TPU v7x, 32 devices: a whole 2x2x4 slice. The times are simulated.
32 devices in a mesh: img: 8 (over z, y), win: 4 (over x, core).
Axes of the slice: x: 2, y: 2, z: 4, core: 2. Of those that a mesh axis runs over, the one named last changes fastest.
Arguments:
- tokens: bfloat16 [64, 4, 49, 768], P('img', 'win'), may hold values from -6 to 6
- crop_count: int32 [8], P('img'), may hold values from 1 to 8, 40 in all
- ln1_gain: float32 [2, 768], replicated, may hold values from 0.1 to 1.9
- ln1_bias: float32 [2, 768], replicated, may hold values from -1.75 to 1.75
- w_qkv: bfloat16 [2, 768, 2304], replicated, may hold values from -0.21875 to 0.21875
- b_query: float32 [2, 768], replicated, may hold values from -1.75 to 1.75
- b_value: float32 [2, 768], replicated, may hold values from -1.75 to 1.75
- bias_table: float32 [2, 169, 24], replicated, may hold values from -4 to 4
- w_out: bfloat16 [2, 768, 768], replicated, may hold values from -0.875 to 0.875
- b_out: float32 [2, 768], replicated, may hold values from -1.75 to 1.75
- ln2_gain: float32 [2, 768], replicated, may hold values from 0.1 to 1.9
- ln2_bias: float32 [2, 768], replicated, may hold values from -1.75 to 1.75
- w_up: bfloat16 [2, 768, 3072], replicated, may hold values from -0.21875 to 0.21875
- b_up: float32 [2, 3072], replicated, may hold values from -1.75 to 1.75
- w_down: bfloat16 [2, 3072, 768], replicated, may hold values from -0.109375 to 0.109375
- b_down: float32 [2, 768], replicated, may hold values from -1.75 to 1.75
- cotangent: bfloat16 [64, 4, 49, 768], P('img', 'win'), may hold values from -6 to 6
Outputs:
- block_out: bfloat16 [64, 4, 49, 768], P('img', 'win')
- grad_tokens: float32 [64, 4, 49, 768], P('img', 'win')
- grad_ln1_gain: float32 [2, 768], P(None, 'img')
- grad_ln1_bias: float32 [2, 768], P(None, 'img')
- grad_w_qkv: float32 [2, 768, 2304], P(None, 'img', 'win')
- grad_b_query: float32 [2, 768], P(None, 'img')
- grad_b_value: float32 [2, 768], P(None, 'img')
- grad_bias_table: float32 [2, 169, 24], replicated
- grad_w_out: float32 [2, 768, 768], P(None, 'img', 'win')
- grad_b_out: float32 [2, 768], P(None, 'img')
- grad_ln2_gain: float32 [2, 768], P(None, 'img')
- grad_ln2_bias: float32 [2, 768], P(None, 'img')
- grad_w_up: float32 [2, 768, 3072], P(None, 'img', 'win')
- grad_b_up: float32 [2, 3072], P(None, 'img')
- grad_w_down: float32 [2, 3072, 768], P(None, 'img', 'win')
- grad_b_down: float32 [2, 768], P(None, 'img')
Inputs may be any that keep to these rules, and one draw needn't show every extreme that they name: Crop slots 0 to crop_count[i] - 1 of image group i hold crops, the others are padding; some group is full (8) in every draw.
All inputs are finite; a program needn't handle non-finite values.
Results may differ from a plain program's by a relative error of at most 0.018.
Values sent between devices are 32-bit elements; how exact they have to be, the bound alone decides.
No kernel may reach another device: no remote copies, remote signals or barrier semaphores. Data moves between devices by JAX's collectives and lax.ppermute only.
A program may use at most 576 MiB of HBM per device.

v0:
```python
import jax
import jax.numpy as jnp
from jax import lax
from jax.sharding import PartitionSpec as P

HEADS = 24
HD = 32


EPSILON = 1e-05


def exact_gelu(values):
    return jax.nn.gelu(values, approximate=False)


def norm_parts(values):
    average = jnp.mean(values, axis=-1, keepdims=True)
    centered = values - average
    inverse = lax.rsqrt(jnp.mean(centered * centered, axis=-1, keepdims=True) + EPSILON)
    return (centered * inverse, inverse)


def norm_back(grad_out, normed, inverse, gain_vec):
    scaled = grad_out * gain_vec
    return inverse * (
        scaled
        - jnp.mean(scaled, axis=-1, keepdims=True)
        - normed * jnp.mean(scaled * normed, axis=-1, keepdims=True)
    )


def outer_sum(left, right):
    left_flat = left.reshape(-1, left.shape[-1])
    right_flat = right.reshape(-1, right.shape[-1])
    return lax.dot_general(
        left_flat, right_flat, (((0,), (0,)), ((), ())), preferred_element_type=jnp.float32
    )


def back_product(grad_low, weight):
    return lax.dot_general(
        grad_low,
        weight,
        (((grad_low.ndim - 1,), (1,)), ((), ())),
        preferred_element_type=jnp.float32,
    )


def column_sum(values):
    return jnp.sum(values.astype(jnp.float32), axis=(0, 1))


def relative_onehot():
    places = jnp.arange(49, dtype=jnp.int32)
    rows_at = places // 7
    cols_at = places % 7
    offsets = (
        (rows_at[:, None] - rows_at[None, :] + 6) * 13 + cols_at[:, None] - cols_at[None, :] + 6
    )
    return (offsets.reshape(-1)[:, None] == jnp.arange(169, dtype=jnp.int32)[None, :]).astype(
        jnp.float32
    )


def region_of(coords):
    return jnp.where(coords < 7, 0, jnp.where(coords < 11, 1, 2))


def roll_forward(field):
    crops, places, width = field.shape
    square = field.reshape(crops, 7, 7, width)
    quadrant = lax.axis_index("win")
    whole = lax.all_gather(square[:, None], "win", axis=1, tiled=True)
    grid = (
        whole.reshape(crops, 2, 2, 7, 7, width)
        .transpose(0, 1, 3, 2, 4, 5)
        .reshape(crops, 14, 14, width)
    )
    grid = jnp.roll(grid, (-3, -3), (1, 2))
    anchor = quadrant * 0
    moved = lax.dynamic_slice(
        grid, (anchor, quadrant // 2 * 7, quadrant % 2 * 7, anchor), (crops, 7, 7, width)
    )
    return moved.reshape(crops, places, width)


def roll_back(field):
    crops, places, width = field.shape
    square = field.reshape(crops, 7, 7, width)
    quadrant = lax.axis_index("win")
    whole = lax.all_gather(square[:, None], "win", axis=1, tiled=True)
    grid = (
        whole.reshape(crops, 2, 2, 7, 7, width)
        .transpose(0, 1, 3, 2, 4, 5)
        .reshape(crops, 14, 14, width)
    )
    grid = jnp.roll(grid, (3, 3), (1, 2))
    anchor = quadrant * 0
    moved = lax.dynamic_slice(
        grid, (anchor, quadrant // 2 * 7, quadrant % 2 * 7, anchor), (crops, 7, 7, width)
    )
    return moved.reshape(crops, places, width)


def block_forward(inputs, params, bias_heads, mask):
    (
        first_gain,
        first_shift,
        joint_weight,
        query_bias,
        value_bias,
        output_weight,
        output_bias,
        second_gain,
        second_shift,
        upper_weight,
        upper_bias,
        lower_weight,
        lower_bias,
    ) = params
    crops, places, width = inputs.shape
    normed_one, inverse_one = norm_parts(inputs)
    hidden_in = (normed_one * first_gain + first_shift).astype(jnp.bfloat16)
    joint = jnp.dot(hidden_in, joint_weight, preferred_element_type=jnp.float32)
    joint = joint + jnp.concatenate([query_bias, jnp.zeros_like(query_bias), value_bias])
    query = (
        (joint[..., :width] * HD ** (-0.5)).astype(jnp.bfloat16).reshape(crops, places, HEADS, HD)
    )
    keys_in = joint[..., width : 2 * width].astype(jnp.bfloat16).reshape(crops, places, HEADS, HD)
    vals_in = joint[..., 2 * width :].astype(jnp.bfloat16).reshape(crops, places, HEADS, HD)
    scores = jnp.einsum("cthe,cuhe->chtu", query, keys_in, preferred_element_type=jnp.float32)
    probs = jax.nn.softmax(scores + bias_heads + mask, axis=-1)
    attended = jnp.einsum(
        "chtu,cuhe->cthe", probs.astype(jnp.bfloat16), vals_in, preferred_element_type=jnp.float32
    )
    attended = attended.astype(jnp.bfloat16).reshape(crops, places, width)
    middle = (
        inputs + jnp.dot(attended, output_weight, preferred_element_type=jnp.float32) + output_bias
    )
    normed_two, inverse_two = norm_parts(middle)
    hidden_two = (normed_two * second_gain + second_shift).astype(jnp.bfloat16)
    upward = jnp.dot(hidden_two, upper_weight, preferred_element_type=jnp.float32) + upper_bias
    active = exact_gelu(upward).astype(jnp.bfloat16)
    result = middle + jnp.dot(active, lower_weight, preferred_element_type=jnp.float32) + lower_bias
    saved = (
        normed_one,
        inverse_one,
        hidden_in,
        query,
        keys_in,
        vals_in,
        probs,
        attended,
        normed_two,
        inverse_two,
        hidden_two,
        upward,
        active,
    )
    return (result, saved)


def block_backward(grad_out, saved, params, onehot):
    (
        first_gain,
        first_shift,
        joint_weight,
        query_bias,
        value_bias,
        output_weight,
        output_bias,
        second_gain,
        second_shift,
        upper_weight,
        upper_bias,
        lower_weight,
        lower_bias,
    ) = params
    (
        normed_one,
        inverse_one,
        hidden_in,
        query,
        keys_in,
        vals_in,
        probs,
        attended,
        normed_two,
        inverse_two,
        hidden_two,
        upward,
        active,
    ) = saved
    crops, places, width = grad_out.shape
    grad_low = grad_out.astype(jnp.bfloat16)
    grad_lower_w = outer_sum(active, grad_low)
    grad_lower_b = column_sum(grad_low)
    grad_act = back_product(grad_low, lower_weight)
    gelu_value, gelu_pull = jax.vjp(exact_gelu, upward)
    (grad_up,) = gelu_pull(grad_act)
    grad_up_low = grad_up.astype(jnp.bfloat16)
    grad_upper_w = outer_sum(hidden_two, grad_up_low)
    grad_upper_b = column_sum(grad_up_low)
    grad_hidden_two = back_product(grad_up_low, upper_weight)
    grad_second_gain = jnp.sum(grad_hidden_two * normed_two, axis=(0, 1))
    grad_second_shift = jnp.sum(grad_hidden_two, axis=(0, 1))
    grad_mid = grad_out + norm_back(grad_hidden_two, normed_two, inverse_two, second_gain)
    grad_mid_low = grad_mid.astype(jnp.bfloat16)
    grad_output_w = outer_sum(attended, grad_mid_low)
    grad_output_b = column_sum(grad_mid_low)
    grad_att = (
        back_product(grad_mid_low, output_weight)
        .astype(jnp.bfloat16)
        .reshape(crops, places, HEADS, HD)
    )
    probs_low = probs.astype(jnp.bfloat16)
    grad_vals = jnp.einsum(
        "chtu,cthe->cuhe", probs_low, grad_att, preferred_element_type=jnp.float32
    )
    grad_probs = jnp.einsum(
        "cthe,cuhe->chtu", grad_att, vals_in, preferred_element_type=jnp.float32
    )
    grad_scores = probs * (grad_probs - jnp.sum(probs * grad_probs, axis=-1, keepdims=True))
    table_heads = jnp.sum(grad_scores, axis=0).transpose(1, 2, 0).reshape(places * places, HEADS)
    grad_table = lax.dot_general(
        onehot,
        table_heads,
        (((0,), (0,)), ((), ())),
        precision=lax.Precision.HIGHEST,
        preferred_element_type=jnp.float32,
    )
    scores_low = grad_scores.astype(jnp.bfloat16)
    grad_query = jnp.einsum(
        "chtu,cuhe->cthe", scores_low, keys_in, preferred_element_type=jnp.float32
    ) * HD ** (-0.5)
    grad_keys = jnp.einsum("chtu,cthe->cuhe", scores_low, query, preferred_element_type=jnp.float32)
    grad_joint = jnp.concatenate(
        [
            grad_query.reshape(crops, places, width),
            grad_keys.reshape(crops, places, width),
            grad_vals.reshape(crops, places, width),
        ],
        axis=-1,
    ).astype(jnp.bfloat16)
    grad_joint_w = outer_sum(hidden_in, grad_joint)
    grad_query_b = column_sum(grad_joint[..., :width])
    grad_value_b = column_sum(grad_joint[..., 2 * width :])
    grad_hidden_in = back_product(grad_joint, joint_weight)
    grad_first_gain = jnp.sum(grad_hidden_in * normed_one, axis=(0, 1))
    grad_first_shift = jnp.sum(grad_hidden_in, axis=(0, 1))
    grad_in = grad_mid + norm_back(grad_hidden_in, normed_one, inverse_one, first_gain)
    grads = (
        grad_first_gain,
        grad_first_shift,
        grad_joint_w,
        grad_query_b,
        grad_value_b,
        grad_output_w,
        grad_output_b,
        grad_second_gain,
        grad_second_shift,
        grad_upper_w,
        grad_upper_b,
        grad_lower_w,
        grad_lower_b,
    )
    return (grad_in, grads, grad_table)


def per_device(
    tokens,
    crop_count,
    ln1_gain,
    ln1_bias,
    w_qkv,
    b_query,
    b_value,
    bias_table,
    w_out,
    b_out,
    ln2_gain,
    ln2_bias,
    w_up,
    b_up,
    w_down,
    b_down,
    cotangent,
):
    crops = tokens.shape[0]
    quadrant = lax.axis_index("win")
    slots = jnp.arange(crops, dtype=jnp.int32)
    valid = (slots < crop_count[0]).astype(jnp.float32)[:, None, None]
    onehot = relative_onehot()

    def params_of(index):
        return (
            ln1_gain[index],
            ln1_bias[index],
            w_qkv[index],
            b_query[index],
            b_value[index],
            w_out[index],
            b_out[index],
            ln2_gain[index],
            ln2_bias[index],
            w_up[index],
            b_up[index],
            w_down[index],
            b_down[index],
        )

    def heads_of(index):
        table_rows = jnp.dot(
            onehot,
            bias_table[index],
            precision=lax.Precision.HIGHEST,
            preferred_element_type=jnp.float32,
        )
        return table_rows.reshape(49, 49, HEADS).transpose(2, 0, 1)

    places = jnp.arange(49, dtype=jnp.int32)
    labels = 3 * region_of(quadrant // 2 * 7 + places // 7) + region_of(
        quadrant % 2 * 7 + places % 7
    )
    mask = jnp.where(labels[:, None] == labels[None, :], 0.0, -100.0).astype(jnp.float32)
    params_one = params_of(0)
    params_two = params_of(1)
    start = tokens[:, 0].astype(jnp.float32)
    first, saved_one = block_forward(start, params_one, heads_of(0), 0.0)
    rolled = roll_forward(first)
    second_rolled, saved_two = block_forward(rolled, params_two, heads_of(1), mask)
    second = roll_back(second_rolled)
    block_out = (second * valid).astype(jnp.bfloat16)[:, None]
    grad_top = roll_forward(cotangent[:, 0].astype(jnp.float32) * valid)
    grad_rolled, grads_two, table_two = block_backward(grad_top, saved_two, params_two, onehot)
    grad_first = roll_back(grad_rolled)
    grad_in, grads_one, table_one = block_backward(grad_first, saved_one, params_one, onehot)
    stacked = [jnp.stack([one_part, two_part]) for one_part, two_part in zip(grads_one, grads_two)]
    (
        first_gain,
        first_shift,
        joint_weight,
        query_bias,
        value_bias,
        output_weight,
        output_bias,
        second_gain,
        second_shift,
        upper_weight,
        upper_bias,
        lower_weight,
        lower_bias,
    ) = stacked
    joint_weight, output_weight, upper_weight, lower_weight = (
        lax.psum_scatter(joint_weight, "win", scatter_dimension=2, tiled=True),
        lax.psum_scatter(output_weight, "win", scatter_dimension=2, tiled=True),
        lax.psum_scatter(upper_weight, "win", scatter_dimension=2, tiled=True),
        lax.psum_scatter(lower_weight, "win", scatter_dimension=2, tiled=True),
    )
    parts = (
        lax.psum_scatter(joint_weight, "img", scatter_dimension=1, tiled=True),
        lax.psum_scatter(output_weight, "img", scatter_dimension=1, tiled=True),
        lax.psum_scatter(upper_weight, "img", scatter_dimension=1, tiled=True),
        lax.psum_scatter(lower_weight, "img", scatter_dimension=1, tiled=True),
        lax.psum_scatter(first_gain, "img", scatter_dimension=1, tiled=True),
        lax.psum_scatter(first_shift, "img", scatter_dimension=1, tiled=True),
        lax.psum_scatter(query_bias, "img", scatter_dimension=1, tiled=True),
        lax.psum_scatter(value_bias, "img", scatter_dimension=1, tiled=True),
        lax.psum_scatter(output_bias, "img", scatter_dimension=1, tiled=True),
        lax.psum_scatter(second_gain, "img", scatter_dimension=1, tiled=True),
        lax.psum_scatter(second_shift, "img", scatter_dimension=1, tiled=True),
        lax.psum_scatter(upper_bias, "img", scatter_dimension=1, tiled=True),
        lax.psum_scatter(lower_bias, "img", scatter_dimension=1, tiled=True),
    )
    (
        joint_weight,
        output_weight,
        upper_weight,
        lower_weight,
        first_gain,
        first_shift,
        query_bias,
        value_bias,
        output_bias,
        second_gain,
        second_shift,
        upper_bias,
        lower_bias,
    ) = parts
    (
        first_gain,
        first_shift,
        query_bias,
        value_bias,
        output_bias,
        second_gain,
        second_shift,
        upper_bias,
        lower_bias,
    ) = lax.psum(
        (
            first_gain,
            first_shift,
            query_bias,
            value_bias,
            output_bias,
            second_gain,
            second_shift,
            upper_bias,
            lower_bias,
        ),
        "win",
    )
    final = (
        first_gain,
        first_shift,
        joint_weight,
        query_bias,
        value_bias,
        output_weight,
        output_bias,
        second_gain,
        second_shift,
        upper_weight,
        upper_bias,
        lower_weight,
        lower_bias,
    )
    table_grads = lax.psum(jnp.stack([table_one, table_two]), ("img", "win"))
    grad_tokens = grad_in[:, None]
    return (
        block_out,
        grad_tokens,
        final[0],
        final[1],
        final[2],
        final[3],
        final[4],
        table_grads,
        final[5],
        final[6],
        final[7],
        final[8],
        final[9],
        final[10],
        final[11],
        final[12],
    )


def solution(mesh):
    return jax.shard_map(
        per_device,
        mesh=mesh,
        in_specs=(
            P("img", "win", None, None),
            P("img"),
            P(),
            P(),
            P(),
            P(),
            P(),
            P(),
            P(),
            P(),
            P(),
            P(),
            P(),
            P(),
            P(),
            P(),
            P("img", "win", None, None),
        ),
        out_specs=(
            P("img", "win", None, None),
            P("img", "win", None, None),
            P(None, "img"),
            P(None, "img"),
            P(None, "img", "win"),
            P(None, "img"),
            P(None, "img"),
            P(),
            P(None, "img", "win"),
            P(None, "img"),
            P(None, "img"),
            P(None, "img"),
            P(None, "img", "win"),
            P(None, "img"),
            P(None, "img", "win"),
            P(None, "img"),
        ),
        check_vma=False,
    )
```

profile of v0, /device:TPU:0, one launch (start us, length us, event | category | flops | bytes accessed | tf_op | source)
XLA Modules:
  0.0 2184.7 jit_solution(11271217277391378210)
XLA Ops:
  25.5 6.3 fusion.185
  39.9 6.6 fusion.104
  46.5 13.7 multiply_convert_fusion.1
  73.3 31.7 %all-gather.5.cloned.1.call-done = f32[8,4,7,7,768]{4,0,3,2,1:T(8,128)} async-done(((f32[8,1,7,7,768]{4,0,3,2,1:T(8,128)}), f32[8,4,7,7,768]{4,0,3,2,1:T(8,128)}) %all-gather.5.cloned.1.call-update) | async-done | bytes 4816912 | tf_op jit(solution)/shard_map/all_gather | solution.py:74
  125.3 7.0 fusion.188
  137.9 6.4 fusion.105
  144.4 13.7 multiply_convert_fusion
  158.1 6.9 convert_reduce_fusion
  165.0 6.7 multiply_reduce_fusion.2
  176.7 5.9 convolution_convert_fusion.2
  201.7 5.5 multiply_reduce_fusion.4
  235.5 12.9 all-gather.11.cloned.1.call-done
  254.7 6.9 convert_reduce_fusion.1
  261.6 6.1 multiply_reduce_fusion.3
  275.5 5.9 convolution_convert_fusion
  297.4 8.2 copy.477
  312.6 6.5 convolution_bitcast_fusion.5
  319.2 11.0 pad_maximum_fusion.2
  330.2 21.6 copy.471
  360.0 6.8 pad_maximum_fusion.1
  366.8 28.5 %copy.480 = f32[2,3072,768]{1,0,2:T(2,128)} copy(f32[2,3072,768]{2,1,0:T(8,128)} %pad_maximum_fusion.1) | data formatting | bytes 37748736 | tf_op jit(solution)/shard_map/stack | solution.py:339
  403.6 6.9 pad_maximum_fusion
  411.2 5.8 add_add_fusion.4
  425.6 6.2 fusion.90
  441.1 233.1 %all-reduce.14.cloned.1.call-done = (f32[2,768,2304]{1,0,2:T(2,128)}, f32[2,768,768]{1,0,2:T(2,128)}) async-done(((f32[2,768,2304]{1,0,2:T(2,128)}, f32[2,768,768]{1,0,2:T(2,128)}), (f32[2,768,2304]{1,0,2:T(2,128)}, f32[2,768,768]{1,0,2:T(2,128)})) %all-reduce.14.cloned.1.call-update) | async-done | bytes 18874384
  675.9 36.6 %copy.509 = f32[2,768,192]{0,2,1:T(8,128)} copy(f32[2,768,192]{1,0,2:T(2,128)S(1)} %constant_dynamic-slice_fusion.1) | data formatting | bytes 2359296
  712.5 52.9 %reshape.540 = f32[768,384]{1,0:T(8,128)} reshape(f32[768,192,2]{2,1,0:T(8,128)} %bitcast.101) | data formatting | bytes 2359296
  769.4 5.5 copy.472
  775.2 223.6 %all-reduce.12.cloned.1.call-done = f32[2,3072,768]{1,0,2:T(2,128)} async-done(((f32[2,3072,768]{1,0,2:T(2,128)}), f32[2,3072,768]{1,0,2:T(2,128)}) %all-reduce.12.cloned.1.call-update) | async-done | bytes 18874384
  998.8 6.1 constant_dynamic-slice_fusion
  1004.9 144.2 %copy.519 = f32[2,3072,192]{0,2,1:T(8,128)} copy(f32[2,3072,192]{1,0,2:T(2,128)} %constant_dynamic-slice_fusion) | data formatting | bytes 9437184
  1149.1 202.6 %reshape.550 = f32[3072,384]{1,0:T(8,128)} reshape(f32[3072,192,2]{2,1,0:T(8,128)} %bitcast.112) | data formatting | bytes 9437184
  1371.4 40.9 %psum.74 = f32[2,169,24]{1,2,0:T(8,128)} all-reduce(f32[2,169,24]{1,2,0:T(8,128)S(1)} %pad_maximum_fusion.10), channel_id=1, replica_groups=mesh['img'=8,'win'=4] {'img','win'}, use_global_device_ids=true, to_apply=%region_42.43 | all-reduce | flops 8112 | bytes 64896 | tf_op jit(solution)/shard_map/psum | solution.py:430
  1417.2 21.1 reduce-scatter.50.cloned.1.call-done
  1439.2 63.0 %reduce-scatter.46.cloned.1.call-done = f32[96,2]{1,0:T(8,128)} async-done(((f32[768,2]{1,0:T(8,128)}), f32[96,2]{1,0:T(8,128)}) %reduce-scatter.46.cloned.1.call-update) | async-done | bytes 784
  1503.0 63.1 %reduce-scatter.44.cloned.1.call-done = f32[96,2]{1,0:T(8,128)} async-done(((f32[768,2]{1,0:T(8,128)}), f32[96,2]{1,0:T(8,128)}) %reduce-scatter.44.cloned.1.call-update) | async-done | bytes 784
  1567.0 63.6 %reduce-scatter.42.cloned.1.call-done = f32[96,2]{1,0:T(8,128)} async-done(((f32[768,2]{1,0:T(8,128)}), f32[96,2]{1,0:T(8,128)}) %reduce-scatter.42.cloned.1.call-update) | async-done | bytes 784
  1631.4 63.5 %reduce-scatter.40.cloned.1.call-done = f32[96,2]{1,0:T(8,128)} async-done(((f32[768,2]{1,0:T(8,128)}), f32[96,2]{1,0:T(8,128)}) %reduce-scatter.40.cloned.1.call-update) | async-done | bytes 784
  1695.8 66.7 %reduce-scatter.56.cloned.1.call-done = f32[384,2]{1,0:T(8,128)} async-done(((f32[3072,2]{1,0:T(8,128)}), f32[384,2]{1,0:T(8,128)}) %reduce-scatter.56.cloned.1.call-update) | async-done | bytes 3088
  1763.5 10.9 all-reduce.4
  1774.5 54.3 %reduce-scatter.48.cloned.1.call-done = f32[96,384]{1,0:T(8,128)} async-done(((f32[768,384]{1,0:T(8,128)}), f32[96,384]{1,0:T(8,128)}) %reduce-scatter.48.cloned.1.call-update) | async-done | bytes 147472
  1828.8 11.7 reshape.541
  1840.5 6.9 copy.483
  1847.4 133.3 %all-reduce.10.cloned.1.call-done = f32[2,768,576]{2,0,1:T(2,128)} async-done(((f32[2,768,576]{2,0,1:T(2,128)}), f32[2,768,576]{2,0,1:T(2,128)}) %all-reduce.10.cloned.1.call-update) | async-done | bytes 3538960
  1982.6 96.0 %reduce-scatter.58.cloned.1.call-done = f32[384,384]{1,0:T(8,128)} async-done(((f32[3072,384]{1,0:T(8,128)}), f32[384,384]{1,0:T(8,128)}) %reduce-scatter.58.cloned.1.call-update) | async-done | bytes 589840
  2078.6 40.1 %reshape.551 = f32[384,192,2]{2,1,0:T(8,128)} reshape(f32[384,384]{1,0:T(8,128)} %reduce-scatter.58.cloned.1.call-done) | data formatting | bytes 1179648
  2118.7 21.6 copy.484
  2140.3 37.4 %reduce-scatter.38.cloned.1.call-done = f32[2,96,768]{2,1,0:T(8,128)} async-done(((f32[2,768,768]{2,1,0:T(8,128)}), f32[2,96,768]{2,1,0:T(8,128)}) %reduce-scatter.38.cloned.1.call-update) | async-done | bytes 589840 | tf_op jit(solution)/shard_map/reduce_scatter | solution.py:364
  (487 shorter events, 222.9 us)
Async XLA Ops:
  7.2 60.9 %all-gather.9.cloned.1.call-start = ((), (), s32[]{:S(2)}) async-start(), calls=%async_computation.15 | async-start | bytes 6021120 | tf_op jit(solution)/shard_map/all_gather | solution.py:74
  8.0 6.2 copy-start.89
  8.0 6.2 copy-start.90
  10.3 94.7 %all-gather.5.cloned.1.call-start = ((), (), s32[]{:S(2)}) async-start(), calls=%async_computation.13 | async-start | bytes 6021120 | tf_op jit(solution)/shard_map/all_gather | solution.py:74
  11.0 53.2 %copy-start.57 = (s32[49,49]{1,0:T(8,128)}, s32[49,49]{1,0:T(8,128)S(1)}, u32[]{:S(2)}) copy-start(s32[49,49]{1,0:T(8,128)S(1)} %subtract_add_fusion) | copy-start | bytes 28816
  20.9 10.8 copy-start.18
  31.8 6.1 copy-start.38
  37.9 362.8 %copy-start.65 = (f32[768]{0:T(1024)}, f32[768]{0:T(1024)S(1)}, u32[]{:S(2)}) copy-start(f32[768]{0:T(1024)S(1)} %get-tuple-element.235) | copy-start | bytes 9220
  38.8 21.4 copy-start.4
  38.8 361.9 %copy-start.62 = (f32[8,49]{1,0:T(8,128)}, f32[8,49]{1,0:T(8,128)S(1)}, u32[]{:S(2)}) copy-start(f32[8,49]{1,0:T(8,128)S(1)} %broadcast_multiply_fusion.10) | copy-start | bytes 4708
  39.1 7.4 copy-start.69
  39.9 20.4 slice-start.8
  39.9 20.4 slice-start.9
  46.5 13.7 copy-start.24
  46.5 13.7 slice-start.10
  64.1 184.3 %all-gather.11.cloned.1.call-start = ((), (), s32[]{:S(2)}) async-start(), calls=%async_computation.16 | async-start | bytes 6021120 | tf_op jit(solution)/shard_map/all_gather | solution.py:92
  119.8 12.5 copy-start.21
  137.9 33.9 %copy-start.76 = (f32[8,49]{1,0:T(8,128)}, f32[8,49]{1,0:T(8,128)S(1)}, u32[]{:S(2)}) copy-start(f32[8,49]{1,0:T(8,128)S(1)} %add_rsqrt_fusion.1) | copy-start | bytes 4708
  144.4 13.7 copy-start.45
  165.0 6.7 copy-start.113
  165.0 6.8 copy-start.13
  176.7 10.3 slice-start.2
  196.3 10.9 copy-start.33
  210.3 464.0 %all-reduce.14.cloned.1.call-start = ((), (), s32[]{:S(2)}) async-start(), calls=%async_computation.32 | async-start | bytes 37748736
  252.8 14.9 copy-start.10
  254.7 6.9 copy-start.5
  254.7 6.9 copy-start.70
  261.6 6.1 copy-start.114
  275.4 10.3 slice-start
  351.8 647.0 %all-reduce.12.cloned.1.call-start = ((), (), s32[]{:S(2)}) async-start(), calls=%async_computation.31 | async-start | bytes 37748736
  395.3 956.5 %reduce-scatter.36.cloned.1.call-start = ((), (), s32[]{:S(2)}) async-start(), calls=%async_computation.17 | async-start | bytes 23592960 | tf_op jit(solution)/shard_map/reduce_scatter | solution.py:358
  410.5 944.8 %all-gather.7.cloned.1.call-start = ((), (), s32[]{:S(2)}) async-start(), calls=%async_computation.14 | async-start | bytes 6021120 | tf_op jit(solution)/shard_map/all_gather | solution.py:92
  418.5 996.1 %reduce-scatter.60.cloned.1.call-start = ((), (), s32[]{:S(2)}) async-start(), calls=%async_computation.29 | async-start | bytes 442368
  431.9 983.6 %reduce-scatter.54.cloned.1.call-start = ((), (), s32[]{:S(2)}) async-start(), calls=%async_computation.26 | async-start | bytes 442368
  432.0 7.3 copy-start.87
  432.0 7.3 copy-start.88
  433.0 983.4 %reduce-scatter.52.cloned.1.call-start = ((), (), s32[]{:S(2)}) async-start(), calls=%async_computation.25 | async-start | bytes 442368
  434.0 1004.3 %reduce-scatter.50.cloned.1.call-start = ((), (), s32[]{:S(2)}) async-start(), calls=%async_computation.24 | async-start | bytes 442368
  435.1 1067.1 %reduce-scatter.46.cloned.1.call-start = ((), (), s32[]{:S(2)}) async-start(), calls=%async_computation.22 | async-start | bytes 442368
  436.1 1130.0 %reduce-scatter.44.cloned.1.call-start = ((), (), s32[]{:S(2)}) async-start(), calls=%async_computation.21 | async-start | bytes 442368
  437.2 1193.4 %reduce-scatter.42.cloned.1.call-start = ((), (), s32[]{:S(2)}) async-start(), calls=%async_computation.20 | async-start | bytes 442368
  438.2 1256.7 %reduce-scatter.40.cloned.1.call-start = ((), (), s32[]{:S(2)}) async-start(), calls=%async_computation.19 | async-start | bytes 442368
  439.3 1323.3 %reduce-scatter.56.cloned.1.call-start = ((), (), s32[]{:S(2)}) async-start(), calls=%async_computation.27 | async-start | bytes 1769472
  441.1 1387.7 %reduce-scatter.48.cloned.1.call-start = ((), (), s32[]{:S(2)}) async-start(), calls=%async_computation.23 | async-start | bytes 1327104
  765.4 1215.2 %all-reduce.10.cloned.1.call-start = ((), (), s32[]{:S(2)}) async-start(), calls=%async_computation.30 | async-start | bytes 7864320
  774.9 1303.7 %reduce-scatter.58.cloned.1.call-start = ((), (), s32[]{:S(2)}) async-start(), calls=%async_computation.28 | async-start | bytes 5308416
  1351.7 825.9 %reduce-scatter.38.cloned.1.call-start = ((), (), s32[]{:S(2)}) async-start(), calls=%async_computation.18 | async-start | bytes 5308416 | tf_op jit(solution)/shard_map/reduce_scatter | solution.py:364
  1368.2 44.1 %copy-start.28 = (f32[8,3,14,768]{3,0,2,1:T(8,128)S(1)}, f32[8,3,14,768]{3,0,2,1:T(8,128)}, u32[]{:S(2)}) copy-start(f32[8,3,14,768]{3,0,2,1:T(8,128)} %slice.226) | copy-start | bytes 3096580
  (99 other events, 370.1 us)
Sparse Core Ops, SparseCore 0:
  10.4 40.7 all-gather.8
  64.3 40.6 all-gather.4
  210.4 38.0 all-gather.10
  351.9 322.3 all-reduce.13
  676.7 321.9 all-reduce.11
  1001.2 139.6 reduce-scatter.35
  1143.1 38.0 all-gather.6
  1184.8 61.3 reduce-scatter.59
  1249.8 60.3 reduce-scatter.53
  1313.7 60.3 reduce-scatter.51
  1377.7 60.5 reduce-scatter.49
  1441.8 60.3 reduce-scatter.45
  1505.8 60.3 reduce-scatter.43
  1570.2 60.3 reduce-scatter.41
  1634.6 60.3 reduce-scatter.39
  1698.6 63.8 reduce-scatter.55
  1765.8 62.9 reduce-scatter.47
  1832.2 148.3 all-reduce.9
  1984.3 94.2 reduce-scatter.57
  2082.7 94.9 reduce-scatter.37
where the time goes:
time: 2200 us; the launch traced here: 2180 us
  waiting for transfers between devices  1160 us (53%)
  local copies, waits for them, and re-layouts  703 us (32%)
  matrix products  162 us (7%)
  other arithmetic  82.6 us (4%)
  blocking collectives  51.8 us (2%)
    unnamed x34, waiting for transfers between devices  1080 us
    unnamed x288, local copies, waits for them, and re-layouts  557 us
    another operation x19, local copies, waits for them, and re-layouts, per_device(): jnp.stack([one_part, two_part])  58.3 us
  transfers between devices with their start and end apart: 20, of which 14 were waited for; matrix products, arithmetic and copies ran while one was open for 34% of the time, Pallas kernels for 0%

commit v1 on v0

v1 whole, which is shorter than its diff:
```python
import functools

import jax
import jax.numpy as jnp
from jax import lax
from jax.experimental import pallas as pl
from jax.experimental.pallas import tpu as pltpu
from jax.sharding import PartitionSpec as P

HEADS = 24
HD = 32
SIDE = 7
T = SIDE * SIDE
TP = 56
D = 768
FF = 3072
C = 8
ROWS = T * C
PAD_ROWS = TP * C
LANE = 128
NG = D // LANE
PER = LANE // HD
GT = PER * TP
EPSILON = 1e-05
SCALE = HD ** (-0.5)
NEG = -1e30
QCH = 384
FCH = 512
N_Q = 3 * D // QCH
N_F = FF // FCH
VMEM_LIMIT = 58 << 20
F32 = jnp.float32
BF16 = jnp.bfloat16

TAIL_K = 0.3
TAIL = (
    0.11963200491345692,
    0.12071217642148169,
    0.10017566554041868,
    0.12769280877164998,
    -0.052036176065482394,
    0.20455934198696718,
    -0.15616004916725648,
    0.035424145900813254,
)
INV_SQRT_2PI = 0.3989422804014327

LOW, HIGH = range(0, 3), range(3, 7)


def cells(rows, cols):
    return [SIDE * i + j for i in rows for j in cols]


FWD_SEND = (cells(LOW, HIGH), cells(HIGH, LOW), cells(LOW, LOW))
FWD_KEEP = cells(HIGH, HIGH)
FWD_PUT = (cells(range(4, 7), range(0, 4)), cells(range(0, 4), range(4, 7)), cells(range(4, 7), range(4, 7)))
FWD_STAY = cells(range(0, 4), range(0, 4))
BACK_SEND, BACK_KEEP, BACK_PUT, BACK_STAY = FWD_PUT, FWD_STAY, FWD_SEND, FWD_KEEP
N_SEND = (12, 12, 9)


def nt(left, right):
    return lax.dot_general(left, right, (((1,), (1,)), ((), ())), preferred_element_type=F32)


def tn(left, right):
    return lax.dot_general(left, right, (((0,), (0,)), ((), ())), preferred_element_type=F32)


def nn(left, right):
    return jnp.dot(left, right, preferred_element_type=F32)


def norm_parts(values):
    average = jnp.mean(values, axis=-1, keepdims=True)
    centered = values - average
    inverse = lax.rsqrt(jnp.mean(centered * centered, axis=-1, keepdims=True) + EPSILON)
    return centered * inverse, inverse


def norm_back(grad_out, normed, inverse, gain):
    scaled = grad_out * gain
    return inverse * (
        scaled
        - jnp.mean(scaled, axis=-1, keepdims=True)
        - normed * jnp.mean(scaled * normed, axis=-1, keepdims=True)
    )


def gelu_parts(a):
    bell = jnp.exp(-0.5 * a * a)
    size = jnp.abs(a)
    t = 1.0 / (1.0 + TAIL_K * size)
    poly = jnp.full_like(t, TAIL[-1])
    for coef in TAIL[-2::-1]:
        poly = poly * t + coef
    tail = bell * (t * poly)
    phi = jnp.where(a < 0, tail, 1.0 - tail)
    return a * phi, phi + a * (INV_SQRT_2PI * bell)


def head_masks():
    lanes = lax.broadcasted_iota(jnp.int32, (TP, LANE), 1)
    return [(lanes >= HD * h) & (lanes < HD * (h + 1)) for h in range(PER)]


def spread(values, masks):
    return jnp.concatenate([jnp.where(m, values, 0.0) for m in masks], axis=0).astype(BF16)


def gather_heads(stacked, masks):
    out = stacked[(PER - 1) * TP :]
    for h in range(PER - 2, -1, -1):
        out = jnp.where(masks[h], stacked[h * TP : (h + 1) * TP], out)
    return out


def soft(scores):
    e = jnp.exp(scores - jnp.max(scores, axis=0, keepdims=True))
    return e * (1.0 / jnp.sum(e, axis=0, keepdims=True))


def colsum(values):
    return jnp.sum(values, axis=0, keepdims=True)


def crop_rows(c):
    return pl.ds(c, T, stride=C)


def pad_rows(c):
    return pl.ds(c, TP, stride=C)


def lanes_at(n, width):
    return pl.ds(pl.multiple_of(n * width, width), width)


def put_pieces(dest, own, pieces, stay, keep, put):
    for to, src in zip(stay, keep):
        dest[pl.ds(C * to, C), :] = own[src]
    for piece, places in zip(pieces, put):
        for k, to in enumerate(places):
            dest[pl.ds(C * to, C), :] = piece[k]


def take_pieces(values_ref, outs, places):
    for out, tokens in zip(outs, places):
        for k, t in enumerate(tokens):
            out[k] = values_ref[pl.ds(C * t, C), :]


def fwd_body(b, *refs):
    if b == 0:
        (tok, *rest) = refs
    else:
        (own, rx, rc, rd, *rest) = refs
    (
        bias, ln1g, ln1b, bq, bv, bout, ln2g, ln2b, bup, bdown,
        wqkv_h, wout_h, wup_h, wdown_h,
        z_o, h_o, qkvc_o, o_o, y_o, h2_o, g_o, gp_o, zn_o, sx_o, sc_o, sd_o,
        wqkv, wout, wup, wdown, qkv_s, o_s, bqkv, acc, sem_q, sem_o, sem_u, sem_d,
    ) = rest

    def cp_q(n):
        return pltpu.make_async_copy(
            wqkv_h.at[b, :, lanes_at(n, QCH)], wqkv.at[:, lanes_at(n, QCH)], sem_q.at[n]
        )

    def cp_u(n):
        return pltpu.make_async_copy(
            wup_h.at[b, :, lanes_at(n, FCH)], wup.at[:, lanes_at(n, FCH)], sem_u.at[n]
        )

    def cp_d(n):
        return pltpu.make_async_copy(
            wdown_h.at[b, lanes_at(n, FCH), :], wdown.at[lanes_at(n, FCH), :], sem_d.at[n]
        )

    cp_o = pltpu.make_async_copy(wout_h.at[b], wout, sem_o)
    for n in range(N_Q):
        cp_q(n).start()
    cp_o.start()
    for n in range(N_F):
        cp_u(n).start()
        cp_d(n).start()

    if b == 0:
        for c in range(C):
            v = tok[c].astype(F32)
            for g in range(NG):
                o_s[g, crop_rows(c), :] = v[:, LANE * g : LANE * (g + 1)]
        for g in range(NG):
            z_o[:, LANE * g : LANE * (g + 1)] = o_s[g, 0:ROWS, :]
    else:
        put_pieces(z_o, own, (rx, rc, rd), FWD_STAY, FWD_KEEP, FWD_PUT)
    normed, _ = norm_parts(z_o[...])
    h_o[...] = (normed * ln1g[b : b + 1, :] + ln1b[b : b + 1, :]).astype(BF16)
    bqkv[:, 0:D] = bq[b : b + 1, :]
    bqkv[:, D : 2 * D] = jnp.zeros((1, D), F32)
    bqkv[:, 2 * D :] = bv[b : b + 1, :]
    qkv_s[:, ROWS:, :] = jnp.zeros((3 * NG, PAD_ROWS - ROWS, LANE), F32)

    def qkv_step(n, _):
        cp_q(n).wait()
        joint = nn(h_o[...], wqkv[:, lanes_at(n, QCH)]) + bqkv[:, lanes_at(n, QCH)]
        joint = joint * jnp.where(n < D // QCH, SCALE, 1.0)
        joint = joint.astype(BF16).astype(F32)
        for k in range(QCH // LANE):
            qkv_s[n * (QCH // LANE) + k, 0:ROWS, :] = joint[:, LANE * k : LANE * (k + 1)]
        return 0

    lax.fori_loop(0, N_Q, qkv_step, 0)
    masks = head_masks()

    def attend(c, _):
        for g in range(NG):
            q = qkv_s[g, pad_rows(c), :]
            k = qkv_s[NG + g, pad_rows(c), :].astype(BF16)
            v = qkv_s[2 * NG + g, pad_rows(c), :].astype(BF16)
            qkvc_o[c, g] = q.astype(BF16)
            qkvc_o[c, NG + g] = k
            qkvc_o[c, 2 * NG + g] = v
            probs = soft(nt(k, spread(q, masks)) + bias[g])
            o_s[g, pad_rows(c), :] = gather_heads(tn(probs.astype(BF16), v), masks)
        return 0

    lax.fori_loop(0, C, attend, 0)
    for g in range(NG):
        o_o[:, LANE * g : LANE * (g + 1)] = o_s[g, 0:ROWS, :].astype(BF16)
    cp_o.wait()
    y = z_o[...] + (nn(o_o[...], wout[...]) + bout[b : b + 1, :])
    y_o[...] = y
    normed, _ = norm_parts(y)
    h2_o[...] = (normed * ln2g[b : b + 1, :] + ln2b[b : b + 1, :]).astype(BF16)
    acc[...] = jnp.zeros_like(acc)

    def mlp_step(n, _):
        cp_u(n).wait()
        a = nn(h2_o[...], wup[:, lanes_at(n, FCH)]) + bup[b : b + 1, lanes_at(n, FCH)]
        act, slope = gelu_parts(a)
        act = act.astype(BF16)
        g_o[:, lanes_at(n, FCH)] = act
        gp_o[:, lanes_at(n, FCH)] = slope.astype(BF16)
        cp_d(n).wait()
        acc[...] += nn(act, wdown[lanes_at(n, FCH), :])
        return 0

    lax.fori_loop(0, N_F, mlp_step, 0)
    acc[...] = y_o[...] + (acc[...] + bdown[b : b + 1, :])
    zn_o[...] = acc[...].reshape(T, C, D)
    take_pieces(acc, (sx_o, sc_o, sd_o), FWD_SEND if b == 0 else BACK_SEND)


ANY = pl.BlockSpec(memory_space=pl.ANY)
VM = pl.BlockSpec(memory_space=pltpu.VMEM)
SM = pl.BlockSpec(memory_space=pltpu.SMEM)


def params_of():
    return pltpu.CompilerParams(vmem_limit_bytes=VMEM_LIMIT)


def cost(flops, nbytes):
    return pl.CostEstimate(flops=int(flops), bytes_accessed=int(nbytes), transcendentals=0)


def shape(dims, dtype):
    return jax.ShapeDtypeStruct(dims, dtype)


PIECES = [shape((T, C, D), F32)] + [shape((n, C, D), F32) for n in N_SEND]


def block_fwd(b, sources, bias, p):
    outs = [
        shape((ROWS, D), F32),
        shape((ROWS, D), BF16),
        shape((C, 3 * NG, TP, LANE), BF16),
        shape((ROWS, D), BF16),
        shape((ROWS, D), F32),
        shape((ROWS, D), BF16),
        shape((ROWS, FF), BF16),
        shape((ROWS, FF), BF16),
    ] + PIECES
    small = (bias, p["ln1_gain"], p["ln1_bias"], p["b_query"], p["b_value"], p["b_out"],
             p["ln2_gain"], p["ln2_bias"], p["b_up"], p["b_down"])
    big = (p["w_qkv"], p["w_out"], p["w_up"], p["w_down"])
    return pl.pallas_call(
        functools.partial(fwd_body, b),
        in_specs=[VM] * (len(sources) + len(small)) + [ANY] * 4,
        out_specs=[VM] * len(outs),
        out_shape=outs,
        scratch_shapes=[
            pltpu.VMEM((D, 3 * D), BF16),
            pltpu.VMEM((D, D), BF16),
            pltpu.VMEM((D, FF), BF16),
            pltpu.VMEM((FF, D), BF16),
            pltpu.VMEM((3 * NG, PAD_ROWS, LANE), F32),
            pltpu.VMEM((NG, PAD_ROWS, LANE), F32),
            pltpu.VMEM((1, 3 * D), F32),
            pltpu.VMEM((ROWS, D), F32),
            pltpu.SemaphoreType.DMA((N_Q,)),
            pltpu.SemaphoreType.DMA,
            pltpu.SemaphoreType.DMA((N_F,)),
            pltpu.SemaphoreType.DMA((N_F,)),
        ],
        compiler_params=params_of(),
        cost_estimate=cost(2 * ROWS * 12 * D * D, 30e6),
        name=f"forward_{b}",
    )(*sources, *small, *big)


def cot_body(count, ct, own_o, sx_o, sc_o, sd_o, s, full):
    for c in range(C):
        keep = jnp.where(c < count[0], 1.0, 0.0).astype(F32)
        v = ct[c].astype(F32) * keep
        for g in range(NG):
            s[g, crop_rows(c), :] = v[:, LANE * g : LANE * (g + 1)]
    for g in range(NG):
        full[:, LANE * g : LANE * (g + 1)] = s[g]
    own_o[...] = full[...].reshape(T, C, D)
    take_pieces(full, (sx_o, sc_o, sd_o), FWD_SEND)


def cotangent_pieces(count, ct):
    return pl.pallas_call(
        cot_body,
        in_specs=[SM, VM],
        out_specs=[VM] * 4,
        out_shape=PIECES,
        scratch_shapes=[pltpu.VMEM((NG, ROWS, LANE), F32), pltpu.VMEM((ROWS, D), F32)],
        compiler_params=params_of(),
        cost_estimate=cost(0, 6e6),
        name="cotangent_pieces",
    )(count, ct)


def join_body(forward, own, rx, rc, rd, dz_o, dd_o, db_o):
    ways = (FWD_STAY, FWD_KEEP, FWD_PUT) if forward else (BACK_STAY, BACK_KEEP, BACK_PUT)
    put_pieces(dz_o, own, (rx, rc, rd), *ways)
    dd = dz_o[...].astype(BF16)
    db_o[...] = colsum(dd.astype(F32))
    w = D // 4
    for c in range(2):
        dd_o[c] = jnp.concatenate(
            [dd[:, w * c : w * (c + 1)], dd[:, w * (2 + c) : w * (3 + c)]], axis=1
        )


def join_grad(forward, own, received):
    return pl.pallas_call(
        functools.partial(join_body, forward),
        in_specs=[VM] * 4,
        out_specs=[VM] * 3,
        out_shape=[shape((ROWS, D), F32), shape((2, ROWS, D // 2), BF16), shape((1, D), F32)],
        compiler_params=params_of(),
        cost_estimate=cost(0, 5e6),
        name="join_grad",
    )(own, *received)


def block_out_body(count, own, rx, rc, rd, out, full, s):
    put_pieces(full, own, (rx, rc, rd), BACK_STAY, BACK_KEEP, BACK_PUT)
    for g in range(NG):
        s[g] = full[:, LANE * g : LANE * (g + 1)]
    for c in range(C):
        keep = jnp.where(c < count[0], 1.0, 0.0).astype(F32)
        for g in range(NG):
            out[c, :, LANE * g : LANE * (g + 1)] = (s[g, crop_rows(c), :] * keep).astype(BF16)


def block_output(count, own, received):
    return pl.pallas_call(
        block_out_body,
        in_specs=[SM] + [VM] * 4,
        out_specs=VM,
        out_shape=shape((C, T, D), BF16),
        scratch_shapes=[pltpu.VMEM((ROWS, D), F32), pltpu.VMEM((NG, ROWS, LANE), F32)],
        compiler_params=params_of(),
        cost_estimate=cost(0, 4e6),
        name="block_output",
    )(count, own, *received)


def mlp_back_body(b, dz, y, ln2g, gp_h, wdown_h, wup_h, da_o, dy_o, dyr_o, sv_o, dbup_o,
                  gp, wdown, wup, acc, dd, sem_g, sem_d, sem_u):
    def cp_g(n):
        return pltpu.make_async_copy(
            gp_h.at[:, lanes_at(n, FCH)], gp.at[:, lanes_at(n, FCH)], sem_g.at[n]
        )

    def cp_u(n):
        return pltpu.make_async_copy(
            wup_h.at[b, :, lanes_at(n, FCH)], wup.at[:, lanes_at(n, FCH)], sem_u.at[n]
        )

    def cp_d(n):
        return pltpu.make_async_copy(
            wdown_h.at[b, lanes_at(n, FCH), :], wdown.at[lanes_at(n, FCH), :], sem_d.at[n]
        )

    for n in range(N_F):
        cp_d(n).start()
        cp_g(n).start()
        cp_u(n).start()
    dd[...] = dz[...].astype(BF16)
    acc[...] = jnp.zeros_like(acc)

    def step(n, _):
        cp_d(n).wait()
        grad_act = nt(dd[...], wdown[lanes_at(n, FCH), :])
        cp_g(n).wait()
        da = (grad_act * gp[:, lanes_at(n, FCH)].astype(F32)).astype(BF16)
        da_o[:, lanes_at(n, FCH)] = da
        dbup_o[:, lanes_at(n, FCH)] = colsum(da.astype(F32))
        cp_u(n).wait()
        acc[...] += nt(da, wup[:, lanes_at(n, FCH)])
        return 0

    lax.fori_loop(0, N_F, step, 0)
    dh2 = acc[...]
    normed, inverse = norm_parts(y[...])
    sv_o[0:1, :] = colsum(dh2 * normed)
    sv_o[1:2, :] = colsum(dh2)
    dy = dz[...] + norm_back(dh2, normed, inverse, ln2g[b : b + 1, :])
    dy_o[...] = dy
    low = dy.astype(BF16)
    dyr_o[...] = low
    sv_o[2:3, :] = colsum(low.astype(F32))


def mlp_back(b, dz, y, gp, p):
    return pl.pallas_call(
        functools.partial(mlp_back_body, b),
        in_specs=[VM] * 3 + [ANY] * 3,
        out_specs=[VM] * 5,
        out_shape=[
            shape((ROWS, FF), BF16),
            shape((ROWS, D), F32),
            shape((ROWS, D), BF16),
            shape((3, D), F32),
            shape((1, FF), F32),
        ],
        scratch_shapes=[
            pltpu.VMEM((ROWS, FF), BF16),
            pltpu.VMEM((FF, D), BF16),
            pltpu.VMEM((D, FF), BF16),
            pltpu.VMEM((ROWS, D), F32),
            pltpu.VMEM((ROWS, D), BF16),
            pltpu.SemaphoreType.DMA((N_F,)),
            pltpu.SemaphoreType.DMA((N_F,)),
            pltpu.SemaphoreType.DMA((N_F,)),
        ],
        compiler_params=params_of(),
        cost_estimate=cost(2 * ROWS * 8 * D * D, 20e6),
        name=f"mlp_back_{b}",
    )(dz, y, p["ln2_gain"], gp, p["w_down"], p["w_up"])


def attn_back_body(b, dyr, qkvc, bias, dy, z, ln1g, wout_h, wqkv_h, *refs):
    if b == 0:
        (r3_o, sv_o, ds_o, out, wout, wqkv, do_s, dqkv_s, dq, acc, sem_o, sem_q) = refs
    else:
        (r3_o, sv_o, ds_o, own_o, sx_o, sc_o, sd_o,
         wout, wqkv, do_s, dqkv_s, dq, acc, sem_o, sem_q) = refs
    cp_o = pltpu.make_async_copy(wout_h.at[b], wout, sem_o)
    cp_o.start()

    def cp_q(n):
        return pltpu.make_async_copy(
            wqkv_h.at[b, :, lanes_at(n, QCH)], wqkv.at[:, lanes_at(n, QCH)], sem_q.at[n]
        )

    for n in range(N_Q):
        cp_q(n).start()
    do_s[:, ROWS:, :] = jnp.zeros((NG, PAD_ROWS - ROWS, LANE), F32)
    ds_o[...] = jnp.zeros_like(ds_o)
    cp_o.wait()
    do = nt(dyr[...], wout[...]).astype(BF16).astype(F32)
    for g in range(NG):
        do_s[g, 0:ROWS, :] = do[:, LANE * g : LANE * (g + 1)]
    masks = head_masks()

    def attend(c, _):
        for g in range(NG):
            q = qkvc[c, g]
            k = qkvc[c, NG + g]
            v = qkvc[c, 2 * NG + g]
            q_wide = spread(q.astype(F32), masks)
            do_wide = spread(do_s[g, pad_rows(c), :], masks)
            probs = soft(nt(k, q_wide) + bias[g])
            weighted = probs * nt(v, do_wide)
            ds = weighted - probs * jnp.sum(weighted, axis=0, keepdims=True)
            ds_o[g] += ds
            low = ds.astype(BF16)
            dqkv_s[g, pad_rows(c), :] = gather_heads(tn(low, k), masks) * SCALE
            dqkv_s[NG + g, pad_rows(c), :] = nn(low, q_wide)
            dqkv_s[2 * NG + g, pad_rows(c), :] = nn(probs.astype(BF16), do_wide)
        return 0

    lax.fori_loop(0, C, attend, 0)
    for g in range(3 * NG):
        dq[:, LANE * g : LANE * (g + 1)] = dqkv_s[g, 0:ROWS, :].astype(BF16)
    sv_o[2:3, :] = colsum(dq[:, 0:D].astype(F32))
    sv_o[3:4, :] = colsum(dq[:, 2 * D :].astype(F32))
    acc[...] = jnp.zeros_like(acc)

    def step(n, _):
        cp_q(n).wait()
        acc[...] += nt(dq[:, lanes_at(n, QCH)], wqkv[:, lanes_at(n, QCH)])
        return 0

    lax.fori_loop(0, N_Q, step, 0)
    wq, wo = 3 * D // 4, D // 4
    for c in range(2):
        for x in range(2):
            w = 2 * x + c
            r3_o[c, :, D * x : D * (x + 1)] = jnp.concatenate(
                [dq[:, wq * w : wq * (w + 1)], dyr[:, wo * w : wo * (w + 1)]], axis=1
            )
    dh = acc[...]
    normed, inverse = norm_parts(z[...])
    sv_o[0:1, :] = colsum(dh * normed)
    sv_o[1:2, :] = colsum(dh)
    acc[...] = dy[...] + norm_back(dh, normed, inverse, ln1g[b : b + 1, :])
    if b == 0:
        for g in range(NG):
            do_s[g, 0:ROWS, :] = acc[:, LANE * g : LANE * (g + 1)]
        for c in range(C):
            for g in range(NG):
                out[c, :, LANE * g : LANE * (g + 1)] = do_s[g, crop_rows(c), :]
    else:
        own_o[...] = acc[...].reshape(T, C, D)
        take_pieces(acc, (sx_o, sc_o, sd_o), BACK_SEND)


def attn_back(b, dyr, qkvc, bias, dy, z, p):
    outs = [
        shape((2, ROWS, 2 * D), BF16),
        shape((4, D), F32),
        shape((NG, TP, GT), F32),
    ] + ([shape((C, T, D), F32)] if b == 0 else PIECES)
    return pl.pallas_call(
        functools.partial(attn_back_body, b),
        in_specs=[VM] * 6 + [ANY] * 2,
        out_specs=[VM] * len(outs),
        out_shape=outs,
        scratch_shapes=[
            pltpu.VMEM((D, D), BF16),
            pltpu.VMEM((D, 3 * D), BF16),
            pltpu.VMEM((NG, PAD_ROWS, LANE), F32),
            pltpu.VMEM((3 * NG, PAD_ROWS, LANE), F32),
            pltpu.VMEM((ROWS, 3 * D), BF16),
            pltpu.VMEM((ROWS, D), F32),
            pltpu.SemaphoreType.DMA,
            pltpu.SemaphoreType.DMA((N_Q,)),
        ],
        compiler_params=params_of(),
        cost_estimate=cost(2 * ROWS * 6 * D * D, 20e6),
        name=f"attn_back_{b}",
    )(dyr, qkvc, bias, dy, z, p["ln1_gain"], p["w_out"], p["w_qkv"])


def weight_grad(kind, core, left, right, received=None):
    if kind == "up":
        grid = (2, 2)
        specs = [
            pl.BlockSpec((ROWS, D), lambda x, n, s: (0, 0)),
            pl.BlockSpec((ROWS, D // 2), lambda x, n, s: (0, (x * 2 + s[0]) * 2 + n)),
        ]
        out_spec = pl.BlockSpec((1, D, D // 2), lambda x, n, s: (x, 0, n))
        out = shape((2, D, D), F32)
    elif kind == "down":
        grid = (4,)
        specs = [
            pl.BlockSpec((1, ROWS, D // 2), lambda m, s: (s[0], 0, 0)),
            pl.BlockSpec((ROWS, FF // 4), lambda m, s: (0, m)),
        ]
        out_spec = pl.BlockSpec((2, D // 2, FF // 8), lambda m, s: (m, 0, 0))
        out = shape((8, D // 2, FF // 8), F32)
    else:
        grid = (2,)
        specs = [
            pl.BlockSpec((ROWS, D), lambda x, s: (0, 0)),
            pl.BlockSpec((ROWS, D), lambda x, s: (0, 0)),
            pl.BlockSpec((1, ROWS, D), lambda x, s: (s[0], 0, x)),
        ]
        out_spec = pl.BlockSpec((1, D, D), lambda x, s: (x, 0, 0))
        out = shape((2, D, D), F32)

    def body(s, *refs):
        got = None
        if received is not None:
            got = refs[-2]
        o = refs[-1]

        def put(where, value):
            o[where] = value if got is None else value + got[where]

        if kind == "up":
            put((0,), tn(refs[0][...], refs[1][...]))
        elif kind == "down":
            for k in range(2):
                put((k,), tn(refs[0][0], refs[1][:, k * (FF // 8) : (k + 1) * (FF // 8)]))
        else:
            hid, att, r = refs[0][...], refs[1][...], refs[2]
            edge = 3 * D // 4
            lo = edge // LANE * LANE
            put((0, slice(None), slice(0, lo)), tn(hid, r[0, :, 0:lo]))
            mid = r[0, :, lo : lo + LANE]
            lane = lax.broadcasted_iota(jnp.int32, (D, LANE), 1)
            put(
                (0, slice(None), slice(lo, lo + LANE)),
                jnp.where(lane < edge - lo, tn(hid, mid), tn(att, mid)),
            )
            put((0, slice(None), slice(lo + LANE, D)), tn(att, r[0, :, lo + LANE :]))

    args = [*left, right]
    if received is not None:
        args.append(received.reshape(out.shape))
        specs.append(out_spec)
    return pl.pallas_call(
        body,
        grid_spec=pltpu.PrefetchScalarGridSpec(
            num_scalar_prefetch=1, grid=grid, in_specs=specs, out_specs=out_spec
        ),
        out_shape=out,
        compiler_params=params_of(),
        cost_estimate=cost(2 * ROWS * 2 * D * D, 6e6 if received is None else 11e6),
        name=f"weight_grad_{kind}",
    )(core, *args)


def insert_bit(i, place, bit):
    return ((i >> place) << (place + 1)) | (bit << place) | (i & ((1 << place) - 1))


def split_sum(kept, fixed, recv, place, bits):
    n, r, w = recv.shape

    def at_recv(flip):
        return lambda i, s: (insert_bit(i, place, s[0] ^ flip), 0, 0)

    def at_kept(flip):
        if fixed is None:
            return at_recv(flip)
        return lambda i, s: (insert_bit(insert_bit(i, place, s[0] ^ flip), fixed, s[1]), 0, 0)

    def body(s, ka, ra, kb, rb, keep_o, send_o):
        keep_o[...] = ka[...] + ra[...]
        send_o[...] = kb[...] + rb[...]

    block = (1, r, w)
    return pl.pallas_call(
        body,
        grid_spec=pltpu.PrefetchScalarGridSpec(
            num_scalar_prefetch=1,
            grid=(n // 2,),
            in_specs=[
                pl.BlockSpec(block, at_kept(0)),
                pl.BlockSpec(block, at_recv(0)),
                pl.BlockSpec(block, at_kept(1)),
                pl.BlockSpec(block, at_recv(1)),
            ],
            out_specs=[pl.BlockSpec(block, lambda i, s: (i, 0, 0))] * 2,
        ),
        out_shape=[shape((n // 2, r, w), F32)] * 2,
        compiler_params=params_of(),
        cost_estimate=cost(n * r * w, 12 * n * r * w),
        name="split_sum",
    )(bits, kept, recv, kept, recv)


def scatter_sum(full, names, order, links):
    names = list(names)
    place = len(names) - 1 - names.index(order[0])
    axis, perm, bit = links[order[0]]
    n, r, w = full.shape
    view = full.reshape(n >> (place + 1), 2, 1 << place, r, w)
    send = lax.dynamic_index_in_dim(view, 1 - bit, 1, False).reshape(n // 2, r, w)
    recv = lax.ppermute(send, axis, perm)
    kept, fixed, fixed_bit = full, place, bit
    names.remove(order[0])
    for name in order[1:]:
        place = len(names) - 1 - names.index(name)
        axis, perm, bit = links[name]
        kept, send = split_sum(kept, fixed, recv, place, jnp.stack([bit, fixed_bit]))
        recv = lax.ppermute(send, axis, perm)
        fixed, fixed_bit = None, bit * 0
        names.remove(name)
    return (kept + recv)[0]


def scatter_rest(block, dim, img, sub):
    step = sub // 2
    while step:
        bit = (img // step) % 2
        half = block.shape[dim] // 2
        keep = lax.dynamic_slice_in_dim(block, bit * half, half, dim)
        send = lax.dynamic_slice_in_dim(block, (1 - bit) * half, half, dim)
        perm = [(i, i ^ step) for i in range(8 * sub)]
        block = keep + lax.ppermute(send, "img", perm)
        step //= 2
    return block


def relative_onehot():
    places = jnp.arange(TP, dtype=jnp.int32)
    rows_at, cols_at = places // SIDE, places % SIDE
    rel = (rows_at[None, :] - rows_at[:, None] + 6) * 13 + cols_at[None, :] - cols_at[:, None] + 6
    real = (places[:, None] < T) & (places[None, :] < T)
    rel = jnp.where(real, rel, -1)
    return (jnp.arange(169, dtype=jnp.int32)[:, None] == rel.reshape(1, -1)).astype(F32)


def region_of(coords):
    return jnp.where(coords < 7, 0, jnp.where(coords < 11, 1, 2))


def spread_bias(bias_table, onehot, quadrant):
    rows = jnp.dot(
        bias_table.transpose(0, 2, 1).reshape(2 * HEADS, 169),
        onehot,
        precision=lax.Precision.HIGHEST,
        preferred_element_type=F32,
    )
    rows = rows.reshape(2, NG, PER, TP, TP).transpose(0, 1, 3, 2, 4)
    places = jnp.arange(TP, dtype=jnp.int32)
    labels = 3 * region_of(quadrant // 2 * 7 + places // 7) + region_of(quadrant % 2 * 7 + places % 7)
    mask = jnp.where(labels[:, None] == labels[None, :], 0.0, -100.0).astype(F32)
    mask = jnp.stack([jnp.zeros_like(mask), mask])
    mask = jnp.where((places < T)[None, :, None], mask, NEG)
    return (rows + mask[:, None, :, None, :]).reshape(2, NG, TP, GT)


def per_device(
    tokens, crop_count, ln1_gain, ln1_bias, w_qkv, b_query, b_value, bias_table, w_out, b_out,
    ln2_gain, ln2_bias, w_up, b_up, w_down, b_down, cotangent, *, n_img,
):
    win, img = lax.axis_index("win"), lax.axis_index("img")
    sub = n_img // 8
    x_bit, core = win // 2, win % 2
    links = {"x": ("win", [(i, i ^ 2) for i in range(4)], x_bit)}
    for k in range(3):
        links[k] = ("img", [(i, i ^ (sub << k)) for i in range(n_img)], (img // (sub << k)) % 2)
    core_swap = [(i, i ^ 1) for i in range(4)]
    mine, other = jnp.reshape(core, (1,)), jnp.reshape(1 - core, (1,))
    p = dict(
        ln1_gain=ln1_gain, ln1_bias=ln1_bias, w_qkv=w_qkv, b_query=b_query, b_value=b_value,
        w_out=w_out, b_out=b_out, ln2_gain=ln2_gain, ln2_bias=ln2_bias, w_up=w_up, b_up=b_up,
        w_down=w_down, b_down=b_down,
    )

    def exchange(pieces):
        ways = ([(i, i ^ 2) for i in range(4)], core_swap, [(i, i ^ 3) for i in range(4)])
        return [lax.ppermute(a, "win", way) for a, way in zip(pieces, ways)]

    onehot = relative_onehot()
    biases = spread_bias(bias_table, onehot, win)
    fwd = [None, None]
    out = block_fwd(0, (tokens[:, 0],), biases[0], p)
    fwd[0] = out[:8]
    ct_own, *ct_send = cotangent_pieces(crop_count, cotangent[:, 0])
    dz, dd, db_down = join_grad(True, ct_own, exchange(ct_send))
    out = block_fwd(1, (out[8], *exchange(out[9:])), biases[1], p)
    fwd[1] = out[:8]
    block_out = block_output(crop_count, out[8], exchange(out[9:]))

    def core_sum(kind, left, right):
        theirs = weight_grad(kind, other, left, right)
        return weight_grad(kind, mine, left, right, lax.ppermute(theirs, "win", core_swap))

    rows, tables, mats = [None, None], [None, None], [None, None]
    side = ("x", 2, 1, 0)
    for b in (1, 0):
        z, h, qkvc, o, y, h2, g, gp = fwd[b]
        full = core_sum("down", [dd], g)
        g_down = scatter_sum(full.reshape(16, D // 4, FF // 8), (2, 1, 0, "x"), (0, "x", 1, 2), links)
        da, dy, dyr, sv_m, db_up = mlp_back(b, dz, y, gp, p)
        full = core_sum("up", [h2], da)
        g_up = scatter_sum(full.reshape(16, D // 8, D), side, ("x", 0, 1, 2), links)
        outs = attn_back(b, dyr, qkvc, biases[b], dy, z, p)
        r3, sv_a, ds = outs[:3]
        rows[b] = jnp.concatenate([sv_a, sv_m, db_down, db_up.reshape(4, D)], axis=0)
        tables[b] = ds
        if b == 1:
            dz, dd, db_down = join_grad(False, outs[3], exchange(outs[4:]))
        else:
            grad_tokens = outs[3][:, None]
        full = core_sum("attn", [h, o], r3)
        order = (1, "x", 0, 2) if b else (1, 0, "x", 2)
        g_att = scatter_sum(full.reshape(16, D // 8, D), side, order, links)
        g_up, g_att = (scatter_rest(v, 0, img, sub) for v in (g_up, g_att))
        g_down = scatter_rest(g_down, 1, img, sub)
        mats[b] = (g_att[:, : 3 * D // 4], g_att[:, 3 * D // 4 :], g_up, g_down.T)

    g_qkv, g_out, g_up, g_down = (jnp.stack(pair) for pair in zip(*mats))
    ds = jnp.stack(tables).reshape(2, NG, TP, PER, TP).transpose(0, 1, 3, 2, 4)
    table = lax.dot_general(
        ds.reshape(2 * HEADS, TP * TP),
        onehot,
        (((1,), (1,)), ((), ())),
        precision=lax.Precision.HIGHEST,
        preferred_element_type=F32,
    )
    table = jnp.pad(table, ((0, 0), (0, 256 - 169))).reshape(2 * HEADS // 3, D)
    small = jnp.concatenate(rows + [table], axis=0)
    for axis, size in (("win", 4), ("img", n_img)):
        step = 1
        while step < size:
            small = small + lax.ppermute(small, axis, [(i, i ^ step) for i in range(size)])
            step *= 2
    table = small[24:].reshape(2, HEADS, 256)[:, :, :169].transpose(0, 2, 1)
    width = D // n_img

    def share(first, n=1):
        full = small[:24].reshape(2, 12, D)[:, first : first + n].reshape(2, n * D)
        return lax.dynamic_slice_in_dim(full, img * (n * width), n * width, 1)

    return (
        block_out[:, None], grad_tokens, share(0), share(1), g_qkv, share(2), share(3), table,
        g_out, share(6), share(4), share(5), g_up, share(8, 4), g_down, share(7),
    )


def solution(mesh):
    shard = P("img", "win", None, None)
    vec, mat = P(None, "img"), P(None, "img", "win")
    return jax.shard_map(
        functools.partial(per_device, n_img=mesh.shape["img"]),
        mesh=mesh,
        in_specs=(shard, P("img")) + (P(),) * 14 + (shard,),
        out_specs=(shard, shard, vec, vec, mat, vec, vec, P(), mat, vec, vec, vec, mat, vec, mat, vec),
        check_vma=False,
    )
```

time: 2200 us -> 614 us (0.28)
  waiting for transfers between devices: 1160 us -> 179 us
  local copies, waits for them, and re-layouts: 703 us -> 53 us
  Pallas kernels: 0 us -> 305 us
  matrix products: 162 us -> 2.45 us
  other arithmetic: 82.6 us -> 11.7 us
  starting transfers between devices: 1.62 us -> 55.4 us
  blocking collectives: 51.8 us -> 0 us
    unnamed x34 -> x0, waiting for transfers between devices: 1080 us -> none
    unnamed x288 -> x108, local copies, waits for them, and re-layouts: 557 us -> 15.9 us
    pallas_call x0 -> x40, Pallas kernels: none -> 305 us  [the longest x12 72.5 us: weight_grad(): pl.pallas_call(body, grid_spec=pltpu.PrefetchScalarGridSpec(num_scalar_pr...]
    ppermute x0 -> x47, waiting for transfers between devices: none -> 179 us  [the longest x24 122 us: scatter_sum(): recv = lax.ppermute(send, axis, perm)]
    dot_general x38 -> x2, matrix products: 149 us -> 2.45 us  [the longest x1 1.36 us: per_device(): lax.dot_general(ds.reshape(2 * HEADS, TP * TP), onehot, (((1,), (1,)), ((...]
    another operation x22 -> x8, local copies, waits for them, and re-layouts: 65 us -> 2 us  [the longest x4 1.81 us: per_device(): ds = jnp.stack(tables).reshape(2, NG, TP, PER, TP).transpose(0, 1, 3, 2, 4)]
    ppermute x0 -> x47, starting transfers between devices: none -> 55.4 us  [the longest x24 36.4 us: scatter_sum(): recv = lax.ppermute(send, axis, perm)]
    psum x2 -> x0, blocking collectives: 51.8 us -> none  [the longest x1 40.9 us: per_device(): table_grads = lax.psum(jnp.stack([table_one, table_two]), ('img', 'win'))]
  transfers between devices with their start and end apart: 20 -> 47, of which waited for: 14 -> 16; matrix products, arithmetic and copies ran while one was open for 34% -> 9% of each run, Pallas kernels for 0% -> 36%
where the time goes in v1:
time: 614 us; the launch traced here: 608 us
  Pallas kernels  305 us (50%)
  waiting for transfers between devices  179 us (29%)
  starting transfers between devices  55.4 us (9%)
  local copies, waits for them, and re-layouts  53 us (9%)
  other arithmetic  11.7 us (2%)
    ppermute x24, waiting for transfers between devices, scatter_sum(): recv = lax.ppermute(send, axis, perm)  122 us
    pallas_call x12, Pallas kernels, weight_grad(): pl.pallas_call(body, grid_spec=pltpu.PrefetchScalarGridSpec(num_scalar_pr...  72.5 us
    pallas_call x2, Pallas kernels, block_fwd(): pl.pallas_call(functools.partial(fwd_body, b), in_specs=[VM] * (len(sourc...  71.4 us
    pallas_call x18, Pallas kernels, split_sum(): pl.pallas_call(body, grid_spec=pltpu.PrefetchScalarGridSpec(num_scalar_pr...  66 us
    pallas_call x2, Pallas kernels, attn_back(): pl.pallas_call(functools.partial(attn_back_body, b), in_specs=[VM] * 6 +...  57 us
    ppermute x5, waiting for transfers between devices, per_device(): lax.ppermute(small, axis, [(i, i ^ step) for i in range(size)])  38.4 us
    ppermute x24, starting transfers between devices, scatter_sum(): recv = lax.ppermute(send, axis, perm)  36.4 us
    pallas_call x2, Pallas kernels, mlp_back(): pl.pallas_call(functools.partial(mlp_back_body, b), in_specs=[VM] * 3 + [...  26.9 us
  transfers between devices with their start and end apart: 47, of which 16 were waited for; matrix products, arithmetic and copies ran while one was open for 9% of the time, Pallas kernels for 36%

profile of v1, /device:TPU:0, one launch (start us, length us, event | category | flops | bytes accessed | tf_op | source)
XLA Modules:
  0.0 608.5 jit_solution(16140871612594520424)
XLA Ops:
  13.9 35.4 %forward_0.1 = (f32[392,768]{1,0:T(8,128)}, bf16[392,768]{1,0:T(8,128)(2,1)}, bf16[8,18,56,128]{3,2,1,0:T(8,128)(2,1)}, bf16[392,768]{1,0:T(8,128)(2,1)}, f32[39...) custom-call(bf16[8,49,768]{2,1,0:T(8,128)(2,1)} %bitcast.113, ...), custom_call_target="tpu_custom_call" | custom-call | flops 5549064192 | bytes 30000000 | tf_op jit(solution)/shard_map/forward_0/pallas_call | solution.py:290
  56.3 6.8 %collective-permute-done.2.refs_3_ = f32[9,8,768]{2,1,0:T(8,128)S(1)} collective-permute-done((f32[9,8,768]{2,1,0:T(8,128)}, f32[9,8,768]{2,1,0:T(8,128)S(1)}, u32[]{:S(2)}, u32[]{:S(2)}) %collective-permute-start.2) | collective-permute-done | bytes 221216 | tf_op jit(solution)/shard_map/ppermute | solution.py:758
  63.9 36.0 %forward_1.1 = (f32[392,768]{1,0:T(8,128)}, bf16[392,768]{1,0:T(8,128)(2,1)}, bf16[8,18,56,128]{3,2,1,0:T(8,128)(2,1)}, bf16[392,768]{1,0:T(8,128)(2,1)}, f32[39...) custom-call(f32[49,8,768]{2,1,0:T(8,128)} %get-tuple-element.107.ref, ...), custom_call_target="tpu_custom_call" | custom-call | flops 5549064192 | bytes 30000000 | tf_op jit(solution)/shard_map/forward_1/pallas_call | solution.py:290
  99.9 13.4 %mlp_back_1.1 = (bf16[392,3072]{1,0:T(8,128)(2,1)}, f32[392,768]{1,0:T(8,128)}, bf16[392,768]{1,0:T(8,128)(2,1)}, f32[3,768]{1,0:T(4,128)}, f32[1,3072]{1,0:T(1,128)}) custom-call(f32[392,768]{1,0:T(8,128)} %get-tuple-element.119.dz, f32[392,768]{1,0:T(8,128)} %get-tuple-element.120.y, f32[2,768]{1,0:T(2,128)} %ln2g.3, ...), custom_call_target="tpu_custom_call" | custom-call | flops 3699376128 | bytes 20000000 | tf_op jit(solution)/shard_map/mlp_back_1/pallas_call | solution.py:435
  113.3 28.4 %attn_back_1.1 = (bf16[2,392,1536]{2,1,0:T(8,128)(2,1)}, f32[4,768]{1,0:T(4,128)}, f32[6,56,224]{2,1,0:T(8,128)}, f32[49,8,768]{2,1,0:T(8,128)}, f32[12,8,768]{2...) custom-call(bf16[392,768]{1,0:T(8,128)(2,1)} %get-tuple-element.122.dyr, ...), custom_call_target="tpu_custom_call" | custom-call | flops 2774532096 | bytes 20000000 | tf_op jit(solution)/shard_map/attn_back_1/pallas_call | solution.py:545
  141.7 5.4 weight_grad_attn.6
  151.3 5.5 weight_grad_up.6
  156.9 3.6 collective-permute-done.11.rd
  164.2 13.5 %mlp_back_0.1 = (bf16[392,3072]{1,0:T(8,128)(2,1)}, f32[392,768]{1,0:T(8,128)}, bf16[392,768]{1,0:T(8,128)(2,1)}, f32[3,768]{1,0:T(4,128)}, f32[1,3072]{1,0:T(1,128)}) custom-call(f32[392,768]{1,0:T(8,128)} %get-tuple-element.130.dz, f32[392,768]{1,0:T(8,128)} %get-tuple-element.131.y, f32[2,768]{1,0:T(2,128)} %ln2g.3, ...), custom_call_target="tpu_custom_call" | custom-call | flops 3699376128 | bytes 20000000 | tf_op jit(solution)/shard_map/mlp_back_0/pallas_call | solution.py:435
  179.1 28.6 %attn_back_0.1 = (bf16[2,392,1536]{2,1,0:T(8,128)(2,1)}, f32[4,768]{1,0:T(4,128)}, f32[6,56,224]{2,1,0:T(8,128)}, f32[8,49,768]{2,1,0:T(8,128)}) custom-call(bf16[392,768]{1,0:T(8,128)(2,1)} %get-tuple-element.133.dyr, bf16[8,18,56,128]{3,2,1,0:T(8,128)(2,1)} %get-tuple-element.134.qkvc, f32[6,56,224]{2,1,0:T(8,128)} %squeeze.36.refs_1_.bias, ...), custom_call_target="tpu_custom_call" | custom-call | flops 2774532096 | bytes 20000000 | tf_op jit(solution)/shard_map/attn_back_0/pallas_call | solution.py:545
  212.0 5.7 weight_grad_down.6
  219.6 4.3 collective-permute-done.13
  229.5 5.4 weight_grad_attn.4
  235.5 5.6 collective-permute-done.4.rc
  242.7 5.6 weight_grad_up.4
  248.3 5.5 weight_grad_down.4
  254.3 6.1 weight_grad_attn.7
  260.4 3.3 constant_dynamic-slice_fusion.9
  264.1 6.7 %weight_grad_up.7 = f32[2,768,768]{2,1,0:T(8,128)} custom-call(s32[1]{0:T(128)} %bitcast.15.s, bf16[392,768]{1,0:T(8,128)(2,1)} %get-tuple-element.174.refs_0_, bf16[392,3072]{1,0:T(8,128)(2,1)} %get-tuple-element.175.refs_1_, f32[2,768,768]{2,1,0:T(8,128)} %collective-permute-done.32.refs_2_), custom_call_target="tpu_custom_call" | custom-call | flops 924844032 | bytes 11000000 | tf_op jit(solution)/shard_map/weight_grad_up/pallas_call | solution.py:624
  273.6 3.3 dynamic-slice_bitcast_fusion
  276.8 6.8 %weight_grad_down.7 = f32[8,384,384]{2,1,0:T(8,128)} custom-call(s32[1]{0:T(128)} %bitcast.15.s, bf16[2,392,384]{2,1,0:T(8,128)(2,1)} %get-tuple-element.190.refs_0_, bf16[392,3072]{1,0:T(8,128)(2,1)} %get-tuple-element.191.refs_1_, f32[8,384,384]{2,1,0:T(8,128)} %collective-permute-done.42.refs_2_), custom_call_target="tpu_custom_call" | custom-call | flops 924844032 | bytes 11000000 | tf_op jit(solution)/shard_map/weight_grad_down/pallas_call | solution.py:624
  283.6 34.1 %collective-permute-done.16 = f32[40,768]{1,0:T(8,128)S(1)} collective-permute-done((f32[40,768]{1,0:T(8,128)S(1)}, f32[40,768]{1,0:T(8,128)S(1)}, u32[]{:S(2)}, u32[]{:S(2)}) %collective-permute-start.16) | collective-permute-done | bytes 122912 | tf_op jit(solution)/shard_map/ppermute | solution.py:813
  319.2 3.2 constant_dynamic-slice_fusion.1
  324.3 6.1 %weight_grad_attn.5 = f32[2,768,768]{2,1,0:T(8,128)} custom-call(s32[1]{0:T(128)} %bitcast.15.s, bf16[392,768]{1,0:T(8,128)(2,1)} %get-tuple-element.148.refs_0_, bf16[392,768]{1,0:T(8,128)(2,1)} %get-tuple-element.149.refs_1_, bf16[2,392,1536]{2,1,0:T(8,128)(2,1)} %get-tuple-element.150.refs_2_, f32[2,768,768]{2,1,0:T(8,128)} %collective-permute-done.17.refs_3_), custom_call_target="tpu_custom_call" | custom-call | flops 924844032 | bytes 11000000 | tf_op jit(solution)/shard_map/weight_grad_attn/pallas_call | solution.py:624
  333.6 4.6 collective-permute-start.18
  338.3 6.7 %weight_grad_up.5 = f32[2,768,768]{2,1,0:T(8,128)} custom-call(s32[1]{0:T(128)} %bitcast.15.s, bf16[392,768]{1,0:T(8,128)(2,1)} %get-tuple-element.166.refs_0_, bf16[392,3072]{1,0:T(8,128)(2,1)} %get-tuple-element.167.refs_1_, f32[2,768,768]{2,1,0:T(8,128)} %collective-permute-done.27.refs_2_), custom_call_target="tpu_custom_call" | custom-call | flops 924844032 | bytes 11000000 | tf_op jit(solution)/shard_map/weight_grad_up/pallas_call | solution.py:624
  345.0 3.2 dynamic-slice_bitcast_fusion.1
  348.7 6.9 %weight_grad_down.5 = f32[8,384,384]{2,1,0:T(8,128)} custom-call(s32[1]{0:T(128)} %bitcast.15.s, bf16[2,392,384]{2,1,0:T(8,128)(2,1)} %get-tuple-element.182.refs_0_, bf16[392,3072]{1,0:T(8,128)(2,1)} %get-tuple-element.183.refs_1_, f32[8,384,384]{2,1,0:T(8,128)} %collective-permute-done.37.refs_2_), custom_call_target="tpu_custom_call" | custom-call | flops 924844032 | bytes 11000000 | tf_op jit(solution)/shard_map/weight_grad_down/pallas_call | solution.py:624
  355.6 3.2 constant_dynamic-slice_fusion.2
  360.9 5.0 split_sum.21
  365.9 6.3 %collective-permute-done.33.ra.rb = f32[8,96,768]{2,1,0:T(8,128)} collective-permute-done((f32[8,96,768]{2,1,0:T(8,128)}, f32[8,96,768]{2,1,0:T(8,128)}, u32[]{:S(2)}, u32[]{:S(2)}) %collective-permute-start.33) | collective-permute-done | bytes 2359328 | tf_op jit(solution)/shard_map/ppermute | solution.py:683
  374.3 5.1 split_sum.27
  383.7 5.0 split_sum.33
  401.2 5.1 split_sum.18
  406.3 16.4 %collective-permute-done.28.ra.rb = f32[8,96,768]{2,1,0:T(8,128)} collective-permute-done((f32[8,96,768]{2,1,0:T(8,128)}, f32[8,96,768]{2,1,0:T(8,128)}, u32[]{:S(2)}, u32[]{:S(2)}) %collective-permute-start.28) | collective-permute-done | bytes 2359328 | tf_op jit(solution)/shard_map/ppermute | solution.py:683
  425.3 5.0 split_sum.24
  430.4 17.7 %collective-permute-done.24.ra.rb = f32[4,96,768]{2,1,0:T(8,128)} collective-permute-done((f32[4,96,768]{2,1,0:T(8,128)}, f32[4,96,768]{2,1,0:T(8,128)}, u32[]{:S(2)}, u32[]{:S(2)}) %collective-permute-start.24) | collective-permute-done | bytes 1179680 | tf_op jit(solution)/shard_map/ppermute | solution.py:690
  454.6 5.0 split_sum.30
  466.9 6.5 %collective-permute-done.44.ra.rb = f32[4,192,384]{2,1,0:T(8,128)} collective-permute-done((f32[4,192,384]{2,1,0:T(8,128)}, f32[4,192,384]{2,1,0:T(8,128)}, u32[]{:S(2)}, u32[]{:S(2)}) %collective-permute-start.44) | collective-permute-done | bytes 1179680 | tf_op jit(solution)/shard_map/ppermute | solution.py:690
  473.3 4.6 collective-permute-start.35
  477.9 3.3 split_sum.34
  481.2 32.7 %collective-permute-done.25.ra.rb = f32[2,96,768]{2,1,0:T(8,128)S(1)} collective-permute-done((f32[2,96,768]{2,1,0:T(8,128)}, f32[2,96,768]{2,1,0:T(8,128)S(1)}, u32[]{:S(2)}, u32[]{:S(2)}) %collective-permute-start.25) | collective-permute-done | bytes 589856 | tf_op jit(solution)/shard_map/ppermute | solution.py:690
  514.7 4.6 collective-permute-start.45
  555.0 17.0 %collective-permute-done.30.ra.rb = f32[2,96,768]{2,1,0:T(8,128)S(1)} collective-permute-done((f32[2,96,768]{2,1,0:T(8,128)}, f32[2,96,768]{2,1,0:T(8,128)S(1)}, u32[]{:S(2)}, u32[]{:S(2)}) %collective-permute-start.30) | collective-permute-done | bytes 589856 | tf_op jit(solution)/shard_map/ppermute | solution.py:690
  575.7 6.1 collective-permute-done.40.ra.rb
  585.5 9.4 %collective-permute-done.21 = f32[1,96,768]{2,1,0:T(8,128)S(1)} collective-permute-done((f32[1,96,768]{2,1,0:T(8,128)}, f32[1,96,768]{2,1,0:T(8,128)S(1)}, u32[]{:S(2)}, u32[]{:S(2)}) %collective-permute-start.21) | collective-permute-done | bytes 294944 | tf_op jit(solution)/shard_map/ppermute | solution.py:690
  595.8 5.5 collective-permute-done.31
  602.9 4.4 collective-permute-done.41
  (270 shorter events, 138.7 us)
Async XLA Ops:
  6.1 46.5 %collective-permute-start.6 = (f32[12,8,768]{2,1,0:T(8,128)}, f32[12,8,768]{2,1,0:T(8,128)S(1)}, u32[]{:S(2)}, u32[]{:S(2)}) collective-permute-start(f32[12,8,768]{2,1,0:T(8,128)} %get-tuple-element.116), channel_id=1, source_target_pairs={{0,2},{1,3},{2,0},{3,1},{4,6},{5,7},{6,4},{7,5},{8,10},{9,11},{10,... | collective-permute-start | bytes 884744 | tf_op jit(solution)/shard_map/ppermute | solution.py:758
  9.1 43.5 %collective-permute-start.7 = (f32[12,8,768]{2,1,0:T(8,128)}, f32[12,8,768]{2,1,0:T(8,128)S(1)}, u32[]{:S(2)}, u32[]{:S(2)}) collective-permute-start(f32[12,8,768]{2,1,0:T(8,128)} %get-tuple-element.117), channel_id=1, source_target_pairs={{0,1},{1,0},{2,3},{3,2},{4,5},{5,4},{6,7},{7,6},{8,9},{9,8},{10,11... | collective-permute-start | bytes 884744 | tf_op jit(solution)/shard_map/ppermute | solution.py:758
  9.1 42.3 %collective-permute-start.8 = (f32[9,8,768]{2,1,0:T(8,128)}, f32[9,8,768]{2,1,0:T(8,128)S(1)}, u32[]{:S(2)}, u32[]{:S(2)}) collective-permute-start(f32[9,8,768]{2,1,0:T(8,128)} %get-tuple-element.118), channel_id=1, source_target_pairs={{0,3},{1,2},{2,1},{3,0},{4,7},{5,6},{6,5},{7,4},{8,11},{9,10},{10,... | collective-permute-start | bytes 663560 | tf_op jit(solution)/shard_map/ppermute | solution.py:758
  49.3 13.8 %collective-permute-start = (f32[12,8,768]{2,1,0:T(8,128)}, f32[12,8,768]{2,1,0:T(8,128)S(1)}, u32[]{:S(2)}, u32[]{:S(2)}) collective-permute-start(f32[12,8,768]{2,1,0:T(8,128)} %get-tuple-element.108), channel_id=1, source_target_pairs={{0,2},{1,3},{2,0},{3,1},{4,6},{5,7},{6,4},{7,5},{8,10},{9,11},{10,... | collective-permute-start | bytes 884744 | tf_op jit(solution)/shard_map/ppermute | solution.py:758
  51.3 11.7 %collective-permute-start.1 = (f32[12,8,768]{2,1,0:T(8,128)}, f32[12,8,768]{2,1,0:T(8,128)S(1)}, u32[]{:S(2)}, u32[]{:S(2)}) collective-permute-start(f32[12,8,768]{2,1,0:T(8,128)} %get-tuple-element.109), channel_id=1, source_target_pairs={{0,1},{1,0},{2,3},{3,2},{4,5},{5,4},{6,7},{7,6},{8,9},{9,8},{10,11... | collective-permute-start | bytes 884744 | tf_op jit(solution)/shard_map/ppermute | solution.py:758
  51.4 11.7 %collective-permute-start.2 = (f32[9,8,768]{2,1,0:T(8,128)}, f32[9,8,768]{2,1,0:T(8,128)S(1)}, u32[]{:S(2)}, u32[]{:S(2)}) collective-permute-start(f32[9,8,768]{2,1,0:T(8,128)} %get-tuple-element.110), channel_id=1, source_target_pairs={{0,3},{1,2},{2,1},{3,0},{4,7},{5,6},{6,5},{7,4},{8,11},{9,10},{10,... | collective-permute-start | bytes 663560 | tf_op jit(solution)/shard_map/ppermute | solution.py:758
  147.2 106.7 %collective-permute-start.22 = (f32[2,768,768]{2,1,0:T(8,128)}, f32[2,768,768]{2,1,0:T(8,128)}, u32[]{:S(2)}, u32[]{:S(2)}) collective-permute-start(f32[2,768,768]{2,1,0:T(8,128)} %weight_grad_attn.6), channel_id=1, source_target_pairs={{0,1},{1,0},{2,3},{3,2},{4,5},{5,4},{6,7},{7,6},{8,9},{9,8},{10,11... | collective-permute-start | bytes 14155784 | tf_op jit(solution)/shard_map/ppermute | solution.py:773
  147.5 13.0 %collective-permute-start.9 = (f32[12,8,768]{2,1,0:T(8,128)S(1)}, f32[12,8,768]{2,1,0:T(8,128)S(1)}, u32[]{:S(2)}, u32[]{:S(2)}) collective-permute-start(f32[12,8,768]{2,1,0:T(8,128)S(1)} %copy-done.49), channel_id=1, source_target_pairs={{0,2},{1,3},{2,0},{3,1},{4,6},{5,7},{6,4},{7,5},{8,10},{9,11},{10,... | collective-permute-start | bytes 884744 | tf_op jit(solution)/shard_map/ppermute | solution.py:758
  149.2 11.4 %collective-permute-start.10 = (f32[12,8,768]{2,1,0:T(8,128)S(1)}, f32[12,8,768]{2,1,0:T(8,128)S(1)}, u32[]{:S(2)}, u32[]{:S(2)}) collective-permute-start(f32[12,8,768]{2,1,0:T(8,128)S(1)} %copy-done.48), channel_id=1, source_target_pairs={{0,1},{1,0},{2,3},{3,2},{4,5},{5,4},{6,7},{7,6},{8,9},{9,8},{10,11... | collective-permute-start | bytes 884744 | tf_op jit(solution)/shard_map/ppermute | solution.py:758
  149.2 11.3 %collective-permute-start.11 = (f32[9,8,768]{2,1,0:T(8,128)}, f32[9,8,768]{2,1,0:T(8,128)S(1)}, u32[]{:S(2)}, u32[]{:S(2)}) collective-permute-start(f32[9,8,768]{2,1,0:T(8,128)} %get-tuple-element.129), channel_id=1, source_target_pairs={{0,3},{1,2},{2,1},{3,0},{4,7},{5,6},{6,5},{7,4},{8,11},{9,10},{10,... | collective-permute-start | bytes 663560 | tf_op jit(solution)/shard_map/ppermute | solution.py:758
  156.9 106.8 %collective-permute-start.32 = (f32[2,768,768]{2,1,0:T(8,128)}, f32[2,768,768]{2,1,0:T(8,128)}, u32[]{:S(2)}, u32[]{:S(2)}) collective-permute-start(f32[2,768,768]{2,1,0:T(8,128)} %weight_grad_up.6), channel_id=1, source_target_pairs={{0,1},{1,0},{2,3},{3,2},{4,5},{5,4},{6,7},{7,6},{8,9},{9,8},{10,11... | collective-permute-start | bytes 14155784 | tf_op jit(solution)/shard_map/ppermute | solution.py:773
  211.3 6.4 %collective-permute-start.12 = (f32[40,768]{1,0:T(8,128)S(1)}, f32[40,768]{1,0:T(8,128)S(1)}, u32[]{:S(2)}, u32[]{:S(2)}) collective-permute-start(f32[40,768]{1,0:T(8,128)S(1)} %concatenate.4), channel_id=1, source_target_pairs={{0,1},{1,0},{2,3},{3,2},{4,5},{5,4},{6,7},{7,6},{8,9},{9,8},{10,11... | collective-permute-start | bytes 368648 | tf_op jit(solution)/shard_map/ppermute | solution.py:813
  217.7 53.2 %collective-permute-start.42 = (f32[8,384,384]{2,1,0:T(8,128)}, f32[8,384,384]{2,1,0:T(8,128)}, u32[]{:S(2)}, u32[]{:S(2)}) collective-permute-start(f32[8,384,384]{2,1,0:T(8,128)} %weight_grad_down.6), channel_id=1, source_target_pairs={{0,1},{1,0},{2,3},{3,2},{4,5},{5,4},{6,7},{7,6},{8,9},{9,8},{10,11... | collective-permute-start | bytes 14155784 | tf_op jit(solution)/shard_map/ppermute | solution.py:773
  217.7 6.2 %collective-permute-start.13 = (f32[40,768]{1,0:T(8,128)S(1)}, f32[40,768]{1,0:T(8,128)S(1)}, u32[]{:S(2)}, u32[]{:S(2)}) collective-permute-start(f32[40,768]{1,0:T(8,128)S(1)} %add.232), channel_id=1, source_target_pairs={{0,2},{1,3},{2,0},{3,1},{4,6},{5,7},{6,4},{7,5},{8,10},{9,11},{10,... | collective-permute-start | bytes 368648 | tf_op jit(solution)/shard_map/ppermute | solution.py:813
  219.4 8.5 %collective-permute-start.5 = (f32[9,8,768]{2,1,0:T(8,128)S(1)}, f32[9,8,768]{2,1,0:T(8,128)}, u32[]{:S(2)}, u32[]{:S(2)}) collective-permute-start(f32[9,8,768]{2,1,0:T(8,128)S(1)} %copy-done.50), channel_id=1, source_target_pairs={{0,3},{1,2},{2,1},{3,0},{4,7},{5,6},{6,5},{7,4},{8,11},{9,10},{10,... | collective-permute-start | bytes 663560 | tf_op jit(solution)/shard_map/ppermute | solution.py:758
  223.9 11.0 %collective-permute-start.3 = (f32[12,8,768]{2,1,0:T(8,128)S(1)}, f32[12,8,768]{2,1,0:T(8,128)S(1)}, u32[]{:S(2)}, u32[]{:S(2)}) collective-permute-start(f32[12,8,768]{2,1,0:T(8,128)S(1)} %copy-done.47), channel_id=1, source_target_pairs={{0,2},{1,3},{2,0},{3,1},{4,6},{5,7},{6,4},{7,5},{8,10},{9,11},{10,... | collective-permute-start | bytes 884744 | tf_op jit(solution)/shard_map/ppermute | solution.py:758
  227.9 7.5 %collective-permute-start.14 = (f32[40,768]{1,0:T(8,128)S(1)}, f32[40,768]{1,0:T(8,128)S(1)}, u32[]{:S(2)}, u32[]{:S(2)}) collective-permute-start(f32[40,768]{1,0:T(8,128)S(1)} %add.233), channel_id=1, source_target_pairs={{0,4},{4,0},{8,12},{12,8},{16,20},{20,16},{24,28},{28,24},{1,5},{5... | collective-permute-start | bytes 368648 | tf_op jit(solution)/shard_map/ppermute | solution.py:813
  234.9 87.5 %collective-permute-start.17 = (f32[2,768,768]{2,1,0:T(8,128)}, f32[2,768,768]{2,1,0:T(8,128)}, u32[]{:S(2)}, u32[]{:S(2)}) collective-permute-start(f32[2,768,768]{2,1,0:T(8,128)} %weight_grad_attn.4), channel_id=1, source_target_pairs={{0,1},{1,0},{2,3},{3,2},{4,5},{5,4},{6,7},{7,6},{8,9},{9,8},{10,11... | collective-permute-start | bytes 14155784 | tf_op jit(solution)/shard_map/ppermute | solution.py:773
  235.4 5.7 collective-permute-start.4
  241.1 7.1 %collective-permute-start.15 = (f32[40,768]{1,0:T(8,128)S(1)}, f32[40,768]{1,0:T(8,128)S(1)}, u32[]{:S(2)}, u32[]{:S(2)}) collective-permute-start(f32[40,768]{1,0:T(8,128)S(1)} %add.234), channel_id=1, source_target_pairs={{0,8},{4,12},{8,0},{12,4},{16,24},{20,28},{24,16},{28,20},{1,9},{5... | collective-permute-start | bytes 368648 | tf_op jit(solution)/shard_map/ppermute | solution.py:813
  248.2 85.4 %collective-permute-start.27 = (f32[2,768,768]{2,1,0:T(8,128)}, f32[2,768,768]{2,1,0:T(8,128)}, u32[]{:S(2)}, u32[]{:S(2)}) collective-permute-start(f32[2,768,768]{2,1,0:T(8,128)} %weight_grad_up.4), channel_id=1, source_target_pairs={{0,1},{1,0},{2,3},{3,2},{4,5},{5,4},{6,7},{7,6},{8,9},{9,8},{10,11... | collective-permute-start | bytes 14155784 | tf_op jit(solution)/shard_map/ppermute | solution.py:773
  253.9 94.3 %collective-permute-start.37 = (f32[8,384,384]{2,1,0:T(8,128)}, f32[8,384,384]{2,1,0:T(8,128)}, u32[]{:S(2)}, u32[]{:S(2)}) collective-permute-start(f32[8,384,384]{2,1,0:T(8,128)} %weight_grad_down.4), channel_id=1, source_target_pairs={{0,1},{1,0},{2,3},{3,2},{4,5},{5,4},{6,7},{7,6},{8,9},{9,8},{10,11... | collective-permute-start | bytes 14155784 | tf_op jit(solution)/shard_map/ppermute | solution.py:773
  263.7 95.2 %collective-permute-start.23 = (f32[8,96,768]{2,1,0:T(8,128)}, f32[8,96,768]{2,1,0:T(8,128)S(1)}, u32[]{:S(2)}, u32[]{:S(2)}) collective-permute-start(f32[8,96,768]{2,1,0:T(8,128)} %bitcast.24), channel_id=1, source_target_pairs={{0,8},{4,12},{8,0},{12,4},{16,24},{20,28},{24,16},{28,20},{1,9},{5... | collective-permute-start | bytes 7077896 | tf_op jit(solution)/shard_map/ppermute | solution.py:683
  270.9 46.8 %collective-permute-start.16 = (f32[40,768]{1,0:T(8,128)S(1)}, f32[40,768]{1,0:T(8,128)S(1)}, u32[]{:S(2)}, u32[]{:S(2)}) collective-permute-start(f32[40,768]{1,0:T(8,128)S(1)} %add.235), channel_id=1, source_target_pairs={{0,16},{4,20},{8,24},{12,28},{16,0},{20,4},{24,8},{28,12},{1,17},{... | collective-permute-start | bytes 368648 | tf_op jit(solution)/shard_map/ppermute | solution.py:813
  317.7 54.5 %collective-permute-start.33 = (f32[8,96,768]{2,1,0:T(8,128)}, f32[8,96,768]{2,1,0:T(8,128)}, u32[]{:S(2)}, u32[]{:S(2)}) collective-permute-start(f32[8,96,768]{2,1,0:T(8,128)} %dynamic-slice_bitcast_fusion), channel_id=1, source_target_pairs={{0,2},{1,3},{2,0},{3,1},{4,6},{5,7},{6,4},{7,5},{8,10},{9,11},{10,... | collective-permute-start | bytes 7077896 | tf_op jit(solution)/shard_map/ppermute | solution.py:683
  322.4 56.9 %collective-permute-start.43 = (f32[8,192,384]{2,1,0:T(8,128)}, f32[8,192,384]{2,1,0:T(8,128)S(1)}, u32[]{:S(2)}, u32[]{:S(2)}) collective-permute-start(f32[8,192,384]{2,1,0:T(8,128)} %bitcast.49), channel_id=1, source_target_pairs={{0,4},{4,0},{8,12},{12,8},{16,20},{20,16},{24,28},{28,24},{1,5},{5... | collective-permute-start | bytes 7077896 | tf_op jit(solution)/shard_map/ppermute | solution.py:683
  333.6 55.0 %collective-permute-start.18 = (f32[8,96,768]{2,1,0:T(8,128)}, f32[8,96,768]{2,1,0:T(8,128)}, u32[]{:S(2)}, u32[]{:S(2)}) collective-permute-start(f32[8,96,768]{2,1,0:T(8,128)} %bitcast.19), channel_id=1, source_target_pairs={{0,8},{4,12},{8,0},{12,4},{16,24},{20,28},{24,16},{28,20},{1,9},{5... | collective-permute-start | bytes 7077896 | tf_op jit(solution)/shard_map/ppermute | solution.py:683
  348.2 74.6 %collective-permute-start.28 = (f32[8,96,768]{2,1,0:T(8,128)}, f32[8,96,768]{2,1,0:T(8,128)}, u32[]{:S(2)}, u32[]{:S(2)}) collective-permute-start(f32[8,96,768]{2,1,0:T(8,128)} %dynamic-slice_bitcast_fusion.1), channel_id=1, source_target_pairs={{0,2},{1,3},{2,0},{3,1},{4,6},{5,7},{6,4},{7,5},{8,10},{9,11},{10,... | collective-permute-start | bytes 7077896 | tf_op jit(solution)/shard_map/ppermute | solution.py:683
  360.2 92.9 %collective-permute-start.38 = (f32[8,192,384]{2,1,0:T(8,128)}, f32[8,192,384]{2,1,0:T(8,128)S(1)}, u32[]{:S(2)}, u32[]{:S(2)}) collective-permute-start(f32[8,192,384]{2,1,0:T(8,128)} %bitcast.43), channel_id=1, source_target_pairs={{0,4},{4,0},{8,12},{12,8},{16,20},{20,16},{24,28},{28,24},{1,5},{5... | collective-permute-start | bytes 7077896 | tf_op jit(solution)/shard_map/ppermute | solution.py:683
  372.2 75.8 %collective-permute-start.24 = (f32[4,96,768]{2,1,0:T(8,128)}, f32[4,96,768]{2,1,0:T(8,128)}, u32[]{:S(2)}, u32[]{:S(2)}) collective-permute-start(f32[4,96,768]{2,1,0:T(8,128)} %get-tuple-element.161), channel_id=1, source_target_pairs={{0,2},{1,3},{2,0},{3,1},{4,6},{5,7},{6,4},{7,5},{8,10},{9,11},{10,... | collective-permute-start | bytes 3538952 | tf_op jit(solution)/shard_map/ppermute | solution.py:690
  379.4 80.3 %collective-permute-start.34 = (f32[4,96,768]{2,1,0:T(8,128)}, f32[4,96,768]{2,1,0:T(8,128)S(1)}, u32[]{:S(2)}, u32[]{:S(2)}) collective-permute-start(f32[4,96,768]{2,1,0:T(8,128)} %get-tuple-element.177), channel_id=1, source_target_pairs={{0,4},{4,0},{8,12},{12,8},{16,20},{20,16},{24,28},{28,24},{1,5},{5... | collective-permute-start | bytes 3538952 | tf_op jit(solution)/shard_map/ppermute | solution.py:690
  388.7 84.7 %collective-permute-start.44 = (f32[4,192,384]{2,1,0:T(8,128)}, f32[4,192,384]{2,1,0:T(8,128)}, u32[]{:S(2)}, u32[]{:S(2)}) collective-permute-start(f32[4,192,384]{2,1,0:T(8,128)} %get-tuple-element.193), channel_id=1, source_target_pairs={{0,2},{1,3},{2,0},{3,1},{4,6},{5,7},{6,4},{7,5},{8,10},{9,11},{10,... | collective-permute-start | bytes 3538952 | tf_op jit(solution)/shard_map/ppermute | solution.py:690
  422.8 103.4 %collective-permute-start.19 = (f32[4,96,768]{2,1,0:T(8,128)}, f32[4,96,768]{2,1,0:T(8,128)}, u32[]{:S(2)}, u32[]{:S(2)}) collective-permute-start(f32[4,96,768]{2,1,0:T(8,128)} %get-tuple-element.152), channel_id=1, source_target_pairs={{0,4},{4,0},{8,12},{12,8},{16,20},{20,16},{24,28},{28,24},{1,5},{5... | collective-permute-start | bytes 3538952 | tf_op jit(solution)/shard_map/ppermute | solution.py:690
  448.0 82.0 %collective-permute-start.29 = (f32[4,96,768]{2,1,0:T(8,128)}, f32[4,96,768]{2,1,0:T(8,128)}, u32[]{:S(2)}, u32[]{:S(2)}) collective-permute-start(f32[4,96,768]{2,1,0:T(8,128)} %get-tuple-element.169), channel_id=1, source_target_pairs={{0,4},{4,0},{8,12},{12,8},{16,20},{20,16},{24,28},{28,24},{1,5},{5... | collective-permute-start | bytes 3538952 | tf_op jit(solution)/shard_map/ppermute | solution.py:690
  453.1 60.8 %collective-permute-start.25 = (f32[2,96,768]{2,1,0:T(8,128)}, f32[2,96,768]{2,1,0:T(8,128)S(1)}, u32[]{:S(2)}, u32[]{:S(2)}) collective-permute-start(f32[2,96,768]{2,1,0:T(8,128)} %get-tuple-element.163), channel_id=1, source_target_pairs={{0,4},{4,0},{8,12},{12,8},{16,20},{20,16},{24,28},{28,24},{1,5},{5... | collective-permute-start | bytes 1769480 | tf_op jit(solution)/shard_map/ppermute | solution.py:690
  459.6 74.8 %collective-permute-start.39 = (f32[4,192,384]{2,1,0:T(8,128)}, f32[4,192,384]{2,1,0:T(8,128)S(1)}, u32[]{:S(2)}, u32[]{:S(2)}) collective-permute-start(f32[4,192,384]{2,1,0:T(8,128)} %get-tuple-element.185), channel_id=1, source_target_pairs={{0,2},{1,3},{2,0},{3,1},{4,6},{5,7},{6,4},{7,5},{8,10},{9,11},{10,... | collective-permute-start | bytes 3538952 | tf_op jit(solution)/shard_map/ppermute | solution.py:690
  473.3 65.3 %collective-permute-start.35 = (f32[2,96,768]{2,1,0:T(8,128)}, f32[2,96,768]{2,1,0:T(8,128)S(1)}, u32[]{:S(2)}, u32[]{:S(2)}) collective-permute-start(f32[2,96,768]{2,1,0:T(8,128)} %get-tuple-element.179), channel_id=1, source_target_pairs={{0,8},{4,12},{8,0},{12,4},{16,24},{20,28},{24,16},{28,20},{1,9},{5... | collective-permute-start | bytes 1769480 | tf_op jit(solution)/shard_map/ppermute | solution.py:690
  477.9 44.3 %copy-start.38 = (f32[1,2,4,768]{3,2,1,0:T(4,128)S(1)}, f32[1,2,4,768]{3,2,1,0:T(4,128)}, u32[]{:S(2)}) copy-start(f32[1,2,4,768]{3,2,1,0:T(4,128)} %slice_bitcast_fusion.5) | copy-start | bytes 73732
  514.7 27.9 %collective-permute-start.45 = (f32[2,192,384]{2,1,0:T(8,128)}, f32[2,192,384]{2,1,0:T(8,128)S(1)}, u32[]{:S(2)}, u32[]{:S(2)}) collective-permute-start(f32[2,192,384]{2,1,0:T(8,128)} %get-tuple-element.195), channel_id=1, source_target_pairs={{0,8},{4,12},{8,0},{12,4},{16,24},{20,28},{24,16},{28,20},{1,9},{5... | collective-permute-start | bytes 1769480 | tf_op jit(solution)/shard_map/ppermute | solution.py:690
  526.2 22.1 %collective-permute-start.26 = (f32[1,96,768]{2,1,0:T(8,128)}, f32[1,96,768]{2,1,0:T(8,128)S(1)}, u32[]{:S(2)}, u32[]{:S(2)}) collective-permute-start(f32[1,96,768]{2,1,0:T(8,128)} %get-tuple-element.165), channel_id=1, source_target_pairs={{0,16},{4,20},{8,24},{12,28},{16,0},{20,4},{24,8},{28,12},{1,17},{... | collective-permute-start | bytes 884744 | tf_op jit(solution)/shard_map/ppermute | solution.py:690
  530.0 19.2 %collective-permute-start.20 = (f32[2,96,768]{2,1,0:T(8,128)}, f32[2,96,768]{2,1,0:T(8,128)S(1)}, u32[]{:S(2)}, u32[]{:S(2)}) collective-permute-start(f32[2,96,768]{2,1,0:T(8,128)} %get-tuple-element.154), channel_id=1, source_target_pairs={{0,2},{1,3},{2,0},{3,1},{4,6},{5,7},{6,4},{7,5},{8,10},{9,11},{10,... | collective-permute-start | bytes 1769480 | tf_op jit(solution)/shard_map/ppermute | solution.py:690
  534.4 37.6 %collective-permute-start.30 = (f32[2,96,768]{2,1,0:T(8,128)}, f32[2,96,768]{2,1,0:T(8,128)S(1)}, u32[]{:S(2)}, u32[]{:S(2)}) collective-permute-start(f32[2,96,768]{2,1,0:T(8,128)} %get-tuple-element.171), channel_id=1, source_target_pairs={{0,8},{4,12},{8,0},{12,4},{16,24},{20,28},{24,16},{28,20},{1,9},{5... | collective-permute-start | bytes 1769480 | tf_op jit(solution)/shard_map/ppermute | solution.py:690
  538.6 43.1 %collective-permute-start.40 = (f32[2,192,384]{2,1,0:T(8,128)}, f32[2,192,384]{2,1,0:T(8,128)S(1)}, u32[]{:S(2)}, u32[]{:S(2)}) collective-permute-start(f32[2,192,384]{2,1,0:T(8,128)} %get-tuple-element.187), channel_id=1, source_target_pairs={{0,8},{4,12},{8,0},{12,4},{16,24},{20,28},{24,16},{28,20},{1,9},{5... | collective-permute-start | bytes 1769480 | tf_op jit(solution)/shard_map/ppermute | solution.py:690
  542.6 42.7 %collective-permute-start.36 = (f32[1,96,768]{2,1,0:T(8,128)}, f32[1,96,768]{2,1,0:T(8,128)S(1)}, u32[]{:S(2)}, u32[]{:S(2)}) collective-permute-start(f32[1,96,768]{2,1,0:T(8,128)} %get-tuple-element.181), channel_id=1, source_target_pairs={{0,16},{4,20},{8,24},{12,28},{16,0},{20,4},{24,8},{28,12},{1,17},{... | collective-permute-start | bytes 884744 | tf_op jit(solution)/shard_map/ppermute | solution.py:690
  548.4 37.0 %collective-permute-start.46 = (f32[1,192,384]{2,1,0:T(8,128)}, f32[1,192,384]{2,1,0:T(8,128)S(1)}, u32[]{:S(2)}, u32[]{:S(2)}) collective-permute-start(f32[1,192,384]{2,1,0:T(8,128)} %get-tuple-element.197), channel_id=1, source_target_pairs={{0,16},{4,20},{8,24},{12,28},{16,0},{20,4},{24,8},{28,12},{1,17},{... | collective-permute-start | bytes 884744 | tf_op jit(solution)/shard_map/ppermute | solution.py:690
  552.7 42.2 %collective-permute-start.21 = (f32[1,96,768]{2,1,0:T(8,128)}, f32[1,96,768]{2,1,0:T(8,128)S(1)}, u32[]{:S(2)}, u32[]{:S(2)}) collective-permute-start(f32[1,96,768]{2,1,0:T(8,128)} %get-tuple-element.156), channel_id=1, source_target_pairs={{0,16},{4,20},{8,24},{12,28},{16,0},{20,4},{24,8},{28,12},{1,17},{... | collective-permute-start | bytes 884744 | tf_op jit(solution)/shard_map/ppermute | solution.py:690
  575.7 25.5 %collective-permute-start.31 = (f32[1,96,768]{2,1,0:T(8,128)}, f32[1,96,768]{2,1,0:T(8,128)S(1)}, u32[]{:S(2)}, u32[]{:S(2)}) collective-permute-start(f32[1,96,768]{2,1,0:T(8,128)} %get-tuple-element.173), channel_id=1, source_target_pairs={{0,16},{4,20},{8,24},{12,28},{16,0},{20,4},{24,8},{28,12},{1,17},{... | collective-permute-start | bytes 884744 | tf_op jit(solution)/shard_map/ppermute | solution.py:690
  585.3 22.0 %collective-permute-start.41 = (f32[1,192,384]{2,1,0:T(8,128)}, f32[1,192,384]{2,1,0:T(8,128)S(1)}, u32[]{:S(2)}, u32[]{:S(2)}) collective-permute-start(f32[1,192,384]{2,1,0:T(8,128)} %get-tuple-element.189), channel_id=1, source_target_pairs={{0,16},{4,20},{8,24},{12,28},{16,0},{20,4},{24,8},{28,12},{1,17},{... | collective-permute-start | bytes 884744 | tf_op jit(solution)/shard_map/ppermute | solution.py:690
  (50 other events, 272.3 us)

commit v2 on v1

v2 whole, which is shorter than its diff:
```python
import functools

import jax
import jax.numpy as jnp
from jax import lax
from jax.experimental import pallas as pl
from jax.experimental.pallas import tpu as pltpu
from jax.sharding import PartitionSpec as P

HEADS = 24
HD = 32
SIDE = 7
T = SIDE * SIDE
TP = 56
TQ = 64
D = 768
FF = 3072
C = 8
ROWS = T * C
PAD_ROWS = TQ * C
HALF = C // 2
PIECE = T * HALF
LANE = 128
NG = D // LANE
PER = LANE // HD
GT = PER * TQ
EPSILON = 1e-05
SCALE = HD ** (-0.5)
NEG = -1e30
QCH = 384
FCH = 768
N_Q = 3 * D // QCH
N_F = FF // FCH
W_UP = D // 2
MINE = D // 4
VMEM_LIMIT = 58 << 20
COST = 0.4
F32 = jnp.float32
BF16 = jnp.bfloat16

TAIL_K = 0.3
TAIL = (
    0.11963200491345692,
    0.12071217642148169,
    0.10017566554041868,
    0.12769280877164998,
    -0.052036176065482394,
    0.20455934198696718,
    -0.15616004916725648,
    0.035424145900813254,
)
INV_SQRT_2PI = 0.3989422804014327

def nt(left, right):
    return lax.dot_general(left, right, (((1,), (1,)), ((), ())), preferred_element_type=F32)


def tn(left, right):
    return lax.dot_general(left, right, (((0,), (0,)), ((), ())), preferred_element_type=F32)


def nn(left, right):
    return jnp.dot(left, right, preferred_element_type=F32)


def norm_parts(values):
    average = jnp.mean(values, axis=-1, keepdims=True)
    centered = values - average
    inverse = lax.rsqrt(jnp.mean(centered * centered, axis=-1, keepdims=True) + EPSILON)
    return centered * inverse, inverse


def norm_back(grad_out, normed, inverse, gain):
    scaled = grad_out * gain
    return inverse * (
        scaled
        - jnp.mean(scaled, axis=-1, keepdims=True)
        - normed * jnp.mean(scaled * normed, axis=-1, keepdims=True)
    )


def gelu_parts(a):
    bell = jnp.exp(-0.5 * a * a)
    size = jnp.abs(a)
    t = 1.0 / (1.0 + TAIL_K * size)
    poly = jnp.full_like(t, TAIL[-1])
    for coef in TAIL[-2::-1]:
        poly = poly * t + coef
    tail = bell * (t * poly)
    phi = jnp.where(a < 0, tail, 1.0 - tail)
    return a * phi, phi + a * (INV_SQRT_2PI * bell)


def head_masks(rows):
    lanes = lax.broadcasted_iota(jnp.int32, (rows, LANE), 1)
    return [(lanes >= HD * h) & (lanes < HD * (h + 1)) for h in range(PER)]


def spread(values, ones):
    return jnp.concatenate([values * m for m in ones], axis=0)


def gather_heads(stacked, masks):
    out = stacked[(PER - 1) * TQ : (PER - 1) * TQ + TP]
    for h in range(PER - 2, -1, -1):
        out = jnp.where(masks[h], stacked[h * TQ : h * TQ + TP], out)
    return out


def soft(scores):
    e = jnp.exp(scores - jnp.max(scores, axis=0, keepdims=True))
    return e * (1.0 / jnp.sum(e, axis=0, keepdims=True))


def colsum(values):
    return jnp.sum(values, axis=0, keepdims=True)


def rows_of(w, n=T, stride=C):
    return pl.ds(w, n, stride=stride)


def lanes_at(n, width):
    return pl.ds(pl.multiple_of(n * width, width), width)


def put_rolled(dest, source, a, back):
    shift, kept = (-3, range(3, 7)) if back else (3, range(0, 4))
    for i in range(SIDE):
        for j in range(SIDE):
            half = a if i in kept else 1 - a
            tile = source[half, SIDE * ((i + shift) % SIDE) + (j + shift) % SIDE]
            if j not in kept:
                tile = pltpu.roll(tile, HALF, 0)
            t = SIDE * i + j
            dest[C * t : C * (t + 1), :] = tile


ANY = pl.BlockSpec(memory_space=pl.ANY)
VM = pl.BlockSpec(memory_space=pltpu.VMEM)
SM = pl.BlockSpec(memory_space=pltpu.SMEM)


def cost(micros):
    return pl.CostEstimate(flops=int(micros * COST * 1.15e9), bytes_accessed=0, transcendentals=0)


def shape(dims, dtype):
    return jax.ShapeDtypeStruct(dims, dtype)


def fixed(dims, single=False):
    mode = dict(pipeline_mode=pl.Buffered(1)) if single else {}
    return pl.BlockSpec(dims, lambda *_: (0,) * len(dims), **mode)


def per_half(dims):
    return pl.BlockSpec((1, *dims), lambda a, *_: (a, *(0,) * len(dims)))


def call(body, args, in_specs, outs, out_specs, estimate, name, after=(), grid=(), scalars=0, scratch=(), reuse=False):
    n_in, n_after = len(args), len(after)

    def wrapped(*refs):
        return body(*refs[:n_in], *refs[n_in + n_after :])

    return pl.pallas_call(
        wrapped,
        grid_spec=pltpu.PrefetchScalarGridSpec(
            num_scalar_prefetch=scalars,
            grid=grid,
            in_specs=list(in_specs) + [ANY] * n_after,
            out_specs=out_specs,
            scratch_shapes=list(scratch),
        ),
        out_shape=outs,
        input_output_aliases={n_in + k: k for k in range(n_after)} if reuse else {},
        compiler_params=pltpu.CompilerParams(vmem_limit_bytes=VMEM_LIMIT),
        cost_estimate=estimate,
        name=name,
    )(*args, *after)


def crop_rows(core, count, crops, after=()):
    def body(at, n, src, mine, other, s):
        wide = src[...].astype(F32).reshape(ROWS, D)
        for g in range(NG):
            s[g] = wide[:, LANE * g : LANE * (g + 1)]
        for k in range(HALF):
            for out, c in ((mine, at[0]), (other, 1 - at[0])):
                crop = HALF * c + k
                keep = jnp.where(crop < n[0], 1.0, 0.0).astype(F32)
                for g in range(NG):
                    out[g, rows_of(k, stride=HALF), :] = s[g, rows_of(crop), :] * keep

    return call(
        body, (core, count, crops), [SM, SM, VM], [shape((NG, PIECE, LANE), F32)] * 2, [VM] * 2, cost(2.5), "crop_rows", after, scratch=[pltpu.VMEM((NG, ROWS, LANE), F32)],
    )


def weave(dest, pieces):
    for b, piece in enumerate(pieces):
        for k in range(HALF):
            for g in range(NG):
                dest[g, rows_of(HALF * b + k), :] = piece[g, rows_of(k, stride=HALF), :]


def join_pieces(x_at, pieces, after=()):
    def body(x, *refs):
        *src, out, s = refs
        for k in range(2):
            weave(s, src[2 * k : 2 * k + 2])
            for g in range(NG):
                out[x[0] ^ k, :, :, LANE * g : LANE * (g + 1)] = s[g].reshape(T, C, LANE)

    return call(
        body, (x_at, *pieces), [SM] + [VM] * 4, shape((2, T, C, D), F32), VM, cost(4), "join_pieces", after,
        scratch=[pltpu.VMEM((NG, ROWS, LANE), F32)],
    )


def own_quadrants(x_at, both_halves, rolled, after=()):
    def body(x, src, mine, other, full, s):
        if rolled:
            put_rolled(full, src, x[0], True)
        else:
            full[...] = src[x[0]].reshape(ROWS, D)
        for g in range(NG):
            s[g] = full[:, LANE * g : LANE * (g + 1)]
        for b, out in enumerate((mine, other)):
            for k in range(HALF):
                for g in range(NG):
                    out[g, rows_of(k, stride=HALF), :] = s[g, rows_of(HALF * b + k), :]

    return call(
        body, (x_at, both_halves), [SM, VM], [shape((NG, PIECE, LANE), F32)] * 2, [VM] * 2, cost(3), "own_quadrants", after, scratch=[pltpu.VMEM((ROWS, D), F32), pltpu.VMEM((NG, ROWS, LANE), F32)],
    )


def token_major(core, count, mine, theirs, after=()):
    def body(at, n, a, b, out, s):
        for k in range(HALF):
            for src, c in ((a, at[0]), (b, 1 - at[0])):
                crop = HALF * c + k
                keep = jnp.where(crop < n[0], 1.0, 0.0).astype(F32)
                for g in range(NG):
                    s[g, rows_of(crop), :] = src[g, rows_of(k, stride=HALF), :] * keep
        for g in range(NG):
            out[:, :, LANE * g : LANE * (g + 1)] = s[g].reshape(T, C, LANE).astype(BF16)

    return call(
        body, (core, count, mine, theirs), [SM, SM, VM, VM], shape((T, C, D), BF16), VM, cost(2.5), "token_major", after, scratch=[pltpu.VMEM((NG, ROWS, LANE), F32)],
    )


def crop_major(core, mine, theirs, after=()):
    def body(at, a, b, out):
        for k in range(HALF):
            for src, c in ((a, at[0]), (b, 1 - at[0])):
                for g in range(NG):
                    out[pl.ds((HALF * c + k) * (T * NG) + g, T, stride=NG), :] = src[g, rows_of(k, stride=HALF), :]

    return call(
        body, (core, mine, theirs), [SM, VM, VM], shape((C * T * NG, LANE), F32), VM, cost(2.5), "crop_major", after,
    )


def fwd_body(b, *refs):
    a = pl.program_id(0)
    if b == 0:
        _, p0, p1, *rest = refs
    else:
        src, mask, *rest = refs
    (
        bias, ln1g, ln1b, bq, bv, bout, ln2g, ln2b, bup, bdown,
        wqkv_h, wout_h, wup_h, wdown_h,
        z_o, h_o, qkvc_o, o_o, y_o, h2_o, g_o, gp_o, zn_o,
        wqkv, wout, wup, wdown, qkv_s, o_s, bqkv, acc, bias_s, sem_q, sem_o, sem_u, sem_d,
    ) = rest

    def cp_q(n):
        return pltpu.make_async_copy(
            wqkv_h.at[b, :, lanes_at(n, QCH)], wqkv.at[:, lanes_at(n, QCH)], sem_q.at[n]
        )

    def cp_u(n):
        return pltpu.make_async_copy(
            wup_h.at[b, :, lanes_at(n, FCH)], wup.at[:, lanes_at(n, FCH)], sem_u.at[n]
        )

    def cp_d(n):
        return pltpu.make_async_copy(
            wdown_h.at[b, lanes_at(n, FCH), :], wdown.at[lanes_at(n, FCH), :], sem_d.at[n]
        )

    cp_o = pltpu.make_async_copy(wout_h.at[b], wout, sem_o)

    def wait(copy):
        @pl.when(a == 0)
        def _():
            copy.wait()

    @pl.when(a == 0)
    def _():
        for n in range(N_Q):
            cp_q(n).start()
        cp_o.start()
        for n in range(N_F):
            cp_u(n).start()
            cp_d(n).start()
        bqkv[:, 0:D] = bq[b : b + 1, :]
        bqkv[:, D : 2 * D] = jnp.zeros((1, D), F32)
        bqkv[:, 2 * D :] = bv[b : b + 1, :]
        qkv_s[:, ROWS:, :] = jnp.zeros((3 * NG, PAD_ROWS - ROWS, LANE), F32)

    if b == 0:
        weave(o_s, (p0, p1))
        for g in range(NG):
            z_o[0, :, LANE * g : LANE * (g + 1)] = o_s[g, 0:ROWS, :]
    else:
        put_rolled(z_o.at[0], src, a, False)
        for w in range(2):
            for g in range(NG):
                bias_s[w * NG + g] = bias[NG + g] + mask[0, w]
    normed, _ = norm_parts(z_o[0])
    h_o[0] = (normed * ln1g[b : b + 1, :] + ln1b[b : b + 1, :]).astype(BF16)

    def qkv_step(n, _):
        wait(cp_q(n))
        joint = nn(h_o[0], wqkv[:, lanes_at(n, QCH)]) + bqkv[:, lanes_at(n, QCH)]
        joint = joint * jnp.where(n < D // QCH, SCALE, 1.0)
        joint = joint.astype(BF16).astype(F32)
        for k in range(QCH // LANE):
            qkv_s[n * (QCH // LANE) + k, 0:ROWS, :] = joint[:, LANE * k : LANE * (k + 1)]
        return 0

    lax.fori_loop(0, N_Q, qkv_step, 0)
    masks = head_masks(TP)
    ones = [m.astype(F32).astype(BF16) for m in head_masks(TQ)]

    def attend(w, _):
        for g in range(NG):
            q = qkv_s[g, rows_of(w, TQ), :].astype(BF16)
            k = qkv_s[NG + g, rows_of(w, TP), :].astype(BF16)
            v = qkv_s[2 * NG + g, rows_of(w, TP), :].astype(BF16)
            qkvc_o[0, w, g] = q
            qkvc_o[0, w, NG + g, 0:TP] = k
            qkvc_o[0, w, 2 * NG + g, 0:TP] = v
            added = bias[g] if b == 0 else bias_s[w // HALF * NG + g]
            probs = soft(nt(k, spread(q, ones)) + added)
            o_s[g, rows_of(w, TP), :] = gather_heads(tn(probs.astype(BF16), v), masks)
        return 0

    lax.fori_loop(0, C, attend, 0, unroll=2)
    for g in range(NG):
        o_o[0, :, LANE * g : LANE * (g + 1)] = o_s[g, 0:ROWS, :].astype(BF16)
    wait(cp_o)
    y_o[0] = z_o[0] + (nn(o_o[0], wout[...]) + bout[b : b + 1, :])
    normed, _ = norm_parts(y_o[0])
    h2_o[0] = (normed * ln2g[b : b + 1, :] + ln2b[b : b + 1, :]).astype(BF16)
    acc[...] = jnp.zeros_like(acc)

    def mlp_step(n, _):
        wait(cp_u(n))
        up = nn(h2_o[0], wup[:, lanes_at(n, FCH)]) + bup[b : b + 1, lanes_at(n, FCH)]
        act, slope = gelu_parts(up)
        act = act.astype(BF16)
        g_o[0, :, lanes_at(n, FCH)] = act
        gp_o[0, :, lanes_at(n, FCH)] = slope.astype(BF16)
        wait(cp_d(n))
        acc[...] += nn(act, wdown[lanes_at(n, FCH), :])
        return 0

    lax.fori_loop(0, N_F, mlp_step, 0)
    zn_o[0] = (y_o[0] + (acc[...] + bdown[b : b + 1, :])).reshape(T, C, D)


def block_fwd(b, sources, bias, p, which=None, after=()):
    outs = [
        shape((2, ROWS, D), F32),
        shape((2, ROWS, D), BF16),
        shape((2, C, 3 * NG, TQ, LANE), BF16),
        shape((2, ROWS, D), BF16),
        shape((2, ROWS, D), F32),
        shape((2, ROWS, D), BF16),
        shape((2, ROWS, FF), BF16),
        shape((2, ROWS, FF), BF16),
        shape((2, T, C, D), F32),
    ]
    if b == 0:
        specs = [fixed((NG, PIECE, LANE), True)] * 2
        out_specs = [
            pl.BlockSpec((1, *o.shape[1:]), lambda a, s, n=len(o.shape) - 1: (s[0] ^ which, *(0,) * n)) for o in outs
        ]
    else:
        specs = [fixed((2, T, C, D), True), per_half((2, TP, GT))]
        out_specs = [per_half(o.shape[1:]) for o in outs]
    small = (bias, p["ln1_gain"], p["ln1_bias"], p["b_query"], p["b_value"], p["b_out"],
             p["ln2_gain"], p["ln2_bias"], p["b_up"], p["b_down"])
    big = (p["w_qkv"], p["w_out"], p["w_up"], p["w_down"])
    return call(
        functools.partial(fwd_body, b),
        (*sources, *small, *big),
        specs + [fixed(v.shape, True) for v in small] + [ANY] * 4,
        outs,
        out_specs,
        cost(25 if which is not None else 46),
        f"forward_{b}",
        after,
        grid=(2 if which is None else 1,),
        scalars=int(which is not None),
        reuse=which == 1,
        scratch=[
            pltpu.VMEM((D, 3 * D), BF16),
            pltpu.VMEM((D, D), BF16),
            pltpu.VMEM((D, FF), BF16),
            pltpu.VMEM((FF, D), BF16),
            pltpu.VMEM((3 * NG, PAD_ROWS, LANE), F32),
            pltpu.VMEM((NG, PAD_ROWS, LANE), F32),
            pltpu.VMEM((1, 3 * D), F32),
            pltpu.VMEM((ROWS, D), F32),
            pltpu.VMEM((2 * NG, TP, GT), F32),
            pltpu.SemaphoreType.DMA((N_Q,)),
            pltpu.SemaphoreType.DMA,
            pltpu.SemaphoreType.DMA((N_F,)),
            pltpu.SemaphoreType.DMA((N_F,)),
        ],
    )


def mlp_back_body(b, x_at, src, y, gp, ln2g, wdown_h, wup_h, dd_o, da_o, dy_o, dyr_o, sv_o,
                  wdown, wup, acc, dz, dd, sem_d, sem_u):
    a = pl.program_id(0)

    def cp_u(n):
        return pltpu.make_async_copy(
            wup_h.at[b, :, lanes_at(n, D)], wup.at[:, lanes_at(n, D)], sem_u.at[n]
        )

    def cp_d(n):
        return pltpu.make_async_copy(
            wdown_h.at[b, lanes_at(n, D), :], wdown.at[lanes_at(n, D), :], sem_d.at[n]
        )

    def wait(copy):
        @pl.when(a == 0)
        def _():
            copy.wait()

    @pl.when(a == 0)
    def _():
        for n in range(4):
            cp_d(n).start()
            cp_u(n).start()
        sv_o[...] = jnp.zeros_like(sv_o)

    put_rolled(dz, src, a, b == 0)
    low = dz[...].astype(BF16)
    dd[...] = low
    sv_o[3:4, :] += colsum(low.astype(F32))
    for x in range(2):

        @pl.when(x_at[0] == x)
        def _():
            for c in range(2):
                w = 2 * x + c
                dd_o[c, 0] = dd[:, MINE * w : MINE * (w + 1)]

    acc[...] = jnp.zeros_like(acc)

    def step(n, _):
        wait(cp_d(n))
        grad_act = nt(dd[...], wdown[lanes_at(n, D), :])
        da = (grad_act * gp[0, :, lanes_at(n, D)].astype(F32)).astype(BF16)

        @pl.when(n // 2 == x_at[0])
        def _():
            da_o[0, :, lanes_at(n % 2, D)] = da

        sv_o[pl.ds(4 + n, 1), :] += colsum(da.astype(F32))
        wait(cp_u(n))
        acc[...] += nt(da, wup[:, lanes_at(n, D)])
        return 0

    lax.fori_loop(0, 4, step, 0)
    dh2 = acc[...]
    normed, inverse = norm_parts(y[0])
    sv_o[0:1, :] += colsum(dh2 * normed)
    sv_o[1:2, :] += colsum(dh2)
    dy = dz[...] + norm_back(dh2, normed, inverse, ln2g[b : b + 1, :])
    dy_o[0] = dy
    low = dy.astype(BF16)
    dyr_o[0] = low
    sv_o[2:3, :] += colsum(low.astype(F32))


def mlp_back(b, x_at, src, y, gp, p, after=()):
    return call(
        functools.partial(mlp_back_body, b),
        (x_at, src, y, gp, p["ln2_gain"], p["w_down"], p["w_up"]),
        [SM, fixed((2, T, C, D), True), per_half((ROWS, D)), per_half((ROWS, FF)), fixed((2, D)), ANY, ANY],
        [
            shape((2, 2, ROWS, MINE), BF16),
            shape((2, ROWS, FF // 2), BF16),
            shape((2, ROWS, D), F32),
            shape((2, ROWS, D), BF16),
            shape((8, D), F32),
        ],
        [
            pl.BlockSpec((2, 1, ROWS, MINE), lambda a: (0, a, 0, 0)),
            per_half((ROWS, FF // 2)),
            per_half((ROWS, D)),
            per_half((ROWS, D)),
            fixed((8, D)),
        ],
        cost(23),
        f"mlp_back_{b}",
        after,
        grid=(2,),
        scratch=[
            pltpu.VMEM((FF, D), BF16),
            pltpu.VMEM((D, FF), BF16),
            pltpu.VMEM((ROWS, D), F32),
            pltpu.VMEM((ROWS, D), F32),
            pltpu.VMEM((ROWS, D), BF16),
            pltpu.SemaphoreType.DMA((4,)),
            pltpu.SemaphoreType.DMA((4,)),
        ],
    )


TABLE = 256
BLOCK = (D // 8, D)


def table_sums(ds, moved):
    row = lax.broadcasted_iota(jnp.int32, (GT, PER * LANE), 0)
    col = lax.broadcasted_iota(jnp.int32, (GT, PER * LANE), 1)
    t = row & (TQ - 1)
    i = sum((t >= SIDE * k).astype(jnp.int32) for k in range(1, SIDE))
    there = (row >> 6 == col >> 7) & (t < T) & ((col & (LANE - 1)) == t + 6 * i)
    onehot = there.astype(F32).astype(BF16)
    moved[:, NG * TP :, :] = jnp.zeros((PER, (8 - NG) * TP, LANE), F32)
    for g in range(NG):
        rest = ds[g]
        total = jnp.zeros((TP, PER * LANE), F32)
        for _ in range(3):
            part = rest.astype(BF16)
            total += nn(part, onehot)
            rest = rest - part.astype(F32)
        for h in range(PER):
            moved[h, TP * g : TP * (g + 1), :] = total[:, LANE * h : LANE * (h + 1)]


def sum_table(moved, put):
    for h in range(PER):
        total = jnp.zeros((8, TABLE), F32)
        for u in range(T):
            v = moved[h, pl.ds(u, 8, stride=TP), :]
            shift = 13 * (6 - u // SIDE) + 6 - u % SIDE
            total += pltpu.roll(jnp.concatenate([v, jnp.zeros_like(v)], axis=1), shift, 1)
        put(h, total)


def attn_back_body(b, x_at, dyr, qkvc, dy, z, *refs):
    if b == 1:
        mask, *refs = refs
    bias, ln1g, *refs = refs
    if b == 0:
        sv_m0, sv_a1, sv_m1, table1, *refs = refs
    (wout_h, wqkv_h, r3_o, sv_o, sum_o, grad_o,
     wout, wqkv, do_s, dqkv_s, dq, acc, bias_s, ds_o, moved, sem_o, sem_q) = refs
    a = pl.program_id(0)
    cp_o = pltpu.make_async_copy(wout_h.at[b], wout, sem_o)

    def cp_q(n):
        return pltpu.make_async_copy(
            wqkv_h.at[b, :, lanes_at(n, QCH)], wqkv.at[:, lanes_at(n, QCH)], sem_q.at[n]
        )

    def wait(copy):
        @pl.when(a == 0)
        def _():
            copy.wait()

    @pl.when(a == 0)
    def _():
        cp_o.start()
        for n in range(N_Q):
            cp_q(n).start()
        do_s[:, ROWS:, :] = jnp.zeros((NG, PAD_ROWS - ROWS, LANE), F32)
        ds_o[...] = jnp.zeros_like(ds_o)
        sv_o[...] = jnp.zeros_like(sv_o)

    if b == 1:
        for w in range(2):
            for g in range(NG):
                bias_s[w * NG + g] = bias[NG + g] + mask[0, w]
    wait(cp_o)
    do = nt(dyr[0], wout[...]).astype(BF16).astype(F32)
    for g in range(NG):
        do_s[g, 0:ROWS, :] = do[:, LANE * g : LANE * (g + 1)]
    masks = head_masks(TP)
    ones = [m.astype(F32).astype(BF16) for m in head_masks(TQ)]

    def attend(w, _):
        for g in range(NG):
            q = qkvc[0, w, g]
            k = qkvc[0, w, NG + g, 0:TP]
            v = qkvc[0, w, 2 * NG + g, 0:TP]
            q_wide = spread(q, ones)
            do_wide = spread(do_s[g, rows_of(w, TQ), :].astype(BF16), ones)
            added = bias[g] if b == 0 else bias_s[w // HALF * NG + g]
            probs = soft(nt(k, q_wide) + added)
            weighted = probs * nt(v, do_wide)
            ds = weighted - probs * jnp.sum(weighted, axis=0, keepdims=True)
            ds_o[g] += ds
            low = ds.astype(BF16)
            dqkv_s[g, rows_of(w, TP), :] = gather_heads(tn(low, k), masks) * SCALE
            dqkv_s[NG + g, rows_of(w, TP), :] = nn(low, q_wide)
            dqkv_s[2 * NG + g, rows_of(w, TP), :] = nn(probs.astype(BF16), do_wide)
        return 0

    lax.fori_loop(0, C, attend, 0, unroll=2)
    for g in range(3 * NG):
        dq[:, LANE * g : LANE * (g + 1)] = dqkv_s[g, 0:ROWS, :].astype(BF16)
    sv_o[2:3, :] += colsum(dq[:, 0:D].astype(F32))
    sv_o[3:4, :] += colsum(dq[:, 2 * D :].astype(F32))
    acc[...] = jnp.zeros_like(acc)

    def step(n, _):
        wait(cp_q(n))
        acc[...] += nt(dq[:, lanes_at(n, QCH)], wqkv[:, lanes_at(n, QCH)])
        return 0

    lax.fori_loop(0, N_Q, step, 0)
    for x in range(2):

        @pl.when(x_at[0] == x)
        def _():
            for c in range(2):
                w = 2 * x + c
                r3_o[c, 0] = jnp.concatenate(
                    [dq[:, 3 * MINE * w : 3 * MINE * (w + 1)], dyr[0, :, MINE * w : MINE * (w + 1)]], axis=1
                )

    dh = acc[...]
    normed, inverse = norm_parts(z[0])
    sv_o[0:1, :] += colsum(dh * normed)
    sv_o[1:2, :] += colsum(dh)
    grad_o[0] = (dy[0] + norm_back(dh, normed, inverse, ln1g[b : b + 1, :])).reshape(T, C, D)

    @pl.when(a == 1)
    def _():
        table_sums(ds_o, moved)
        if b == 1:
            sum_table(moved, lambda h, v: sum_o.__setitem__(h, v))
            return
        sum_o[...] = jnp.zeros_like(sum_o)
        for at, ref in ((0, sv_o), (4, sv_m0), (12, sv_a1), (16, sv_m1)):
            sum_o[at : at + ref.shape[0], :] = ref[...]
        for h in range(PER):
            sum_o[24 + 8 * h : 32 + 8 * h, TABLE : 2 * TABLE] = table1[h]
        sum_table(moved, lambda h, v: sum_o.__setitem__((slice(24 + 8 * h, 32 + 8 * h), slice(0, TABLE)), v))


def attn_back(b, x_at, dyr, qkvc, dy, z, mask, bias, p, sums=(), after=()):
    masks = [mask] if b else []
    sum_shape = (PER, 8, TABLE) if b else BLOCK
    return call(
        functools.partial(attn_back_body, b),
        (x_at, dyr, qkvc, dy, z, *masks, bias, p["ln1_gain"], *sums, p["w_out"], p["w_qkv"]),
        [SM, per_half((ROWS, D)), per_half((C, 3 * NG, TQ, LANE)), per_half((ROWS, D)), per_half((ROWS, D))]
        + [per_half((2, TP, GT))] * b
        + [fixed(bias.shape, True), fixed((2, D)), *(fixed(v.shape) for v in sums), ANY, ANY],
        [shape((2, 2, ROWS, D), BF16), shape((4, D), F32), shape(sum_shape, F32), shape((2, T, C, D), F32)],
        [
            pl.BlockSpec((2, 1, ROWS, D), lambda a: (0, a, 0, 0)),
            fixed((4, D)),
            fixed(sum_shape),
            per_half((T, C, D)),
        ],
        cost(48),
        f"attn_back_{b}",
        after,
        grid=(2,),
        scratch=[
            pltpu.VMEM((D, D), BF16),
            pltpu.VMEM((D, 3 * D), BF16),
            pltpu.VMEM((NG, PAD_ROWS, LANE), F32),
            pltpu.VMEM((3 * NG, PAD_ROWS, LANE), F32),
            pltpu.VMEM((ROWS, 3 * D), BF16),
            pltpu.VMEM((ROWS, D), F32),
            pltpu.VMEM((2 * NG, TP, GT), F32),
            pltpu.VMEM((NG, TP, GT), F32),
            pltpu.VMEM((PER, 8 * TP, LANE), F32),
            pltpu.SemaphoreType.DMA,
            pltpu.SemaphoreType.DMA((N_Q,)),
        ],
    )


def halves(left, right):
    return tn(left(0), right(0)) + tn(left(1), right(1))


def insert_bit(i, place, bit):
    return ((i >> place) << (place + 1)) | (bit << place) | (i & ((1 << place) - 1))


def row_pairs(values, k):
    height = values.shape[0] // 8
    for i in range(4):
        low = insert_bit(i, k, 0)
        high = low | (1 << k)
        yield i, low, high, values[height * low : height * (low + 1)], values[height * high : height * (high + 1)]


def put_down(out, i, total):
    half = MINE // 2
    out[i, :, 0:W_UP] = total[0:half]
    out[i, :, W_UP:] = total[half:]


def get_down(block):
    return jnp.concatenate([block[:, 0:W_UP], block[:, W_UP:]], axis=0)


def mlp_other(bits, dd, act, hid, da, after=()):
    def down(s, l, r, out):
        for k in range(2):
            lanes = slice(k * W_UP, (k + 1) * W_UP)
            put_down(out, k, halves(lambda a: l[0, a], lambda a: r[a, :, lanes]))

    out = shape((16, *BLOCK), F32)
    first = call(
        down, (bits, dd, act),
        [pl.BlockSpec((1, 2, ROWS, MINE), lambda i, s: (1 - s[0], 0, 0, 0)),
         pl.BlockSpec((2, ROWS, D), lambda i, s: (0, 0, i))],
        out, pl.BlockSpec((2, *BLOCK), lambda i, s: (i, 0, 0)),
        cost(6.5), "down_other", after, (4,), 1,
    )

    def up(s, l, r, out):
        out[...] = halves(lambda a: l[a], lambda a: r[a]).reshape(8, D // 8, W_UP)

    return call(
        up, (bits, hid, da),
        [fixed((2, ROWS, D)), pl.BlockSpec((2, ROWS, W_UP), lambda n, s: (0, 0, 2 * (1 - s[0]) + n))],
        [out], [pl.BlockSpec((8, D // 8, W_UP), lambda n, s: (1, 0, n))],
        cost(5.4), "up_other", (first,), (2,), 1, reuse=True,
    )[0]


def mlp_mine(bits, dd, act, hid, da, recv, first, after=()):
    def down(s, l, rk, rs, gk, gs, keep, send):
        put_down(keep, 0, halves(lambda a: l[0, a], lambda a: rk[a]) + get_down(gk[0]))
        put_down(send, 0, halves(lambda a: l[0, a], lambda a: rs[a]) + get_down(gs[0]))

    def block(flip):
        return lambda i, s: insert_bit(i, first, s[1 + first] ^ flip)

    outs = [shape((8, *BLOCK), F32)] * 2
    half = call(
        down, (bits, dd, act, act, recv, recv),
        [pl.BlockSpec((1, 2, ROWS, MINE), lambda i, s: (s[0], 0, 0, 0))]
        + [pl.BlockSpec((2, ROWS, W_UP), lambda i, s, m=block(f): (0, 0, m(i, s))) for f in (0, 1)]
        + [pl.BlockSpec((1, *BLOCK), lambda i, s, m=block(f): (m(i, s), 0, 0)) for f in (0, 1)],
        outs, [pl.BlockSpec((1, *BLOCK), lambda i, s: (i, 0, 0))] * 2,
        cost(6.9), "down_mine", after, (4,), 1,
    )

    def up(s, l, r, got, keep, send):
        total = halves(lambda a: l[a], lambda a: r[a])
        mine = s[1 + first] == 0
        for i, j, k, p, q in row_pairs(total, first):
            p, q = p + got[j], q + got[k]
            keep[i] = jnp.where(mine, p, q)
            send[i] = jnp.where(mine, q, p)

    return call(
        up, (bits, hid, da, recv),
        [fixed((2, ROWS, D)), pl.BlockSpec((2, ROWS, W_UP), lambda n, s: (0, 0, 2 * s[0] + n)),
         pl.BlockSpec((8, D // 8, W_UP), lambda n, s: (1, 0, n))],
        outs, [pl.BlockSpec((4, D // 8, W_UP), lambda n, s: (1, 0, n))] * 2,
        cost(5.7), "up_mine", half, (2,), 1, reuse=True,
    )


def attn_total(hid, att, r, lo, width):
    edge = 3 * MINE
    cut = edge // LANE * LANE

    def product(left, a, b):
        return halves(lambda k: left[k], lambda k: r[k, :, a - lo : b - lo])

    parts = []
    if lo < cut:
        parts.append(product(hid, lo, min(cut, lo + width)))
    if lo + width > cut:
        lane = lax.broadcasted_iota(jnp.int32, (D, LANE), 1)
        span = (cut, cut + LANE)
        parts.append(jnp.where(lane < edge - cut, product(hid, *span), product(att, *span)))
    if lo + width > cut + LANE:
        parts.append(product(att, cut + LANE, lo + width))
    return parts[0] if len(parts) == 1 else jnp.concatenate(parts, axis=1)


def attn_other(bits, hid, att, r3, after=()):
    def body(s, h, o, r, *outs):
        for n in range(2):

            @pl.when(pl.program_id(0) == n)
            def _():
                total = attn_total(h, o, r.at[0], n * W_UP, W_UP).reshape(8, D // 8, W_UP)
                outs[2 * n][...] = total[0:4]
                outs[2 * n + 1][...] = total[4:8]

    right = pl.BlockSpec((1, 2, ROWS, W_UP), lambda n, s: (1 - s[0], 0, 0, n))
    return call(
        body, (bits, hid, att, r3), [fixed((2, ROWS, D)), fixed((2, ROWS, D)), right],
        [shape((4, D // 8, W_UP), F32)] * 4, [fixed((4, D // 8, W_UP))] * 4,
        cost(7), "attn_other", after, (2,), 1,
    )


def attn_mine(bits, hid, att, r3, recv, first, cols, small=None, after=()):
    extra = small is not None
    width = W_UP * len(cols)

    def body(s, h, o, r, *refs):
        gots, more, (keep, send) = refs[: 2 * len(cols)], refs[2 * len(cols) : -2], refs[-2:]
        for k, n in enumerate(cols):

            @pl.when(pl.program_id(0) == k)
            def _():
                total = attn_total(h, o, r.at[0], n * W_UP, W_UP)
                mine = s[1 + first] == 0
                for i, j, jj, p, q in row_pairs(total, first):
                    p, q = p + gots[2 * k + j // 4][j % 4], q + gots[2 * k + jj // 4][jj % 4]
                    keep[i] = jnp.where(mine, p, q)
                    send[i] = jnp.where(mine, q, p)
                if extra:
                    added = more[0][...] + more[1][...]
                    keep[4] = added
                    send[4] = added

    at = lambda n: n + cols[0]
    specs = [
        fixed((2, ROWS, D)),
        fixed((2, ROWS, D)),
        pl.BlockSpec((1, 2, ROWS, W_UP), lambda n, s: (s[0], 0, 0, at(n))),
    ]
    args = [bits, hid, att, r3]
    for n in cols:
        args += recv[2 * n : 2 * n + 2]
        specs += [fixed((4, D // 8, W_UP))] * 2
    if extra:
        args += small
        specs += [pl.BlockSpec((D // 8, W_UP), lambda n, s: (0, at(n)))] * 2
    out = pl.BlockSpec((4 + extra, D // 8, W_UP), lambda n, s: (0, 0, n))
    return call(
        body, args, specs, [shape((4 + extra, D // 8, width), F32)] * 2, [out] * 2,
        cost(1.5 + 2.8 * len(cols)), "attn_mine", after, (len(cols),), 1,
    )


def split_sum(kept, recv, place, bit, extra, after=()):
    n, r, w = recv.shape
    half = (n - extra) // 2

    def body(s, ka, ra, kb, rb, keep_o, send_o):
        keep_o[...] = ka[...] + ra[...]
        send_o[...] = kb[...] + rb[...]

    def at(flip):
        def index(i, s):
            j = insert_bit(i, place, s[0] ^ flip)
            return (jnp.where(i == half, 2 * half, j) if extra else j, 0, 0)

        return pl.BlockSpec((1, r, w), index)

    return call(
        body, (jnp.reshape(bit, (1,)), kept, recv, kept, recv), [at(0), at(0), at(1), at(1)],
        [shape((half + extra, r, w), F32)] * 2, [pl.BlockSpec((1, r, w), lambda i, s: (i, 0, 0))] * 2,
        cost(1.5 + n * r * w * 5e-6), "split_sum", after, (half + extra,), 1,
    )


class Halving:
    def __init__(self, names, links, extra=0):
        self.names, self.links, self.extra = list(names), links, extra

    def send(self, name, kept, out):
        axis, perm, _ = self.links[name]
        if name in self.names:
            self.names.remove(name)
        self.kept, self.recv = kept, lax.ppermute(out, axis, perm)
        return kept

    def step(self, name, after=()):
        place = len(self.names) - 1 - self.names.index(name)
        kept, out = split_sum(self.kept, self.recv, place, self.links[name][2], self.extra, after)
        return self.send(name, kept, out)

    def result(self):
        return self.kept + self.recv


def scatter_rest(block, dim, img, sub):
    step = sub // 2
    while step:
        bit = (img // step) % 2
        half = block.shape[dim] // 2
        keep = lax.dynamic_slice_in_dim(block, bit * half, half, dim)
        send = lax.dynamic_slice_in_dim(block, (1 - bit) * half, half, dim)
        perm = [(i, i ^ step) for i in range(8 * sub)]
        block = keep + lax.ppermute(send, "img", perm)
        step //= 2
    return block


def relative_onehot():
    at = jnp.arange(TP * TQ, dtype=jnp.int32)
    u, t = at // TQ, at % TQ
    rel = (t // SIDE - u // SIDE + 6) * 13 + t % SIDE - u % SIDE + 6
    rel = jnp.where((u < T) & (t < T), rel, -1)
    return (jnp.arange(169, dtype=jnp.int32)[:, None] == rel[None, :]).astype(F32)


def region_of(coords):
    return jnp.where(coords < 7, 0, jnp.where(coords < 11, 1, 2))


def spread_bias(bias_table, onehot):
    rows = jnp.dot(
        bias_table.transpose(0, 2, 1).reshape(2 * HEADS, 169),
        onehot,
        precision=lax.Precision.HIGHEST,
        preferred_element_type=F32,
    )
    rows = rows.reshape(2, NG, PER, TP, TQ).transpose(0, 1, 3, 2, 4).reshape(2 * NG, TP, GT)
    return jnp.where((jnp.arange(TP) < T)[None, :, None], rows, NEG)


def shift_masks(core):
    places = jnp.arange(TQ, dtype=jnp.int32)
    step = jnp.arange(2, dtype=jnp.int32)
    rows = region_of(step[:, None] * SIDE + places // SIDE)
    cols = region_of((core ^ step)[:, None] * SIDE + places % SIDE)
    labels = 3 * rows[:, None] + cols[None, :]
    mask = jnp.where(labels[:, :, :TP, None] == labels[:, :, None, :], 0.0, -100.0).astype(F32)
    return jnp.tile(mask, (1, 1, 1, PER))


def per_device(
    tokens, crop_count, ln1_gain, ln1_bias, w_qkv, b_query, b_value, bias_table, w_out, b_out,
    ln2_gain, ln2_bias, w_up, b_up, w_down, b_down, cotangent, *, n_img,
):
    win, img = lax.axis_index("win"), lax.axis_index("img")
    sub = n_img // 8
    x_bit, core = win // 2, win % 2
    links = {}
    for k in range(3):
        links[k] = ("img", [(i, i ^ (sub << k)) for i in range(n_img)], (img // (sub << k)) % 2)
    bits = jnp.stack([core, links[0][2], links[1][2], links[2][2]])
    at_core, at_x = jnp.reshape(core, (1,)), jnp.reshape(x_bit, (1,))
    all_valid = jnp.full((1,), C, jnp.int32)
    p = dict(
        ln1_gain=ln1_gain, ln1_bias=ln1_bias, w_qkv=w_qkv, b_query=b_query, b_value=b_value,
        w_out=w_out, b_out=b_out, ln2_gain=ln2_gain, ln2_bias=ln2_bias, w_up=w_up, b_up=b_up,
        w_down=w_down, b_down=b_down,
    )

    def over(way, a):
        return lax.ppermute(a, "win", [(i, i ^ way) for i in range(4)])

    def swap(a):
        return over(1, a)

    onehot = relative_onehot()
    bias = spread_bias(bias_table, onehot)
    mask = shift_masks(core)

    mine, other = crop_rows(at_core, all_valid, tokens[:, 0].transpose(1, 0, 2))
    near, far = swap(other), (over(2, mine), over(3, other))
    ct_mine, ct_other = crop_rows(at_core, crop_count, cotangent[:, 0].transpose(1, 0, 2), (mine,))
    ct_near, ct_far = swap(ct_other), (over(2, ct_mine), over(3, ct_other))
    fwd0 = block_fwd(0, (at_x, mine, near), bias, p, 0, (ct_mine,))
    fwd0 = block_fwd(0, (at_x, *far), bias, p, 1, fwd0)
    fwd1 = block_fwd(1, (fwd0[8], mask), bias, p)
    z0, h0, qkvc0, o0, y0, h20, g0, gp0, _ = fwd0
    z1, h1, qkvc1, o1, y1, h21, g1, gp1, zn = fwd1
    ct = join_pieces(at_x, (ct_mine, ct_near, *ct_far), (zn,))

    def stream(first, extra=0, more=()):
        return Halving([*more, *(k for k in (2, 1, 0) if k != first)], links, extra)

    mlp1, mlp0 = (stream(0, 0, ("which",)) for _ in range(2))
    att1, att0 = stream(0), [stream(0, 1), stream(1, 1)]

    dd1, da1, dy, dyr, sv_m1 = mlp_back(1, at_x, ct, y1, gp1, p)
    part = mlp_other(bits, dd1, g1, h21, da1)
    mlp_x = swap(part)
    r31, sv_a1, table1, grad1 = attn_back(1, at_x, dyr, qkvc1, dy, z1, mask, bias, p, (), (part,))
    last = mlp1.send(0, *mlp_mine(bits, dd1, g1, h21, da1, mlp_x, 0, (sv_a1,)))
    part = attn_other(bits, h1, o1, r31, (last,))
    att_x = [swap(a) for a in part]

    dd0, da0, dy, dyr, sv_m0 = mlp_back(0, at_x, grad1, y0, gp0, p, (part[3],))
    last = att1.send(0, *attn_mine(bits, h1, o1, r31, att_x, 0, (0, 1), None, (sv_m0,)))
    out_mine, out_other = own_quadrants(at_x, zn, True, (last,))
    last = mlp1.step(1, (out_mine,))
    part = mlp_other(bits, dd0, g0, h20, da0, (last,))
    mlp_x = swap(part)
    out_x = swap(out_other)
    block_out = token_major(at_core, crop_count, out_mine, out_x, (part,))
    last = mlp0.send(0, *mlp_mine(bits, dd0, g0, h20, da0, mlp_x, 0, (block_out,)))
    last = att1.step(1, (last,))
    last = mlp1.step(2, (last,))
    r30, sv_a0, small, grad0 = attn_back(
        0, at_x, dyr, qkvc0, dy, z0, mask, bias, p, (sv_m0, sv_a1, sv_m1, table1), (last,)
    )
    part = attn_other(bits, h0, o0, r30)
    att_x = [swap(a) for a in part]
    small = [small, swap(small)]
    last = mlp0.step(1, (part[3],))
    for k in range(2):
        kept, out = attn_mine(bits, h0, o0, r30, att_x, k, (k,), small, (last,))
        last = att0[k].send(k, kept, out)
    last = att1.step(2, (last,))
    in_mine, in_other = own_quadrants(at_x, grad0, False, (last,))
    in_x = swap(in_other)
    last = in_mine
    for s, name in ((mlp0, 2), (att0[0], 1), (att0[1], 0), (att0[0], 2), (att0[1], 2)):
        last = s.step(name, (last,))
    grad_tokens = crop_major(at_core, in_mine, in_x, (last,)).reshape(C, 1, T, D)

    parts = [a.result() for a in att0]
    g_att = (jnp.concatenate([a[0] for a in parts], axis=1), att1.result()[0])
    small = jnp.concatenate([a[1] for a in parts], axis=1)[:56]
    for k in range(sub.bit_length() - 1):
        small = small + lax.ppermute(small, "img", [(i, i ^ (1 << k)) for i in range(n_img)])
    mats = []
    for b, mlp in enumerate((mlp0, mlp1)):
        att = scatter_rest(g_att[b], 0, img, sub)
        down, up = mlp.result()
        g_down = scatter_rest(get_down(down), 1, img, sub)
        g_up = scatter_rest(up, 0, img, sub)
        mats.append((att[:, : 3 * D // 4], att[:, 3 * D // 4 :], g_up, g_down.T))

    g_qkv, g_out, g_up, g_down = (jnp.stack(pair) for pair in zip(*mats))
    table = small[24:].reshape(PER, 8, 3, TABLE)[:, :NG, :2, :169].transpose(2, 3, 1, 0).reshape(2, 169, HEADS)
    width = D // n_img

    vectors = small[:24].reshape(2, 12, D)
    mine = lax.dynamic_slice_in_dim(vectors[:, :8], img * width, width, 2)
    up_bias = lax.dynamic_slice_in_dim(vectors[:, 8:].reshape(2, FF), img * (4 * width), 4 * width, 1)

    return (
        block_out.transpose(1, 0, 2)[:, None], grad_tokens, mine[:, 0], mine[:, 1], g_qkv, mine[:, 2], mine[:, 3], table,
        g_out, mine[:, 6], mine[:, 4], mine[:, 5], g_up, up_bias, g_down, mine[:, 7],
    )


def solution(mesh):
    shard = P("img", "win", None, None)
    vec, mat = P(None, "img"), P(None, "img", "win")
    return jax.shard_map(
        functools.partial(per_device, n_img=mesh.shape["img"]),
        mesh=mesh,
        in_specs=(shard, P("img")) + (P(),) * 14 + (shard,),
        out_specs=(shard, shard, vec, vec, mat, vec, vec, P(), mat, vec, vec, vec, mat, vec, mat, vec),
        check_vma=False,
    )
```

time: 614 us -> 513 us (0.84)
  waiting for transfers between devices: 179 us -> 78.1 us
  Pallas kernels: 305 us -> 369 us
  local copies, waits for them, and re-layouts: 53 us -> 19.6 us
  starting transfers between devices: 55.4 us -> 30.6 us
    ppermute x47 -> x34, waiting for transfers between devices: 179 us -> 78.1 us  [the longest x15 74.2 us: send(): self.kept, self.recv = (kept, lax.ppermute(out, axis, perm))]
    pallas_call x40 -> x37, Pallas kernels: 305 us -> 369 us  [call(): pl.pallas_call(wrapped, grid_spec=pltpu.PrefetchScalarGridSpec(num_scalar...]
    ppermute x47 -> x34, starting transfers between devices: 55.4 us -> 30.6 us  [the longest x15 22.6 us: send(): self.kept, self.recv = (kept, lax.ppermute(out, axis, perm))]
    dynamic_slice x13 -> x1, local copies, waits for them, and re-layouts: 18.8 us -> 0.58 us  [per_device(): lax.dynamic_slice_in_dim(vectors[:, 8:].reshape(2, FF), img * (4 * width)...]
    reshape x9 -> x5, local copies, waits for them, and re-layouts: 9.88 us -> 2.06 us  [the longest x3 1.41 us: spread_bias(): rows.reshape(2, NG, PER, TP, TQ).transpose(0, 1, 3, 2, 4)]
    unnamed x108 -> x64, local copies, waits for them, and re-layouts: 15.9 us -> 14.8 us
  transfers between devices with their start and end apart: 47 -> 34, of which waited for: 16 -> 9; matrix products, arithmetic and copies ran while one was open for 9% -> 2% of each run, Pallas kernels for 36% -> 59%
where the time goes in v2:
time: 513 us; the launch traced here: 507 us
  Pallas kernels  369 us (72%)
  waiting for transfers between devices  78.1 us (15%)
  starting transfers between devices  30.6 us (6%)
  local copies, waits for them, and re-layouts  19.6 us (4%)
  other arithmetic  6.46 us (1%)
    pallas_call x37, Pallas kernels, call(): pl.pallas_call(wrapped, grid_spec=pltpu.PrefetchScalarGridSpec(num_scalar...  369 us
    ppermute x15, waiting for transfers between devices, send(): self.kept, self.recv = (kept, lax.ppermute(out, axis, perm))  74.2 us
    ppermute x15, starting transfers between devices, send(): self.kept, self.recv = (kept, lax.ppermute(out, axis, perm))  22.6 us
    unnamed x64, local copies, waits for them, and re-layouts  14.8 us
  transfers between devices with their start and end apart: 34, of which 9 were waited for; matrix products, arithmetic and copies ran while one was open for 2% of the time, Pallas kernels for 59%

profile of v2, /device:TPU:0, one launch (start us, length us, event | category | flops | bytes accessed | tf_op | source)
XLA Modules:
  0.0 507.3 jit_solution(1228318596646021006)
XLA Ops:
  0.7 2.5 crop_rows.2
  3.7 2.6 collective-permute-start.1
  6.9 2.5 crop_rows.3
  17.3 25.8 %forward_0.2 = (f32[2,392,768]{2,1,0:T(8,128)}, bf16[2,392,768]{2,1,0:T(8,128)(2,1)}, bf16[2,8,18,64,128]{4,3,2,1,0:T(8,128)(2,1)}, bf16[2,392,768]{2,1,0:T(8,12...) custom-call(s32[1]{0:T(128)} %bitcast.1.refs_0_, ...), custom_call_target="tpu_custom_call" | custom-call | flops 11500000256 | tf_op jit(solution)/shard_map/forward_0/pallas_call | solution.py:167
  43.9 25.8 %forward_0.3 = (f32[2,392,768]{2,1,0:T(8,128)}, bf16[2,392,768]{2,1,0:T(8,128)(2,1)}, bf16[2,8,18,64,128]{4,3,2,1,0:T(8,128)(2,1)}, bf16[2,392,768]{2,1,0:T(8,12...) custom-call(s32[1]{0:T(128)} %bitcast.1.refs_0_, ...), custom_call_target="tpu_custom_call", output_to_operand_aliasing={{0}: (17, {}), {1}: (18, {}), {2}: (19, {}), {3}: (20, {}),... | custom-call | flops 11500000256 | tf_op jit(solution)/shard_map/forward_0/pallas_call | solution.py:167
  69.7 46.5 %forward_1.1 = (f32[2,392,768]{2,1,0:T(8,128)}, bf16[2,392,768]{2,1,0:T(8,128)(2,1)}, bf16[2,8,18,64,128]{4,3,2,1,0:T(8,128)(2,1)}, bf16[2,392,768]{2,1,0:T(8,12...) custom-call(f32[2,49,8,768]{3,2,1,0:T(8,128)} %get-tuple-element.122, ...), custom_call_target="tpu_custom_call" | custom-call | flops 21159999488 | tf_op jit(solution)/shard_map/forward_1/pallas_call | solution.py:167
  117.1 3.9 join_pieces.1.refs_1_
  121.0 22.9 %mlp_back_1.1 = (bf16[2,2,392,192]{3,2,1,0:T(8,128)(2,1)}, bf16[2,392,1536]{2,1,0:T(8,128)(2,1)}, f32[2,392,768]{2,1,0:T(8,128)}, bf16[2,392,768]{2,1,0:T(8,128)(2,1)}, f32[8,768]{1,0:T(8,128)}) custom-call(s32[1]{0:T(128)} %bitcast.1.refs_0_, f32[2,49,8,768]{3,2,1,0:T(8,128)} %join_pieces.1.refs_1_, f32[2,392,768]{2,1,0:T(8,128)} %get-tuple-element.127.refs_2_, ...), custom_call_target="tpu_custom_call" | custom-call | flops 10579999744 | tf_op jit(solution)/shard_map/mlp_back_1/pallas_call | solution.py:167
  143.9 6.4 %down_other.2.refs_3_ = f32[16,96,768]{2,1,0:T(8,128)} custom-call(s32[4]{0:T(128)} %pad_add_fusion.refs_0_, bf16[2,2,392,192]{3,2,1,0:T(8,128)(2,1)} %get-tuple-element.135.refs_1_, bf16[2,392,3072]{2,1,0:T(8,128)(2,1)} %get-tuple-element.136.refs_2_.refs_3_), custom_call_target="tpu_custom_call" | custom-call | flops 2990000128 | tf_op jit(solution)/shard_map/down_other/pallas_call | solution.py:167
  150.3 5.3 %up_other.2.refs_10_ = f32[16,96,768]{2,1,0:T(8,128)} custom-call(s32[4]{0:T(128)} %pad_add_fusion.refs_0_, bf16[2,392,768]{2,1,0:T(8,128)(2,1)} %get-tuple-element.133.refs_1_, bf16[2,392,1536]{2,1,0:T(8,128)(2,1)} %get-tuple-element.134.refs_2_, f32[16,96,768]{2,1,0:T(8,128)} %down_other.2.refs_3_), custom_call_target="tpu_custom_call", output_to_operand_aliasing={{}: (3, {})} | custom-call | flops 2484000000 | tf_op jit(solution)/shard_map/up_other/pallas_call | solution.py:167
  155.7 48.0 %attn_back_1.1 = (bf16[2,2,392,768]{3,2,1,0:T(8,128)(2,1)}, f32[4,768]{1,0:T(4,128)}, f32[4,8,256]{2,1,0:T(8,128)}, f32[2,49,8,768]{3,2,1,0:T(8,128)}) custom-call(s32[1]{0:T(128)} %bitcast.1.refs_0_, bf16[2,392,768]{2,1,0:T(8,128)(2,1)} %get-tuple-element.129.refs_1_, bf16[2,8,18,64,128]{4,3,2,1,0:T(8,128)(2,1)} %get-tuple-element.130.refs_2_, ...), custom_call_target="tpu_custom_call" | custom-call | flops 22080000000 | tf_op jit(solution)/shard_map/attn_back_1/pallas_call | solution.py:167
  203.7 2.1 copy-done.2
  205.8 6.9 %down_mine.2 = (f32[8,96,768]{2,1,0:T(8,128)}, f32[8,96,768]{2,1,0:T(8,128)}) custom-call(s32[4]{0:T(128)} %pad_add_fusion.refs_0_, bf16[2,2,392,192]{3,2,1,0:T(8,128)(2,1)} %get-tuple-element.135.refs_1_, bf16[2,392,3072]{2,1,0:T(8,128)(2,1)} %get-tuple-element.136.refs_2_.refs_3_, bf16[2,392,3072]{2,1,0:T(8,128)(2,1)} %get-tuple-element.136.refs_2_.refs_3_, ...), custom_call_target="tpu_custom_call" | custom-call | flops 3174000128 | tf_op jit(solution)/shard_map/down_mine/pallas_call | solution.py:167
  212.7 5.6 %up_mine.2 = (f32[8,96,768]{2,1,0:T(8,128)}, f32[8,96,768]{2,1,0:T(8,128)}) custom-call(s32[4]{0:T(128)} %pad_add_fusion.refs_0_, bf16[2,392,768]{2,1,0:T(8,128)(2,1)} %get-tuple-element.133.refs_1_, bf16[2,392,1536]{2,1,0:T(8,128)(2,1)} %get-tuple-element.134.refs_2_, f32[16,96,768]{2,1,0:T(8,128)} %copy-done.2, ...), custom_call_target="tpu_custom_call", output_to_operand_aliasing={{0}: (4, {}), {1}: (5, {})} | custom-call | flops 2622000128 | tf_op jit(solution)/shard_map/up_mine/pallas_call | solution.py:167
  220.3 6.8 %attn_other.2 = (f32[4,96,384]{2,1,0:T(8,128)}, f32[4,96,384]{2,1,0:T(8,128)}, f32[4,96,384]{2,1,0:T(8,128)}, f32[4,96,384]{2,1,0:T(8,128)}) custom-call(s32[4]{0:T(128)} %pad_add_fusion.refs_0_, bf16[2,392,768]{2,1,0:T(8,128)(2,1)} %get-tuple-element.124.refs_1_, bf16[2,392,768]{2,1,0:T(8,128)(2,1)} %get-tuple-element.125.refs_2_, ...), custom_call_target="tpu_custom_call" | custom-call | flops 3220000000 | tf_op jit(solution)/shard_map/attn_other/pallas_call | solution.py:167
  228.1 23.0 %mlp_back_0.1 = (bf16[2,2,392,192]{3,2,1,0:T(8,128)(2,1)}, bf16[2,392,1536]{2,1,0:T(8,128)(2,1)}, f32[2,392,768]{2,1,0:T(8,128)}, bf16[2,392,768]{2,1,0:T(8,128)(2,1)}, f32[8,768]{1,0:T(8,128)}) custom-call(s32[1]{0:T(128)} %bitcast.1.refs_0_, f32[2,49,8,768]{3,2,1,0:T(8,128)} %get-tuple-element.146.refs_1_, f32[2,392,768]{2,1,0:T(8,128)} %get-tuple-element.147.refs_2_, ...), custom_call_target="tpu_custom_call" | custom-call | flops 10579999744 | tf_op jit(solution)/shard_map/mlp_back_0/pallas_call | solution.py:167
  252.6 7.2 %attn_mine.3 = (f32[4,96,768]{2,1,0:T(8,128)}, f32[4,96,768]{2,1,0:T(8,128)}) custom-call(s32[4]{0:T(128)} %pad_add_fusion.refs_0_, bf16[2,392,768]{2,1,0:T(8,128)(2,1)} %get-tuple-element.124.refs_1_, bf16[2,392,768]{2,1,0:T(8,128)(2,1)} %get-tuple-element.125.refs_2_, bf16[2,2,392,768]{3,2,1,0:T(8,128)(2,1)} %get-tuple-element.137.refs_3_, ...), custom_call_target="tpu_custom_call" | custom-call | flops 3265999872 | tf_op jit(solution)/shard_map/attn_mine/pallas_call | solution.py:167
  259.8 2.9 own_quadrants.2
  262.7 9.7 %collective-permute-done.12.refs_2_.refs_4_ = f32[8,96,768]{2,1,0:T(8,128)S(1)} collective-permute-done((f32[8,96,768]{2,1,0:T(8,128)}, f32[8,96,768]{2,1,0:T(8,128)S(1)}, u32[]{:S(2)}, u32[]{:S(2)}) %collective-permute-start.12) | collective-permute-done | bytes 2359328 | tf_op jit(solution)/shard_map/ppermute | solution.py:898
  273.9 4.3 split_sum.10
  278.2 6.3 %down_other.3.refs_3_ = f32[16,96,768]{2,1,0:T(8,128)} custom-call(s32[4]{0:T(128)} %pad_add_fusion.refs_0_, bf16[2,2,392,192]{3,2,1,0:T(8,128)(2,1)} %get-tuple-element.155.refs_1_, bf16[2,392,3072]{2,1,0:T(8,128)(2,1)} %get-tuple-element.156.refs_2_.refs_3_, f32[4,96,768]{2,1,0:T(8,128)} %get-tuple-element.158.refs_3_.refs_1_), custom_call_target="tpu_custom_call" | custom-call | flops 2990000128 | tf_op jit(solution)/shard_map/down_other/pallas_call | solution.py:167
  284.5 5.4 %up_other.3.refs_4_ = f32[16,96,768]{2,1,0:T(8,128)} custom-call(s32[4]{0:T(128)} %pad_add_fusion.refs_0_, bf16[2,392,768]{2,1,0:T(8,128)(2,1)} %get-tuple-element.153.refs_1_, bf16[2,392,1536]{2,1,0:T(8,128)(2,1)} %get-tuple-element.154.refs_2_, f32[16,96,768]{2,1,0:T(8,128)} %down_other.3.refs_3_), custom_call_target="tpu_custom_call", output_to_operand_aliasing={{}: (3, {})} | custom-call | flops 2484000000 | tf_op jit(solution)/shard_map/up_other/pallas_call | solution.py:167
  293.8 3.8 collective-permute-done.11.refs_3_
  298.4 2.5 token_major.1.refs_6_
  300.9 2.2 copy-done.3
  303.1 6.9 %down_mine.3 = (f32[8,96,768]{2,1,0:T(8,128)}, f32[8,96,768]{2,1,0:T(8,128)}) custom-call(s32[4]{0:T(128)} %pad_add_fusion.refs_0_, bf16[2,2,392,192]{3,2,1,0:T(8,128)(2,1)} %get-tuple-element.155.refs_1_, bf16[2,392,3072]{2,1,0:T(8,128)(2,1)} %get-tuple-element.156.refs_2_.refs_3_, bf16[2,392,3072]{2,1,0:T(8,128)(2,1)} %get-tuple-element.156.refs_2_.refs_3_, ...), custom_call_target="tpu_custom_call" | custom-call | flops 3174000128 | tf_op jit(solution)/shard_map/down_mine/pallas_call | solution.py:167
  310.0 5.7 %up_mine.3 = (f32[8,96,768]{2,1,0:T(8,128)}, f32[8,96,768]{2,1,0:T(8,128)}) custom-call(s32[4]{0:T(128)} %pad_add_fusion.refs_0_, bf16[2,392,768]{2,1,0:T(8,128)(2,1)} %get-tuple-element.153.refs_1_, bf16[2,392,1536]{2,1,0:T(8,128)(2,1)} %get-tuple-element.154.refs_2_, f32[16,96,768]{2,1,0:T(8,128)} %copy-done.3, ...), custom_call_target="tpu_custom_call", output_to_operand_aliasing={{0}: (4, {}), {1}: (5, {})} | custom-call | flops 2622000128 | tf_op jit(solution)/shard_map/up_mine/pallas_call | solution.py:167
  318.7 2.5 split_sum.11
  321.2 2.5 split_sum.12
  323.7 2.8 collective-permute-start.33
  326.5 47.7 %attn_back_0.1 = (bf16[2,2,392,768]{3,2,1,0:T(8,128)(2,1)}, f32[4,768]{1,0:T(4,128)}, f32[96,768]{1,0:T(8,128)}, f32[2,49,8,768]{3,2,1,0:T(8,128)}) custom-call(s32[1]{0:T(128)} %bitcast.1.refs_0_, bf16[2,392,768]{2,1,0:T(8,128)(2,1)} %get-tuple-element.159.refs_1_, bf16[2,8,18,64,128]{4,3,2,1,0:T(8,128)(2,1)} %get-tuple-element.160.refs_2_, ...), custom_call_target="tpu_custom_call" | custom-call | flops 22080000000 | tf_op jit(solution)/shard_map/attn_back_0/pallas_call | solution.py:167
  374.3 7.0 %attn_other.3 = (f32[4,96,384]{2,1,0:T(8,128)}, f32[4,96,384]{2,1,0:T(8,128)}, f32[4,96,384]{2,1,0:T(8,128)}, f32[4,96,384]{2,1,0:T(8,128)}) custom-call(s32[4]{0:T(128)} %pad_add_fusion.refs_0_, bf16[2,392,768]{2,1,0:T(8,128)(2,1)} %get-tuple-element.174.refs_1_, bf16[2,392,768]{2,1,0:T(8,128)(2,1)} %get-tuple-element.175.refs_2_, ...), custom_call_target="tpu_custom_call" | custom-call | flops 3220000000 | tf_op jit(solution)/shard_map/attn_other/pallas_call | solution.py:167
  385.2 4.6 split_sum.13
  391.1 5.0 attn_mine.4
  397.1 5.9 %attn_mine.5 = (f32[5,96,384]{2,1,0:T(8,128)}, f32[5,96,384]{2,1,0:T(8,128)}) custom-call(s32[4]{0:T(128)} %pad_add_fusion.refs_0_, bf16[2,392,768]{2,1,0:T(8,128)(2,1)} %get-tuple-element.174.refs_1_, bf16[2,392,768]{2,1,0:T(8,128)(2,1)} %get-tuple-element.175.refs_2_, bf16[2,2,392,768]{3,2,1,0:T(8,128)(2,1)} %get-tuple-element.176.refs_3_, ...), custom_call_target="tpu_custom_call" | custom-call | flops 1978000000 | tf_op jit(solution)/shard_map/attn_mine/pallas_call | solution.py:167
  403.0 2.2 split_sum.14
  407.9 3.0 own_quadrants.3
  410.9 19.8 %collective-permute-done.31 = f32[1,96,768]{2,1,0:T(8,128)S(1)} collective-permute-done((f32[1,96,768]{2,1,0:T(8,128)}, f32[1,96,768]{2,1,0:T(8,128)S(1)}, u32[]{:S(2)}, u32[]{:S(2)}) %collective-permute-start.31) | collective-permute-done | bytes 294944 | tf_op jit(solution)/shard_map/ppermute | solution.py:898
  432.5 2.5 split_sum.15
  435.0 2.5 collective-permute-start.32
  438.4 3.2 split_sum.16
  441.6 14.3 %collective-permute-done.24.refs_2_.refs_4_ = f32[5,96,384]{2,1,0:T(8,128)S(1)} collective-permute-done((f32[5,96,384]{2,1,0:T(8,128)S(1)}, f32[5,96,384]{2,1,0:T(8,128)S(1)}, u32[]{:S(2)}, u32[]{:S(2)}) %collective-permute-start.24) | collective-permute-done | bytes 737312 | tf_op jit(solution)/shard_map/ppermute | solution.py:898
  456.8 3.2 split_sum.17
  461.8 7.1 %collective-permute-done.28.refs_2_.refs_4_ = f32[3,96,384]{2,1,0:T(8,128)S(1)} collective-permute-done((f32[3,96,384]{2,1,0:T(8,128)}, f32[3,96,384]{2,1,0:T(8,128)S(1)}, u32[]{:S(2)}, u32[]{:S(2)}) %collective-permute-start.28) | collective-permute-done | bytes 442400 | tf_op jit(solution)/shard_map/ppermute | solution.py:898
  469.7 2.1 split_sum.18
  477.6 2.4 crop_major.1
  482.0 16.2 %collective-permute-done.30 = f32[2,96,384]{2,1,0:T(8,128)S(1)} collective-permute-done((f32[2,96,384]{2,1,0:T(8,128)}, f32[2,96,384]{2,1,0:T(8,128)S(1)}, u32[]{:S(2)}, u32[]{:S(2)}) %collective-permute-start.30) | collective-permute-done | bytes 294944 | tf_op jit(solution)/shard_map/ppermute | solution.py:898
  498.3 5.0 collective-permute-done.29
  (168 shorter events, 49.8 us)
Async XLA Ops:
  0.6 11.1 %copy-start = (f32[2,169,24]{1,2,0:T(8,128)S(1)}, f32[2,169,24]{1,2,0:T(8,128)}, u32[]{:S(2)}) copy-start(f32[2,169,24]{1,2,0:T(8,128)} %param.24) | copy-start | bytes 97348
  3.2 14.0 %collective-permute-start.2 = (f32[6,196,128]{2,1,0:T(8,128)}, f32[6,196,128]{2,1,0:T(8,128)}, u32[]{:S(2)}, u32[]{:S(2)}) collective-permute-start(f32[6,196,128]{2,1,0:T(8,128)} %get-tuple-element.111), channel_id=1, source_target_pairs={{0,1},{1,0},{2,3},{3,2},{4,5},{5,4},{6,7},{7,6},{8,9},{9,8},{10,11... | collective-permute-start | bytes 1806344 | tf_op jit(solution)/shard_map/ppermute | solution.py:976
  3.7 39.4 %collective-permute-start.1 = (f32[6,196,128]{2,1,0:T(8,128)}, f32[6,196,128]{2,1,0:T(8,128)S(1)}, u32[]{:S(2)}, u32[]{:S(2)}) collective-permute-start(f32[6,196,128]{2,1,0:T(8,128)} %get-tuple-element.111), channel_id=1, source_target_pairs={{0,3},{1,2},{2,1},{3,0},{4,7},{5,6},{6,5},{7,4},{8,11},{9,10},{10,... | collective-permute-start | bytes 1806344 | tf_op jit(solution)/shard_map/ppermute | solution.py:976
  6.3 36.8 %collective-permute-start = (f32[6,196,128]{2,1,0:T(8,128)}, f32[6,196,128]{2,1,0:T(8,128)}, u32[]{:S(2)}, u32[]{:S(2)}) collective-permute-start(f32[6,196,128]{2,1,0:T(8,128)} %get-tuple-element.110.refs_3_.refs_1_), channel_id=1, source_target_pairs={{0,2},{1,3},{2,0},{3,1},{4,6},{5,7},{6,4},{7,5},{8,10},{9,11},{10,... | collective-permute-start | bytes 1806344 | tf_op jit(solution)/shard_map/ppermute | solution.py:976
  9.4 106.8 %collective-permute-start.3 = (f32[6,196,128]{2,1,0:T(8,128)}, f32[6,196,128]{2,1,0:T(8,128)}, u32[]{:S(2)}, u32[]{:S(2)}) collective-permute-start(f32[6,196,128]{2,1,0:T(8,128)} %get-tuple-element.126), channel_id=1, source_target_pairs={{0,1},{1,0},{2,3},{3,2},{4,5},{5,4},{6,7},{7,6},{8,9},{9,8},{10,11... | collective-permute-start | bytes 1806344 | tf_op jit(solution)/shard_map/ppermute | solution.py:976
  9.6 106.7 %collective-permute-start.5 = (f32[6,196,128]{2,1,0:T(8,128)}, f32[6,196,128]{2,1,0:T(8,128)}, u32[]{:S(2)}, u32[]{:S(2)}) collective-permute-start(f32[6,196,128]{2,1,0:T(8,128)} %get-tuple-element.126), channel_id=1, source_target_pairs={{0,3},{1,2},{2,1},{3,0},{4,7},{5,6},{6,5},{7,4},{8,11},{9,10},{10,... | collective-permute-start | bytes 1806344 | tf_op jit(solution)/shard_map/ppermute | solution.py:976
  13.6 3.6 copy-start.9
  17.2 99.0 %collective-permute-start.4 = (f32[6,196,128]{2,1,0:T(8,128)S(1)}, f32[6,196,128]{2,1,0:T(8,128)S(1)}, u32[]{:S(2)}, u32[]{:S(2)}) collective-permute-start(f32[6,196,128]{2,1,0:T(8,128)S(1)} %copy-done.9), channel_id=1, source_target_pairs={{0,2},{1,3},{2,0},{3,1},{4,6},{5,7},{6,4},{7,5},{8,10},{9,11},{10,... | collective-permute-start | bytes 1806344 | tf_op jit(solution)/shard_map/ppermute | solution.py:976
  155.6 48.1 %collective-permute-start.6 = (f32[16,96,768]{2,1,0:T(8,128)}, f32[16,96,768]{2,1,0:T(8,128)S(1)}, u32[]{:S(2)}, u32[]{:S(2)}) collective-permute-start(f32[16,96,768]{2,1,0:T(8,128)} %up_other.2.refs_10_), channel_id=1, source_target_pairs={{0,1},{1,0},{2,3},{3,2},{4,5},{5,4},{6,7},{7,6},{8,9},{9,8},{10,11... | collective-permute-start | bytes 14155784 | tf_op jit(solution)/shard_map/ppermute | solution.py:976
  218.4 54.1 %collective-permute-start.12 = (f32[8,96,768]{2,1,0:T(8,128)}, f32[8,96,768]{2,1,0:T(8,128)S(1)}, u32[]{:S(2)}, u32[]{:S(2)}) collective-permute-start(f32[8,96,768]{2,1,0:T(8,128)} %get-tuple-element.157), channel_id=1, source_target_pairs={{0,4},{4,0},{8,12},{12,8},{16,20},{20,16},{24,28},{28,24},{1,5},{5... | collective-permute-start | bytes 7077896 | tf_op jit(solution)/shard_map/ppermute | solution.py:898
  227.1 24.1 %collective-permute-start.10 = (f32[4,96,384]{2,1,0:T(8,128)}, f32[4,96,384]{2,1,0:T(8,128)S(1)}, u32[]{:S(2)}, u32[]{:S(2)}) collective-permute-start(f32[4,96,384]{2,1,0:T(8,128)} %get-tuple-element.145.refs_7_), channel_id=1, source_target_pairs={{0,1},{1,0},{2,3},{3,2},{4,5},{5,4},{6,7},{7,6},{8,9},{9,8},{10,11... | collective-permute-start | bytes 1769480 | tf_op jit(solution)/shard_map/ppermute | solution.py:976
  227.3 23.8 %collective-permute-start.7 = (f32[4,96,384]{2,1,0:T(8,128)}, f32[4,96,384]{2,1,0:T(8,128)S(1)}, u32[]{:S(2)}, u32[]{:S(2)}) collective-permute-start(f32[4,96,384]{2,1,0:T(8,128)} %get-tuple-element.142), channel_id=1, source_target_pairs={{0,1},{1,0},{2,3},{3,2},{4,5},{5,4},{6,7},{7,6},{8,9},{9,8},{10,11... | collective-permute-start | bytes 1769480 | tf_op jit(solution)/shard_map/ppermute | solution.py:976
  227.6 23.6 %collective-permute-start.8 = (f32[4,96,384]{2,1,0:T(8,128)}, f32[4,96,384]{2,1,0:T(8,128)S(1)}, u32[]{:S(2)}, u32[]{:S(2)}) collective-permute-start(f32[4,96,384]{2,1,0:T(8,128)} %get-tuple-element.143), channel_id=1, source_target_pairs={{0,1},{1,0},{2,3},{3,2},{4,5},{5,4},{6,7},{7,6},{8,9},{9,8},{10,11... | collective-permute-start | bytes 1769480 | tf_op jit(solution)/shard_map/ppermute | solution.py:976
  227.8 23.4 %collective-permute-start.9 = (f32[4,96,384]{2,1,0:T(8,128)}, f32[4,96,384]{2,1,0:T(8,128)S(1)}, u32[]{:S(2)}, u32[]{:S(2)}) collective-permute-start(f32[4,96,384]{2,1,0:T(8,128)} %get-tuple-element.144), channel_id=1, source_target_pairs={{0,1},{1,0},{2,3},{3,2},{4,5},{5,4},{6,7},{7,6},{8,9},{9,8},{10,11... | collective-permute-start | bytes 1769480 | tf_op jit(solution)/shard_map/ppermute | solution.py:976
  284.5 5.4 %copy-start.23 = (f32[6,196,128]{2,1,0:T(8,128)S(1)}, f32[6,196,128]{2,1,0:T(8,128)}, u32[]{:S(2)}) copy-start(f32[6,196,128]{2,1,0:T(8,128)} %get-tuple-element.152) | copy-start | bytes 1806340
  289.9 11.0 %collective-permute-start.15 = (f32[16,96,768]{2,1,0:T(8,128)}, f32[16,96,768]{2,1,0:T(8,128)S(1)}, u32[]{:S(2)}, u32[]{:S(2)}) collective-permute-start(f32[16,96,768]{2,1,0:T(8,128)} %up_other.3.refs_4_), channel_id=1, source_target_pairs={{0,1},{1,0},{2,3},{3,2},{4,5},{5,4},{6,7},{7,6},{8,9},{9,8},{10,11... | collective-permute-start | bytes 14155784 | tf_op jit(solution)/shard_map/ppermute | solution.py:976
  289.9 7.6 %collective-permute-start.11 = (f32[6,196,128]{2,1,0:T(8,128)S(1)}, f32[6,196,128]{2,1,0:T(8,128)S(1)}, u32[]{:S(2)}, u32[]{:S(2)}) collective-permute-start(f32[6,196,128]{2,1,0:T(8,128)S(1)} %copy-done.23), channel_id=1, source_target_pairs={{0,1},{1,0},{2,3},{3,2},{4,5},{5,4},{6,7},{7,6},{8,9},{9,8},{10,11... | collective-permute-start | bytes 1806344 | tf_op jit(solution)/shard_map/ppermute | solution.py:976
  290.4 28.3 %collective-permute-start.14 = (f32[4,96,768]{2,1,0:T(8,128)}, f32[4,96,768]{2,1,0:T(8,128)}, u32[]{:S(2)}, u32[]{:S(2)}) collective-permute-start(f32[4,96,768]{2,1,0:T(8,128)} %get-tuple-element.166), channel_id=1, source_target_pairs={{0,4},{4,0},{8,12},{12,8},{16,20},{20,16},{24,28},{28,24},{1,5},{5... | collective-permute-start | bytes 3538952 | tf_op jit(solution)/shard_map/ppermute | solution.py:898
  292.2 29.0 %collective-permute-start.13 = (f32[4,96,768]{2,1,0:T(8,128)}, f32[4,96,768]{2,1,0:T(8,128)}, u32[]{:S(2)}, u32[]{:S(2)}) collective-permute-start(f32[4,96,768]{2,1,0:T(8,128)} %get-tuple-element.165), channel_id=1, source_target_pairs={{0,8},{4,12},{8,0},{12,4},{16,24},{20,28},{24,16},{28,20},{1,9},{5... | collective-permute-start | bytes 3538952 | tf_op jit(solution)/shard_map/ppermute | solution.py:898
  300.9 2.2 copy-start.3
  315.7 67.8 %collective-permute-start.22 = (f32[8,96,768]{2,1,0:T(8,128)}, f32[8,96,768]{2,1,0:T(8,128)S(1)}, u32[]{:S(2)}, u32[]{:S(2)}) collective-permute-start(f32[8,96,768]{2,1,0:T(8,128)} %get-tuple-element.182), channel_id=1, source_target_pairs={{0,4},{4,0},{8,12},{12,8},{16,20},{20,16},{24,28},{28,24},{1,5},{5... | collective-permute-start | bytes 7077896 | tf_op jit(solution)/shard_map/ppermute | solution.py:898
  323.7 58.1 %collective-permute-start.33 = (f32[2,96,768]{2,1,0:T(8,128)}, f32[2,96,768]{2,1,0:T(8,128)}, u32[]{:S(2)}, u32[]{:S(2)}) collective-permute-start(f32[2,96,768]{2,1,0:T(8,128)} %get-tuple-element.203), channel_id=1, source_target_pairs={{0,16},{4,20},{8,24},{12,28},{16,0},{20,4},{24,8},{28,12},{1,17},{... | collective-permute-start | bytes 1769480 | tf_op jit(solution)/shard_map/ppermute | solution.py:898
  374.2 9.2 %collective-permute-start.19 = (f32[96,768]{1,0:T(8,128)}, f32[96,768]{1,0:T(8,128)S(1)}, u32[]{:S(2)}, u32[]{:S(2)}) collective-permute-start(f32[96,768]{1,0:T(8,128)} %get-tuple-element.179.refs_6_), channel_id=1, source_target_pairs={{0,1},{1,0},{2,3},{3,2},{4,5},{5,4},{6,7},{7,6},{8,9},{9,8},{10,11... | collective-permute-start | bytes 884744 | tf_op jit(solution)/shard_map/ppermute | solution.py:976
  374.3 8.0 %copy-start.12 = (f32[2,96,768]{2,1,0:T(8,128)S(1)}, f32[2,96,768]{2,1,0:T(8,128)}, u32[]{:S(2)}) copy-start(f32[2,96,768]{2,1,0:T(8,128)} %get-tuple-element.171.refs_13_) | copy-start | bytes 1769476
  381.3 8.5 %collective-permute-start.20 = (f32[4,96,384]{2,1,0:T(8,128)}, f32[4,96,384]{2,1,0:T(8,128)}, u32[]{:S(2)}, u32[]{:S(2)}) collective-permute-start(f32[4,96,384]{2,1,0:T(8,128)} %get-tuple-element.180), channel_id=1, source_target_pairs={{0,1},{1,0},{2,3},{3,2},{4,5},{5,4},{6,7},{7,6},{8,9},{9,8},{10,11... | collective-permute-start | bytes 1769480 | tf_op jit(solution)/shard_map/ppermute | solution.py:976
  381.7 9.4 %collective-permute-start.21 = (f32[4,96,384]{2,1,0:T(8,128)}, f32[4,96,384]{2,1,0:T(8,128)}, u32[]{:S(2)}, u32[]{:S(2)}) collective-permute-start(f32[4,96,384]{2,1,0:T(8,128)} %get-tuple-element.181), channel_id=1, source_target_pairs={{0,1},{1,0},{2,3},{3,2},{4,5},{5,4},{6,7},{7,6},{8,9},{9,8},{10,11... | collective-permute-start | bytes 1769480 | tf_op jit(solution)/shard_map/ppermute | solution.py:976
  381.8 14.3 %collective-permute-start.17 = (f32[4,96,384]{2,1,0:T(8,128)}, f32[4,96,384]{2,1,0:T(8,128)S(1)}, u32[]{:S(2)}, u32[]{:S(2)}) collective-permute-start(f32[4,96,384]{2,1,0:T(8,128)} %get-tuple-element.177), channel_id=1, source_target_pairs={{0,1},{1,0},{2,3},{3,2},{4,5},{5,4},{6,7},{7,6},{8,9},{9,8},{10,11... | collective-permute-start | bytes 1769480 | tf_op jit(solution)/shard_map/ppermute | solution.py:976
  383.4 6.4 %copy-start.7 = (f32[96,768]{1,0:T(8,128)}, f32[96,768]{1,0:T(8,128)S(1)}, u32[]{:S(2)}) copy-start(f32[96,768]{1,0:T(8,128)S(1)} %collective-permute-done.19.refs_7_) | copy-start | bytes 884740
  383.4 12.7 %collective-permute-start.18 = (f32[4,96,384]{2,1,0:T(8,128)}, f32[4,96,384]{2,1,0:T(8,128)S(1)}, u32[]{:S(2)}, u32[]{:S(2)}) collective-permute-start(f32[4,96,384]{2,1,0:T(8,128)} %get-tuple-element.178.refs_5_), channel_id=1, source_target_pairs={{0,1},{1,0},{2,3},{3,2},{4,5},{5,4},{6,7},{7,6},{8,9},{9,8},{10,11... | collective-permute-start | bytes 1769480 | tf_op jit(solution)/shard_map/ppermute | solution.py:976
  383.5 19.5 %collective-permute-start.16 = (f32[2,96,768]{2,1,0:T(8,128)}, f32[2,96,768]{2,1,0:T(8,128)}, u32[]{:S(2)}, u32[]{:S(2)}) collective-permute-start(f32[2,96,768]{2,1,0:T(8,128)} %get-tuple-element.173), channel_id=1, source_target_pairs={{0,8},{4,12},{8,0},{12,4},{16,24},{20,28},{24,16},{28,20},{1,9},{5... | collective-permute-start | bytes 1769480 | tf_op jit(solution)/shard_map/ppermute | solution.py:898
  389.8 41.7 %collective-permute-start.26 = (f32[4,96,768]{2,1,0:T(8,128)}, f32[4,96,768]{2,1,0:T(8,128)S(1)}, u32[]{:S(2)}, u32[]{:S(2)}) collective-permute-start(f32[4,96,768]{2,1,0:T(8,128)} %get-tuple-element.191), channel_id=1, source_target_pairs={{0,8},{4,12},{8,0},{12,4},{16,24},{20,28},{24,16},{28,20},{1,9},{5... | collective-permute-start | bytes 3538952 | tf_op jit(solution)/shard_map/ppermute | solution.py:898
  403.0 2.5 copy-start.20
  403.0 4.1 copy-start.19
  405.2 25.5 %collective-permute-start.31 = (f32[1,96,768]{2,1,0:T(8,128)}, f32[1,96,768]{2,1,0:T(8,128)S(1)}, u32[]{:S(2)}, u32[]{:S(2)}) collective-permute-start(f32[1,96,768]{2,1,0:T(8,128)} %get-tuple-element.201), channel_id=1, source_target_pairs={{0,16},{4,20},{8,24},{12,28},{16,0},{20,4},{24,8},{28,12},{1,17},{... | collective-permute-start | bytes 884744 | tf_op jit(solution)/shard_map/ppermute | solution.py:898
  405.5 32.0 %collective-permute-start.25 = (f32[5,96,384]{2,1,0:T(8,128)S(1)}, f32[5,96,384]{2,1,0:T(8,128)S(1)}, u32[]{:S(2)}, u32[]{:S(2)}) collective-permute-start(f32[5,96,384]{2,1,0:T(8,128)S(1)} %copy-done.20), channel_id=1, source_target_pairs={{0,4},{4,0},{8,12},{12,8},{16,20},{20,16},{24,28},{28,24},{1,5},{5... | collective-permute-start | bytes 2211848 | tf_op jit(solution)/shard_map/ppermute | solution.py:898
  407.1 48.9 %collective-permute-start.24 = (f32[5,96,384]{2,1,0:T(8,128)S(1)}, f32[5,96,384]{2,1,0:T(8,128)S(1)}, u32[]{:S(2)}, u32[]{:S(2)}) collective-permute-start(f32[5,96,384]{2,1,0:T(8,128)S(1)} %copy-done.19), channel_id=1, source_target_pairs={{0,8},{4,12},{8,0},{12,4},{16,24},{20,28},{24,16},{28,20},{1,9},{5... | collective-permute-start | bytes 2211848 | tf_op jit(solution)/shard_map/ppermute | solution.py:898
  407.9 22.8 %copy-start.18 = (f32[1,96,768]{2,1,0:T(8,128)S(1)}, f32[1,96,768]{2,1,0:T(8,128)}, u32[]{:S(2)}) copy-start(f32[1,96,768]{2,1,0:T(8,128)} %get-tuple-element.186.refs_2_) | copy-start | bytes 884740
  410.9 66.7 %collective-permute-start.23 = (f32[6,196,128]{2,1,0:T(8,128)}, f32[6,196,128]{2,1,0:T(8,128)}, u32[]{:S(2)}, u32[]{:S(2)}) collective-permute-start(f32[6,196,128]{2,1,0:T(8,128)} %get-tuple-element.188), channel_id=1, source_target_pairs={{0,1},{1,0},{2,3},{3,2},{4,5},{5,4},{6,7},{7,6},{8,9},{9,8},{10,11... | collective-permute-start | bytes 1806344 | tf_op jit(solution)/shard_map/ppermute | solution.py:976
  435.0 45.1 %collective-permute-start.32 = (f32[2,96,768]{2,1,0:T(8,128)}, f32[2,96,768]{2,1,0:T(8,128)S(1)}, u32[]{:S(2)}, u32[]{:S(2)}) collective-permute-start(f32[2,96,768]{2,1,0:T(8,128)} %get-tuple-element.202), channel_id=1, source_target_pairs={{0,16},{4,20},{8,24},{12,28},{16,0},{20,4},{24,8},{28,12},{1,17},{... | collective-permute-start | bytes 1769480 | tf_op jit(solution)/shard_map/ppermute | solution.py:898
  441.6 27.4 %collective-permute-start.28 = (f32[3,96,384]{2,1,0:T(8,128)}, f32[3,96,384]{2,1,0:T(8,128)S(1)}, u32[]{:S(2)}, u32[]{:S(2)}) collective-permute-start(f32[3,96,384]{2,1,0:T(8,128)} %get-tuple-element.196), channel_id=1, source_target_pairs={{0,8},{4,12},{8,0},{12,4},{16,24},{20,28},{24,16},{28,20},{1,9},{5... | collective-permute-start | bytes 1327112 | tf_op jit(solution)/shard_map/ppermute | solution.py:898
  460.0 11.8 %collective-permute-start.27 = (f32[3,96,384]{2,1,0:T(8,128)}, f32[3,96,384]{2,1,0:T(8,128)S(1)}, u32[]{:S(2)}, u32[]{:S(2)}) collective-permute-start(f32[3,96,384]{2,1,0:T(8,128)} %get-tuple-element.195), channel_id=1, source_target_pairs={{0,4},{4,0},{8,12},{12,8},{16,20},{20,16},{24,28},{28,24},{1,5},{5... | collective-permute-start | bytes 1327112 | tf_op jit(solution)/shard_map/ppermute | solution.py:898
  471.8 4.4 copy-start.30
  474.7 5.4 %copy-start.13 = (f32[2,96,768]{2,1,0:T(8,128)S(1)}, f32[2,96,768]{2,1,0:T(8,128)}, u32[]{:S(2)}) copy-start(f32[2,96,768]{2,1,0:T(8,128)} %get-tuple-element.192.refs_5_) | copy-start | bytes 1769476
  474.7 23.5 %collective-permute-start.30 = (f32[2,96,384]{2,1,0:T(8,128)}, f32[2,96,384]{2,1,0:T(8,128)S(1)}, u32[]{:S(2)}, u32[]{:S(2)}) collective-permute-start(f32[2,96,384]{2,1,0:T(8,128)} %get-tuple-element.200), channel_id=1, source_target_pairs={{0,16},{4,20},{8,24},{12,28},{16,0},{20,4},{24,8},{28,12},{1,17},{... | collective-permute-start | bytes 884744 | tf_op jit(solution)/shard_map/ppermute | solution.py:898
  476.2 27.1 %collective-permute-start.29 = (f32[2,96,384]{2,1,0:T(8,128)S(1)}, f32[2,96,384]{2,1,0:T(8,128)S(1)}, u32[]{:S(2)}, u32[]{:S(2)}) collective-permute-start(f32[2,96,384]{2,1,0:T(8,128)S(1)} %copy-done.30), channel_id=1, source_target_pairs={{0,16},{4,20},{8,24},{12,28},{16,0},{20,4},{24,8},{28,12},{1,17},{... | collective-permute-start | bytes 884744 | tf_op jit(solution)/shard_map/ppermute | solution.py:898
  480.1 18.1 %copy-start.17 = (f32[2,96,384]{2,1,0:T(8,128)S(1)}, f32[2,96,384]{2,1,0:T(8,128)}, u32[]{:S(2)}) copy-start(f32[2,96,384]{2,1,0:T(8,128)} %get-tuple-element.198.refs_3_) | copy-start | bytes 884740
  480.2 23.1 %copy-start.16 = (f32[2,96,384]{2,1,0:T(8,128)S(1)}, f32[2,96,384]{2,1,0:T(8,128)}, u32[]{:S(2)}) copy-start(f32[2,96,384]{2,1,0:T(8,128)} %get-tuple-element.197.refs_5_) | copy-start | bytes 884740
  498.3 8.8 %copy-start.1 = (f32[2,169,24]{1,2,0:T(8,128)S(1)}, f32[2,169,24]{1,2,0:T(8,128)}, u32[]{:S(2)}) copy-start(f32[2,169,24]{1,2,0:T(8,128)} %param.24) | copy-start | bytes 97348
  (17 other events, 18.1 us)

commit v3 on v2

--- a/solution.py
+++ b/solution.py
@@ -27,8 +27,9 @@
 EPSILON = 1e-05
 SCALE = HD ** (-0.5)
 NEG = -1e30
-QCH = 384
-FCH = 768
+QCH = 768
+FCH = 1536
+WIN = 2
 N_Q = 3 * D // QCH
 N_F = FF // FCH
 W_UP = D // 2
@@ -158,7 +159,7 @@
     return pl.BlockSpec((1, *dims), lambda a, *_: (a, *(0,) * len(dims)))
 
 
-def call(body, args, in_specs, outs, out_specs, estimate, name, after=(), grid=(), scalars=0, scratch=(), reuse=False):
+def call(body, args, in_specs, outs, out_specs, estimate, name, after=(), grid=(), scalars=0, scratch=(), reuse=0):
     n_in, n_after = len(args), len(after)
 
     def wrapped(*refs):
@@ -174,7 +175,7 @@
             scratch_shapes=list(scratch),
         ),
         out_shape=outs,
-        input_output_aliases={n_in + k: k for k in range(n_after)} if reuse else {},
+        input_output_aliases={n_in + k: k for k in range(reuse)},
         compiler_params=pltpu.CompilerParams(vmem_limit_bytes=VMEM_LIMIT),
         cost_estimate=estimate,
         name=name,
@@ -265,18 +266,31 @@
     )
 
 
-def fwd_body(b, *refs):
+def fwd_body(b, which, *refs):
     a = pl.program_id(0)
     if b == 0:
-        _, p0, p1, *rest = refs
+        at_x, p0, p1, *rest = refs
     else:
         src, mask, *rest = refs
     (
         bias, ln1g, ln1b, bq, bv, bout, ln2g, ln2b, bup, bdown,
         wqkv_h, wout_h, wup_h, wdown_h,
-        z_o, h_o, qkvc_o, o_o, y_o, h2_o, g_o, gp_o, zn_o,
-        wqkv, wout, wup, wdown, qkv_s, o_s, bqkv, acc, bias_s, sem_q, sem_o, sem_u, sem_d,
+        z_h, h_h, qkvc_h, o_h, y_h, h2_h, g_h, gp_h, zn_o,
+        wqkv, wout, wup, wdown, qkv_s, o_s, bqkv, bias_s,
+        z_o, h_o, qkvc_o, o_o, y_o, h2_o, g_o, gp_o, sem_q, sem_o, sem_u, sem_d, sem_out,
     ) = rest
+    at = at_x[0] ^ which if b == 0 else a
+    results = (
+        (z_o, z_h), (h_o, h_h), (qkvc_o, qkvc_h), (o_o, o_h), (y_o, y_h), (h2_o, h2_h), (g_o, g_h), (gp_o, gp_h),
+    )
+
+    def out(k):
+        return pltpu.make_async_copy(results[k][0].at[0], results[k][1].at[at], sem_out.at[k])
+
+    def free(k):
+        @pl.when(a > 0)
+        def _():
+            out(k).wait()
 
     def cp_q(n):
         return pltpu.make_async_copy(
@@ -313,6 +327,7 @@
         bqkv[:, 2 * D :] = bv[b : b + 1, :]
         qkv_s[:, ROWS:, :] = jnp.zeros((3 * NG, PAD_ROWS - ROWS, LANE), F32)
 
+    free(0)
     if b == 0:
         weave(o_s, (p0, p1))
         for g in range(NG):
@@ -322,8 +337,11 @@
         for w in range(2):
             for g in range(NG):
                 bias_s[w * NG + g] = bias[NG + g] + mask[0, w]
+    out(0).start()
     normed, _ = norm_parts(z_o[0])
+    free(1)
     h_o[0] = (normed * ln1g[b : b + 1, :] + ln1b[b : b + 1, :]).astype(BF16)
+    out(1).start()
 
     def qkv_step(n, _):
         wait(cp_q(n))
@@ -338,41 +356,58 @@
     masks = head_masks(TP)
     ones = [m.astype(F32).astype(BF16) for m in head_masks(TQ)]
 
-    def attend(w, _):
-        for g in range(NG):
-            q = qkv_s[g, rows_of(w, TQ), :].astype(BF16)
-            k = qkv_s[NG + g, rows_of(w, TP), :].astype(BF16)
-            v = qkv_s[2 * NG + g, rows_of(w, TP), :].astype(BF16)
+    def attend(step, _):
+        items = [(step * WIN + i, g) for i in range(WIN) for g in range(NG)]
+        qs = [qkv_s[g, rows_of(w, TQ), :].astype(BF16) for w, g in items]
+        ks = [qkv_s[NG + g, rows_of(w, TP), :].astype(BF16) for w, g in items]
+        vs = [qkv_s[2 * NG + g, rows_of(w, TP), :].astype(BF16) for w, g in items]
+        for (w, g), q, k, v in zip(items, qs, ks, vs):
             qkvc_o[0, w, g] = q
             qkvc_o[0, w, NG + g, 0:TP] = k
             qkvc_o[0, w, 2 * NG + g, 0:TP] = v
-            added = bias[g] if b == 0 else bias_s[w // HALF * NG + g]
-            probs = soft(nt(k, spread(q, ones)) + added)
-            o_s[g, rows_of(w, TP), :] = gather_heads(tn(probs.astype(BF16), v), masks)
+        added = [bias[g] if b == 0 else bias_s[w // HALF * NG + g] for w, g in items]
+        scores = [nt(k, spread(q, ones)) + extra for k, q, extra in zip(ks, qs, added)]
+        probs = [soft(score).astype(BF16) for score in scores]
+        for (w, g), prob, v in zip(items, probs, vs):
+            o_s[g, rows_of(w, TP), :] = gather_heads(tn(prob, v), masks)
         return 0
 
-    lax.fori_loop(0, C, attend, 0, unroll=2)
+    free(2)
+    lax.fori_loop(0, C // WIN, attend, 0, unroll=2)
+    out(2).start()
+    free(3)
     for g in range(NG):
         o_o[0, :, LANE * g : LANE * (g + 1)] = o_s[g, 0:ROWS, :].astype(BF16)
+    out(3).start()
     wait(cp_o)
+    free(4)
     y_o[0] = z_o[0] + (nn(o_o[0], wout[...]) + bout[b : b + 1, :])
+    out(4).start()
     normed, _ = norm_parts(y_o[0])
+    free(5)
     h2_o[0] = (normed * ln2g[b : b + 1, :] + ln2b[b : b + 1, :]).astype(BF16)
-    acc[...] = jnp.zeros_like(acc)
-
+    out(5).start()
+    free(6)
+    free(7)
     def mlp_step(n, _):
         wait(cp_u(n))
         up = nn(h2_o[0], wup[:, lanes_at(n, FCH)]) + bup[b : b + 1, lanes_at(n, FCH)]
         act, slope = gelu_parts(up)
-        act = act.astype(BF16)
-        g_o[0, :, lanes_at(n, FCH)] = act
+        g_o[0, :, lanes_at(n, FCH)] = act.astype(BF16)
         gp_o[0, :, lanes_at(n, FCH)] = slope.astype(BF16)
+        return 0
+
+    lax.fori_loop(0, N_F, mlp_step, 0)
+    out(6).start()
+    out(7).start()
+    for n in range(N_F):
         wait(cp_d(n))
-        acc[...] += nn(act, wdown[lanes_at(n, FCH), :])
-        return 0
-
-    lax.fori_loop(0, N_F, mlp_step, 0)
-    zn_o[0] = (y_o[0] + (acc[...] + bdown[b : b + 1, :])).reshape(T, C, D)
+    zn_o[0] = (y_o[0] + (nn(g_o[0], wdown[...]) + bdown[b : b + 1, :])).reshape(T, C, D)
+
+    @pl.when(a == pl.num_programs(0) - 1)
+    def _():
+        for k in range(len(results)):
+            out(k).wait()
 
 
 def block_fwd(b, sources, bias, p, which=None, after=()):
@@ -389,27 +424,25 @@
     ]
     if b == 0:
         specs = [fixed((NG, PIECE, LANE), True)] * 2
-        out_specs = [
-            pl.BlockSpec((1, *o.shape[1:]), lambda a, s, n=len(o.shape) - 1: (s[0] ^ which, *(0,) * n)) for o in outs
-        ]
+        out_specs = [pl.BlockSpec((1, T, C, D), lambda a, s: (s[0] ^ which, 0, 0, 0))]
     else:
         specs = [fixed((2, T, C, D), True), per_half((2, TP, GT))]
-        out_specs = [per_half(o.shape[1:]) for o in outs]
+        out_specs = [per_half((T, C, D))]
     small = (bias, p["ln1_gain"], p["ln1_bias"], p["b_query"], p["b_value"], p["b_out"],
              p["ln2_gain"], p["ln2_bias"], p["b_up"], p["b_down"])
     big = (p["w_qkv"], p["w_out"], p["w_up"], p["w_down"])
     return call(
-        functools.partial(fwd_body, b),
+        functools.partial(fwd_body, b, which),
         (*sources, *small, *big),
         specs + [fixed(v.shape, True) for v in small] + [ANY] * 4,
         outs,
-        out_specs,
-        cost(25 if which is not None else 46),
+        [ANY] * 8 + out_specs,
+        cost(21 if which is not None else 36),
         f"forward_{b}",
         after,
         grid=(2 if which is None else 1,),
         scalars=int(which is not None),
-        reuse=which == 1,
+        reuse=len(outs) if which == 1 else 0,
         scratch=[
             pltpu.VMEM((D, 3 * D), BF16),
             pltpu.VMEM((D, D), BF16),
@@ -418,18 +451,19 @@
             pltpu.VMEM((3 * NG, PAD_ROWS, LANE), F32),
             pltpu.VMEM((NG, PAD_ROWS, LANE), F32),
             pltpu.VMEM((1, 3 * D), F32),
-            pltpu.VMEM((ROWS, D), F32),
             pltpu.VMEM((2 * NG, TP, GT), F32),
+            *(pltpu.VMEM((1, *o.shape[1:]), o.dtype) for o in outs[:8]),
             pltpu.SemaphoreType.DMA((N_Q,)),
             pltpu.SemaphoreType.DMA,
             pltpu.SemaphoreType.DMA((N_F,)),
             pltpu.SemaphoreType.DMA((N_F,)),
+            pltpu.SemaphoreType.DMA((8,)),
         ],
     )
 
 
-def mlp_back_body(b, x_at, src, y, gp, ln2g, wdown_h, wup_h, dd_o, da_o, dy_o, dyr_o, sv_o,
-                  wdown, wup, acc, dz, dd, sem_d, sem_u):
+def mlp_back_body(b, x_at, core, src, y, gp, act, hid, ln2g, wdown_h, wup_h, dd_o, da_o, dy_o, dyr_o, sv_o, down_o, up_o,
+                  wdown, wup, dz, dd, da_s, sem_d, sem_u):
     a = pl.program_id(0)
 
     def cp_u(n):
@@ -466,24 +500,24 @@
                 w = 2 * x + c
                 dd_o[c, 0] = dd[:, MINE * w : MINE * (w + 1)]
 
-    acc[...] = jnp.zeros_like(acc)
-
     def step(n, _):
         wait(cp_d(n))
         grad_act = nt(dd[...], wdown[lanes_at(n, D), :])
         da = (grad_act * gp[0, :, lanes_at(n, D)].astype(F32)).astype(BF16)
 
+        da_s[:, lanes_at(n, D)] = da
+
         @pl.when(n // 2 == x_at[0])
         def _():
             da_o[0, :, lanes_at(n % 2, D)] = da
 
         sv_o[pl.ds(4 + n, 1), :] += colsum(da.astype(F32))
+        return 0
+
+    lax.fori_loop(0, 4, step, 0)
+    for n in range(4):
         wait(cp_u(n))
-        acc[...] += nt(da, wup[:, lanes_at(n, D)])
-        return 0
-
-    lax.fori_loop(0, 4, step, 0)
-    dh2 = acc[...]
+    dh2 = nt(da_s[...], wup[...])
     normed, inverse = norm_parts(y[0])
     sv_o[0:1, :] += colsum(dh2 * normed)
     sv_o[1:2, :] += colsum(dh2)
@@ -492,19 +526,33 @@
     low = dy.astype(BF16)
     dyr_o[0] = low
     sv_o[2:3, :] += colsum(low.astype(F32))
-
-
-def mlp_back(b, x_at, src, y, gp, p, after=()):
+    down = tn(dd_o[1 - core[0], 0], act[0])
+    up = tn(hid[0], da_o[0, :, lanes_at(1 - core[0], D)])
+
+    def put(add):
+        for k in range(8):
+            add_down(down_o, k, down[:, W_UP * k : W_UP * (k + 1)], add)
+            rows = up[D // 8 * k : D // 8 * (k + 1)]
+            up_o[k] = up_o[k] + rows if add else rows
+
+    for half in range(2):
+        pl.when(a == half)(functools.partial(put, half == 1))
+
+
+def mlp_back(b, x_at, core, src, y, gp, act, hid, p, after=()):
     return call(
         functools.partial(mlp_back_body, b),
-        (x_at, src, y, gp, p["ln2_gain"], p["w_down"], p["w_up"]),
-        [SM, fixed((2, T, C, D), True), per_half((ROWS, D)), per_half((ROWS, FF)), fixed((2, D)), ANY, ANY],
+        (x_at, core, src, y, gp, act, hid, p["ln2_gain"], p["w_down"], p["w_up"]),
+        [SM, SM, fixed((2, T, C, D), True), per_half((ROWS, D)), per_half((ROWS, FF)), per_half((ROWS, FF)),
+         per_half((ROWS, D)), fixed((2, D)), ANY, ANY],
         [
             shape((2, 2, ROWS, MINE), BF16),
             shape((2, ROWS, FF // 2), BF16),
             shape((2, ROWS, D), F32),
             shape((2, ROWS, D), BF16),
             shape((8, D), F32),
+            shape((8, *BLOCK), F32),
+            shape((8, *BLOCK), F32),
         ],
         [
             pl.BlockSpec((2, 1, ROWS, MINE), lambda a: (0, a, 0, 0)),
@@ -512,8 +560,10 @@
             per_half((ROWS, D)),
             per_half((ROWS, D)),
             fixed((8, D)),
+            fixed((8, *BLOCK), True),
+            fixed((8, *BLOCK), True),
         ],
-        cost(23),
+        cost(22),
         f"mlp_back_{b}",
         after,
         grid=(2,),
@@ -521,8 +571,8 @@
             pltpu.VMEM((FF, D), BF16),
             pltpu.VMEM((D, FF), BF16),
             pltpu.VMEM((ROWS, D), F32),
-            pltpu.VMEM((ROWS, D), F32),
             pltpu.VMEM((ROWS, D), BF16),
+            pltpu.VMEM((ROWS, FF), BF16),
             pltpu.SemaphoreType.DMA((4,)),
             pltpu.SemaphoreType.DMA((4,)),
         ],
@@ -562,14 +612,14 @@
         put(h, total)
 
 
-def attn_back_body(b, x_at, dyr, qkvc, dy, z, *refs):
+def attn_back_body(b, x_at, core, dyr, qkvc, dy, z, hid, att, *refs):
     if b == 1:
         mask, *refs = refs
     bias, ln1g, *refs = refs
     if b == 0:
         sv_m0, sv_a1, sv_m1, table1, *refs = refs
-    (wout_h, wqkv_h, r3_o, sv_o, sum_o, grad_o,
-     wout, wqkv, do_s, dqkv_s, dq, acc, bias_s, ds_o, moved, sem_o, sem_q) = refs
+    (wout_h, wqkv_h, r3_o, sv_o, sum_o, grad_o, *part_o,
+     wout, wqkv, do_s, dqkv_s, dq, bias_s, ds_o, moved, sem_o, sem_q) = refs
     a = pl.program_id(0)
     cp_o = pltpu.make_async_copy(wout_h.at[b], wout, sem_o)
 
@@ -603,37 +653,37 @@
     masks = head_masks(TP)
     ones = [m.astype(F32).astype(BF16) for m in head_masks(TQ)]
 
-    def attend(w, _):
-        for g in range(NG):
-            q = qkvc[0, w, g]
-            k = qkvc[0, w, NG + g, 0:TP]
-            v = qkvc[0, w, 2 * NG + g, 0:TP]
-            q_wide = spread(q, ones)
-            do_wide = spread(do_s[g, rows_of(w, TQ), :].astype(BF16), ones)
-            added = bias[g] if b == 0 else bias_s[w // HALF * NG + g]
-            probs = soft(nt(k, q_wide) + added)
-            weighted = probs * nt(v, do_wide)
-            ds = weighted - probs * jnp.sum(weighted, axis=0, keepdims=True)
-            ds_o[g] += ds
-            low = ds.astype(BF16)
-            dqkv_s[g, rows_of(w, TP), :] = gather_heads(tn(low, k), masks) * SCALE
-            dqkv_s[NG + g, rows_of(w, TP), :] = nn(low, q_wide)
-            dqkv_s[2 * NG + g, rows_of(w, TP), :] = nn(probs.astype(BF16), do_wide)
+    def attend(step, _):
+        items = [(step * WIN + i, g) for i in range(WIN) for g in range(NG)]
+        ks = [qkvc[0, w, NG + g, 0:TP] for w, g in items]
+        q_wide = [spread(qkvc[0, w, g], ones) for w, g in items]
+        do_wide = [spread(do_s[g, rows_of(w, TQ), :].astype(BF16), ones) for w, g in items]
+        added = [bias[g] if b == 0 else bias_s[w // HALF * NG + g] for w, g in items]
+        scores = [nt(k, q) + extra for k, q, extra in zip(ks, q_wide, added)]
+        dprobs = [nt(qkvc[0, w, 2 * NG + g, 0:TP], d) for (w, g), d in zip(items, do_wide)]
+        probs = [soft(score) for score in scores]
+        weighted = [p * d for p, d in zip(probs, dprobs)]
+        ds = [x - p * jnp.sum(x, axis=0, keepdims=True) for x, p in zip(weighted, probs)]
+        for (w, g), d in zip(items, ds):
+            ds_o[g] += d
+        low = [d.astype(BF16) for d in ds]
+        dks = [nn(x, q) for x, q in zip(low, q_wide)]
+        dvs = [nn(p.astype(BF16), d) for p, d in zip(probs, do_wide)]
+        dqs = [tn(x, k) for x, k in zip(low, ks)]
+        for (w, g), d_q, d_k, d_v in zip(items, dqs, dks, dvs):
+            dqkv_s[g, rows_of(w, TP), :] = gather_heads(d_q, masks) * SCALE
+            dqkv_s[NG + g, rows_of(w, TP), :] = d_k
+            dqkv_s[2 * NG + g, rows_of(w, TP), :] = d_v
         return 0
 
-    lax.fori_loop(0, C, attend, 0, unroll=2)
+    lax.fori_loop(0, C // WIN, attend, 0)
     for g in range(3 * NG):
         dq[:, LANE * g : LANE * (g + 1)] = dqkv_s[g, 0:ROWS, :].astype(BF16)
     sv_o[2:3, :] += colsum(dq[:, 0:D].astype(F32))
     sv_o[3:4, :] += colsum(dq[:, 2 * D :].astype(F32))
-    acc[...] = jnp.zeros_like(acc)
-
-    def step(n, _):
+    for n in range(N_Q):
         wait(cp_q(n))
-        acc[...] += nt(dq[:, lanes_at(n, QCH)], wqkv[:, lanes_at(n, QCH)])
-        return 0
-
-    lax.fori_loop(0, N_Q, step, 0)
+    dh = nt(dq[...], wqkv[...])
     for x in range(2):
 
         @pl.when(x_at[0] == x)
@@ -644,11 +694,20 @@
                     [dq[:, 3 * MINE * w : 3 * MINE * (w + 1)], dyr[0, :, MINE * w : MINE * (w + 1)]], axis=1
                 )
 
-    dh = acc[...]
     normed, inverse = norm_parts(z[0])
     sv_o[0:1, :] += colsum(dh * normed)
     sv_o[1:2, :] += colsum(dh)
     grad_o[0] = (dy[0] + norm_back(dh, normed, inverse, ln1g[b : b + 1, :])).reshape(T, C, D)
+    other = r3_o[1 - core[0], 0]
+    parts = [attn_columns(tn, hid[0], att[0], other[:, W_UP * n : W_UP * (n + 1)], W_UP * n, W_UP) for n in range(2)]
+
+    def put_parts(add):
+        for out, part in zip(part_o, parts):
+            blocks = part.reshape(8, D // 8, W_UP)
+            out[...] = out[...] + blocks if add else blocks
+
+    for half in range(2):
+        pl.when(a == half)(functools.partial(put_parts, half == 1))
 
     @pl.when(a == 1)
     def _():
@@ -658,29 +717,36 @@
             return
         sum_o[...] = jnp.zeros_like(sum_o)
         for at, ref in ((0, sv_o), (4, sv_m0), (12, sv_a1), (16, sv_m1)):
-            sum_o[at : at + ref.shape[0], :] = ref[...]
+            for k in range(2):
+                sum_o[24 * k + at : 24 * k + at + ref.shape[0], :] = ref[:, W_UP * k : W_UP * (k + 1)]
+
+        def put(h, v, at=48):
+            sum_o[at + NG * h : at + NG * (h + 1), 0:TABLE] = v[0:NG]
+
+        sum_table(moved, put)
         for h in range(PER):
-            sum_o[24 + 8 * h : 32 + 8 * h, TABLE : 2 * TABLE] = table1[h]
-        sum_table(moved, lambda h, v: sum_o.__setitem__((slice(24 + 8 * h, 32 + 8 * h), slice(0, TABLE)), v))
-
-
-def attn_back(b, x_at, dyr, qkvc, dy, z, mask, bias, p, sums=(), after=()):
+            put(h, table1[h], 72)
+
+
+def attn_back(b, x_at, core, dyr, qkvc, dy, z, hid, att, mask, bias, p, sums=(), after=()):
     masks = [mask] if b else []
-    sum_shape = (PER, 8, TABLE) if b else BLOCK
+    sum_shape = (PER, 8, TABLE) if b else (D // 8, W_UP)
     return call(
         functools.partial(attn_back_body, b),
-        (x_at, dyr, qkvc, dy, z, *masks, bias, p["ln1_gain"], *sums, p["w_out"], p["w_qkv"]),
-        [SM, per_half((ROWS, D)), per_half((C, 3 * NG, TQ, LANE)), per_half((ROWS, D)), per_half((ROWS, D))]
+        (x_at, core, dyr, qkvc, dy, z, hid, att, *masks, bias, p["ln1_gain"], *sums, p["w_out"], p["w_qkv"]),
+        [SM, SM, per_half((ROWS, D)), per_half((C, 3 * NG, TQ, LANE))] + [per_half((ROWS, D))] * 4
         + [per_half((2, TP, GT))] * b
         + [fixed(bias.shape, True), fixed((2, D)), *(fixed(v.shape) for v in sums), ANY, ANY],
-        [shape((2, 2, ROWS, D), BF16), shape((4, D), F32), shape(sum_shape, F32), shape((2, T, C, D), F32)],
+        [shape((2, 2, ROWS, D), BF16), shape((4, D), F32), shape(sum_shape, F32), shape((2, T, C, D), F32)]
+        + [shape((8, D // 8, W_UP), F32)] * 2,
         [
             pl.BlockSpec((2, 1, ROWS, D), lambda a: (0, a, 0, 0)),
             fixed((4, D)),
             fixed(sum_shape),
             per_half((T, C, D)),
-        ],
-        cost(48),
+        ]
+        + [fixed((8, D // 8, W_UP), True)] * 2,
+        cost(31),
         f"attn_back_{b}",
         after,
         grid=(2,),
@@ -690,7 +756,6 @@
             pltpu.VMEM((NG, PAD_ROWS, LANE), F32),
             pltpu.VMEM((3 * NG, PAD_ROWS, LANE), F32),
             pltpu.VMEM((ROWS, 3 * D), BF16),
-            pltpu.VMEM((ROWS, D), F32),
             pltpu.VMEM((2 * NG, TP, GT), F32),
             pltpu.VMEM((NG, TP, GT), F32),
             pltpu.VMEM((PER, 8 * TP, LANE), F32),
@@ -722,55 +787,34 @@
     out[i, :, W_UP:] = total[half:]
 
 
+def add_down(out, i, total, add):
+    put_down(out, i, total + get_down(out[i]) if add else total)
+
+
 def get_down(block):
     return jnp.concatenate([block[:, 0:W_UP], block[:, W_UP:]], axis=0)
 
 
-def mlp_other(bits, dd, act, hid, da, after=()):
-    def down(s, l, r, out):
-        for k in range(2):
-            lanes = slice(k * W_UP, (k + 1) * W_UP)
-            put_down(out, k, halves(lambda a: l[0, a], lambda a: r[a, :, lanes]))
-
-    out = shape((16, *BLOCK), F32)
-    first = call(
-        down, (bits, dd, act),
-        [pl.BlockSpec((1, 2, ROWS, MINE), lambda i, s: (1 - s[0], 0, 0, 0)),
-         pl.BlockSpec((2, ROWS, D), lambda i, s: (0, 0, i))],
-        out, pl.BlockSpec((2, *BLOCK), lambda i, s: (i, 0, 0)),
-        cost(6.5), "down_other", after, (4,), 1,
-    )
-
-    def up(s, l, r, out):
-        out[...] = halves(lambda a: l[a], lambda a: r[a]).reshape(8, D // 8, W_UP)
-
-    return call(
-        up, (bits, hid, da),
-        [fixed((2, ROWS, D)), pl.BlockSpec((2, ROWS, W_UP), lambda n, s: (0, 0, 2 * (1 - s[0]) + n))],
-        [out], [pl.BlockSpec((8, D // 8, W_UP), lambda n, s: (1, 0, n))],
-        cost(5.4), "up_other", (first,), (2,), 1, reuse=True,
-    )[0]
-
-
-def mlp_mine(bits, dd, act, hid, da, recv, first, after=()):
-    def down(s, l, rk, rs, gk, gs, keep, send):
+def down_mine(bits, dd, act, recv, first, after=()):
+    def body(s, l, rk, rs, gk, gs, keep, send):
         put_down(keep, 0, halves(lambda a: l[0, a], lambda a: rk[a]) + get_down(gk[0]))
         put_down(send, 0, halves(lambda a: l[0, a], lambda a: rs[a]) + get_down(gs[0]))
 
     def block(flip):
         return lambda i, s: insert_bit(i, first, s[1 + first] ^ flip)
 
-    outs = [shape((8, *BLOCK), F32)] * 2
-    half = call(
-        down, (bits, dd, act, act, recv, recv),
+    return call(
+        body, (bits, dd, act, act, recv, recv),
         [pl.BlockSpec((1, 2, ROWS, MINE), lambda i, s: (s[0], 0, 0, 0))]
         + [pl.BlockSpec((2, ROWS, W_UP), lambda i, s, m=block(f): (0, 0, m(i, s))) for f in (0, 1)]
         + [pl.BlockSpec((1, *BLOCK), lambda i, s, m=block(f): (m(i, s), 0, 0)) for f in (0, 1)],
-        outs, [pl.BlockSpec((1, *BLOCK), lambda i, s: (i, 0, 0))] * 2,
+        [shape((4, *BLOCK), F32)] * 2, [pl.BlockSpec((1, *BLOCK), lambda i, s: (i, 0, 0))] * 2,
         cost(6.9), "down_mine", after, (4,), 1,
     )
 
-    def up(s, l, r, got, keep, send):
+
+def up_mine(bits, hid, da, recv, first, after=()):
+    def body(s, l, r, got, keep, send):
         total = halves(lambda a: l[a], lambda a: r[a])
         mine = s[1 + first] == 0
         for i, j, k, p, q in row_pairs(total, first):
@@ -779,49 +823,31 @@
             send[i] = jnp.where(mine, q, p)
 
     return call(
-        up, (bits, hid, da, recv),
+        body, (bits, hid, da, recv),
         [fixed((2, ROWS, D)), pl.BlockSpec((2, ROWS, W_UP), lambda n, s: (0, 0, 2 * s[0] + n)),
-         pl.BlockSpec((8, D // 8, W_UP), lambda n, s: (1, 0, n))],
-        outs, [pl.BlockSpec((4, D // 8, W_UP), lambda n, s: (1, 0, n))] * 2,
-        cost(5.7), "up_mine", half, (2,), 1, reuse=True,
-    )
-
-
-def attn_total(hid, att, r, lo, width):
+         pl.BlockSpec((8, D // 8, W_UP), lambda n, s: (0, 0, n))],
+        [shape((4, *BLOCK), F32)] * 2, [pl.BlockSpec((4, D // 8, W_UP), lambda n, s: (0, 0, n))] * 2,
+        cost(5.7), "up_mine", after, (2,), 1,
+    )
+
+
+def attn_columns(product, hid, att, r, lo, width):
     edge = 3 * MINE
     cut = edge // LANE * LANE
-
-    def product(left, a, b):
-        return halves(lambda k: left[k], lambda k: r[k, :, a - lo : b - lo])
-
     parts = []
     if lo < cut:
-        parts.append(product(hid, lo, min(cut, lo + width)))
+        parts.append(product(hid, r[..., 0 : min(cut - lo, width)]))
     if lo + width > cut:
         lane = lax.broadcasted_iota(jnp.int32, (D, LANE), 1)
-        span = (cut, cut + LANE)
-        parts.append(jnp.where(lane < edge - cut, product(hid, *span), product(att, *span)))
+        right = r[..., cut - lo : cut - lo + LANE]
+        parts.append(jnp.where(lane < edge - cut, product(hid, right), product(att, right)))
     if lo + width > cut + LANE:
-        parts.append(product(att, cut + LANE, lo + width))
+        parts.append(product(att, r[..., cut - lo + LANE : width]))
     return parts[0] if len(parts) == 1 else jnp.concatenate(parts, axis=1)
 
 
-def attn_other(bits, hid, att, r3, after=()):
-    def body(s, h, o, r, *outs):
-        for n in range(2):
-
-            @pl.when(pl.program_id(0) == n)
-            def _():
-                total = attn_total(h, o, r.at[0], n * W_UP, W_UP).reshape(8, D // 8, W_UP)
-                outs[2 * n][...] = total[0:4]
-                outs[2 * n + 1][...] = total[4:8]
-
-    right = pl.BlockSpec((1, 2, ROWS, W_UP), lambda n, s: (1 - s[0], 0, 0, n))
-    return call(
-        body, (bits, hid, att, r3), [fixed((2, ROWS, D)), fixed((2, ROWS, D)), right],
-        [shape((4, D // 8, W_UP), F32)] * 4, [fixed((4, D // 8, W_UP))] * 4,
-        cost(7), "attn_other", after, (2,), 1,
-    )
+def two_halves(left, right):
+    return tn(left[0], right[0]) + tn(left[1], right[1])
 
 
 def attn_mine(bits, hid, att, r3, recv, first, cols, small=None, after=()):
@@ -829,15 +855,15 @@
     width = W_UP * len(cols)
 
     def body(s, h, o, r, *refs):
-        gots, more, (keep, send) = refs[: 2 * len(cols)], refs[2 * len(cols) : -2], refs[-2:]
+        gots, more, (keep, send) = refs[: len(cols)], refs[len(cols) : -2], refs[-2:]
         for k, n in enumerate(cols):
 
             @pl.when(pl.program_id(0) == k)
             def _():
-                total = attn_total(h, o, r.at[0], n * W_UP, W_UP)
+                total = attn_columns(two_halves, h, o, r[0], n * W_UP, W_UP)
                 mine = s[1 + first] == 0
                 for i, j, jj, p, q in row_pairs(total, first):
-                    p, q = p + gots[2 * k + j // 4][j % 4], q + gots[2 * k + jj // 4][jj % 4]
+                    p, q = p + gots[k][j], q + gots[k][jj]
                     keep[i] = jnp.where(mine, p, q)
                     send[i] = jnp.where(mine, q, p)
                 if extra:
@@ -853,11 +879,11 @@
     ]
     args = [bits, hid, att, r3]
     for n in cols:
-        args += recv[2 * n : 2 * n + 2]
-        specs += [fixed((4, D // 8, W_UP))] * 2
+        args.append(recv[n])
+        specs.append(fixed((8, D // 8, W_UP)))
     if extra:
         args += small
-        specs += [pl.BlockSpec((D // 8, W_UP), lambda n, s: (0, at(n)))] * 2
+        specs += [fixed((D // 8, W_UP))] * 2
     out = pl.BlockSpec((4 + extra, D // 8, W_UP), lambda n, s: (0, 0, n))
     return call(
         body, args, specs, [shape((4 + extra, D // 8, width), F32)] * 2, [out] * 2,
@@ -865,26 +891,49 @@
     )
 
 
-def split_sum(kept, recv, place, bit, extra, after=()):
-    n, r, w = recv.shape
+def split_sum(streams, extra, after=(), through=()):
+    n = streams[0][1].shape[0]
     half = (n - extra) // 2
 
-    def body(s, ka, ra, kb, rb, keep_o, send_o):
-        keep_o[...] = ka[...] + ra[...]
-        send_o[...] = kb[...] + rb[...]
-
-    def at(flip):
-        def index(i, s):
-            j = insert_bit(i, place, s[0] ^ flip)
-            return (jnp.where(i == half, 2 * half, j) if extra else j, 0, 0)
-
-        return pl.BlockSpec((1, r, w), index)
-
-    return call(
-        body, (jnp.reshape(bit, (1,)), kept, recv, kept, recv), [at(0), at(0), at(1), at(1)],
-        [shape((half + extra, r, w), F32)] * 2, [pl.BlockSpec((1, r, w), lambda i, s: (i, 0, 0))] * 2,
-        cost(1.5 + n * r * w * 5e-6), "split_sum", after, (half + extra,), 1,
-    )
+    def body(s, *refs):
+        ins, outs = refs[: 4 * len(streams)], refs[4 * len(streams) + len(through) :]
+        for k in range(len(streams)):
+            ka, ra, kb, rb = ins[4 * k : 4 * k + 4]
+            outs[2 * k][...] = ka[...] + ra[...]
+            outs[2 * k + 1][...] = kb[...] + rb[...]
+
+    args, specs = [jnp.stack([bit for *_, bit in streams])], []
+    outs, out_specs = [shape(a.shape, a.dtype) for a in through], [ANY] * len(through)
+    for k, (kept, recv, place, _) in enumerate(streams):
+        block = (1, *recv.shape[1:])
+
+        def at(flip, k=k, place=place, block=block):
+            def index(i, s):
+                j = insert_bit(i, place, s[k] ^ flip)
+                return (jnp.where(i == half, 2 * half, j) if extra else j, 0, 0)
+
+            return pl.BlockSpec(block, index)
+
+        args += [kept, recv, kept, recv]
+        specs += [at(0), at(0), at(1), at(1)]
+        outs += [shape((half + extra, *recv.shape[1:]), F32)] * 2
+        out_specs += [pl.BlockSpec(block, lambda i, s: (i, 0, 0))] * 2
+    size = sum(recv.size for _, recv, *_ in streams)
+    return call(
+        body, args, specs, outs, out_specs, cost(1.5 + size * 5e-6), "split_sum", (*through, *after), (half + extra,), 1,
+        reuse=len(through),
+    )
+
+
+def steps(*pairs, after=(), through=()):
+    args = []
+    for s, name in pairs:
+        args.append((s.kept, s.recv, len(s.names) - 1 - s.names.index(name), s.links[name][2]))
+    outs = split_sum(args, pairs[0][0].extra, after, through)
+    passed, outs = outs[: len(through)], outs[len(through) :]
+    for k, (s, name) in enumerate(pairs):
+        s.send(name, outs[2 * k], outs[2 * k + 1])
+    return (outs[0], *passed) if through else outs[0]
 
 
 class Halving:
@@ -899,12 +948,34 @@
         return kept
 
     def step(self, name, after=()):
-        place = len(self.names) - 1 - self.names.index(name)
-        kept, out = split_sum(self.kept, self.recv, place, self.links[name][2], self.extra, after)
-        return self.send(name, kept, out)
-
-    def result(self):
-        return self.kept + self.recv
+        return steps((self, name), after=after)
+
+    def pair(self):
+        return self.kept, self.recv
+
+
+def last_sums(downs, ups, att0, att1, after=()):
+    pairs = [*downs, *ups, *att0, att1]
+
+    def body(*refs):
+        ins, (qkv, out, up, down, small) = refs[: 2 * len(pairs)], refs[2 * len(pairs) :]
+        total = [ins[2 * i][0] + ins[2 * i + 1][0] for i in range(len(pairs))]
+        for b in range(2):
+            down[b] = get_down(total[b])
+            up[b] = total[2 + b]
+        edge = 3 * MINE
+        for b, att in enumerate((jnp.concatenate([total[4], total[5]], axis=1), total[6])):
+            qkv[b] = att[:, 0:edge]
+            out[b] = att[:, edge:]
+        small[...] = ins[8][1] + ins[9][1]
+
+    rows = D // 8
+    return call(
+        body, [a for pair in pairs for a in pair], [VM] * (2 * len(pairs)),
+        [shape((2, rows, 3 * MINE), F32), shape((2, rows, MINE), F32), shape((2, rows, D), F32),
+         shape((2, MINE, W_UP), F32), shape((rows, W_UP), F32)],
+        [VM] * 5, cost(4), "last_sums", after,
+    )
 
 
 def scatter_rest(block, dim, img, sub):
@@ -993,72 +1064,68 @@
     z1, h1, qkvc1, o1, y1, h21, g1, gp1, zn = fwd1
     ct = join_pieces(at_x, (ct_mine, ct_near, *ct_far), (zn,))
 
-    def stream(first, extra=0, more=()):
-        return Halving([*more, *(k for k in (2, 1, 0) if k != first)], links, extra)
-
-    mlp1, mlp0 = (stream(0, 0, ("which",)) for _ in range(2))
-    att1, att0 = stream(0), [stream(0, 1), stream(1, 1)]
-
-    dd1, da1, dy, dyr, sv_m1 = mlp_back(1, at_x, ct, y1, gp1, p)
-    part = mlp_other(bits, dd1, g1, h21, da1)
-    mlp_x = swap(part)
-    r31, sv_a1, table1, grad1 = attn_back(1, at_x, dyr, qkvc1, dy, z1, mask, bias, p, (), (part,))
-    last = mlp1.send(0, *mlp_mine(bits, dd1, g1, h21, da1, mlp_x, 0, (sv_a1,)))
-    part = attn_other(bits, h1, o1, r31, (last,))
+    def stream(first, extra=0):
+        return Halving([k for k in (2, 1, 0) if k != first], links, extra)
+
+    down1, up1, att1, down0, up0 = (stream(k) for k in (0, 1, 0, 0, 1))
+    att0 = [stream(0, 1), stream(1)]
+
+    dd1, da1, dy, dyr, sv_m1, *part = mlp_back(1, at_x, at_core, ct, y1, gp1, g1, h21, p)
+    down_x, up_x = (swap(a) for a in part)
+    r31, sv_a1, table1, grad1, *part = attn_back(
+        1, at_x, at_core, dyr, qkvc1, dy, z1, h1, o1, mask, bias, p, (), (part[0],)
+    )
     att_x = [swap(a) for a in part]
-
-    dd0, da0, dy, dyr, sv_m0 = mlp_back(0, at_x, grad1, y0, gp0, p, (part[3],))
-    last = att1.send(0, *attn_mine(bits, h1, o1, r31, att_x, 0, (0, 1), None, (sv_m0,)))
+    last = down1.send(0, *down_mine(bits, dd1, g1, down_x, 0, (sv_a1,)))
+    last = up1.send(1, *up_mine(bits, h21, da1, up_x, 1, (last,)))
+
+    dd0, da0, dy, dyr, sv_m0, *part = mlp_back(0, at_x, at_core, grad1, y0, gp0, g0, h20, p, (last, *att_x))
+    last, *part = steps((down1, 1), (up1, 0), after=(sv_m0,), through=part)
+    down_x, up_x = (swap(a) for a in part)
+    last = att1.send(0, *attn_mine(bits, h1, o1, r31, att_x, 0, (0, 1), None, (last,)))
     out_mine, out_other = own_quadrants(at_x, zn, True, (last,))
-    last = mlp1.step(1, (out_mine,))
-    part = mlp_other(bits, dd0, g0, h20, da0, (last,))
-    mlp_x = swap(part)
     out_x = swap(out_other)
-    block_out = token_major(at_core, crop_count, out_mine, out_x, (part,))
-    last = mlp0.send(0, *mlp_mine(bits, dd0, g0, h20, da0, mlp_x, 0, (block_out,)))
-    last = att1.step(1, (last,))
-    last = mlp1.step(2, (last,))
-    r30, sv_a0, small, grad0 = attn_back(
-        0, at_x, dyr, qkvc0, dy, z0, mask, bias, p, (sv_m0, sv_a1, sv_m1, table1), (last,)
-    )
-    part = attn_other(bits, h0, o0, r30)
+    last = down0.send(0, *down_mine(bits, dd0, g0, down_x, 0, (out_mine,)))
+    last = up0.send(1, *up_mine(bits, h20, da0, up_x, 1, (last,)))
+    last = steps((down1, 2), (up1, 2), after=(last,))
+    r30, sv_a0, small, grad0, *part = attn_back(
+        0, at_x, at_core, dyr, qkvc0, dy, z0, h0, o0, mask, bias, p, (sv_m0, sv_a1, sv_m1, table1), (last,)
+    )
+    last, small, *part = steps(
+        (up0, 0), (down0, 1), (att1, 1), after=(sv_a0, down1.recv, up1.recv), through=(small, *part)
+    )
     att_x = [swap(a) for a in part]
     small = [small, swap(small)]
-    last = mlp0.step(1, (part[3],))
-    for k in range(2):
-        kept, out = attn_mine(bits, h0, o0, r30, att_x, k, (k,), small, (last,))
-        last = att0[k].send(k, kept, out)
-    last = att1.step(2, (last,))
-    in_mine, in_other = own_quadrants(at_x, grad0, False, (last,))
+    block_out = token_major(at_core, crop_count, out_mine, out_x, (last,))
+    in_mine, in_other = own_quadrants(at_x, grad0, False, (block_out,))
     in_x = swap(in_other)
     last = in_mine
-    for s, name in ((mlp0, 2), (att0[0], 1), (att0[1], 0), (att0[0], 2), (att0[1], 2)):
-        last = s.step(name, (last,))
-    grad_tokens = crop_major(at_core, in_mine, in_x, (last,)).reshape(C, 1, T, D)
-
-    parts = [a.result() for a in att0]
-    g_att = (jnp.concatenate([a[0] for a in parts], axis=1), att1.result()[0])
-    small = jnp.concatenate([a[1] for a in parts], axis=1)[:56]
+    for k in range(2):
+        kept, out = attn_mine(bits, h0, o0, r30, att_x, k, (k,), None if k else small, (last,))
+        last = att0[k].send(k, kept, out)
+    last = steps((up0, 2), (down0, 2), (att1, 2), after=(last,))
+    last = att0[0].step(1, (last, up0.recv))
+    last = att0[1].step(0, (last, down0.recv))
+    last = att0[0].step(2, (last,))
+    last = att0[1].step(2, (last,))
+    grad_tokens = crop_major(at_core, in_mine, in_x, (last,))
+
+    g_qkv, g_out, g_up, g_down, small = last_sums(
+        (down0.pair(), down1.pair()), (up0.pair(), up1.pair()), [a.pair() for a in att0], att1.pair(), (grad_tokens,)
+    )
     for k in range(sub.bit_length() - 1):
         small = small + lax.ppermute(small, "img", [(i, i ^ (1 << k)) for i in range(n_img)])
-    mats = []
-    for b, mlp in enumerate((mlp0, mlp1)):
-        att = scatter_rest(g_att[b], 0, img, sub)
-        down, up = mlp.result()
-        g_down = scatter_rest(get_down(down), 1, img, sub)
-        g_up = scatter_rest(up, 0, img, sub)
-        mats.append((att[:, : 3 * D // 4], att[:, 3 * D // 4 :], g_up, g_down.T))
-
-    g_qkv, g_out, g_up, g_down = (jnp.stack(pair) for pair in zip(*mats))
-    table = small[24:].reshape(PER, 8, 3, TABLE)[:, :NG, :2, :169].transpose(2, 3, 1, 0).reshape(2, 169, HEADS)
+    g_qkv, g_out, g_up = (scatter_rest(g, 1, img, sub) for g in (g_qkv, g_out, g_up))
+    g_down = scatter_rest(g_down, 2, img, sub).transpose(0, 2, 1)
+    table = small[48:, :169].reshape(2, PER, NG, 169).transpose(0, 3, 2, 1).reshape(2, 169, HEADS)
     width = D // n_img
 
-    vectors = small[:24].reshape(2, 12, D)
+    vectors = jnp.concatenate([small[:24], small[24:48]], axis=1).reshape(2, 12, D)
     mine = lax.dynamic_slice_in_dim(vectors[:, :8], img * width, width, 2)
     up_bias = lax.dynamic_slice_in_dim(vectors[:, 8:].reshape(2, FF), img * (4 * width), 4 * width, 1)
 
     return (
-        block_out.transpose(1, 0, 2)[:, None], grad_tokens, mine[:, 0], mine[:, 1], g_qkv, mine[:, 2], mine[:, 3], table,
+        block_out.transpose(1, 0, 2)[:, None], grad_tokens.reshape(C, 1, T, D), mine[:, 0], mine[:, 1], g_qkv, mine[:, 2], mine[:, 3], table,
         g_out, mine[:, 6], mine[:, 4], mine[:, 5], g_up, up_bias, g_down, mine[:, 7],
     )
 

time: 513 us -> 407 us (0.79)
  Pallas kernels: 369 us -> 284 us
  waiting for transfers between devices: 78.1 us -> 52.2 us
    pallas_call x37 -> x30, Pallas kernels: 369 us -> 284 us  [call(): pl.pallas_call(wrapped, grid_spec=pltpu.PrefetchScalarGridSpec(num_scalar...]
    ppermute x15 -> x21, waiting for transfers between devices: 74.2 us -> 50.1 us  [send(): self.kept, self.recv = (kept, lax.ppermute(out, axis, perm))]
    ppermute x15 -> x21, starting transfers between devices: 22.6 us -> 27.4 us  [send(): self.kept, self.recv = (kept, lax.ppermute(out, axis, perm))]
    unnamed x64 -> x85, local copies, waits for them, and re-layouts: 14.8 us -> 17.1 us
  transfers between devices with their start and end apart: 34 -> 38, of which waited for: 9 -> 8; matrix products, arithmetic and copies ran while one was open for 2% -> 2% of each run, Pallas kernels for 59% -> 60%
where the time goes in v3:
time: 407 us; the launch traced here: 402 us
  Pallas kernels  284 us (70%)
  waiting for transfers between devices  52.2 us (13%)
  starting transfers between devices  35.5 us (9%)
  local copies, waits for them, and re-layouts  23 us (6%)
    pallas_call x30, Pallas kernels, call(): pl.pallas_call(wrapped, grid_spec=pltpu.PrefetchScalarGridSpec(num_scalar...  284 us
    ppermute x21, waiting for transfers between devices, send(): self.kept, self.recv = (kept, lax.ppermute(out, axis, perm))  50.1 us
    ppermute x21, starting transfers between devices, send(): self.kept, self.recv = (kept, lax.ppermute(out, axis, perm))  27.4 us
    unnamed x85, local copies, waits for them, and re-layouts  17.1 us
  transfers between devices with their start and end apart: 38, of which 8 were waited for; matrix products, arithmetic and copies ran while one was open for 2% of the time, Pallas kernels for 60%

profile of v3, /device:TPU:0, one launch (start us, length us, event | category | flops | bytes accessed | tf_op | source)
XLA Modules:
  0.0 401.9 jit_solution(15075030479625203187)
XLA Ops:
  0.7 2.5 crop_rows.2
  3.7 2.6 collective-permute-start.1
  6.9 2.5 crop_rows.3
  9.6 2.0 collective-permute-start.5
  16.6 20.2 %forward_0.2 = (f32[2,392,768]{2,1,0:T(8,128)}, bf16[2,392,768]{2,1,0:T(8,128)(2,1)}, bf16[2,8,18,64,128]{4,3,2,1,0:T(8,128)(2,1)}, bf16[2,392,768]{2,1,0:T(8,12...) custom-call(s32[1]{0:T(128)} %bitcast.1.refs_0_, ...), custom_call_target="tpu_custom_call" | custom-call | flops 9660000256 | tf_op jit(solution)/shard_map/forward_0/pallas_call | solution.py:168
  37.6 20.3 %forward_0.3 = (f32[2,392,768]{2,1,0:T(8,128)}, bf16[2,392,768]{2,1,0:T(8,128)(2,1)}, bf16[2,8,18,64,128]{4,3,2,1,0:T(8,128)(2,1)}, bf16[2,392,768]{2,1,0:T(8,12...) custom-call(s32[1]{0:T(128)} %bitcast.1.refs_0_, ...), custom_call_target="tpu_custom_call", output_to_operand_aliasing={{0}: (17, {}), {1}: (18, {}), {2}: (19, {}), {3}: (20, {}),... | custom-call | flops 9660000256 | tf_op jit(solution)/shard_map/forward_0/pallas_call | solution.py:168
  57.9 36.0 %forward_1.1 = (f32[2,392,768]{2,1,0:T(8,128)}, bf16[2,392,768]{2,1,0:T(8,128)(2,1)}, bf16[2,8,18,64,128]{4,3,2,1,0:T(8,128)(2,1)}, bf16[2,392,768]{2,1,0:T(8,12...) custom-call(f32[2,49,8,768]{3,2,1,0:T(8,128)} %get-tuple-element.141, ...), custom_call_target="tpu_custom_call" | custom-call | flops 16560000000 | tf_op jit(solution)/shard_map/forward_1/pallas_call | solution.py:168
  94.7 3.9 join_pieces.1.refs_2_
  98.7 25.1 %mlp_back_1.1 = (bf16[2,2,392,192]{3,2,1,0:T(8,128)(2,1)}, bf16[2,392,1536]{2,1,0:T(8,128)(2,1)}, f32[2,392,768]{2,1,0:T(8,128)}, bf16[2,392,768]{2,1,0:T(8,128)...) custom-call(s32[1]{0:T(128)} %bitcast.1.refs_0_, s32[1]{0:T(128)} %bitcast.refs_0_.refs_1_, ...), custom_call_target="tpu_custom_call" | custom-call | flops 10119999488 | tf_op jit(solution)/shard_map/mlp_back_1/pallas_call | solution.py:168
  124.3 32.2 %attn_back_1.1 = (bf16[2,2,392,768]{3,2,1,0:T(8,128)(2,1)}, f32[4,768]{1,0:T(4,128)}, f32[4,8,256]{2,1,0:T(8,128)}, f32[2,49,8,768]{3,2,1,0:T(8,128)}, f32[8,96,384]{2,1,0:T(8,128)}, /*index=5*/f32[8,96,384]{2,1,0:T(8,128)}) custom-call(s32[1]{0:T(128)} %bitcast.1.refs_0_, s32[1]{0:T(128)} %bitcast.refs_0_.refs_1_, ...), custom_call_target="tpu_custom_call" | custom-call | flops 14259999744 | tf_op jit(solution)/shard_map/attn_back_1/pallas_call | solution.py:168
  159.1 6.9 %down_mine.2 = (f32[4,96,768]{2,1,0:T(8,128)}, f32[4,96,768]{2,1,0:T(8,128)}) custom-call(s32[4]{0:T(128)} %pad_add_fusion.refs_0_, bf16[2,2,392,192]{3,2,1,0:T(8,128)(2,1)} %get-tuple-element.158.refs_1_, bf16[2,392,3072]{2,1,0:T(8,128)(2,1)} %get-tuple-element.148.refs_5_.refs_2_.refs_3_, bf16[2,392,3072]{2,1,0:T(8,128)(2,1)} %get-tuple-element.148.refs_5_.refs_2_.refs_3_, ...), custom_call_target="tpu_custom_call" | custom-call | flops 3174000128 | tf_op jit(solution)/shard_map/down_mine/pallas_call | solution.py:168
  166.0 5.8 %up_mine.2 = (f32[4,96,768]{2,1,0:T(8,128)}, f32[4,96,768]{2,1,0:T(8,128)}) custom-call(s32[4]{0:T(128)} %pad_add_fusion.refs_0_, bf16[2,392,768]{2,1,0:T(8,128)(2,1)} %get-tuple-element.149.refs_6_.refs_1_, bf16[2,392,1536]{2,1,0:T(8,128)(2,1)} %get-tuple-element.162.refs_2_, f32[8,96,768]{2,1,0:T(8,128)} %collective-permute-done.10.refs_3_, ...), custom_call_target="tpu_custom_call" | custom-call | flops 2622000128 | tf_op jit(solution)/shard_map/up_mine/pallas_call | solution.py:168
  171.9 2.1 collective-permute-start.11
  173.9 1.5 collective-permute-start.9
  177.1 25.0 %mlp_back_0.1 = (bf16[2,2,392,192]{3,2,1,0:T(8,128)(2,1)}, bf16[2,392,1536]{2,1,0:T(8,128)(2,1)}, f32[2,392,768]{2,1,0:T(8,128)}, bf16[2,392,768]{2,1,0:T(8,128)...) custom-call(s32[1]{0:T(128)} %bitcast.1.refs_0_, s32[1]{0:T(128)} %bitcast.refs_0_.refs_1_, ...), custom_call_target="tpu_custom_call" | custom-call | flops 10119999488 | tf_op jit(solution)/shard_map/mlp_back_0/pallas_call | solution.py:168
  203.4 4.2 %split_sum.8 = (f32[8,96,768]{2,1,0:T(8,128)}, f32[8,96,768]{2,1,0:T(8,128)}, f32[2,96,768]{2,1,0:T(8,128)}, f32[2,96,768]{2,1,0:T(8,128)}, f32[2,96,768]{2,1,0:T(8,128)}, /*index=5*/f32[2,96,768]{2,1,0:T(8,128)}) custom-call(s32[2]{0:T(128)} %pad_add_fusion.1.refs_0_, ...), custom_call_target="tpu_custom_call", output_to_operand_aliasing={{0}: (9, {}), {1}: (10, {})} | custom-call | flops 2046595200 | tf_op jit(solution)/shard_map/split_sum/pallas_call | solution.py:168
  210.9 7.2 %attn_mine.3 = (f32[4,96,768]{2,1,0:T(8,128)}, f32[4,96,768]{2,1,0:T(8,128)}) custom-call(s32[4]{0:T(128)} %pad_add_fusion.refs_0_, bf16[2,392,768]{2,1,0:T(8,128)(2,1)} %get-tuple-element.143.refs_6_.refs_1_, bf16[2,392,768]{2,1,0:T(8,128)(2,1)} %get-tuple-element.144.refs_7_.refs_2_, bf16[2,2,392,768]{3,2,1,0:T(8,128)(2,1)} %get-tuple-element.155.refs_3_, ...), custom_call_target="tpu_custom_call" | custom-call | flops 3265999872 | tf_op jit(solution)/shard_map/attn_mine/pallas_call | solution.py:168
  218.2 3.0 own_quadrants.2
  223.4 6.9 %down_mine.3 = (f32[4,96,768]{2,1,0:T(8,128)}, f32[4,96,768]{2,1,0:T(8,128)}) custom-call(s32[4]{0:T(128)} %pad_add_fusion.refs_0_, bf16[2,2,392,192]{3,2,1,0:T(8,128)(2,1)} %get-tuple-element.180.refs_1_, bf16[2,392,3072]{2,1,0:T(8,128)(2,1)} %get-tuple-element.169.refs_5_.refs_2_.refs_3_, bf16[2,392,3072]{2,1,0:T(8,128)(2,1)} %get-tuple-element.169.refs_5_.refs_2_.refs_3_, ...), custom_call_target="tpu_custom_call" | custom-call | flops 3174000128 | tf_op jit(solution)/shard_map/down_mine/pallas_call | solution.py:168
  230.3 5.7 %up_mine.3 = (f32[4,96,768]{2,1,0:T(8,128)}, f32[4,96,768]{2,1,0:T(8,128)}) custom-call(s32[4]{0:T(128)} %pad_add_fusion.refs_0_, bf16[2,392,768]{2,1,0:T(8,128)(2,1)} %get-tuple-element.170.refs_6_.refs_1_, bf16[2,392,1536]{2,1,0:T(8,128)(2,1)} %get-tuple-element.178.refs_2_, f32[8,96,768]{2,1,0:T(8,128)} %collective-permute-done.13.refs_3_, ...), custom_call_target="tpu_custom_call" | custom-call | flops 2622000128 | tf_op jit(solution)/shard_map/up_mine/pallas_call | solution.py:168
  237.0 3.3 split_sum.9
  240.3 2.6 collective-permute-start.20
  243.2 1.6 collective-permute-start.15
  245.6 32.6 %attn_back_0.1 = (bf16[2,2,392,768]{3,2,1,0:T(8,128)(2,1)}, f32[4,768]{1,0:T(4,128)}, f32[96,384]{1,0:T(8,128)}, f32[2,49,8,768]{3,2,1,0:T(8,128)}, f32[8,96,384]{2,1,0:T(8,128)}, /*index=5*/f32[8,96,384]{2,1,0:T(8,128)}) custom-call(s32[1]{0:T(128)} %bitcast.1.refs_0_, s32[1]{0:T(128)} %bitcast.refs_0_.refs_1_, ...), custom_call_target="tpu_custom_call" | custom-call | flops 14259999744 | tf_op jit(solution)/shard_map/attn_back_0/pallas_call | solution.py:168
  278.2 3.3 collective-permute-done.15.refs_2_.refs_4_
  282.9 5.6 %split_sum.10 = (f32[96,384]{1,0:T(8,128)}, f32[8,96,384]{2,1,0:T(8,128)}, f32[8,96,384]{2,1,0:T(8,128)}, f32[2,96,768]{2,1,0:T(8,128)}, f32[2,96,768]{2,1,0:T(8...) custom-call(s32[3]{0:T(128)} %pad_add_fusion.2.refs_0_, ...), custom_call_target="tpu_custom_call", output_to_operand_aliasing={{0}: (13, {}), {1}: (14, {}), {2}: (15, {})} | custom-call | flops 2724892672 | tf_op jit(solution)/shard_map/split_sum/pallas_call | solution.py:168
  289.6 1.5 collective-permute-start.28
  291.1 2.0 collective-permute-done.12.refs_3_
  294.6 2.5 token_major.1.refs_2_
  298.0 2.9 own_quadrants.3
  302.0 5.1 %attn_mine.4 = (f32[5,96,384]{2,1,0:T(8,128)}, f32[5,96,384]{2,1,0:T(8,128)}) custom-call(s32[4]{0:T(128)} %pad_add_fusion.refs_0_, bf16[2,392,768]{2,1,0:T(8,128)(2,1)} %get-tuple-element.191.refs_6_.refs_1_, bf16[2,392,768]{2,1,0:T(8,128)(2,1)} %get-tuple-element.192.refs_7_.refs_2_, bf16[2,2,392,768]{3,2,1,0:T(8,128)(2,1)} %get-tuple-element.209.refs_3_, ...), custom_call_target="tpu_custom_call" | custom-call | flops 1978000000 | tf_op jit(solution)/shard_map/attn_mine/pallas_call | solution.py:168
  309.4 5.8 %attn_mine.5 = (f32[4,96,384]{2,1,0:T(8,128)}, f32[4,96,384]{2,1,0:T(8,128)}) custom-call(s32[4]{0:T(128)} %pad_add_fusion.refs_0_, bf16[2,392,768]{2,1,0:T(8,128)(2,1)} %get-tuple-element.191.refs_6_.refs_1_, bf16[2,392,768]{2,1,0:T(8,128)(2,1)} %get-tuple-element.192.refs_7_.refs_2_, bf16[2,2,392,768]{3,2,1,0:T(8,128)(2,1)} %get-tuple-element.209.refs_3_, ...), custom_call_target="tpu_custom_call" | custom-call | flops 1978000000 | tf_op jit(solution)/shard_map/attn_mine/pallas_call | solution.py:168
  315.2 6.2 %collective-permute-done.30.refs_10_.refs_12_ = f32[2,96,768]{2,1,0:T(8,128)S(1)} collective-permute-done((f32[2,96,768]{2,1,0:T(8,128)S(1)}, f32[2,96,768]{2,1,0:T(8,128)S(1)}, u32[]{:S(2)}, u32[]{:S(2)}) %collective-permute-start.30) | collective-permute-done | bytes 589856 | tf_op jit(solution)/shard_map/ppermute | solution.py:947
  322.3 4.0 split_sum.11
  326.2 3.5 collective-permute-start.31
  329.7 1.7 collective-permute-start.26
  331.5 12.6 %collective-permute-done.31.refs_6_.refs_5_ = f32[1,96,768]{2,1,0:T(8,128)S(1)} collective-permute-done((f32[1,96,768]{2,1,0:T(8,128)}, f32[1,96,768]{2,1,0:T(8,128)S(1)}, u32[]{:S(2)}, u32[]{:S(2)}) %collective-permute-start.31) | collective-permute-done | bytes 294944 | tf_op jit(solution)/shard_map/ppermute | solution.py:947
  345.1 3.2 split_sum.12
  348.4 8.0 %collective-permute-done.32.refs_6_.refs_1_ = f32[1,96,768]{2,1,0:T(8,128)S(1)} collective-permute-done((f32[1,96,768]{2,1,0:T(8,128)}, f32[1,96,768]{2,1,0:T(8,128)S(1)}, u32[]{:S(2)}, u32[]{:S(2)}) %collective-permute-start.32) | collective-permute-done | bytes 294944 | tf_op jit(solution)/shard_map/ppermute | solution.py:947
  358.5 2.1 split_sum.13
  361.0 2.1 collective-permute-start.37
  363.1 6.5 %collective-permute-done.34.refs_2_.refs_4_ = f32[3,96,384]{2,1,0:T(8,128)S(1)} collective-permute-done((f32[3,96,384]{2,1,0:T(8,128)}, f32[3,96,384]{2,1,0:T(8,128)S(1)}, u32[]{:S(2)}, u32[]{:S(2)}) %collective-permute-start.34) | collective-permute-done | bytes 442400 | tf_op jit(solution)/shard_map/ppermute | solution.py:947
  370.5 2.1 split_sum.14
  373.9 1.8 split_sum.15
  375.8 2.3 collective-permute-start.36
  378.9 2.4 crop_major.1.refs_14_
  381.3 12.2 %collective-permute-done.36.refs_11_ = f32[1,96,384]{2,1,0:T(8,128)S(1)} collective-permute-done((f32[1,96,384]{2,1,0:T(8,128)}, f32[1,96,384]{2,1,0:T(8,128)S(1)}, u32[]{:S(2)}, u32[]{:S(2)}) %collective-permute-start.36) | collective-permute-done | bytes 147488 | tf_op jit(solution)/shard_map/ppermute | solution.py:947
  394.3 3.4 last_sums.1
  (173 shorter events, 41.0 us)
Async XLA Ops:
  0.6 11.0 %copy-start = (f32[2,169,24]{1,2,0:T(8,128)S(1)}, f32[2,169,24]{1,2,0:T(8,128)}, u32[]{:S(2)}) copy-start(f32[2,169,24]{1,2,0:T(8,128)} %param.24) | copy-start | bytes 97348
  3.2 13.3 %collective-permute-start.2 = (f32[6,196,128]{2,1,0:T(8,128)}, f32[6,196,128]{2,1,0:T(8,128)}, u32[]{:S(2)}, u32[]{:S(2)}) collective-permute-start(f32[6,196,128]{2,1,0:T(8,128)} %get-tuple-element.130), channel_id=1, source_target_pairs={{0,1},{1,0},{2,3},{3,2},{4,5},{5,4},{6,7},{7,6},{8,9},{9,8},{10,11... | collective-permute-start | bytes 1806344 | tf_op jit(solution)/shard_map/ppermute | solution.py:1047
  3.7 33.1 %collective-permute-start.1 = (f32[6,196,128]{2,1,0:T(8,128)}, f32[6,196,128]{2,1,0:T(8,128)S(1)}, u32[]{:S(2)}, u32[]{:S(2)}) collective-permute-start(f32[6,196,128]{2,1,0:T(8,128)} %get-tuple-element.130), channel_id=1, source_target_pairs={{0,3},{1,2},{2,1},{3,0},{4,7},{5,6},{6,5},{7,4},{8,11},{9,10},{10,... | collective-permute-start | bytes 1806344 | tf_op jit(solution)/shard_map/ppermute | solution.py:1047
  6.3 30.5 %collective-permute-start = (f32[6,196,128]{2,1,0:T(8,128)}, f32[6,196,128]{2,1,0:T(8,128)}, u32[]{:S(2)}, u32[]{:S(2)}) collective-permute-start(f32[6,196,128]{2,1,0:T(8,128)} %get-tuple-element.129.refs_3_.refs_1_), channel_id=1, source_target_pairs={{0,2},{1,3},{2,0},{3,1},{4,6},{5,7},{6,4},{7,5},{8,10},{9,11},{10,... | collective-permute-start | bytes 1806344 | tf_op jit(solution)/shard_map/ppermute | solution.py:1047
  9.4 84.5 %collective-permute-start.3 = (f32[6,196,128]{2,1,0:T(8,128)}, f32[6,196,128]{2,1,0:T(8,128)}, u32[]{:S(2)}, u32[]{:S(2)}) collective-permute-start(f32[6,196,128]{2,1,0:T(8,128)} %get-tuple-element.145), channel_id=1, source_target_pairs={{0,1},{1,0},{2,3},{3,2},{4,5},{5,4},{6,7},{7,6},{8,9},{9,8},{10,11... | collective-permute-start | bytes 1806344 | tf_op jit(solution)/shard_map/ppermute | solution.py:1047
  9.6 84.4 %collective-permute-start.5 = (f32[6,196,128]{2,1,0:T(8,128)}, f32[6,196,128]{2,1,0:T(8,128)}, u32[]{:S(2)}, u32[]{:S(2)}) collective-permute-start(f32[6,196,128]{2,1,0:T(8,128)} %get-tuple-element.145), channel_id=1, source_target_pairs={{0,3},{1,2},{2,1},{3,0},{4,7},{5,6},{6,5},{7,4},{8,11},{9,10},{10,... | collective-permute-start | bytes 1806344 | tf_op jit(solution)/shard_map/ppermute | solution.py:1047
  16.5 77.4 %collective-permute-start.4 = (f32[6,196,128]{2,1,0:T(8,128)S(1)}, f32[6,196,128]{2,1,0:T(8,128)S(1)}, u32[]{:S(2)}, u32[]{:S(2)}) collective-permute-start(f32[6,196,128]{2,1,0:T(8,128)S(1)} %copy-done.16), channel_id=1, source_target_pairs={{0,2},{1,3},{2,0},{3,1},{4,6},{5,7},{6,4},{7,5},{8,10},{9,11},{10,... | collective-permute-start | bytes 1806344 | tf_op jit(solution)/shard_map/ppermute | solution.py:1047
  123.8 33.9 %collective-permute-start.8 = (f32[8,96,768]{2,1,0:T(8,128)}, f32[8,96,768]{2,1,0:T(8,128)S(1)}, u32[]{:S(2)}, u32[]{:S(2)}) collective-permute-start(f32[8,96,768]{2,1,0:T(8,128)} %get-tuple-element.154.refs_13_), channel_id=1, source_target_pairs={{0,1},{1,0},{2,3},{3,2},{4,5},{5,4},{6,7},{7,6},{8,9},{9,8},{10,11... | collective-permute-start | bytes 7077896 | tf_op jit(solution)/shard_map/ppermute | solution.py:1047
  123.9 42.1 %collective-permute-start.10 = (f32[8,96,768]{2,1,0:T(8,128)}, f32[8,96,768]{2,1,0:T(8,128)}, u32[]{:S(2)}, u32[]{:S(2)}) collective-permute-start(f32[8,96,768]{2,1,0:T(8,128)} %get-tuple-element.163), channel_id=1, source_target_pairs={{0,1},{1,0},{2,3},{3,2},{4,5},{5,4},{6,7},{7,6},{8,9},{9,8},{10,11... | collective-permute-start | bytes 7077896 | tf_op jit(solution)/shard_map/ppermute | solution.py:1047
  156.5 19.5 %collective-permute-start.6 = (f32[8,96,384]{2,1,0:T(8,128)}, f32[8,96,384]{2,1,0:T(8,128)S(1)}, u32[]{:S(2)}, u32[]{:S(2)}) collective-permute-start(f32[8,96,384]{2,1,0:T(8,128)} %get-tuple-element.156), channel_id=1, source_target_pairs={{0,1},{1,0},{2,3},{3,2},{4,5},{5,4},{6,7},{7,6},{8,9},{9,8},{10,11... | collective-permute-start | bytes 3538952 | tf_op jit(solution)/shard_map/ppermute | solution.py:1047
  156.7 19.4 %collective-permute-start.7 = (f32[8,96,384]{2,1,0:T(8,128)}, f32[8,96,384]{2,1,0:T(8,128)}, u32[]{:S(2)}, u32[]{:S(2)}) collective-permute-start(f32[8,96,384]{2,1,0:T(8,128)} %get-tuple-element.157), channel_id=1, source_target_pairs={{0,1},{1,0},{2,3},{3,2},{4,5},{5,4},{6,7},{7,6},{8,9},{9,8},{10,11... | collective-permute-start | bytes 3538952 | tf_op jit(solution)/shard_map/ppermute | solution.py:1047
  166.0 7.9 %copy-start.23 = (f32[4,96,768]{2,1,0:T(8,128)S(1)}, f32[4,96,768]{2,1,0:T(8,128)}, u32[]{:S(2)}) copy-start(f32[4,96,768]{2,1,0:T(8,128)} %get-tuple-element.161) | copy-start | bytes 3538948
  171.9 30.2 %collective-permute-start.11 = (f32[4,96,768]{2,1,0:T(8,128)}, f32[4,96,768]{2,1,0:T(8,128)S(1)}, u32[]{:S(2)}, u32[]{:S(2)}) collective-permute-start(f32[4,96,768]{2,1,0:T(8,128)} %get-tuple-element.165), channel_id=1, source_target_pairs={{0,8},{4,12},{8,0},{12,4},{16,24},{20,28},{24,16},{28,20},{1,9},{5... | collective-permute-start | bytes 3538952 | tf_op jit(solution)/shard_map/ppermute | solution.py:947
  173.9 28.1 %collective-permute-start.9 = (f32[4,96,768]{2,1,0:T(8,128)S(1)}, f32[4,96,768]{2,1,0:T(8,128)S(1)}, u32[]{:S(2)}, u32[]{:S(2)}) collective-permute-start(f32[4,96,768]{2,1,0:T(8,128)S(1)} %copy-done.23), channel_id=1, source_target_pairs={{0,4},{4,0},{8,12},{12,8},{16,20},{20,16},{24,28},{28,24},{1,5},{5... | collective-permute-start | bytes 3538952 | tf_op jit(solution)/shard_map/ppermute | solution.py:947
  207.6 14.5 %collective-permute-start.14 = (f32[8,96,768]{2,1,0:T(8,128)}, f32[8,96,768]{2,1,0:T(8,128)S(1)}, u32[]{:S(2)}, u32[]{:S(2)}) collective-permute-start(f32[8,96,768]{2,1,0:T(8,128)} %get-tuple-element.181), channel_id=1, source_target_pairs={{0,1},{1,0},{2,3},{3,2},{4,5},{5,4},{6,7},{7,6},{8,9},{9,8},{10,11... | collective-permute-start | bytes 7077896 | tf_op jit(solution)/shard_map/ppermute | solution.py:1047
  207.7 22.6 %collective-permute-start.13 = (f32[8,96,768]{2,1,0:T(8,128)}, f32[8,96,768]{2,1,0:T(8,128)}, u32[]{:S(2)}, u32[]{:S(2)}) collective-permute-start(f32[8,96,768]{2,1,0:T(8,128)} %get-tuple-element.179), channel_id=1, source_target_pairs={{0,1},{1,0},{2,3},{3,2},{4,5},{5,4},{6,7},{7,6},{8,9},{9,8},{10,11... | collective-permute-start | bytes 7077896 | tf_op jit(solution)/shard_map/ppermute | solution.py:1047
  209.3 26.6 %collective-permute-start.18 = (f32[2,96,768]{2,1,0:T(8,128)}, f32[2,96,768]{2,1,0:T(8,128)S(1)}, u32[]{:S(2)}, u32[]{:S(2)}) collective-permute-start(f32[2,96,768]{2,1,0:T(8,128)} %get-tuple-element.195), channel_id=1, source_target_pairs={{0,8},{4,12},{8,0},{12,4},{16,24},{20,28},{24,16},{28,20},{1,9},{5... | collective-permute-start | bytes 1769480 | tf_op jit(solution)/shard_map/ppermute | solution.py:947
  209.8 26.2 %collective-permute-start.19 = (f32[2,96,768]{2,1,0:T(8,128)}, f32[2,96,768]{2,1,0:T(8,128)S(1)}, u32[]{:S(2)}, u32[]{:S(2)}) collective-permute-start(f32[2,96,768]{2,1,0:T(8,128)} %get-tuple-element.197), channel_id=1, source_target_pairs={{0,4},{4,0},{8,12},{12,8},{16,20},{20,16},{24,28},{28,24},{1,5},{5... | collective-permute-start | bytes 1769480 | tf_op jit(solution)/shard_map/ppermute | solution.py:947
  221.2 57.0 %collective-permute-start.17 = (f32[4,96,768]{2,1,0:T(8,128)S(1)}, f32[4,96,768]{2,1,0:T(8,128)S(1)}, u32[]{:S(2)}, u32[]{:S(2)}) collective-permute-start(f32[4,96,768]{2,1,0:T(8,128)S(1)} %copy-done.20), channel_id=1, source_target_pairs={{0,4},{4,0},{8,12},{12,8},{16,20},{20,16},{24,28},{28,24},{1,5},{5... | collective-permute-start | bytes 3538952 | tf_op jit(solution)/shard_map/ppermute | solution.py:947
  240.3 37.9 %collective-permute-start.20 = (f32[1,96,768]{2,1,0:T(8,128)}, f32[1,96,768]{2,1,0:T(8,128)S(1)}, u32[]{:S(2)}, u32[]{:S(2)}) collective-permute-start(f32[1,96,768]{2,1,0:T(8,128)} %get-tuple-element.203), channel_id=1, source_target_pairs={{0,16},{4,20},{8,24},{12,28},{16,0},{20,4},{24,8},{28,12},{1,17},{... | collective-permute-start | bytes 884744 | tf_op jit(solution)/shard_map/ppermute | solution.py:947
  242.9 35.3 %collective-permute-start.21 = (f32[1,96,768]{2,1,0:T(8,128)}, f32[1,96,768]{2,1,0:T(8,128)S(1)}, u32[]{:S(2)}, u32[]{:S(2)}) collective-permute-start(f32[1,96,768]{2,1,0:T(8,128)} %get-tuple-element.204), channel_id=1, source_target_pairs={{0,16},{4,20},{8,24},{12,28},{16,0},{20,4},{24,8},{28,12},{1,17},{... | collective-permute-start | bytes 884744 | tf_op jit(solution)/shard_map/ppermute | solution.py:947
  243.2 38.3 %collective-permute-start.15 = (f32[4,96,768]{2,1,0:T(8,128)}, f32[4,96,768]{2,1,0:T(8,128)S(1)}, u32[]{:S(2)}, u32[]{:S(2)}) collective-permute-start(f32[4,96,768]{2,1,0:T(8,128)} %get-tuple-element.184), channel_id=1, source_target_pairs={{0,8},{4,12},{8,0},{12,4},{16,24},{20,28},{24,16},{28,20},{1,9},{5... | collective-permute-start | bytes 3538952 | tf_op jit(solution)/shard_map/ppermute | solution.py:947
  244.8 36.7 %collective-permute-start.16 = (f32[4,96,768]{2,1,0:T(8,128)}, f32[4,96,768]{2,1,0:T(8,128)S(1)}, u32[]{:S(2)}, u32[]{:S(2)}) collective-permute-start(f32[4,96,768]{2,1,0:T(8,128)} %get-tuple-element.185), channel_id=1, source_target_pairs={{0,4},{4,0},{8,12},{12,8},{16,20},{20,16},{24,28},{28,24},{1,5},{5... | collective-permute-start | bytes 3538952 | tf_op jit(solution)/shard_map/ppermute | solution.py:947
  288.5 8.6 %copy-start.29 = (f32[2,96,768]{2,1,0:T(8,128)S(1)}, f32[2,96,768]{2,1,0:T(8,128)}, u32[]{:S(2)}) copy-start(f32[2,96,768]{2,1,0:T(8,128)} %get-tuple-element.221) | copy-start | bytes 1769476
  288.5 12.4 %collective-permute-start.24 = (f32[8,96,384]{2,1,0:T(8,128)}, f32[8,96,384]{2,1,0:T(8,128)S(1)}, u32[]{:S(2)}, u32[]{:S(2)}) collective-permute-start(f32[8,96,384]{2,1,0:T(8,128)} %get-tuple-element.211), channel_id=1, source_target_pairs={{0,1},{1,0},{2,3},{3,2},{4,5},{5,4},{6,7},{7,6},{8,9},{9,8},{10,11... | collective-permute-start | bytes 3538952 | tf_op jit(solution)/shard_map/ppermute | solution.py:1047
  288.6 19.8 %collective-permute-start.23 = (f32[8,96,384]{2,1,0:T(8,128)}, f32[8,96,384]{2,1,0:T(8,128)S(1)}, u32[]{:S(2)}, u32[]{:S(2)}) collective-permute-start(f32[8,96,384]{2,1,0:T(8,128)} %get-tuple-element.210), channel_id=1, source_target_pairs={{0,1},{1,0},{2,3},{3,2},{4,5},{5,4},{6,7},{7,6},{8,9},{9,8},{10,11... | collective-permute-start | bytes 3538952 | tf_op jit(solution)/shard_map/ppermute | solution.py:1047
  289.1 4.1 %collective-permute-start.12 = (f32[6,196,128]{2,1,0:T(8,128)S(1)}, f32[6,196,128]{2,1,0:T(8,128)S(1)}, u32[]{:S(2)}, u32[]{:S(2)}) collective-permute-start(f32[6,196,128]{2,1,0:T(8,128)S(1)} %copy-done.26), channel_id=1, source_target_pairs={{0,1},{1,0},{2,3},{3,2},{4,5},{5,4},{6,7},{7,6},{8,9},{9,8},{10,11... | collective-permute-start | bytes 1806344 | tf_op jit(solution)/shard_map/ppermute | solution.py:1047
  289.2 7.9 %collective-permute-start.25 = (f32[96,384]{1,0:T(8,128)}, f32[96,384]{1,0:T(8,128)S(1)}, u32[]{:S(2)}, u32[]{:S(2)}) collective-permute-start(f32[96,384]{1,0:T(8,128)} %get-tuple-element.212.refs_5_), channel_id=1, source_target_pairs={{0,1},{1,0},{2,3},{3,2},{4,5},{5,4},{6,7},{7,6},{8,9},{9,8},{10,11... | collective-permute-start | bytes 442376 | tf_op jit(solution)/shard_map/ppermute | solution.py:1047
  289.6 25.6 %collective-permute-start.28 = (f32[2,96,768]{2,1,0:T(8,128)}, f32[2,96,768]{2,1,0:T(8,128)S(1)}, u32[]{:S(2)}, u32[]{:S(2)}) collective-permute-start(f32[2,96,768]{2,1,0:T(8,128)} %get-tuple-element.217), channel_id=1, source_target_pairs={{0,4},{4,0},{8,12},{12,8},{16,20},{20,16},{24,28},{28,24},{1,5},{5... | collective-permute-start | bytes 1769480 | tf_op jit(solution)/shard_map/ppermute | solution.py:947
  293.2 22.0 %collective-permute-start.29 = (f32[2,96,768]{2,1,0:T(8,128)}, f32[2,96,768]{2,1,0:T(8,128)S(1)}, u32[]{:S(2)}, u32[]{:S(2)}) collective-permute-start(f32[2,96,768]{2,1,0:T(8,128)} %get-tuple-element.219), channel_id=1, source_target_pairs={{0,8},{4,12},{8,0},{12,4},{16,24},{20,28},{24,16},{28,20},{1,9},{5... | collective-permute-start | bytes 1769480 | tf_op jit(solution)/shard_map/ppermute | solution.py:947
  297.1 24.3 %collective-permute-start.30 = (f32[2,96,768]{2,1,0:T(8,128)S(1)}, f32[2,96,768]{2,1,0:T(8,128)S(1)}, u32[]{:S(2)}, u32[]{:S(2)}) collective-permute-start(f32[2,96,768]{2,1,0:T(8,128)S(1)} %copy-done.29), channel_id=1, source_target_pairs={{0,8},{4,12},{8,0},{12,4},{16,24},{20,28},{24,16},{28,20},{1,9},{5... | collective-permute-start | bytes 1769480 | tf_op jit(solution)/shard_map/ppermute | solution.py:947
  307.0 37.1 %collective-permute-start.27 = (f32[5,96,384]{2,1,0:T(8,128)}, f32[5,96,384]{2,1,0:T(8,128)S(1)}, u32[]{:S(2)}, u32[]{:S(2)}) collective-permute-start(f32[5,96,384]{2,1,0:T(8,128)} %get-tuple-element.216), channel_id=1, source_target_pairs={{0,4},{4,0},{8,12},{12,8},{16,20},{20,16},{24,28},{28,24},{1,5},{5... | collective-permute-start | bytes 2211848 | tf_op jit(solution)/shard_map/ppermute | solution.py:947
  315.2 6.8 %copy-start.11 = (f32[2,96,768]{2,1,0:T(8,128)}, f32[2,96,768]{2,1,0:T(8,128)S(1)}, u32[]{:S(2)}) copy-start(f32[2,96,768]{2,1,0:T(8,128)S(1)} %collective-permute-done.28.refs_2_.refs_4_) | copy-start | bytes 1769476
  315.2 6.8 %copy-start.12 = (f32[2,96,768]{2,1,0:T(8,128)}, f32[2,96,768]{2,1,0:T(8,128)S(1)}, u32[]{:S(2)}) copy-start(f32[2,96,768]{2,1,0:T(8,128)S(1)} %collective-permute-done.29.refs_6_.refs_8_) | copy-start | bytes 1769476
  322.2 7.5 %copy-start.30 = (f32[4,96,384]{2,1,0:T(8,128)S(1)}, f32[4,96,384]{2,1,0:T(8,128)}, u32[]{:S(2)}) copy-start(f32[4,96,384]{2,1,0:T(8,128)} %get-tuple-element.215) | copy-start | bytes 1769476
  326.2 22.1 %copy-start.25 = (f32[6,196,128]{2,1,0:T(8,128)S(1)}, f32[6,196,128]{2,1,0:T(8,128)}, u32[]{:S(2)}) copy-start(f32[6,196,128]{2,1,0:T(8,128)} %get-tuple-element.208) | copy-start | bytes 1806340
  326.2 17.9 %collective-permute-start.31 = (f32[1,96,768]{2,1,0:T(8,128)}, f32[1,96,768]{2,1,0:T(8,128)S(1)}, u32[]{:S(2)}, u32[]{:S(2)}) collective-permute-start(f32[1,96,768]{2,1,0:T(8,128)} %get-tuple-element.223), channel_id=1, source_target_pairs={{0,16},{4,20},{8,24},{12,28},{16,0},{20,4},{24,8},{28,12},{1,17},{... | collective-permute-start | bytes 884744 | tf_op jit(solution)/shard_map/ppermute | solution.py:947
  329.7 27.9 %collective-permute-start.26 = (f32[4,96,384]{2,1,0:T(8,128)S(1)}, f32[4,96,384]{2,1,0:T(8,128)S(1)}, u32[]{:S(2)}, u32[]{:S(2)}) collective-permute-start(f32[4,96,384]{2,1,0:T(8,128)S(1)} %copy-done.30), channel_id=1, source_target_pairs={{0,8},{4,12},{8,0},{12,4},{16,24},{20,28},{24,16},{28,20},{1,9},{5... | collective-permute-start | bytes 1769480 | tf_op jit(solution)/shard_map/ppermute | solution.py:947
  331.4 25.0 %collective-permute-start.32 = (f32[1,96,768]{2,1,0:T(8,128)}, f32[1,96,768]{2,1,0:T(8,128)S(1)}, u32[]{:S(2)}, u32[]{:S(2)}) collective-permute-start(f32[1,96,768]{2,1,0:T(8,128)} %get-tuple-element.225), channel_id=1, source_target_pairs={{0,16},{4,20},{8,24},{12,28},{16,0},{20,4},{24,8},{28,12},{1,17},{... | collective-permute-start | bytes 884744 | tf_op jit(solution)/shard_map/ppermute | solution.py:947
  348.3 12.7 %copy-start.35 = (f32[1,96,768]{2,1,0:T(8,128)S(1)}, f32[1,96,768]{2,1,0:T(8,128)}, u32[]{:S(2)}) copy-start(f32[1,96,768]{2,1,0:T(8,128)} %get-tuple-element.236) | copy-start | bytes 884740
  348.3 21.4 %collective-permute-start.34 = (f32[3,96,384]{2,1,0:T(8,128)}, f32[3,96,384]{2,1,0:T(8,128)S(1)}, u32[]{:S(2)}, u32[]{:S(2)}) collective-permute-start(f32[3,96,384]{2,1,0:T(8,128)} %get-tuple-element.228), channel_id=1, source_target_pairs={{0,8},{4,12},{8,0},{12,4},{16,24},{20,28},{24,16},{28,20},{1,9},{5... | collective-permute-start | bytes 1327112 | tf_op jit(solution)/shard_map/ppermute | solution.py:947
  348.3 29.7 %collective-permute-start.22 = (f32[6,196,128]{2,1,0:T(8,128)S(1)}, f32[6,196,128]{2,1,0:T(8,128)S(1)}, u32[]{:S(2)}, u32[]{:S(2)}) collective-permute-start(f32[6,196,128]{2,1,0:T(8,128)S(1)} %copy-done.25), channel_id=1, source_target_pairs={{0,1},{1,0},{2,3},{3,2},{4,5},{5,4},{6,7},{7,6},{8,9},{9,8},{10,11... | collective-permute-start | bytes 1806344 | tf_op jit(solution)/shard_map/ppermute | solution.py:1047
  360.5 12.6 %collective-permute-start.33 = (f32[2,96,384]{2,1,0:T(8,128)}, f32[2,96,384]{2,1,0:T(8,128)S(1)}, u32[]{:S(2)}, u32[]{:S(2)}) collective-permute-start(f32[2,96,384]{2,1,0:T(8,128)} %get-tuple-element.227), channel_id=1, source_target_pairs={{0,4},{4,0},{8,12},{12,8},{16,20},{20,16},{24,28},{28,24},{1,5},{5... | collective-permute-start | bytes 884744 | tf_op jit(solution)/shard_map/ppermute | solution.py:947
  361.0 20.3 %collective-permute-start.37 = (f32[1,96,768]{2,1,0:T(8,128)S(1)}, f32[1,96,768]{2,1,0:T(8,128)S(1)}, u32[]{:S(2)}, u32[]{:S(2)}) collective-permute-start(f32[1,96,768]{2,1,0:T(8,128)S(1)} %copy-done.35), channel_id=1, source_target_pairs={{0,16},{4,20},{8,24},{12,28},{16,0},{20,4},{24,8},{28,12},{1,17},{... | collective-permute-start | bytes 884744 | tf_op jit(solution)/shard_map/ppermute | solution.py:947
  372.5 21.0 %collective-permute-start.35 = (f32[2,96,384]{2,1,0:T(8,128)}, f32[2,96,384]{2,1,0:T(8,128)S(1)}, u32[]{:S(2)}, u32[]{:S(2)}) collective-permute-start(f32[2,96,384]{2,1,0:T(8,128)} %get-tuple-element.233), channel_id=1, source_target_pairs={{0,16},{4,20},{8,24},{12,28},{16,0},{20,4},{24,8},{28,12},{1,17},{... | collective-permute-start | bytes 884744 | tf_op jit(solution)/shard_map/ppermute | solution.py:947
  375.8 17.8 %collective-permute-start.36 = (f32[1,96,384]{2,1,0:T(8,128)}, f32[1,96,384]{2,1,0:T(8,128)S(1)}, u32[]{:S(2)}, u32[]{:S(2)}) collective-permute-start(f32[1,96,384]{2,1,0:T(8,128)} %get-tuple-element.234), channel_id=1, source_target_pairs={{0,16},{4,20},{8,24},{12,28},{16,0},{20,4},{24,8},{28,12},{1,17},{... | collective-permute-start | bytes 442376 | tf_op jit(solution)/shard_map/ppermute | solution.py:947
  381.3 12.3 %copy-start.36 = (f32[1,96,768]{2,1,0:T(8,128)}, f32[1,96,768]{2,1,0:T(8,128)S(1)}, u32[]{:S(2)}) copy-start(f32[1,96,768]{2,1,0:T(8,128)S(1)} %collective-permute-done.37.refs_13_) | copy-start | bytes 884740
  393.5 7.8 %copy-start.1 = (f32[2,169,24]{1,2,0:T(8,128)S(1)}, f32[2,169,24]{1,2,0:T(8,128)}, u32[]{:S(2)}) copy-start(f32[2,169,24]{1,2,0:T(8,128)} %param.24) | copy-start | bytes 97348
  (31 other events, 49.2 us)

commit v4 on v3

--- a/solution.py
+++ b/solution.py
@@ -34,7 +34,9 @@
 N_F = FF // FCH
 W_UP = D // 2
 MINE = D // 4
-VMEM_LIMIT = 58 << 20
+VMEM_LIMIT = 44 << 20
+VMEM_SMALL = 24 << 20
+BIG = ("forw", "mlp_", "attn")
 COST = 0.4
 F32 = jnp.float32
 BF16 = jnp.bfloat16
@@ -176,7 +178,7 @@
         ),
         out_shape=outs,
         input_output_aliases={n_in + k: k for k in range(reuse)},
-        compiler_params=pltpu.CompilerParams(vmem_limit_bytes=VMEM_LIMIT),
+        compiler_params=pltpu.CompilerParams(vmem_limit_bytes=VMEM_LIMIT if name[:4] in BIG else VMEM_SMALL),
         cost_estimate=estimate,
         name=name,
     )(*args, *after)
@@ -271,7 +273,7 @@
     if b == 0:
         at_x, p0, p1, *rest = refs
     else:
-        src, mask, *rest = refs
+        core, src, *rest = refs
     (
         bias, ln1g, ln1b, bq, bv, bout, ln2g, ln2b, bup, bdown,
         wqkv_h, wout_h, wup_h, wdown_h,
@@ -335,8 +337,9 @@
     else:
         put_rolled(z_o.at[0], src, a, False)
         for w in range(2):
+            mask = shift_mask(a, core[0] ^ w)
             for g in range(NG):
-                bias_s[w * NG + g] = bias[NG + g] + mask[0, w]
+                bias_s[w * NG + g] = bias[NG + g] + mask
     out(0).start()
     normed, _ = norm_parts(z_o[0])
     free(1)
@@ -426,7 +429,7 @@
         specs = [fixed((NG, PIECE, LANE), True)] * 2
         out_specs = [pl.BlockSpec((1, T, C, D), lambda a, s: (s[0] ^ which, 0, 0, 0))]
     else:
-        specs = [fixed((2, T, C, D), True), per_half((2, TP, GT))]
+        specs = [SM, fixed((2, T, C, D), True)]
         out_specs = [per_half((T, C, D))]
     small = (bias, p["ln1_gain"], p["ln1_bias"], p["b_query"], p["b_value"], p["b_out"],
              p["ln2_gain"], p["ln2_bias"], p["b_up"], p["b_down"])
@@ -462,7 +465,7 @@
     )
 
 
-def mlp_back_body(b, x_at, core, src, y, gp, act, hid, ln2g, wdown_h, wup_h, dd_o, da_o, dy_o, dyr_o, sv_o, down_o, up_o,
+def mlp_back_body(b, x_at, core, src, y, gp, act, hid, ln2g, wdown_h, wup_h, dd_o, da_o, dy_o, sv_o, down_o, up_o,
                   wdown, wup, dz, dd, da_s, sem_d, sem_u):
     a = pl.program_id(0)
 
@@ -523,9 +526,7 @@
     sv_o[1:2, :] += colsum(dh2)
     dy = dz[...] + norm_back(dh2, normed, inverse, ln2g[b : b + 1, :])
     dy_o[0] = dy
-    low = dy.astype(BF16)
-    dyr_o[0] = low
-    sv_o[2:3, :] += colsum(low.astype(F32))
+    sv_o[2:3, :] += colsum(dy.astype(BF16).astype(F32))
     down = tn(dd_o[1 - core[0], 0], act[0])
     up = tn(hid[0], da_o[0, :, lanes_at(1 - core[0], D)])
 
@@ -549,7 +550,6 @@
             shape((2, 2, ROWS, MINE), BF16),
             shape((2, ROWS, FF // 2), BF16),
             shape((2, ROWS, D), F32),
-            shape((2, ROWS, D), BF16),
             shape((8, D), F32),
             shape((8, *BLOCK), F32),
             shape((8, *BLOCK), F32),
@@ -557,7 +557,6 @@
         [
             pl.BlockSpec((2, 1, ROWS, MINE), lambda a: (0, a, 0, 0)),
             per_half((ROWS, FF // 2)),
-            per_half((ROWS, D)),
             per_half((ROWS, D)),
             fixed((8, D)),
             fixed((8, *BLOCK), True),
@@ -583,12 +582,24 @@
 BLOCK = (D // 8, D)
 
 
+def row_of(t):
+    return sum((t >= SIDE * k).astype(jnp.int32) for k in range(1, 10))
+
+
+def shift_mask(a, column):
+    u = lax.broadcasted_iota(jnp.int32, (TP, GT), 0)
+    t = lax.broadcasted_iota(jnp.int32, (TP, GT), 1) & (TQ - 1)
+    iu, it = row_of(u), row_of(t)
+    rows = (iu >= 4) != (it >= 4)
+    cols = (u - SIDE * iu >= 4) != (t - SIDE * it >= 4)
+    return jnp.where((rows & (a == 1)) | (cols & (column == 1)), -100.0, 0.0)
+
+
 def table_sums(ds, moved):
     row = lax.broadcasted_iota(jnp.int32, (GT, PER * LANE), 0)
     col = lax.broadcasted_iota(jnp.int32, (GT, PER * LANE), 1)
     t = row & (TQ - 1)
-    i = sum((t >= SIDE * k).astype(jnp.int32) for k in range(1, SIDE))
-    there = (row >> 6 == col >> 7) & (t < T) & ((col & (LANE - 1)) == t + 6 * i)
+    there = (row >> 6 == col >> 7) & (t < T) & ((col & (LANE - 1)) == t + 6 * row_of(t))
     onehot = there.astype(F32).astype(BF16)
     moved[:, NG * TP :, :] = jnp.zeros((PER, (8 - NG) * TP, LANE), F32)
     for g in range(NG):
@@ -612,14 +623,12 @@
         put(h, total)
 
 
-def attn_back_body(b, x_at, core, dyr, qkvc, dy, z, hid, att, *refs):
-    if b == 1:
-        mask, *refs = refs
+def attn_back_body(b, x_at, core, dy, qkvc, z, hid, att, *refs):
     bias, ln1g, *refs = refs
     if b == 0:
         sv_m0, sv_a1, sv_m1, table1, *refs = refs
     (wout_h, wqkv_h, r3_o, sv_o, sum_o, grad_o, *part_o,
-     wout, wqkv, do_s, dqkv_s, dq, bias_s, ds_o, moved, sem_o, sem_q) = refs
+     wout, wqkv, do_s, dqkv_s, dq, bias_s, ds_o, moved, dyr, sem_o, sem_q) = refs
     a = pl.program_id(0)
     cp_o = pltpu.make_async_copy(wout_h.at[b], wout, sem_o)
 
@@ -644,10 +653,12 @@
 
     if b == 1:
         for w in range(2):
+            mask = shift_mask(a, core[0] ^ w)
             for g in range(NG):
-                bias_s[w * NG + g] = bias[NG + g] + mask[0, w]
+                bias_s[w * NG + g] = bias[NG + g] + mask
+    dyr[...] = dy[0].astype(BF16)
     wait(cp_o)
-    do = nt(dyr[0], wout[...]).astype(BF16).astype(F32)
+    do = nt(dyr[...], wout[...]).astype(BF16).astype(F32)
     for g in range(NG):
         do_s[g, 0:ROWS, :] = do[:, LANE * g : LANE * (g + 1)]
     masks = head_masks(TP)
@@ -691,7 +702,7 @@
             for c in range(2):
                 w = 2 * x + c
                 r3_o[c, 0] = jnp.concatenate(
-                    [dq[:, 3 * MINE * w : 3 * MINE * (w + 1)], dyr[0, :, MINE * w : MINE * (w + 1)]], axis=1
+                    [dq[:, 3 * MINE * w : 3 * MINE * (w + 1)], dyr[:, MINE * w : MINE * (w + 1)]], axis=1
                 )
 
     normed, inverse = norm_parts(z[0])
@@ -728,14 +739,12 @@
             put(h, table1[h], 72)
 
 
-def attn_back(b, x_at, core, dyr, qkvc, dy, z, hid, att, mask, bias, p, sums=(), after=()):
-    masks = [mask] if b else []
+def attn_back(b, x_at, core, dy, qkvc, z, hid, att, bias, p, sums=(), after=()):
     sum_shape = (PER, 8, TABLE) if b else (D // 8, W_UP)
     return call(
         functools.partial(attn_back_body, b),
-        (x_at, core, dyr, qkvc, dy, z, hid, att, *masks, bias, p["ln1_gain"], *sums, p["w_out"], p["w_qkv"]),
-        [SM, SM, per_half((ROWS, D)), per_half((C, 3 * NG, TQ, LANE))] + [per_half((ROWS, D))] * 4
-        + [per_half((2, TP, GT))] * b
+        (x_at, core, dy, qkvc, z, hid, att, bias, p["ln1_gain"], *sums, p["w_out"], p["w_qkv"]),
+        [SM, SM, per_half((ROWS, D)), per_half((C, 3 * NG, TQ, LANE))] + [per_half((ROWS, D))] * 3
         + [fixed(bias.shape, True), fixed((2, D)), *(fixed(v.shape) for v in sums), ANY, ANY],
         [shape((2, 2, ROWS, D), BF16), shape((4, D), F32), shape(sum_shape, F32), shape((2, T, C, D), F32)]
         + [shape((8, D // 8, W_UP), F32)] * 2,
@@ -759,6 +768,7 @@
             pltpu.VMEM((2 * NG, TP, GT), F32),
             pltpu.VMEM((NG, TP, GT), F32),
             pltpu.VMEM((PER, 8 * TP, LANE), F32),
+            pltpu.VMEM((ROWS, D), BF16),
             pltpu.SemaphoreType.DMA,
             pltpu.SemaphoreType.DMA((N_Q,)),
         ],
@@ -925,6 +935,29 @@
     )
 
 
+def join_steps(joint, *pairs, after=()):
+    kept = [s.kept for s, _ in pairs]
+    recv = [s.recv for s, _ in pairs]
+
+    def body(s, *refs):
+        ins, (keep, send) = refs[:-2], refs[-2:]
+        for k in range(len(pairs)):
+            mine = s[k] == 0
+            low, high = (ins[k][i] + ins[len(pairs) + k][i] for i in range(2))
+            keep[k] = jnp.where(mine, low, high)
+            send[k] = jnp.where(mine, high, low)
+
+    bits = jnp.stack([s.links[name][2] for s, name in pairs])
+    block = kept[0].shape
+    keep, send = call(
+        body, (bits, *kept, *recv), [fixed(block)] * (2 * len(pairs)),
+        [shape((len(pairs), *block[1:]), F32)] * 2, [fixed((len(pairs), *block[1:]))] * 2,
+        cost(2), "join_steps", after, (1,), 1,
+    )
+    joint.send(pairs[0][1], keep, send)
+    return keep
+
+
 def steps(*pairs, after=(), through=()):
     args = []
     for s, name in pairs:
@@ -954,20 +987,20 @@
         return self.kept, self.recv
 
 
-def last_sums(downs, ups, att0, att1, after=()):
-    pairs = [*downs, *ups, *att0, att1]
+def last_sums(mlps, att0, att1, after=()):
+    pairs = [*mlps, *att0, att1]
 
     def body(*refs):
         ins, (qkv, out, up, down, small) = refs[: 2 * len(pairs)], refs[2 * len(pairs) :]
-        total = [ins[2 * i][0] + ins[2 * i + 1][0] for i in range(len(pairs))]
         for b in range(2):
-            down[b] = get_down(total[b])
-            up[b] = total[2 + b]
+            up[b] = ins[2 * b][0] + ins[2 * b + 1][0]
+            down[b] = get_down(ins[2 * b][1] + ins[2 * b + 1][1])
+        total = [ins[2 * i][0] + ins[2 * i + 1][0] for i in range(2, 5)]
         edge = 3 * MINE
-        for b, att in enumerate((jnp.concatenate([total[4], total[5]], axis=1), total[6])):
+        for b, att in enumerate((jnp.concatenate(total[0:2], axis=1), total[2])):
             qkv[b] = att[:, 0:edge]
             out[b] = att[:, edge:]
-        small[...] = ins[8][1] + ins[9][1]
+        small[...] = ins[4][1] + ins[5][1]
 
     rows = D // 8
     return call(
@@ -991,37 +1024,39 @@
     return block
 
 
-def relative_onehot():
-    at = jnp.arange(TP * TQ, dtype=jnp.int32)
-    u, t = at // TQ, at % TQ
-    rel = (t // SIDE - u // SIDE + 6) * 13 + t % SIDE - u % SIDE + 6
-    rel = jnp.where((u < T) & (t < T), rel, -1)
-    return (jnp.arange(169, dtype=jnp.int32)[:, None] == rel[None, :]).astype(F32)
-
-
-def region_of(coords):
-    return jnp.where(coords < 7, 0, jnp.where(coords < 11, 1, 2))
-
-
-def spread_bias(bias_table, onehot):
-    rows = jnp.dot(
-        bias_table.transpose(0, 2, 1).reshape(2 * HEADS, 169),
-        onehot,
-        precision=lax.Precision.HIGHEST,
-        preferred_element_type=F32,
-    )
-    rows = rows.reshape(2, NG, PER, TP, TQ).transpose(0, 1, 3, 2, 4).reshape(2 * NG, TP, GT)
-    return jnp.where((jnp.arange(TP) < T)[None, :, None], rows, NEG)
-
-
-def shift_masks(core):
-    places = jnp.arange(TQ, dtype=jnp.int32)
-    step = jnp.arange(2, dtype=jnp.int32)
-    rows = region_of(step[:, None] * SIDE + places // SIDE)
-    cols = region_of((core ^ step)[:, None] * SIDE + places % SIDE)
-    labels = 3 * rows[:, None] + cols[None, :]
-    mask = jnp.where(labels[:, :, :TP, None] == labels[:, :, None, :], 0.0, -100.0).astype(F32)
-    return jnp.tile(mask, (1, 1, 1, PER))
+def window_bias(table, after=()):
+    pairs = 16
+
+    def body(src, out, rolled, wide):
+        l = lax.broadcasted_iota(jnp.int32, (LANE, GT), 0)
+        t = lax.broadcasted_iota(jnp.int32, (LANE, GT), 1) & (TQ - 1)
+        at = lax.broadcasted_iota(jnp.int32, (LANE, GT), 1) >> 6
+        there = (t < T) & (l == t + 6 * row_of(t))
+        wide[...] = jnp.zeros_like(wide)
+        for h in range(PER):
+            rows = [src[k // NG, PER * (k % NG) + h : PER * (k % NG) + h + 1] for k in range(2 * NG)]
+            rows = jnp.concatenate(rows + [jnp.zeros((pairs - 2 * NG, TABLE), F32)], axis=0)
+            for u in range(T):
+                shift = 13 * (6 - u // SIDE) + 6 - u % SIDE
+                rolled[pairs * u : pairs * (u + 1), :] = pltpu.roll(rows, (TABLE - shift) % TABLE, 1)[:, 0:LANE]
+            ones = (there & (at == h)).astype(F32).astype(BF16)
+            rest = rolled[...]
+            for _ in range(3):
+                part = rest.astype(BF16)
+                moved = nn(part, ones)
+                for k in range(2):
+                    wide[k, 0 : pairs * T, :] += moved[:, LANE * k : LANE * (k + 1)]
+                rest = rest - part.astype(F32)
+        real = lax.broadcasted_iota(jnp.int32, (TP, LANE), 0) < T
+        for b in range(2 * NG):
+            for k in range(2):
+                v = wide[k, pl.ds(b, TP, stride=pairs), :]
+                out[b, :, LANE * k : LANE * (k + 1)] = jnp.where(real, v, NEG)
+
+    return call(
+        body, (table,), [VM], shape((2 * NG, TP, GT), F32), VM, cost(4), "window_bias", after,
+        scratch=[pltpu.VMEM((pairs * T, LANE), F32), pltpu.VMEM((2, pairs * TP, LANE), F32)],
+    )
 
 
 def per_device(
@@ -1049,9 +1084,8 @@
     def swap(a):
         return over(1, a)
 
-    onehot = relative_onehot()
-    bias = spread_bias(bias_table, onehot)
-    mask = shift_masks(core)
+    table = jnp.pad(bias_table.transpose(0, 2, 1), ((0, 0), (0, 0), (0, TABLE - 169)))
+    bias = window_bias(table)
 
     mine, other = crop_rows(at_core, all_valid, tokens[:, 0].transpose(1, 0, 2))
     near, far = swap(other), (over(2, mine), over(3, other))
@@ -1059,7 +1093,7 @@
     ct_near, ct_far = swap(ct_other), (over(2, ct_mine), over(3, ct_other))
     fwd0 = block_fwd(0, (at_x, mine, near), bias, p, 0, (ct_mine,))
     fwd0 = block_fwd(0, (at_x, *far), bias, p, 1, fwd0)
-    fwd1 = block_fwd(1, (fwd0[8], mask), bias, p)
+    fwd1 = block_fwd(1, (at_core, fwd0[8]), bias, p)
     z0, h0, qkvc0, o0, y0, h20, g0, gp0, _ = fwd0
     z1, h1, qkvc1, o1, y1, h21, g1, gp1, zn = fwd1
     ct = join_pieces(at_x, (ct_mine, ct_near, *ct_far), (zn,))
@@ -1068,31 +1102,32 @@
         return Halving([k for k in (2, 1, 0) if k != first], links, extra)
 
     down1, up1, att1, down0, up0 = (stream(k) for k in (0, 1, 0, 0, 1))
-    att0 = [stream(0, 1), stream(1)]
-
-    dd1, da1, dy, dyr, sv_m1, *part = mlp_back(1, at_x, at_core, ct, y1, gp1, g1, h21, p)
+    mlp1, mlp0 = (Halving([], links) for _ in range(2))
+    att0 = [stream(0, 1), stream(0)]
+
+    dd1, da1, dy, sv_m1, *part = mlp_back(1, at_x, at_core, ct, y1, gp1, g1, h21, p)
     down_x, up_x = (swap(a) for a in part)
     r31, sv_a1, table1, grad1, *part = attn_back(
-        1, at_x, at_core, dyr, qkvc1, dy, z1, h1, o1, mask, bias, p, (), (part[0],)
+        1, at_x, at_core, dy, qkvc1, z1, h1, o1, bias, p, (), (part[0],)
     )
     att_x = [swap(a) for a in part]
     last = down1.send(0, *down_mine(bits, dd1, g1, down_x, 0, (sv_a1,)))
     last = up1.send(1, *up_mine(bits, h21, da1, up_x, 1, (last,)))
 
-    dd0, da0, dy, dyr, sv_m0, *part = mlp_back(0, at_x, at_core, grad1, y0, gp0, g0, h20, p, (last, *att_x))
+    dd0, da0, dy, sv_m0, *part = mlp_back(0, at_x, at_core, grad1, y0, gp0, g0, h20, p, (last, *att_x))
     last, *part = steps((down1, 1), (up1, 0), after=(sv_m0,), through=part)
     down_x, up_x = (swap(a) for a in part)
     last = att1.send(0, *attn_mine(bits, h1, o1, r31, att_x, 0, (0, 1), None, (last,)))
     out_mine, out_other = own_quadrants(at_x, zn, True, (last,))
     out_x = swap(out_other)
-    last = down0.send(0, *down_mine(bits, dd0, g0, down_x, 0, (out_mine,)))
+    last = join_steps(mlp1, (up1, 2), (down1, 2), after=(out_mine,))
+    last = down0.send(0, *down_mine(bits, dd0, g0, down_x, 0, (last,)))
     last = up0.send(1, *up_mine(bits, h20, da0, up_x, 1, (last,)))
-    last = steps((down1, 2), (up1, 2), after=(last,))
     r30, sv_a0, small, grad0, *part = attn_back(
-        0, at_x, at_core, dyr, qkvc0, dy, z0, h0, o0, mask, bias, p, (sv_m0, sv_a1, sv_m1, table1), (last,)
+        0, at_x, at_core, dy, qkvc0, z0, h0, o0, bias, p, (sv_m0, sv_a1, sv_m1, table1), (last,)
     )
     last, small, *part = steps(
-        (up0, 0), (down0, 1), (att1, 1), after=(sv_a0, down1.recv, up1.recv), through=(small, *part)
+        (up0, 0), (down0, 1), (att1, 1), after=(sv_a0, mlp1.recv), through=(small, *part)
     )
     att_x = [swap(a) for a in part]
     small = [small, swap(small)]
@@ -1100,18 +1135,20 @@
     in_mine, in_other = own_quadrants(at_x, grad0, False, (block_out,))
     in_x = swap(in_other)
     last = in_mine
-    for k in range(2):
-        kept, out = attn_mine(bits, h0, o0, r30, att_x, k, (k,), None if k else small, (last,))
-        last = att0[k].send(k, kept, out)
-    last = steps((up0, 2), (down0, 2), (att1, 2), after=(last,))
-    last = att0[0].step(1, (last, up0.recv))
-    last = att0[1].step(0, (last, down0.recv))
-    last = att0[0].step(2, (last,))
+    kept, out = attn_mine(bits, h0, o0, r30, att_x, 0, (0,), small, (last,))
+    last = att0[0].send(0, kept, out)
+    last = join_steps(mlp0, (up0, 2), (down0, 2), after=(last,))
+    kept, out = attn_mine(bits, h0, o0, r30, att_x, 0, (1,), None, (last,))
+    last = att0[1].send(0, kept, out)
+    last = att0[0].step(1, (last,))
+    last = att1.step(2, (last,))
+    last = att0[1].step(1, (last,))
+    last = att0[0].step(2, (last, mlp0.recv))
     last = att0[1].step(2, (last,))
     grad_tokens = crop_major(at_core, in_mine, in_x, (last,))
 
     g_qkv, g_out, g_up, g_down, small = last_sums(
-        (down0.pair(), down1.pair()), (up0.pair(), up1.pair()), [a.pair() for a in att0], att1.pair(), (grad_tokens,)
+        (mlp0.pair(), mlp1.pair()), [a.pair() for a in att0], att1.pair(), (grad_tokens,)
     )
     for k in range(sub.bit_length() - 1):
         small = small + lax.ppermute(small, "img", [(i, i ^ (1 << k)) for i in range(n_img)])

time: 407 us -> 367 us (0.902)
  Pallas kernels: 284 us -> 225 us
  waiting for transfers between devices: 52.2 us -> 75.5 us
  local copies, waits for them, and re-layouts: 23 us -> 35 us
  starting transfers between devices: 35.5 us -> 25.3 us
    pallas_call x30 -> x32, Pallas kernels: 284 us -> 225 us  [call(): pl.pallas_call(wrapped, grid_spec=pltpu.PrefetchScalarGridSpec(num_scalar...]
    ppermute x21 -> x19, waiting for transfers between devices: 50.1 us -> 70.1 us  [send(): self.kept, self.recv = (kept, lax.ppermute(out, axis, perm))]
    unnamed x85 -> x175, local copies, waits for them, and re-layouts: 17.1 us -> 33.7 us
    ppermute x21 -> x19, starting transfers between devices: 27.4 us -> 17.4 us  [send(): self.kept, self.recv = (kept, lax.ppermute(out, axis, perm))]
  transfers between devices with their start and end apart: 38 -> 36, of which waited for: 8 -> 16; matrix products, arithmetic and copies ran while one was open for 2% -> 0% of each run, Pallas kernels for 60% -> 53%
where the time goes in v4:
time: 367 us; the launch traced here: 363 us
  Pallas kernels  225 us (61%)
  waiting for transfers between devices  75.5 us (21%)
  local copies, waits for them, and re-layouts  35 us (10%)
  starting transfers between devices  25.3 us (7%)
    pallas_call x32, Pallas kernels, call(): pl.pallas_call(wrapped, grid_spec=pltpu.PrefetchScalarGridSpec(num_scalar...  225 us
    ppermute x19, waiting for transfers between devices, send(): self.kept, self.recv = (kept, lax.ppermute(out, axis, perm))  70.1 us
    unnamed x175, local copies, waits for them, and re-layouts  33.7 us
    ppermute x19, starting transfers between devices, send(): self.kept, self.recv = (kept, lax.ppermute(out, axis, perm))  17.4 us
    ppermute x17, starting transfers between devices, over(): return lax.ppermute(a, 'win', [(i, i ^ way) for i in range(4)])  7.93 us
  transfers between devices with their start and end apart: 36, of which 16 were waited for; matrix products, arithmetic and copies ran while one was open for 0% of the time, Pallas kernels for 53%

profile of v4, /device:TPU:0, one launch (start us, length us, event | category | flops | bytes accessed | tf_op | source)
XLA Modules:
  0.0 363.4 jit_solution(15185281588471510062)
XLA Ops:
  3.6 2.6 collective-permute-start.1
  8.3 2.0 collective-permute-start.5
  10.4 1.7 window_bias.1.refs_3_.refs_2_.refs_7_
  12.3 18.8 %forward_0.2 = (f32[2,392,768]{2,1,0:T(8,128)}, bf16[2,392,768]{2,1,0:T(8,128)(2,1)S(1)}, bf16[2,8,18,64,128]{4,3,2,1,0:T(8,128)(2,1)}, bf16[2,392,768]{2,1,0:T(...) custom-call(s32[1]{0:T(128)} %bitcast.1.refs_0_, ...), custom_call_target="tpu_custom_call" | custom-call | flops 9660000256 | tf_op jit(solution)/shard_map/forward_0/pallas_call | solution.py:170
  31.1 3.1 collective-permute-done.refs_1_
  34.2 1.7 copy-done.5
  35.9 17.9 %forward_0.3 = (f32[2,392,768]{2,1,0:T(8,128)S(1)}, bf16[2,392,768]{2,1,0:T(8,128)(2,1)S(1)}, bf16[2,8,18,64,128]{4,3,2,1,0:T(8,128)(2,1)}, bf16[2,392,768]{2,1,...) custom-call(s32[1]{0:T(128)} %bitcast.1.refs_0_, ...), custom_call_target="tpu_custom_call", output_to_operand_aliasing={{0}: (17, {}), {1}: (18, {}), {2}: (19, {}), {3}: (20, {}),... | custom-call | flops 9660000256 | tf_op jit(solution)/shard_map/forward_0/pallas_call | solution.py:170
  57.3 35.5 %forward_1.1 = (f32[2,392,768]{2,1,0:T(8,128)S(1)}, bf16[2,392,768]{2,1,0:T(8,128)(2,1)S(1)}, bf16[2,8,18,64,128]{4,3,2,1,0:T(8,128)(2,1)}, bf16[2,392,768]{2,1,...) custom-call(s32[1]{0:T(128)} %bitcast.refs_0_.refs_1_, ...), custom_call_target="tpu_custom_call" | custom-call | flops 16560000000 | tf_op jit(solution)/shard_map/forward_1/pallas_call | solution.py:170
  92.9 3.5 copy-done.7
  97.3 1.5 copy-done.9
  98.7 24.1 %mlp_back_1.1 = (bf16[2,2,392,192]{3,2,1,0:T(8,128)(2,1)S(1)}, bf16[2,392,1536]{2,1,0:T(8,128)(2,1)S(1)}, f32[2,392,768]{2,1,0:T(8,128)}, f32[8,768]{1,0:T(8,128...) custom-call(s32[1]{0:T(128)} %bitcast.1.refs_0_, s32[1]{0:T(128)} %bitcast.refs_0_.refs_1_, ...), custom_call_target="tpu_custom_call" | custom-call | flops 10119999488 | tf_op jit(solution)/shard_map/mlp_back_1/pallas_call | solution.py:170
  124.8 28.6 %attn_back_1.1 = (bf16[2,2,392,768]{3,2,1,0:T(8,128)(2,1)}, f32[4,768]{1,0:T(4,128)S(1)}, f32[4,8,256]{2,1,0:T(8,128)S(1)}, f32[2,49,8,768]{3,2,1,0:T(8,128)}, f...) custom-call(s32[1]{0:T(128)} %bitcast.1.refs_0_, s32[1]{0:T(128)} %bitcast.refs_0_.refs_1_, ...), custom_call_target="tpu_custom_call" | custom-call | flops 14259999744 | tf_op jit(solution)/shard_map/attn_back_1/pallas_call | solution.py:170
  155.2 2.4 copy-done
  159.4 3.7 %down_mine.2 = (f32[4,96,768]{2,1,0:T(8,128)S(1)}, f32[4,96,768]{2,1,0:T(8,128)S(1)}) custom-call(s32[4]{0:T(128)S(1)} %pad_add_fusion.refs_0_, bf16[2,2,392,192]{3,2,1,0:T(8,128)(2,1)S(1)} %copy-done.17, bf16[2,392,3072]{2,1,0:T(8,128)(2,1)S(1)} %copy-done, bf16[2,392,3072]{2,1,0:T(8,128)(2,1)S(1)} %copy-done, ...), custom_call_target="tpu_custom_call" | custom-call | flops 3174000128 | tf_op jit(solution)/shard_map/down_mine/pallas_call | solution.py:170
  163.2 4.1 %up_mine.2 = (f32[4,96,768]{2,1,0:T(8,128)S(1)}, f32[4,96,768]{2,1,0:T(8,128)S(1)}) custom-call(s32[4]{0:T(128)S(1)} %pad_add_fusion.refs_0_, bf16[2,392,768]{2,1,0:T(8,128)(2,1)S(1)} %copy-done.69, bf16[2,392,1536]{2,1,0:T(8,128)(2,1)S(1)} %copy-done.65, f32[8,96,768]{2,1,0:T(8,128)} %collective-permute-done.10.refs_3_, ...), custom_call_target="tpu_custom_call" | custom-call | flops 2622000128 | tf_op jit(solution)/shard_map/up_mine/pallas_call | solution.py:170
  167.4 2.2 collective-permute-start.11
  169.6 1.5 collective-permute-start.9
  171.2 24.4 %mlp_back_0.1 = (bf16[2,2,392,192]{3,2,1,0:T(8,128)(2,1)S(1)}, bf16[2,392,1536]{2,1,0:T(8,128)(2,1)}, f32[2,392,768]{2,1,0:T(8,128)}, f32[8,768]{1,0:T(8,128)S(1...) custom-call(s32[1]{0:T(128)} %bitcast.1.refs_0_, s32[1]{0:T(128)} %bitcast.refs_0_.refs_1_, ...), custom_call_target="tpu_custom_call" | custom-call | flops 10119999488 | tf_op jit(solution)/shard_map/mlp_back_0/pallas_call | solution.py:170
  195.8 1.5 collective-permute-done.9.refs_2_.refs_4_
  197.2 1.6 split_sum.7
  199.3 1.5 collective-permute-start.15
  201.4 1.8 copy-done.70
  206.0 5.8 %attn_mine.3 = (f32[4,96,768]{2,1,0:T(8,128)S(1)}, f32[4,96,768]{2,1,0:T(8,128)}) custom-call(s32[4]{0:T(128)S(1)} %pad_add_fusion.refs_0_, bf16[2,392,768]{2,1,0:T(8,128)(2,1)S(1)} %copy-done.72, bf16[2,392,768]{2,1,0:T(8,128)(2,1)S(1)} %copy-done.74, bf16[2,2,392,768]{3,2,1,0:T(8,128)(2,1)S(1)} %copy-done.70, ...), custom_call_target="tpu_custom_call" | custom-call | flops 3265999872 | tf_op jit(solution)/shard_map/attn_mine/pallas_call | solution.py:170
  212.2 1.7 copy-done.8
  216.0 2.6 join_steps.2
  218.6 2.6 collective-permute-start.20
  221.2 4.5 %down_mine.3 = (f32[4,96,768]{2,1,0:T(8,128)S(1)}, f32[4,96,768]{2,1,0:T(8,128)}) custom-call(s32[4]{0:T(128)S(1)} %pad_add_fusion.refs_0_, bf16[2,2,392,192]{3,2,1,0:T(8,128)(2,1)S(1)} %copy-done.19, bf16[2,392,3072]{2,1,0:T(8,128)(2,1)S(1)} %bitcast.31, bf16[2,392,3072]{2,1,0:T(8,128)(2,1)S(1)} %bitcast.31, ...), custom_call_target="tpu_custom_call" | custom-call | flops 3174000128 | tf_op jit(solution)/shard_map/down_mine/pallas_call | solution.py:170
  226.5 5.2 %up_mine.3 = (f32[4,96,768]{2,1,0:T(8,128)S(1)}, f32[4,96,768]{2,1,0:T(8,128)}) custom-call(s32[4]{0:T(128)S(1)} %copy-done.41, bf16[2,392,768]{2,1,0:T(8,128)(2,1)S(1)} %copy-done.2, bf16[2,392,1536]{2,1,0:T(8,128)(2,1)S(1)} %copy-done.43, f32[8,96,768]{2,1,0:T(8,128)} %collective-permute-done.13.refs_3_, ...), custom_call_target="tpu_custom_call" | custom-call | flops 2622000128 | tf_op jit(solution)/shard_map/up_mine/pallas_call | solution.py:170
  232.5 1.5 collective-permute-start.18
  234.1 28.0 %attn_back_0.1 = (bf16[2,2,392,768]{3,2,1,0:T(8,128)(2,1)}, f32[4,768]{1,0:T(4,128)S(1)}, f32[96,384]{1,0:T(8,128)S(1)}, f32[2,49,8,768]{3,2,1,0:T(8,128)}, f32[...) custom-call(s32[1]{0:T(128)} %bitcast.1.refs_0_, s32[1]{0:T(128)} %bitcast.refs_0_.refs_1_, ...), custom_call_target="tpu_custom_call" | custom-call | flops 14259999744 | tf_op jit(solution)/shard_map/attn_back_0/pallas_call | solution.py:170
  262.1 8.4 %collective-permute-done.17.refs_2_.refs_4_ = f32[4,96,768]{2,1,0:T(8,128)S(1)} collective-permute-done((f32[4,96,768]{2,1,0:T(8,128)}, f32[4,96,768]{2,1,0:T(8,128)S(1)}, u32[]{:S(2)}, u32[]{:S(2)}) %collective-permute-start.17) | collective-permute-done | bytes 1179680 | tf_op jit(solution)/shard_map/ppermute | solution.py:980
  270.5 1.8 split_sum.8
  273.9 2.2 collective-permute-done.12.refs_3_
  279.1 1.7 copy-done.54
  280.8 1.6 attn_mine.4
  283.0 2.0 collective-permute-start.28
  285.0 4.8 %collective-permute-done.23.refs_3_ = f32[2,96,768]{2,1,0:T(8,128)S(1)} collective-permute-done((f32[2,96,768]{2,1,0:T(8,128)}, f32[2,96,768]{2,1,0:T(8,128)S(1)}, u32[]{:S(2)}, u32[]{:S(2)}) %collective-permute-start.23) | collective-permute-done | bytes 589856 | tf_op jit(solution)/shard_map/ppermute | solution.py:980
  289.8 2.7 collective-permute-done.24.refs_4_
  293.2 2.4 attn_mine.5
  297.1 8.5 %collective-permute-done.29.refs_2_.refs_4_ = f32[5,96,384]{2,1,0:T(8,128)S(1)} collective-permute-done((f32[5,96,384]{2,1,0:T(8,128)S(1)}, f32[5,96,384]{2,1,0:T(8,128)S(1)}, u32[]{:S(2)}, u32[]{:S(2)}) %collective-permute-start.29) | collective-permute-done | bytes 737312 | tf_op jit(solution)/shard_map/ppermute | solution.py:980
  305.9 4.8 %collective-permute-done.28.refs_2_.refs_4_ = f32[2,96,768]{2,1,0:T(8,128)S(1)} collective-permute-done((f32[2,96,768]{2,1,0:T(8,128)S(1)}, f32[2,96,768]{2,1,0:T(8,128)S(1)}, u32[]{:S(2)}, u32[]{:S(2)}) %collective-permute-start.28) | collective-permute-done | bytes 589856 | tf_op jit(solution)/shard_map/ppermute | solution.py:980
  311.5 5.8 %collective-permute-done.27.refs_2_.refs_4_ = f32[4,96,384]{2,1,0:T(8,128)S(1)} collective-permute-done((f32[4,96,384]{2,1,0:T(8,128)S(1)}, f32[4,96,384]{2,1,0:T(8,128)S(1)}, u32[]{:S(2)}, u32[]{:S(2)}) %collective-permute-start.27) | collective-permute-done | bytes 589856 | tf_op jit(solution)/shard_map/ppermute | solution.py:980
  317.6 1.7 collective-permute-start.35
  319.3 6.9 %collective-permute-done.32.refs_6_.refs_1_ = f32[2,96,768]{2,1,0:T(8,128)S(1)} collective-permute-done((f32[2,96,768]{2,1,0:T(8,128)S(1)}, f32[2,96,768]{2,1,0:T(8,128)S(1)}, u32[]{:S(2)}, u32[]{:S(2)}) %collective-permute-start.32) | collective-permute-done | bytes 589856 | tf_op jit(solution)/shard_map/ppermute | solution.py:980
  326.2 7.4 %collective-permute-done.31.refs_2_.refs_4_ = f32[3,96,384]{2,1,0:T(8,128)S(1)} collective-permute-done((f32[3,96,384]{2,1,0:T(8,128)S(1)}, f32[3,96,384]{2,1,0:T(8,128)S(1)}, u32[]{:S(2)}, u32[]{:S(2)}) %collective-permute-start.31) | collective-permute-done | bytes 442400 | tf_op jit(solution)/shard_map/ppermute | solution.py:980
  334.3 4.9 %collective-permute-done.30.refs_2_.refs_4_ = f32[2,96,384]{2,1,0:T(8,128)S(1)} collective-permute-done((f32[2,96,384]{2,1,0:T(8,128)S(1)}, f32[2,96,384]{2,1,0:T(8,128)S(1)}, u32[]{:S(2)}, u32[]{:S(2)}) %collective-permute-start.30) | collective-permute-done | bytes 294944 | tf_op jit(solution)/shard_map/ppermute | solution.py:980
  343.9 13.4 %collective-permute-done.34.refs_7_ = f32[1,96,384]{2,1,0:T(8,128)S(1)} collective-permute-done((f32[1,96,384]{2,1,0:T(8,128)}, f32[1,96,384]{2,1,0:T(8,128)S(1)}, u32[]{:S(2)}, u32[]{:S(2)}) %collective-permute-start.34) | collective-permute-done | bytes 147488 | tf_op jit(solution)/shard_map/ppermute | solution.py:980
  358.6 2.3 last_sums.1
  (246 shorter events, 39.7 us)
Async XLA Ops:
  3.2 9.0 %collective-permute-start.2 = (f32[6,196,128]{2,1,0:T(8,128)}, f32[6,196,128]{2,1,0:T(8,128)}, u32[]{:S(2)}, u32[]{:S(2)}) collective-permute-start(f32[6,196,128]{2,1,0:T(8,128)} %get-tuple-element.124), channel_id=1, source_target_pairs={{0,1},{1,0},{2,3},{3,2},{4,5},{5,4},{6,7},{7,6},{8,9},{9,8},{10,11... | collective-permute-start | bytes 1806344 | tf_op jit(solution)/shard_map/ppermute | solution.py:1082
  3.6 30.6 %collective-permute-start.1 = (f32[6,196,128]{2,1,0:T(8,128)}, f32[6,196,128]{2,1,0:T(8,128)S(1)}, u32[]{:S(2)}, u32[]{:S(2)}) collective-permute-start(f32[6,196,128]{2,1,0:T(8,128)} %get-tuple-element.124), channel_id=1, source_target_pairs={{0,3},{1,2},{2,1},{3,0},{4,7},{5,6},{6,5},{7,4},{8,11},{9,10},{10,... | collective-permute-start | bytes 1806344 | tf_op jit(solution)/shard_map/ppermute | solution.py:1082
  6.2 28.0 %collective-permute-start = (f32[6,196,128]{2,1,0:T(8,128)}, f32[6,196,128]{2,1,0:T(8,128)S(1)}, u32[]{:S(2)}, u32[]{:S(2)}) collective-permute-start(f32[6,196,128]{2,1,0:T(8,128)} %get-tuple-element.123.refs_3_.refs_1_), channel_id=1, source_target_pairs={{0,2},{1,3},{2,0},{3,1},{4,6},{5,7},{6,4},{7,5},{8,10},{9,11},{10,... | collective-permute-start | bytes 1806344 | tf_op jit(solution)/shard_map/ppermute | solution.py:1082
  8.1 84.7 %collective-permute-start.3 = (f32[6,196,128]{2,1,0:T(8,128)}, f32[6,196,128]{2,1,0:T(8,128)S(1)}, u32[]{:S(2)}, u32[]{:S(2)}) collective-permute-start(f32[6,196,128]{2,1,0:T(8,128)} %get-tuple-element.139), channel_id=1, source_target_pairs={{0,1},{1,0},{2,3},{3,2},{4,5},{5,4},{6,7},{7,6},{8,9},{9,8},{10,11... | collective-permute-start | bytes 1806344 | tf_op jit(solution)/shard_map/ppermute | solution.py:1082
  8.3 84.6 %collective-permute-start.5 = (f32[6,196,128]{2,1,0:T(8,128)}, f32[6,196,128]{2,1,0:T(8,128)S(1)}, u32[]{:S(2)}, u32[]{:S(2)}) collective-permute-start(f32[6,196,128]{2,1,0:T(8,128)} %get-tuple-element.139), channel_id=1, source_target_pairs={{0,3},{1,2},{2,1},{3,0},{4,7},{5,6},{6,5},{7,4},{8,11},{9,10},{10,... | collective-permute-start | bytes 1806344 | tf_op jit(solution)/shard_map/ppermute | solution.py:1082
  12.1 112.6 %copy-start.20 = (f32[12,56,256]{2,1,0:T(8,128)}, f32[12,56,256]{2,1,0:T(8,128)S(1)}, u32[]{:S(2)}) copy-start(f32[12,56,256]{2,1,0:T(8,128)S(1)} %window_bias.1.refs_3_.refs_2_.refs_7_) | copy-start | bytes 2064388
  12.1 80.7 %collective-permute-start.4 = (f32[6,196,128]{2,1,0:T(8,128)S(1)}, f32[6,196,128]{2,1,0:T(8,128)S(1)}, u32[]{:S(2)}, u32[]{:S(2)}) collective-permute-start(f32[6,196,128]{2,1,0:T(8,128)S(1)} %get-tuple-element.125.refs_17_.refs_1_), channel_id=1, source_target_pairs={{0,2},{1,3},{2,0},{3,1},{4,6},{5,7},{6,4},{7,5},{8,10},{9,11},{10,... | collective-permute-start | bytes 1806344 | tf_op jit(solution)/shard_map/ppermute | solution.py:1082
  57.3 35.5 %copy-start.12 = (bf16[2,392,768]{2,1,0:T(8,128)(2,1)}, bf16[2,392,768]{2,1,0:T(8,128)(2,1)S(1)}, u32[]{:S(2)}) copy-start(bf16[2,392,768]{2,1,0:T(8,128)(2,1)S(1)} %get-tuple-element.187.refs_5_.refs_1_) | copy-start | bytes 3612676
  92.8 31.9 %copy-start.71 = (bf16[2,392,768]{2,1,0:T(8,128)(2,1)}, bf16[2,392,768]{2,1,0:T(8,128)(2,1)S(1)}, u32[]{:S(2)}) copy-start(bf16[2,392,768]{2,1,0:T(8,128)(2,1)S(1)} %get-tuple-element.137.refs_5_.refs_1_) | copy-start | bytes 3612676
  92.8 31.9 %copy-start.73 = (bf16[2,392,768]{2,1,0:T(8,128)(2,1)}, bf16[2,392,768]{2,1,0:T(8,128)(2,1)S(1)}, u32[]{:S(2)}) copy-start(bf16[2,392,768]{2,1,0:T(8,128)(2,1)S(1)} %get-tuple-element.138.refs_6_.refs_2_) | copy-start | bytes 3612676
  124.2 29.1 %copy-start.16 = (bf16[2,2,392,192]{3,2,1,0:T(8,128)(2,1)}, bf16[2,2,392,192]{3,2,1,0:T(8,128)(2,1)S(1)}, u32[]{:S(2)}) copy-start(bf16[2,2,392,192]{3,2,1,0:T(8,128)(2,1)S(1)} %get-tuple-element.151.refs_1_) | copy-start | bytes 1806340
  124.2 29.1 %copy-start.79 = (f32[8,768]{1,0:T(8,128)}, f32[8,768]{1,0:T(8,128)S(1)}, u32[]{:S(2)}) copy-start(f32[8,768]{1,0:T(8,128)S(1)} %get-tuple-element.189.refs_11_) | copy-start | bytes 73732
  124.2 31.0 %collective-permute-start.8 = (f32[8,96,768]{2,1,0:T(8,128)}, f32[8,96,768]{2,1,0:T(8,128)S(1)}, u32[]{:S(2)}, u32[]{:S(2)}) collective-permute-start(f32[8,96,768]{2,1,0:T(8,128)} %get-tuple-element.147.refs_11_), channel_id=1, source_target_pairs={{0,1},{1,0},{2,3},{3,2},{4,5},{5,4},{6,7},{7,6},{8,9},{9,8},{10,11... | collective-permute-start | bytes 7077896 | tf_op jit(solution)/shard_map/ppermute | solution.py:1082
  124.2 38.9 %collective-permute-start.10 = (f32[8,96,768]{2,1,0:T(8,128)}, f32[8,96,768]{2,1,0:T(8,128)}, u32[]{:S(2)}, u32[]{:S(2)}) collective-permute-start(f32[8,96,768]{2,1,0:T(8,128)} %get-tuple-element.156), channel_id=1, source_target_pairs={{0,1},{1,0},{2,3},{3,2},{4,5},{5,4},{6,7},{7,6},{8,9},{9,8},{10,11... | collective-permute-start | bytes 7077896 | tf_op jit(solution)/shard_map/ppermute | solution.py:1082
  154.6 16.6 %collective-permute-start.6 = (f32[8,96,384]{2,1,0:T(8,128)}, f32[8,96,384]{2,1,0:T(8,128)S(1)}, u32[]{:S(2)}, u32[]{:S(2)}) collective-permute-start(f32[8,96,384]{2,1,0:T(8,128)} %get-tuple-element.149), channel_id=1, source_target_pairs={{0,1},{1,0},{2,3},{3,2},{4,5},{5,4},{6,7},{7,6},{8,9},{9,8},{10,11... | collective-permute-start | bytes 3538952 | tf_op jit(solution)/shard_map/ppermute | solution.py:1082
  154.6 16.6 %collective-permute-start.7 = (f32[8,96,384]{2,1,0:T(8,128)}, f32[8,96,384]{2,1,0:T(8,128)}, u32[]{:S(2)}, u32[]{:S(2)}) collective-permute-start(f32[8,96,384]{2,1,0:T(8,128)} %get-tuple-element.150), channel_id=1, source_target_pairs={{0,1},{1,0},{2,3},{3,2},{4,5},{5,4},{6,7},{7,6},{8,9},{9,8},{10,11... | collective-permute-start | bytes 3538952 | tf_op jit(solution)/shard_map/ppermute | solution.py:1082
  155.2 66.0 %copy-start.40 = (s32[4]{0:T(128)}, s32[4]{0:T(128)S(1)}, u32[]{:S(2)}) copy-start(s32[4]{0:T(128)S(1)} %pad_add_fusion.refs_0_) | copy-start | bytes 52
  167.4 28.4 %collective-permute-start.11 = (f32[4,96,768]{2,1,0:T(8,128)S(1)}, f32[4,96,768]{2,1,0:T(8,128)S(1)}, u32[]{:S(2)}, u32[]{:S(2)}) collective-permute-start(f32[4,96,768]{2,1,0:T(8,128)S(1)} %get-tuple-element.158), channel_id=1, source_target_pairs={{0,8},{4,12},{8,0},{12,4},{16,24},{20,28},{24,16},{28,20},{1,9},{5... | collective-permute-start | bytes 3538952 | tf_op jit(solution)/shard_map/ppermute | solution.py:980
  169.6 27.6 %collective-permute-start.9 = (f32[4,96,768]{2,1,0:T(8,128)S(1)}, f32[4,96,768]{2,1,0:T(8,128)S(1)}, u32[]{:S(2)}, u32[]{:S(2)}) collective-permute-start(f32[4,96,768]{2,1,0:T(8,128)S(1)} %get-tuple-element.154), channel_id=1, source_target_pairs={{0,4},{4,0},{8,12},{12,8},{16,20},{20,16},{24,28},{28,24},{1,5},{5... | collective-permute-start | bytes 3538952 | tf_op jit(solution)/shard_map/ppermute | solution.py:980
  198.8 22.3 %collective-permute-start.14 = (f32[8,96,768]{2,1,0:T(8,128)}, f32[8,96,768]{2,1,0:T(8,128)S(1)}, u32[]{:S(2)}, u32[]{:S(2)}) collective-permute-start(f32[8,96,768]{2,1,0:T(8,128)} %get-tuple-element.174), channel_id=1, source_target_pairs={{0,1},{1,0},{2,3},{3,2},{4,5},{5,4},{6,7},{7,6},{8,9},{9,8},{10,11... | collective-permute-start | bytes 7077896 | tf_op jit(solution)/shard_map/ppermute | solution.py:1082
  198.8 26.9 %collective-permute-start.13 = (f32[8,96,768]{2,1,0:T(8,128)}, f32[8,96,768]{2,1,0:T(8,128)}, u32[]{:S(2)}, u32[]{:S(2)}) collective-permute-start(f32[8,96,768]{2,1,0:T(8,128)} %get-tuple-element.172), channel_id=1, source_target_pairs={{0,1},{1,0},{2,3},{3,2},{4,5},{5,4},{6,7},{7,6},{8,9},{9,8},{10,11... | collective-permute-start | bytes 7077896 | tf_op jit(solution)/shard_map/ppermute | solution.py:1082
  199.3 16.2 %collective-permute-start.15 = (f32[2,96,768]{2,1,0:T(8,128)}, f32[2,96,768]{2,1,0:T(8,128)S(1)}, u32[]{:S(2)}, u32[]{:S(2)}) collective-permute-start(f32[2,96,768]{2,1,0:T(8,128)} %get-tuple-element.176), channel_id=1, source_target_pairs={{0,4},{4,0},{8,12},{12,8},{16,20},{20,16},{24,28},{28,24},{1,5},{5... | collective-permute-start | bytes 1769480 | tf_op jit(solution)/shard_map/ppermute | solution.py:980
  200.9 15.1 %collective-permute-start.16 = (f32[2,96,768]{2,1,0:T(8,128)S(1)}, f32[2,96,768]{2,1,0:T(8,128)}, u32[]{:S(2)}, u32[]{:S(2)}) collective-permute-start(f32[2,96,768]{2,1,0:T(8,128)S(1)} %get-tuple-element.177), channel_id=1, source_target_pairs={{0,8},{4,12},{8,0},{12,4},{16,24},{20,28},{24,16},{28,20},{1,9},{5... | collective-permute-start | bytes 1769480 | tf_op jit(solution)/shard_map/ppermute | solution.py:980
  201.4 19.7 %slice-start = ((s8[4816896]{0:T(1024)(128)(4,1)}), s8[4194304]{0:T(1024)(128)(4,1)S(1)}, s32[]{:S(2)}) async-start(s8[4816896]{0:T(1024)(128)(4,1)} %bitcast.30), calls=%async_computation | async-start | bytes 8388608
  211.7 50.4 %collective-permute-start.19 = (f32[4,96,768]{2,1,0:T(8,128)}, f32[4,96,768]{2,1,0:T(8,128)S(1)}, u32[]{:S(2)}, u32[]{:S(2)}) collective-permute-start(f32[4,96,768]{2,1,0:T(8,128)} %get-tuple-element.183), channel_id=1, source_target_pairs={{0,4},{4,0},{8,12},{12,8},{16,20},{20,16},{24,28},{28,24},{1,5},{5... | collective-permute-start | bytes 3538952 | tf_op jit(solution)/shard_map/ppermute | solution.py:980
  218.6 43.6 %collective-permute-start.20 = (f32[2,96,768]{2,1,0:T(8,128)}, f32[2,96,768]{2,1,0:T(8,128)S(1)}, u32[]{:S(2)}, u32[]{:S(2)}) collective-permute-start(f32[2,96,768]{2,1,0:T(8,128)} %get-tuple-element.195), channel_id=1, source_target_pairs={{0,16},{4,20},{8,24},{12,28},{16,0},{20,4},{24,8},{28,12},{1,17},{... | collective-permute-start | bytes 1769480 | tf_op jit(solution)/shard_map/ppermute | solution.py:980
  231.8 38.7 %collective-permute-start.17 = (f32[4,96,768]{2,1,0:T(8,128)}, f32[4,96,768]{2,1,0:T(8,128)S(1)}, u32[]{:S(2)}, u32[]{:S(2)}) collective-permute-start(f32[4,96,768]{2,1,0:T(8,128)} %get-tuple-element.181), channel_id=1, source_target_pairs={{0,8},{4,12},{8,0},{12,4},{16,24},{20,28},{24,16},{28,20},{1,9},{5... | collective-permute-start | bytes 3538952 | tf_op jit(solution)/shard_map/ppermute | solution.py:980
  232.5 38.0 %collective-permute-start.18 = (f32[4,96,768]{2,1,0:T(8,128)}, f32[4,96,768]{2,1,0:T(8,128)S(1)}, u32[]{:S(2)}, u32[]{:S(2)}) collective-permute-start(f32[4,96,768]{2,1,0:T(8,128)} %get-tuple-element.182), channel_id=1, source_target_pairs={{0,4},{4,0},{8,12},{12,8},{16,20},{20,16},{24,28},{28,24},{1,5},{5... | collective-permute-start | bytes 3538952 | tf_op jit(solution)/shard_map/ppermute | solution.py:980
  234.1 36.4 %copy-start.4 = (f32[4,96,768]{2,1,0:T(8,128)S(1)}, f32[4,96,768]{2,1,0:T(8,128)}, u32[]{:S(2)}) copy-start(f32[4,96,768]{2,1,0:T(8,128)} %copy-done.3) | copy-start | bytes 3538948
  272.3 6.5 %collective-permute-start.25 = (f32[8,96,384]{2,1,0:T(8,128)S(1)}, f32[8,96,384]{2,1,0:T(8,128)S(1)}, u32[]{:S(2)}, u32[]{:S(2)}) collective-permute-start(f32[8,96,384]{2,1,0:T(8,128)S(1)} %get-tuple-element.205), channel_id=1, source_target_pairs={{0,1},{1,0},{2,3},{3,2},{4,5},{5,4},{6,7},{7,6},{8,9},{9,8},{10,11... | collective-permute-start | bytes 3538952 | tf_op jit(solution)/shard_map/ppermute | solution.py:1082
  272.4 3.7 %collective-permute-start.12 = (f32[6,196,128]{2,1,0:T(8,128)S(1)}, f32[6,196,128]{2,1,0:T(8,128)S(1)}, u32[]{:S(2)}, u32[]{:S(2)}) collective-permute-start(f32[6,196,128]{2,1,0:T(8,128)S(1)} %copy-done.45), channel_id=1, source_target_pairs={{0,1},{1,0},{2,3},{3,2},{4,5},{5,4},{6,7},{7,6},{8,9},{9,8},{10,11... | collective-permute-start | bytes 1806344 | tf_op jit(solution)/shard_map/ppermute | solution.py:1082
  272.9 20.3 %collective-permute-start.22 = (f32[8,96,384]{2,1,0:T(8,128)S(1)}, f32[8,96,384]{2,1,0:T(8,128)S(1)}, u32[]{:S(2)}, u32[]{:S(2)}) collective-permute-start(f32[8,96,384]{2,1,0:T(8,128)S(1)} %get-tuple-element.201), channel_id=1, source_target_pairs={{0,1},{1,0},{2,3},{3,2},{4,5},{5,4},{6,7},{7,6},{8,9},{9,8},{10,11... | collective-permute-start | bytes 3538952 | tf_op jit(solution)/shard_map/ppermute | solution.py:1082
  273.0 5.9 %collective-permute-start.26 = (f32[96,384]{1,0:T(8,128)S(1)}, f32[96,384]{1,0:T(8,128)S(1)}, u32[]{:S(2)}, u32[]{:S(2)}) collective-permute-start(f32[96,384]{1,0:T(8,128)S(1)} %get-tuple-element.206.refs_5_), channel_id=1, source_target_pairs={{0,1},{1,0},{2,3},{3,2},{4,5},{5,4},{6,7},{7,6},{8,9},{9,8},{10,11... | collective-permute-start | bytes 442376 | tf_op jit(solution)/shard_map/ppermute | solution.py:1082
  273.4 16.4 %collective-permute-start.23 = (f32[2,96,768]{2,1,0:T(8,128)}, f32[2,96,768]{2,1,0:T(8,128)S(1)}, u32[]{:S(2)}, u32[]{:S(2)}) collective-permute-start(f32[2,96,768]{2,1,0:T(8,128)} %get-tuple-element.203), channel_id=1, source_target_pairs={{0,4},{4,0},{8,12},{12,8},{16,20},{20,16},{24,28},{28,24},{1,5},{5... | collective-permute-start | bytes 1769480 | tf_op jit(solution)/shard_map/ppermute | solution.py:980
  276.1 16.4 %collective-permute-start.24 = (f32[2,96,768]{2,1,0:T(8,128)}, f32[2,96,768]{2,1,0:T(8,128)S(1)}, u32[]{:S(2)}, u32[]{:S(2)}) collective-permute-start(f32[2,96,768]{2,1,0:T(8,128)} %get-tuple-element.204), channel_id=1, source_target_pairs={{0,8},{4,12},{8,0},{12,4},{16,24},{20,28},{24,16},{28,20},{1,9},{5... | collective-permute-start | bytes 1769480 | tf_op jit(solution)/shard_map/ppermute | solution.py:980
  282.4 23.2 %collective-permute-start.29 = (f32[5,96,384]{2,1,0:T(8,128)S(1)}, f32[5,96,384]{2,1,0:T(8,128)S(1)}, u32[]{:S(2)}, u32[]{:S(2)}) collective-permute-start(f32[5,96,384]{2,1,0:T(8,128)S(1)} %get-tuple-element.213), channel_id=1, source_target_pairs={{0,4},{4,0},{8,12},{12,8},{16,20},{20,16},{24,28},{28,24},{1,5},{5... | collective-permute-start | bytes 2211848 | tf_op jit(solution)/shard_map/ppermute | solution.py:980
  283.0 27.8 %collective-permute-start.28 = (f32[2,96,768]{2,1,0:T(8,128)S(1)}, f32[2,96,768]{2,1,0:T(8,128)S(1)}, u32[]{:S(2)}, u32[]{:S(2)}) collective-permute-start(f32[2,96,768]{2,1,0:T(8,128)S(1)} %get-tuple-element.212), channel_id=1, source_target_pairs={{0,8},{4,12},{8,0},{12,4},{16,24},{20,28},{24,16},{28,20},{1,9},{5... | collective-permute-start | bytes 1769480 | tf_op jit(solution)/shard_map/ppermute | solution.py:980
  295.7 21.7 %collective-permute-start.27 = (f32[4,96,384]{2,1,0:T(8,128)S(1)}, f32[4,96,384]{2,1,0:T(8,128)S(1)}, u32[]{:S(2)}, u32[]{:S(2)}) collective-permute-start(f32[4,96,384]{2,1,0:T(8,128)S(1)} %get-tuple-element.210), channel_id=1, source_target_pairs={{0,4},{4,0},{8,12},{12,8},{16,20},{20,16},{24,28},{28,24},{1,5},{5... | collective-permute-start | bytes 1769480 | tf_op jit(solution)/shard_map/ppermute | solution.py:980
  296.2 29.9 %collective-permute-start.32 = (f32[2,96,768]{2,1,0:T(8,128)S(1)}, f32[2,96,768]{2,1,0:T(8,128)S(1)}, u32[]{:S(2)}, u32[]{:S(2)}) collective-permute-start(f32[2,96,768]{2,1,0:T(8,128)S(1)} %get-tuple-element.219), channel_id=1, source_target_pairs={{0,16},{4,20},{8,24},{12,28},{16,0},{20,4},{24,8},{28,12},{1,17},{... | collective-permute-start | bytes 1769480 | tf_op jit(solution)/shard_map/ppermute | solution.py:980
  305.8 27.8 %collective-permute-start.31 = (f32[3,96,384]{2,1,0:T(8,128)S(1)}, f32[3,96,384]{2,1,0:T(8,128)S(1)}, u32[]{:S(2)}, u32[]{:S(2)}) collective-permute-start(f32[3,96,384]{2,1,0:T(8,128)S(1)} %get-tuple-element.218), channel_id=1, source_target_pairs={{0,8},{4,12},{8,0},{12,4},{16,24},{20,28},{24,16},{28,20},{1,9},{5... | collective-permute-start | bytes 1327112 | tf_op jit(solution)/shard_map/ppermute | solution.py:980
  305.8 34.7 %collective-permute-start.21 = (f32[6,196,128]{2,1,0:T(8,128)S(1)}, f32[6,196,128]{2,1,0:T(8,128)S(1)}, u32[]{:S(2)}, u32[]{:S(2)}) collective-permute-start(f32[6,196,128]{2,1,0:T(8,128)S(1)} %get-tuple-element.199), channel_id=1, source_target_pairs={{0,1},{1,0},{2,3},{3,2},{4,5},{5,4},{6,7},{7,6},{8,9},{9,8},{10,11... | collective-permute-start | bytes 1806344 | tf_op jit(solution)/shard_map/ppermute | solution.py:1082
  311.5 22.8 %copy-start.66 = (f32[1,96,768]{2,1,0:T(8,128)}, f32[1,96,768]{2,1,0:T(8,128)S(1)}, u32[]{:S(2)}) copy-start(f32[1,96,768]{2,1,0:T(8,128)S(1)} %get-tuple-element.215.refs_5_.refs_8_) | copy-start | bytes 884740
  317.5 21.7 %collective-permute-start.30 = (f32[2,96,384]{2,1,0:T(8,128)S(1)}, f32[2,96,384]{2,1,0:T(8,128)S(1)}, u32[]{:S(2)}, u32[]{:S(2)}) collective-permute-start(f32[2,96,384]{2,1,0:T(8,128)S(1)} %get-tuple-element.217), channel_id=1, source_target_pairs={{0,8},{4,12},{8,0},{12,4},{16,24},{20,28},{24,16},{28,20},{1,9},{5... | collective-permute-start | bytes 884744 | tf_op jit(solution)/shard_map/ppermute | solution.py:980
  317.6 26.3 %collective-permute-start.35 = (f32[1,96,768]{2,1,0:T(8,128)}, f32[1,96,768]{2,1,0:T(8,128)S(1)}, u32[]{:S(2)}, u32[]{:S(2)}) collective-permute-start(f32[1,96,768]{2,1,0:T(8,128)} %get-tuple-element.224), channel_id=1, source_target_pairs={{0,16},{4,20},{8,24},{12,28},{16,0},{20,4},{24,8},{28,12},{1,17},{... | collective-permute-start | bytes 884744 | tf_op jit(solution)/shard_map/ppermute | solution.py:980
  334.3 23.0 %collective-permute-start.33 = (f32[2,96,384]{2,1,0:T(8,128)}, f32[2,96,384]{2,1,0:T(8,128)}, u32[]{:S(2)}, u32[]{:S(2)}) collective-permute-start(f32[2,96,384]{2,1,0:T(8,128)} %get-tuple-element.222), channel_id=1, source_target_pairs={{0,16},{4,20},{8,24},{12,28},{16,0},{20,4},{24,8},{28,12},{1,17},{... | collective-permute-start | bytes 884744 | tf_op jit(solution)/shard_map/ppermute | solution.py:980
  340.6 16.8 %copy-start.25 = (f32[2,96,768]{2,1,0:T(8,128)S(1)}, f32[2,96,768]{2,1,0:T(8,128)}, u32[]{:S(2)}) copy-start(f32[2,96,768]{2,1,0:T(8,128)} %copy-done.24) | copy-start | bytes 1769476
  340.6 16.7 %collective-permute-start.34 = (f32[1,96,384]{2,1,0:T(8,128)}, f32[1,96,384]{2,1,0:T(8,128)S(1)}, u32[]{:S(2)}, u32[]{:S(2)}) collective-permute-start(f32[1,96,384]{2,1,0:T(8,128)} %get-tuple-element.223), channel_id=1, source_target_pairs={{0,16},{4,20},{8,24},{12,28},{16,0},{20,4},{24,8},{28,12},{1,17},{... | collective-permute-start | bytes 442376 | tf_op jit(solution)/shard_map/ppermute | solution.py:980
  340.6 16.8 %copy-start.56 = (f32[2,96,768]{2,1,0:T(8,128)S(1)}, f32[2,96,768]{2,1,0:T(8,128)}, u32[]{:S(2)}) copy-start(f32[2,96,768]{2,1,0:T(8,128)} %copy-done.55) | copy-start | bytes 1769476
  (74 other events, 334.5 us)

commit v5 on v4

--- a/solution.py
+++ b/solution.py
@@ -29,14 +29,13 @@
 NEG = -1e30
 QCH = 768
 FCH = 1536
-WIN = 2
+WIN = 4
 N_Q = 3 * D // QCH
 N_F = FF // FCH
 W_UP = D // 2
 MINE = D // 4
-VMEM_LIMIT = 44 << 20
+VMEM_OF = {"forwar": 48 << 20, "mlp_ba": 48 << 20, "attn_b": 44 << 20, "attn_m": 24 << 20}
 VMEM_SMALL = 24 << 20
-BIG = ("forw", "mlp_", "attn")
 COST = 0.4
 F32 = jnp.float32
 BF16 = jnp.bfloat16
@@ -178,7 +177,7 @@
         ),
         out_shape=outs,
         input_output_aliases={n_in + k: k for k in range(reuse)},
-        compiler_params=pltpu.CompilerParams(vmem_limit_bytes=VMEM_LIMIT if name[:4] in BIG else VMEM_SMALL),
+        compiler_params=pltpu.CompilerParams(vmem_limit_bytes=VMEM_OF.get(name[:6], VMEM_SMALL)),
         cost_estimate=estimate,
         name=name,
     )(*args, *after)
@@ -206,20 +205,6 @@
         for k in range(HALF):
             for g in range(NG):
                 dest[g, rows_of(HALF * b + k), :] = piece[g, rows_of(k, stride=HALF), :]
-
-
-def join_pieces(x_at, pieces, after=()):
-    def body(x, *refs):
-        *src, out, s = refs
-        for k in range(2):
-            weave(s, src[2 * k : 2 * k + 2])
-            for g in range(NG):
-                out[x[0] ^ k, :, :, LANE * g : LANE * (g + 1)] = s[g].reshape(T, C, LANE)
-
-    return call(
-        body, (x_at, *pieces), [SM] + [VM] * 4, shape((2, T, C, D), F32), VM, cost(4), "join_pieces", after,
-        scratch=[pltpu.VMEM((NG, ROWS, LANE), F32)],
-    )
 
 
 def own_quadrants(x_at, both_halves, rolled, after=()):
@@ -465,8 +450,15 @@
     )
 
 
-def mlp_back_body(b, x_at, core, src, y, gp, act, hid, ln2g, wdown_h, wup_h, dd_o, da_o, dy_o, sv_o, down_o, up_o,
-                  wdown, wup, dz, dd, da_s, sem_d, sem_u):
+def mlp_back_body(b, x_at, core, *refs):
+    if b == 1:
+        (*pieces, y, gp, act, hid, ln2g,
+         wdown_h, wup_h, dd_o, da_o, dy_o, sv_o, down_o, up_o,
+         wdown, wup, dz, dd, da_s, src, woven, sem_d, sem_u) = refs
+    else:
+        (src, y, gp, act, hid, ln2g,
+         wdown_h, wup_h, dd_o, da_o, dy_o, sv_o, down_o, up_o,
+         wdown, wup, dz, dd, da_s, sem_d, sem_u) = refs
     a = pl.program_id(0)
 
     def cp_u(n):
@@ -490,6 +482,11 @@
             cp_d(n).start()
             cp_u(n).start()
         sv_o[...] = jnp.zeros_like(sv_o)
+        if b == 1:
+            for k in range(2):
+                weave(woven, pieces[2 * k : 2 * k + 2])
+                for g in range(NG):
+                    src[x_at[0] ^ k, :, :, LANE * g : LANE * (g + 1)] = woven[g].reshape(T, C, LANE)
 
     put_rolled(dz, src, a, b == 0)
     low = dz[...].astype(BF16)
@@ -543,8 +540,8 @@
 def mlp_back(b, x_at, core, src, y, gp, act, hid, p, after=()):
     return call(
         functools.partial(mlp_back_body, b),
-        (x_at, core, src, y, gp, act, hid, p["ln2_gain"], p["w_down"], p["w_up"]),
-        [SM, SM, fixed((2, T, C, D), True), per_half((ROWS, D)), per_half((ROWS, FF)), per_half((ROWS, FF)),
+        (x_at, core, *src, y, gp, act, hid, p["ln2_gain"], p["w_down"], p["w_up"]),
+        [SM, SM, *(fixed(v.shape, True) for v in src), per_half((ROWS, D)), per_half((ROWS, FF)), per_half((ROWS, FF)),
          per_half((ROWS, D)), fixed((2, D)), ANY, ANY],
         [
             shape((2, 2, ROWS, MINE), BF16),
@@ -572,6 +569,7 @@
             pltpu.VMEM((ROWS, D), F32),
             pltpu.VMEM((ROWS, D), BF16),
             pltpu.VMEM((ROWS, FF), BF16),
+            *([pltpu.VMEM((2, T, C, D), F32), pltpu.VMEM((NG, ROWS, LANE), F32)] if b else []),
             pltpu.SemaphoreType.DMA((4,)),
             pltpu.SemaphoreType.DMA((4,)),
         ],
@@ -1096,16 +1094,17 @@
     fwd1 = block_fwd(1, (at_core, fwd0[8]), bias, p)
     z0, h0, qkvc0, o0, y0, h20, g0, gp0, _ = fwd0
     z1, h1, qkvc1, o1, y1, h21, g1, gp1, zn = fwd1
-    ct = join_pieces(at_x, (ct_mine, ct_near, *ct_far), (zn,))
 
     def stream(first, extra=0):
         return Halving([k for k in (2, 1, 0) if k != first], links, extra)
 
-    down1, up1, att1, down0, up0 = (stream(k) for k in (0, 1, 0, 0, 1))
+    down1, up1, att1, down0, up0 = (stream(k) for k in (0, 1, 0, 1, 0))
     mlp1, mlp0 = (Halving([], links) for _ in range(2))
     att0 = [stream(0, 1), stream(0)]
 
-    dd1, da1, dy, sv_m1, *part = mlp_back(1, at_x, at_core, ct, y1, gp1, g1, h21, p)
+    dd1, da1, dy, sv_m1, *part = mlp_back(
+        1, at_x, at_core, (ct_mine, ct_near, *ct_far), y1, gp1, g1, h21, p, (zn,)
+    )
     down_x, up_x = (swap(a) for a in part)
     r31, sv_a1, table1, grad1, *part = attn_back(
         1, at_x, at_core, dy, qkvc1, z1, h1, o1, bias, p, (), (part[0],)
@@ -1114,20 +1113,20 @@
     last = down1.send(0, *down_mine(bits, dd1, g1, down_x, 0, (sv_a1,)))
     last = up1.send(1, *up_mine(bits, h21, da1, up_x, 1, (last,)))
 
-    dd0, da0, dy, sv_m0, *part = mlp_back(0, at_x, at_core, grad1, y0, gp0, g0, h20, p, (last, *att_x))
+    dd0, da0, dy, sv_m0, *part = mlp_back(0, at_x, at_core, (grad1,), y0, gp0, g0, h20, p, (last, *att_x))
     last, *part = steps((down1, 1), (up1, 0), after=(sv_m0,), through=part)
     down_x, up_x = (swap(a) for a in part)
     last = att1.send(0, *attn_mine(bits, h1, o1, r31, att_x, 0, (0, 1), None, (last,)))
     out_mine, out_other = own_quadrants(at_x, zn, True, (last,))
     out_x = swap(out_other)
     last = join_steps(mlp1, (up1, 2), (down1, 2), after=(out_mine,))
-    last = down0.send(0, *down_mine(bits, dd0, g0, down_x, 0, (last,)))
-    last = up0.send(1, *up_mine(bits, h20, da0, up_x, 1, (last,)))
+    last = down0.send(1, *down_mine(bits, dd0, g0, down_x, 1, (last,)))
+    last = up0.send(0, *up_mine(bits, h20, da0, up_x, 0, (last,)))
     r30, sv_a0, small, grad0, *part = attn_back(
         0, at_x, at_core, dy, qkvc0, z0, h0, o0, bias, p, (sv_m0, sv_a1, sv_m1, table1), (last,)
     )
     last, small, *part = steps(
-        (up0, 0), (down0, 1), (att1, 1), after=(sv_a0, mlp1.recv), through=(small, *part)
+        (down0, 0), (up0, 1), (att1, 1), after=(sv_a0, mlp1.recv), through=(small, *part)
     )
     att_x = [swap(a) for a in part]
     small = [small, swap(small)]

time: 367 us -> 358 us (0.975)
  local copies, waits for them, and re-layouts: 35 us -> 22.3 us
  waiting for transfers between devices: 75.5 us -> 81.5 us
    unnamed x175 -> x131, local copies, waits for them, and re-layouts: 33.7 us -> 20.9 us
    ppermute x19, waiting for transfers between devices: 70.1 us -> 76.6 us  [send(): self.kept, self.recv = (kept, lax.ppermute(out, axis, perm))]
    pallas_call x32 -> x31, Pallas kernels: 225 us -> 222 us  [call(): pl.pallas_call(wrapped, grid_spec=pltpu.PrefetchScalarGridSpec(num_scalar...]
  transfers between devices with their start and end apart: 36 -> 36, of which waited for: 16 -> 16; matrix products, arithmetic and copies ran while one was open for 0% -> 0% of each run, Pallas kernels for 53% -> 54%
where the time goes in v5:
time: 358 us; the launch traced here: 354 us
  Pallas kernels  222 us (62%)
  waiting for transfers between devices  81.5 us (23%)
  starting transfers between devices  25.7 us (7%)
  local copies, waits for them, and re-layouts  22.3 us (6%)
    pallas_call x31, Pallas kernels, call(): pl.pallas_call(wrapped, grid_spec=pltpu.PrefetchScalarGridSpec(num_scalar...  222 us
    ppermute x19, waiting for transfers between devices, send(): self.kept, self.recv = (kept, lax.ppermute(out, axis, perm))  76.6 us
    unnamed x131, local copies, waits for them, and re-layouts  20.9 us
    ppermute x19, starting transfers between devices, send(): self.kept, self.recv = (kept, lax.ppermute(out, axis, perm))  17.7 us
    ppermute x17, starting transfers between devices, over(): return lax.ppermute(a, 'win', [(i, i ^ way) for i in range(4)])  8 us
  transfers between devices with their start and end apart: 36, of which 16 were waited for; matrix products, arithmetic and copies ran while one was open for 0% of the time, Pallas kernels for 54%

profile of v5, /device:TPU:0, one launch (start us, length us, event | category | flops | bytes accessed | tf_op | source)
XLA Modules:
  0.0 353.9 jit_solution(16748163232078848872)
XLA Ops:
  1.7 1.4 crop_rows.2
  3.6 2.6 collective-permute-start.1
  6.9 1.3 crop_rows.3
  8.3 2.0 collective-permute-start.5
  10.4 1.7 window_bias.1.refs_3_.refs_2_.refs_7_
  12.3 19.7 %forward_0.2 = (f32[2,392,768]{2,1,0:T(8,128)}, bf16[2,392,768]{2,1,0:T(8,128)(2,1)S(1)}, bf16[2,8,18,64,128]{4,3,2,1,0:T(8,128)(2,1)}, bf16[2,392,768]{2,1,0:T(...) custom-call(s32[1]{0:T(128)} %bitcast.1.refs_0_, ...), custom_call_target="tpu_custom_call" | custom-call | flops 9660000256 | tf_op jit(solution)/shard_map/forward_0/pallas_call | solution.py:169
  32.1 2.1 collective-permute-done.refs_1_
  34.2 1.3 copy-done.1
  35.5 19.0 %forward_0.3 = (f32[2,392,768]{2,1,0:T(8,128)}, bf16[2,392,768]{2,1,0:T(8,128)(2,1)S(1)}, bf16[2,8,18,64,128]{4,3,2,1,0:T(8,128)(2,1)}, bf16[2,392,768]{2,1,0:T(...) custom-call(s32[1]{0:T(128)} %bitcast.1.refs_0_, ...), custom_call_target="tpu_custom_call", output_to_operand_aliasing={{0}: (17, {}), {1}: (18, {}), {2}: (19, {}), {3}: (20, {}),... | custom-call | flops 9660000256 | tf_op jit(solution)/shard_map/forward_0/pallas_call | solution.py:169
  55.6 36.5 %forward_1.1 = (f32[2,392,768]{2,1,0:T(8,128)}, bf16[2,392,768]{2,1,0:T(8,128)(2,1)S(1)}, bf16[2,8,18,64,128]{4,3,2,1,0:T(8,128)(2,1)}, bf16[2,392,768]{2,1,0:T(...) custom-call(s32[1]{0:T(128)} %bitcast.refs_0_.refs_1_, ...), custom_call_target="tpu_custom_call" | custom-call | flops 16560000000 | tf_op jit(solution)/shard_map/forward_1/pallas_call | solution.py:169
  92.2 25.2 %mlp_back_1.1 = (bf16[2,2,392,192]{3,2,1,0:T(8,128)(2,1)S(1)}, bf16[2,392,1536]{2,1,0:T(8,128)(2,1)}, f32[2,392,768]{2,1,0:T(8,128)}, f32[8,768]{1,0:T(8,128)S(1...) custom-call(s32[1]{0:T(128)} %bitcast.1.refs_0_, s32[1]{0:T(128)} %bitcast.refs_0_.refs_1_, ...), custom_call_target="tpu_custom_call" | custom-call | flops 10119999488 | tf_op jit(solution)/shard_map/mlp_back_1/pallas_call | solution.py:169
  119.4 1.7 copy-done.27
  121.1 28.0 %attn_back_1.1 = (bf16[2,2,392,768]{3,2,1,0:T(8,128)(2,1)}, f32[4,768]{1,0:T(4,128)S(1)}, f32[4,8,256]{2,1,0:T(8,128)S(1)}, f32[2,49,8,768]{3,2,1,0:T(8,128)}, f...) custom-call(s32[1]{0:T(128)} %bitcast.1.refs_0_, s32[1]{0:T(128)} %bitcast.refs_0_.refs_1_, ...), custom_call_target="tpu_custom_call" | custom-call | flops 14259999744 | tf_op jit(solution)/shard_map/attn_back_1/pallas_call | solution.py:169
  150.9 2.4 copy-done
  155.1 3.7 %down_mine.2 = (f32[4,96,768]{2,1,0:T(8,128)S(1)}, f32[4,96,768]{2,1,0:T(8,128)S(1)}) custom-call(s32[4]{0:T(128)S(1)} %pad_add_fusion.refs_0_, bf16[2,2,392,192]{3,2,1,0:T(8,128)(2,1)S(1)} %copy-done.11, bf16[2,392,3072]{2,1,0:T(8,128)(2,1)S(1)} %copy-done, bf16[2,392,3072]{2,1,0:T(8,128)(2,1)S(1)} %copy-done, ...), custom_call_target="tpu_custom_call" | custom-call | flops 3174000128 | tf_op jit(solution)/shard_map/down_mine/pallas_call | solution.py:169
  158.9 4.1 %up_mine.2 = (f32[4,96,768]{2,1,0:T(8,128)S(1)}, f32[4,96,768]{2,1,0:T(8,128)S(1)}) custom-call(s32[4]{0:T(128)S(1)} %pad_add_fusion.refs_0_, bf16[2,392,768]{2,1,0:T(8,128)(2,1)S(1)} %copy-done.40, bf16[2,392,1536]{2,1,0:T(8,128)(2,1)S(1)} %copy-done.36, f32[8,96,768]{2,1,0:T(8,128)} %collective-permute-done.10.refs_3_, ...), custom_call_target="tpu_custom_call" | custom-call | flops 2622000128 | tf_op jit(solution)/shard_map/up_mine/pallas_call | solution.py:169
  163.0 2.2 collective-permute-start.11
  165.3 1.5 collective-permute-start.9
  166.9 24.2 %mlp_back_0.1 = (bf16[2,2,392,192]{3,2,1,0:T(8,128)(2,1)S(1)}, bf16[2,392,1536]{2,1,0:T(8,128)(2,1)}, f32[2,392,768]{2,1,0:T(8,128)}, f32[8,768]{1,0:T(8,128)S(1...) custom-call(s32[1]{0:T(128)} %bitcast.1.refs_0_, s32[1]{0:T(128)} %bitcast.refs_0_.refs_1_, ...), custom_call_target="tpu_custom_call" | custom-call | flops 10119999488 | tf_op jit(solution)/shard_map/mlp_back_0/pallas_call | solution.py:169
  191.5 1.5 collective-permute-done.9.refs_2_.refs_4_
  194.4 1.5 collective-permute-start.14
  196.5 6.0 %attn_mine.3 = (f32[4,96,768]{2,1,0:T(8,128)S(1)}, f32[4,96,768]{2,1,0:T(8,128)}) custom-call(s32[4]{0:T(128)S(1)} %pad_add_fusion.refs_0_, bf16[2,392,768]{2,1,0:T(8,128)(2,1)S(1)} %copy-done.54, bf16[2,392,768]{2,1,0:T(8,128)(2,1)S(1)} %copy-done.56, bf16[2,2,392,768]{3,2,1,0:T(8,128)(2,1)S(1)} %copy-done.50, ...), custom_call_target="tpu_custom_call" | custom-call | flops 3265999872 | tf_op jit(solution)/shard_map/attn_mine/pallas_call | solution.py:169
  203.3 7.3 %collective-permute-done.14.refs_3_ = f32[2,96,768]{2,1,0:T(8,128)S(1)} collective-permute-done((f32[2,96,768]{2,1,0:T(8,128)S(1)}, f32[2,96,768]{2,1,0:T(8,128)S(1)}, u32[]{:S(2)}, u32[]{:S(2)}) %collective-permute-start.14) | collective-permute-done | bytes 589856 | tf_op jit(solution)/shard_map/ppermute | solution.py:978
  211.6 2.7 collective-permute-start.20
  214.3 3.8 %down_mine.3 = (f32[4,96,768]{2,1,0:T(8,128)S(1)}, f32[4,96,768]{2,1,0:T(8,128)S(1)}) custom-call(s32[4]{0:T(128)S(1)} %pad_add_fusion.refs_0_, bf16[2,2,392,192]{3,2,1,0:T(8,128)(2,1)S(1)} %get-tuple-element.171.refs_1_, bf16[2,392,3072]{2,1,0:T(8,128)(2,1)S(1)} %bitcast.31, bf16[2,392,3072]{2,1,0:T(8,128)(2,1)S(1)} %bitcast.31, ...), custom_call_target="tpu_custom_call" | custom-call | flops 3174000128 | tf_op jit(solution)/shard_map/down_mine/pallas_call | solution.py:169
  218.2 3.8 %up_mine.3 = (f32[4,96,768]{2,1,0:T(8,128)S(1)}, f32[4,96,768]{2,1,0:T(8,128)}) custom-call(s32[4]{0:T(128)S(1)} %pad_add_fusion.refs_0_, bf16[2,392,768]{2,1,0:T(8,128)(2,1)S(1)} %copy-done.3, bf16[2,392,1536]{2,1,0:T(8,128)(2,1)S(1)} %copy-done.26, f32[8,96,768]{2,1,0:T(8,128)S(1)} %collective-permute-done.17.refs_3_, ...), custom_call_target="tpu_custom_call" | custom-call | flops 2622000128 | tf_op jit(solution)/shard_map/up_mine/pallas_call | solution.py:169
  223.7 27.4 %attn_back_0.1 = (bf16[2,2,392,768]{3,2,1,0:T(8,128)(2,1)}, f32[4,768]{1,0:T(4,128)S(1)}, f32[96,384]{1,0:T(8,128)S(1)}, f32[2,49,8,768]{3,2,1,0:T(8,128)}, f32[...) custom-call(s32[1]{0:T(128)} %bitcast.1.refs_0_, s32[1]{0:T(128)} %bitcast.refs_0_.refs_1_, ...), custom_call_target="tpu_custom_call" | custom-call | flops 14259999744 | tf_op jit(solution)/shard_map/attn_back_0/pallas_call | solution.py:169
  251.2 9.0 %collective-permute-done.18.refs_6_.refs_8_ = f32[4,96,768]{2,1,0:T(8,128)S(1)} collective-permute-done((f32[4,96,768]{2,1,0:T(8,128)}, f32[4,96,768]{2,1,0:T(8,128)S(1)}, u32[]{:S(2)}, u32[]{:S(2)}) %collective-permute-start.18) | collective-permute-done | bytes 1179680 | tf_op jit(solution)/shard_map/ppermute | solution.py:978
  261.4 1.4 split_sum.8
  264.0 2.7 collective-permute-done.12.refs_3_
  266.7 1.4 collective-permute-start.24
  268.1 1.3 token_major.1.refs_2_
  270.8 1.5 copy-done.34
  272.3 1.6 attn_mine.4
  274.6 5.5 %collective-permute-done.23.refs_3_ = f32[2,96,768]{2,1,0:T(8,128)S(1)} collective-permute-done((f32[2,96,768]{2,1,0:T(8,128)S(1)}, f32[2,96,768]{2,1,0:T(8,128)S(1)}, u32[]{:S(2)}, u32[]{:S(2)}) %collective-permute-start.23) | collective-permute-done | bytes 589856 | tf_op jit(solution)/shard_map/ppermute | solution.py:978
  280.1 2.7 collective-permute-done.24.refs_4_
  283.6 2.5 attn_mine.5
  286.1 1.5 collective-permute-start.27
  287.5 1.5 collective-permute-start.32
  289.0 9.6 %collective-permute-done.29.refs_2_.refs_4_ = f32[5,96,384]{2,1,0:T(8,128)S(1)} collective-permute-done((f32[5,96,384]{2,1,0:T(8,128)S(1)}, f32[5,96,384]{2,1,0:T(8,128)S(1)}, u32[]{:S(2)}, u32[]{:S(2)}) %collective-permute-start.29) | collective-permute-done | bytes 737312 | tf_op jit(solution)/shard_map/ppermute | solution.py:978
  299.7 10.7 %collective-permute-done.27.refs_2_.refs_4_ = f32[4,96,384]{2,1,0:T(8,128)S(1)} collective-permute-done((f32[4,96,384]{2,1,0:T(8,128)S(1)}, f32[4,96,384]{2,1,0:T(8,128)S(1)}, u32[]{:S(2)}, u32[]{:S(2)}) %collective-permute-start.27) | collective-permute-done | bytes 589856 | tf_op jit(solution)/shard_map/ppermute | solution.py:978
  310.6 1.8 collective-permute-start.35
  312.5 3.0 collective-permute-done.32.refs_6_.refs_1_
  315.5 11.9 %collective-permute-done.31.refs_2_.refs_4_ = f32[3,96,384]{2,1,0:T(8,128)S(1)} collective-permute-done((f32[3,96,384]{2,1,0:T(8,128)S(1)}, f32[3,96,384]{2,1,0:T(8,128)S(1)}, u32[]{:S(2)}, u32[]{:S(2)}) %collective-permute-start.31) | collective-permute-done | bytes 442400 | tf_op jit(solution)/shard_map/ppermute | solution.py:978
  328.2 4.0 %collective-permute-done.30.refs_2_.refs_4_ = f32[2,96,384]{2,1,0:T(8,128)S(1)} collective-permute-done((f32[2,96,384]{2,1,0:T(8,128)S(1)}, f32[2,96,384]{2,1,0:T(8,128)S(1)}, u32[]{:S(2)}, u32[]{:S(2)}) %collective-permute-start.30) | collective-permute-done | bytes 294944 | tf_op jit(solution)/shard_map/ppermute | solution.py:978
  337.0 9.5 %collective-permute-done.34.refs_7_ = f32[1,96,384]{2,1,0:T(8,128)S(1)} collective-permute-done((f32[1,96,384]{2,1,0:T(8,128)}, f32[1,96,384]{2,1,0:T(8,128)S(1)}, u32[]{:S(2)}, u32[]{:S(2)}) %collective-permute-start.34) | collective-permute-done | bytes 147488 | tf_op jit(solution)/shard_map/ppermute | solution.py:978
  348.1 1.3 copy-done.32
  349.4 2.3 last_sums.1
  (201 shorter events, 30.0 us)
Async XLA Ops:
  3.2 9.0 %collective-permute-start.2 = (f32[6,196,128]{2,1,0:T(8,128)}, f32[6,196,128]{2,1,0:T(8,128)}, u32[]{:S(2)}, u32[]{:S(2)}) collective-permute-start(f32[6,196,128]{2,1,0:T(8,128)} %get-tuple-element.124), channel_id=1, source_target_pairs={{0,1},{1,0},{2,3},{3,2},{4,5},{5,4},{6,7},{7,6},{8,9},{9,8},{10,11... | collective-permute-start | bytes 1806344 | tf_op jit(solution)/shard_map/ppermute | solution.py:1080
  3.6 30.6 %collective-permute-start.1 = (f32[6,196,128]{2,1,0:T(8,128)}, f32[6,196,128]{2,1,0:T(8,128)S(1)}, u32[]{:S(2)}, u32[]{:S(2)}) collective-permute-start(f32[6,196,128]{2,1,0:T(8,128)} %get-tuple-element.124), channel_id=1, source_target_pairs={{0,3},{1,2},{2,1},{3,0},{4,7},{5,6},{6,5},{7,4},{8,11},{9,10},{10,... | collective-permute-start | bytes 1806344 | tf_op jit(solution)/shard_map/ppermute | solution.py:1080
  6.2 28.0 %collective-permute-start = (f32[6,196,128]{2,1,0:T(8,128)}, f32[6,196,128]{2,1,0:T(8,128)S(1)}, u32[]{:S(2)}, u32[]{:S(2)}) collective-permute-start(f32[6,196,128]{2,1,0:T(8,128)} %get-tuple-element.123.refs_3_.refs_1_), channel_id=1, source_target_pairs={{0,2},{1,3},{2,0},{3,1},{4,6},{5,7},{6,4},{7,5},{8,10},{9,11},{10,... | collective-permute-start | bytes 1806344 | tf_op jit(solution)/shard_map/ppermute | solution.py:1080
  8.2 84.0 %collective-permute-start.3 = (f32[6,196,128]{2,1,0:T(8,128)}, f32[6,196,128]{2,1,0:T(8,128)S(1)}, u32[]{:S(2)}, u32[]{:S(2)}) collective-permute-start(f32[6,196,128]{2,1,0:T(8,128)} %get-tuple-element.139), channel_id=1, source_target_pairs={{0,1},{1,0},{2,3},{3,2},{4,5},{5,4},{6,7},{7,6},{8,9},{9,8},{10,11... | collective-permute-start | bytes 1806344 | tf_op jit(solution)/shard_map/ppermute | solution.py:1080
  8.3 83.9 %collective-permute-start.5 = (f32[6,196,128]{2,1,0:T(8,128)}, f32[6,196,128]{2,1,0:T(8,128)S(1)}, u32[]{:S(2)}, u32[]{:S(2)}) collective-permute-start(f32[6,196,128]{2,1,0:T(8,128)} %get-tuple-element.139), channel_id=1, source_target_pairs={{0,3},{1,2},{2,1},{3,0},{4,7},{5,6},{6,5},{7,4},{8,11},{9,10},{10,... | collective-permute-start | bytes 1806344 | tf_op jit(solution)/shard_map/ppermute | solution.py:1080
  12.2 107.3 %copy-start.12 = (f32[12,56,256]{2,1,0:T(8,128)}, f32[12,56,256]{2,1,0:T(8,128)S(1)}, u32[]{:S(2)}) copy-start(f32[12,56,256]{2,1,0:T(8,128)S(1)} %window_bias.1.refs_3_.refs_2_.refs_7_) | copy-start | bytes 2064388
  12.2 80.0 %collective-permute-start.4 = (f32[6,196,128]{2,1,0:T(8,128)S(1)}, f32[6,196,128]{2,1,0:T(8,128)S(1)}, u32[]{:S(2)}, u32[]{:S(2)}) collective-permute-start(f32[6,196,128]{2,1,0:T(8,128)S(1)} %get-tuple-element.125.refs_17_.refs_2_), channel_id=1, source_target_pairs={{0,2},{1,3},{2,0},{3,1},{4,6},{5,7},{6,4},{7,5},{8,10},{9,11},{10,... | collective-permute-start | bytes 1806344 | tf_op jit(solution)/shard_map/ppermute | solution.py:1080
  55.6 36.5 %copy-start.6 = (bf16[2,392,768]{2,1,0:T(8,128)(2,1)}, bf16[2,392,768]{2,1,0:T(8,128)(2,1)S(1)}, u32[]{:S(2)}) copy-start(bf16[2,392,768]{2,1,0:T(8,128)(2,1)S(1)} %get-tuple-element.187.refs_5_.refs_1_) | copy-start | bytes 3612676
  55.6 36.5 %copy-start.8 = (bf16[2,392,768]{2,1,0:T(8,128)(2,1)}, bf16[2,392,768]{2,1,0:T(8,128)(2,1)S(1)}, u32[]{:S(2)}) copy-start(bf16[2,392,768]{2,1,0:T(8,128)(2,1)S(1)} %get-tuple-element.188.refs_6_.refs_2_) | copy-start | bytes 3612676
  92.1 25.3 %copy-start.39 = (bf16[2,392,768]{2,1,0:T(8,128)(2,1)}, bf16[2,392,768]{2,1,0:T(8,128)(2,1)S(1)}, u32[]{:S(2)}) copy-start(bf16[2,392,768]{2,1,0:T(8,128)(2,1)S(1)} %get-tuple-element.143.refs_9_.refs_1_) | copy-start | bytes 3612676
  92.1 27.3 %copy-start.53 = (bf16[2,392,768]{2,1,0:T(8,128)(2,1)}, bf16[2,392,768]{2,1,0:T(8,128)(2,1)S(1)}, u32[]{:S(2)}) copy-start(bf16[2,392,768]{2,1,0:T(8,128)(2,1)S(1)} %get-tuple-element.137.refs_5_.refs_1_) | copy-start | bytes 3612676
  92.1 27.3 %copy-start.55 = (bf16[2,392,768]{2,1,0:T(8,128)(2,1)}, bf16[2,392,768]{2,1,0:T(8,128)(2,1)S(1)}, u32[]{:S(2)}) copy-start(bf16[2,392,768]{2,1,0:T(8,128)(2,1)S(1)} %get-tuple-element.138.refs_6_.refs_2_) | copy-start | bytes 3612676
  92.2 27.3 %copy-start.4 = (bf16[2,768,768]{2,1,0:T(8,128)(2,1)S(1)}, bf16[2,768,768]{2,1,0:T(8,128)(2,1)}, u32[]{:S(2)}) copy-start(bf16[2,768,768]{2,1,0:T(8,128)(2,1)} %refs_13_.7) | copy-start | bytes 7077892
  118.9 32.0 %collective-permute-start.8 = (f32[8,96,768]{2,1,0:T(8,128)}, f32[8,96,768]{2,1,0:T(8,128)S(1)}, u32[]{:S(2)}, u32[]{:S(2)}) collective-permute-start(f32[8,96,768]{2,1,0:T(8,128)} %get-tuple-element.147.refs_11_), channel_id=1, source_target_pairs={{0,1},{1,0},{2,3},{3,2},{4,5},{5,4},{6,7},{7,6},{8,9},{9,8},{10,11... | collective-permute-start | bytes 7077896 | tf_op jit(solution)/shard_map/ppermute | solution.py:1080
  118.9 40.0 %collective-permute-start.10 = (f32[8,96,768]{2,1,0:T(8,128)}, f32[8,96,768]{2,1,0:T(8,128)}, u32[]{:S(2)}, u32[]{:S(2)}) collective-permute-start(f32[8,96,768]{2,1,0:T(8,128)} %get-tuple-element.156), channel_id=1, source_target_pairs={{0,1},{1,0},{2,3},{3,2},{4,5},{5,4},{6,7},{7,6},{8,9},{9,8},{10,11... | collective-permute-start | bytes 7077896 | tf_op jit(solution)/shard_map/ppermute | solution.py:1080
  150.3 16.6 %collective-permute-start.6 = (f32[8,96,384]{2,1,0:T(8,128)}, f32[8,96,384]{2,1,0:T(8,128)S(1)}, u32[]{:S(2)}, u32[]{:S(2)}) collective-permute-start(f32[8,96,384]{2,1,0:T(8,128)} %get-tuple-element.149), channel_id=1, source_target_pairs={{0,1},{1,0},{2,3},{3,2},{4,5},{5,4},{6,7},{7,6},{8,9},{9,8},{10,11... | collective-permute-start | bytes 3538952 | tf_op jit(solution)/shard_map/ppermute | solution.py:1080
  150.3 16.6 %collective-permute-start.7 = (f32[8,96,384]{2,1,0:T(8,128)}, f32[8,96,384]{2,1,0:T(8,128)}, u32[]{:S(2)}, u32[]{:S(2)}) collective-permute-start(f32[8,96,384]{2,1,0:T(8,128)} %get-tuple-element.150), channel_id=1, source_target_pairs={{0,1},{1,0},{2,3},{3,2},{4,5},{5,4},{6,7},{7,6},{8,9},{9,8},{10,11... | collective-permute-start | bytes 3538952 | tf_op jit(solution)/shard_map/ppermute | solution.py:1080
  163.0 28.4 %collective-permute-start.11 = (f32[4,96,768]{2,1,0:T(8,128)S(1)}, f32[4,96,768]{2,1,0:T(8,128)S(1)}, u32[]{:S(2)}, u32[]{:S(2)}) collective-permute-start(f32[4,96,768]{2,1,0:T(8,128)S(1)} %get-tuple-element.158), channel_id=1, source_target_pairs={{0,8},{4,12},{8,0},{12,4},{16,24},{20,28},{24,16},{28,20},{1,9},{5... | collective-permute-start | bytes 3538952 | tf_op jit(solution)/shard_map/ppermute | solution.py:978
  165.3 27.6 %collective-permute-start.9 = (f32[4,96,768]{2,1,0:T(8,128)S(1)}, f32[4,96,768]{2,1,0:T(8,128)S(1)}, u32[]{:S(2)}, u32[]{:S(2)}) collective-permute-start(f32[4,96,768]{2,1,0:T(8,128)S(1)} %get-tuple-element.154), channel_id=1, source_target_pairs={{0,4},{4,0},{8,12},{12,8},{16,20},{20,16},{24,28},{28,24},{1,5},{5... | collective-permute-start | bytes 3538952 | tf_op jit(solution)/shard_map/ppermute | solution.py:978
  193.8 20.5 %collective-permute-start.13 = (f32[8,96,768]{2,1,0:T(8,128)}, f32[8,96,768]{2,1,0:T(8,128)S(1)}, u32[]{:S(2)}, u32[]{:S(2)}) collective-permute-start(f32[8,96,768]{2,1,0:T(8,128)} %get-tuple-element.172), channel_id=1, source_target_pairs={{0,1},{1,0},{2,3},{3,2},{4,5},{5,4},{6,7},{7,6},{8,9},{9,8},{10,11... | collective-permute-start | bytes 7077896 | tf_op jit(solution)/shard_map/ppermute | solution.py:1080
  193.9 24.3 %collective-permute-start.17 = (f32[8,96,768]{2,1,0:T(8,128)}, f32[8,96,768]{2,1,0:T(8,128)S(1)}, u32[]{:S(2)}, u32[]{:S(2)}) collective-permute-start(f32[8,96,768]{2,1,0:T(8,128)} %get-tuple-element.180), channel_id=1, source_target_pairs={{0,1},{1,0},{2,3},{3,2},{4,5},{5,4},{6,7},{7,6},{8,9},{9,8},{10,11... | collective-permute-start | bytes 7077896 | tf_op jit(solution)/shard_map/ppermute | solution.py:1080
  194.4 16.2 %collective-permute-start.14 = (f32[2,96,768]{2,1,0:T(8,128)S(1)}, f32[2,96,768]{2,1,0:T(8,128)S(1)}, u32[]{:S(2)}, u32[]{:S(2)}) collective-permute-start(f32[2,96,768]{2,1,0:T(8,128)S(1)} %get-tuple-element.174), channel_id=1, source_target_pairs={{0,4},{4,0},{8,12},{12,8},{16,20},{20,16},{24,28},{28,24},{1,5},{5... | collective-permute-start | bytes 1769480 | tf_op jit(solution)/shard_map/ppermute | solution.py:978
  195.9 15.0 %collective-permute-start.15 = (f32[2,96,768]{2,1,0:T(8,128)S(1)}, f32[2,96,768]{2,1,0:T(8,128)S(1)}, u32[]{:S(2)}, u32[]{:S(2)}) collective-permute-start(f32[2,96,768]{2,1,0:T(8,128)S(1)} %get-tuple-element.175), channel_id=1, source_target_pairs={{0,8},{4,12},{8,0},{12,4},{16,24},{20,28},{24,16},{28,20},{1,9},{5... | collective-permute-start | bytes 1769480 | tf_op jit(solution)/shard_map/ppermute | solution.py:978
  196.5 17.8 %slice-start = ((s8[4816896]{0:T(1024)(128)(4,1)}), s8[4194304]{0:T(1024)(128)(4,1)S(1)}, s32[]{:S(2)}) async-start(s8[4816896]{0:T(1024)(128)(4,1)} %bitcast.30), calls=%async_computation | async-start | bytes 8388608
  196.5 17.8 %slice-start.1 = ((s8[4816896]{0:T(1024)(128)(4,1)}), s8[622592]{0:T(1024)(128)(4,1)S(1)}, s32[]{:S(2)}) async-start(s8[4816896]{0:T(1024)(128)(4,1)} %bitcast.30), calls=%async_computation.1 | async-start | bytes 1245184
  202.5 48.7 %collective-permute-start.19 = (f32[4,96,768]{2,1,0:T(8,128)}, f32[4,96,768]{2,1,0:T(8,128)S(1)}, u32[]{:S(2)}, u32[]{:S(2)}) collective-permute-start(f32[4,96,768]{2,1,0:T(8,128)} %get-tuple-element.183), channel_id=1, source_target_pairs={{0,4},{4,0},{8,12},{12,8},{16,20},{20,16},{24,28},{28,24},{1,5},{5... | collective-permute-start | bytes 3538952 | tf_op jit(solution)/shard_map/ppermute | solution.py:978
  203.3 14.9 %copy-start.43 = (f32[6,196,128]{2,1,0:T(8,128)}, f32[6,196,128]{2,1,0:T(8,128)S(1)}, u32[]{:S(2)}) copy-start(f32[6,196,128]{2,1,0:T(8,128)S(1)} %get-tuple-element.169.refs_5_.refs_2_) | copy-start | bytes 1806340
  211.6 39.6 %collective-permute-start.20 = (f32[2,96,768]{2,1,0:T(8,128)S(1)}, f32[2,96,768]{2,1,0:T(8,128)S(1)}, u32[]{:S(2)}, u32[]{:S(2)}) collective-permute-start(f32[2,96,768]{2,1,0:T(8,128)S(1)} %get-tuple-element.195), channel_id=1, source_target_pairs={{0,16},{4,20},{8,24},{12,28},{16,0},{20,4},{24,8},{28,12},{1,17},{... | collective-permute-start | bytes 1769480 | tf_op jit(solution)/shard_map/ppermute | solution.py:978
  222.1 38.1 %collective-permute-start.18 = (f32[4,96,768]{2,1,0:T(8,128)}, f32[4,96,768]{2,1,0:T(8,128)S(1)}, u32[]{:S(2)}, u32[]{:S(2)}) collective-permute-start(f32[4,96,768]{2,1,0:T(8,128)} %get-tuple-element.182), channel_id=1, source_target_pairs={{0,4},{4,0},{8,12},{12,8},{16,20},{20,16},{24,28},{28,24},{1,5},{5... | collective-permute-start | bytes 3538952 | tf_op jit(solution)/shard_map/ppermute | solution.py:978
  223.2 38.2 %collective-permute-start.16 = (f32[4,96,768]{2,1,0:T(8,128)S(1)}, f32[4,96,768]{2,1,0:T(8,128)S(1)}, u32[]{:S(2)}, u32[]{:S(2)}) collective-permute-start(f32[4,96,768]{2,1,0:T(8,128)S(1)} %get-tuple-element.178), channel_id=1, source_target_pairs={{0,8},{4,12},{8,0},{12,4},{16,24},{20,28},{24,16},{28,20},{1,9},{5... | collective-permute-start | bytes 3538952 | tf_op jit(solution)/shard_map/ppermute | solution.py:978
  262.9 7.9 %collective-permute-start.25 = (f32[8,96,384]{2,1,0:T(8,128)S(1)}, f32[8,96,384]{2,1,0:T(8,128)S(1)}, u32[]{:S(2)}, u32[]{:S(2)}) collective-permute-start(f32[8,96,384]{2,1,0:T(8,128)S(1)} %get-tuple-element.205), channel_id=1, source_target_pairs={{0,1},{1,0},{2,3},{3,2},{4,5},{5,4},{6,7},{7,6},{8,9},{9,8},{10,11... | collective-permute-start | bytes 3538952 | tf_op jit(solution)/shard_map/ppermute | solution.py:1080
  262.9 3.7 %collective-permute-start.12 = (f32[6,196,128]{2,1,0:T(8,128)S(1)}, f32[6,196,128]{2,1,0:T(8,128)S(1)}, u32[]{:S(2)}, u32[]{:S(2)}) collective-permute-start(f32[6,196,128]{2,1,0:T(8,128)S(1)} %get-tuple-element.170), channel_id=1, source_target_pairs={{0,1},{1,0},{2,3},{3,2},{4,5},{5,4},{6,7},{7,6},{8,9},{9,8},{10,11... | collective-permute-start | bytes 1806344 | tf_op jit(solution)/shard_map/ppermute | solution.py:1080
  263.4 20.1 %collective-permute-start.22 = (f32[8,96,384]{2,1,0:T(8,128)S(1)}, f32[8,96,384]{2,1,0:T(8,128)S(1)}, u32[]{:S(2)}, u32[]{:S(2)}) collective-permute-start(f32[8,96,384]{2,1,0:T(8,128)S(1)} %get-tuple-element.201), channel_id=1, source_target_pairs={{0,1},{1,0},{2,3},{3,2},{4,5},{5,4},{6,7},{7,6},{8,9},{9,8},{10,11... | collective-permute-start | bytes 3538952 | tf_op jit(solution)/shard_map/ppermute | solution.py:1080
  263.5 7.3 %collective-permute-start.26 = (f32[96,384]{1,0:T(8,128)S(1)}, f32[96,384]{1,0:T(8,128)S(1)}, u32[]{:S(2)}, u32[]{:S(2)}) collective-permute-start(f32[96,384]{1,0:T(8,128)S(1)} %get-tuple-element.206.refs_5_), channel_id=1, source_target_pairs={{0,1},{1,0},{2,3},{3,2},{4,5},{5,4},{6,7},{7,6},{8,9},{9,8},{10,11... | collective-permute-start | bytes 442376 | tf_op jit(solution)/shard_map/ppermute | solution.py:1080
  263.9 16.2 %collective-permute-start.23 = (f32[2,96,768]{2,1,0:T(8,128)S(1)}, f32[2,96,768]{2,1,0:T(8,128)S(1)}, u32[]{:S(2)}, u32[]{:S(2)}) collective-permute-start(f32[2,96,768]{2,1,0:T(8,128)S(1)} %get-tuple-element.203), channel_id=1, source_target_pairs={{0,8},{4,12},{8,0},{12,4},{16,24},{20,28},{24,16},{28,20},{1,9},{5... | collective-permute-start | bytes 1769480 | tf_op jit(solution)/shard_map/ppermute | solution.py:978
  266.7 16.2 %collective-permute-start.24 = (f32[2,96,768]{2,1,0:T(8,128)S(1)}, f32[2,96,768]{2,1,0:T(8,128)S(1)}, u32[]{:S(2)}, u32[]{:S(2)}) collective-permute-start(f32[2,96,768]{2,1,0:T(8,128)S(1)} %get-tuple-element.204), channel_id=1, source_target_pairs={{0,4},{4,0},{8,12},{12,8},{16,20},{20,16},{24,28},{28,24},{1,5},{5... | collective-permute-start | bytes 1769480 | tf_op jit(solution)/shard_map/ppermute | solution.py:978
  273.9 24.7 %collective-permute-start.29 = (f32[5,96,384]{2,1,0:T(8,128)S(1)}, f32[5,96,384]{2,1,0:T(8,128)S(1)}, u32[]{:S(2)}, u32[]{:S(2)}) collective-permute-start(f32[5,96,384]{2,1,0:T(8,128)S(1)} %get-tuple-element.213), channel_id=1, source_target_pairs={{0,4},{4,0},{8,12},{12,8},{16,20},{20,16},{24,28},{28,24},{1,5},{5... | collective-permute-start | bytes 2211848 | tf_op jit(solution)/shard_map/ppermute | solution.py:978
  274.6 24.3 %collective-permute-start.28 = (f32[2,96,768]{2,1,0:T(8,128)S(1)}, f32[2,96,768]{2,1,0:T(8,128)S(1)}, u32[]{:S(2)}, u32[]{:S(2)}) collective-permute-start(f32[2,96,768]{2,1,0:T(8,128)S(1)} %get-tuple-element.212), channel_id=1, source_target_pairs={{0,8},{4,12},{8,0},{12,4},{16,24},{20,28},{24,16},{28,20},{1,9},{5... | collective-permute-start | bytes 1769480 | tf_op jit(solution)/shard_map/ppermute | solution.py:978
  286.1 24.4 %collective-permute-start.27 = (f32[4,96,384]{2,1,0:T(8,128)S(1)}, f32[4,96,384]{2,1,0:T(8,128)S(1)}, u32[]{:S(2)}, u32[]{:S(2)}) collective-permute-start(f32[4,96,384]{2,1,0:T(8,128)S(1)} %get-tuple-element.210), channel_id=1, source_target_pairs={{0,4},{4,0},{8,12},{12,8},{16,20},{20,16},{24,28},{28,24},{1,5},{5... | collective-permute-start | bytes 1769480 | tf_op jit(solution)/shard_map/ppermute | solution.py:978
  287.5 27.9 %collective-permute-start.32 = (f32[2,96,768]{2,1,0:T(8,128)S(1)}, f32[2,96,768]{2,1,0:T(8,128)S(1)}, u32[]{:S(2)}, u32[]{:S(2)}) collective-permute-start(f32[2,96,768]{2,1,0:T(8,128)S(1)} %get-tuple-element.219), channel_id=1, source_target_pairs={{0,16},{4,20},{8,24},{12,28},{16,0},{20,4},{24,8},{28,12},{1,17},{... | collective-permute-start | bytes 1769480 | tf_op jit(solution)/shard_map/ppermute | solution.py:978
  298.8 28.6 %collective-permute-start.31 = (f32[3,96,384]{2,1,0:T(8,128)S(1)}, f32[3,96,384]{2,1,0:T(8,128)S(1)}, u32[]{:S(2)}, u32[]{:S(2)}) collective-permute-start(f32[3,96,384]{2,1,0:T(8,128)S(1)} %get-tuple-element.218), channel_id=1, source_target_pairs={{0,8},{4,12},{8,0},{12,4},{16,24},{20,28},{24,16},{28,20},{1,9},{5... | collective-permute-start | bytes 1327112 | tf_op jit(solution)/shard_map/ppermute | solution.py:978
  298.9 35.0 %collective-permute-start.21 = (f32[6,196,128]{2,1,0:T(8,128)S(1)}, f32[6,196,128]{2,1,0:T(8,128)S(1)}, u32[]{:S(2)}, u32[]{:S(2)}) collective-permute-start(f32[6,196,128]{2,1,0:T(8,128)S(1)} %get-tuple-element.199), channel_id=1, source_target_pairs={{0,1},{1,0},{2,3},{3,2},{4,5},{5,4},{6,7},{7,6},{8,9},{9,8},{10,11... | collective-permute-start | bytes 1806344 | tf_op jit(solution)/shard_map/ppermute | solution.py:1080
  299.7 28.4 %copy-start.48 = (f32[1,96,768]{2,1,0:T(8,128)}, f32[1,96,768]{2,1,0:T(8,128)S(1)}, u32[]{:S(2)}) copy-start(f32[1,96,768]{2,1,0:T(8,128)S(1)} %get-tuple-element.215.refs_5_.refs_8_) | copy-start | bytes 884740
  310.6 21.6 %collective-permute-start.30 = (f32[2,96,384]{2,1,0:T(8,128)S(1)}, f32[2,96,384]{2,1,0:T(8,128)S(1)}, u32[]{:S(2)}, u32[]{:S(2)}) collective-permute-start(f32[2,96,384]{2,1,0:T(8,128)S(1)} %get-tuple-element.217), channel_id=1, source_target_pairs={{0,8},{4,12},{8,0},{12,4},{16,24},{20,28},{24,16},{28,20},{1,9},{5... | collective-permute-start | bytes 884744 | tf_op jit(solution)/shard_map/ppermute | solution.py:978
  310.6 26.4 %collective-permute-start.35 = (f32[1,96,768]{2,1,0:T(8,128)}, f32[1,96,768]{2,1,0:T(8,128)S(1)}, u32[]{:S(2)}, u32[]{:S(2)}) collective-permute-start(f32[1,96,768]{2,1,0:T(8,128)} %get-tuple-element.224), channel_id=1, source_target_pairs={{0,16},{4,20},{8,24},{12,28},{16,0},{20,4},{24,8},{28,12},{1,17},{... | collective-permute-start | bytes 884744 | tf_op jit(solution)/shard_map/ppermute | solution.py:978
  328.1 19.0 %collective-permute-start.33 = (f32[2,96,384]{2,1,0:T(8,128)}, f32[2,96,384]{2,1,0:T(8,128)}, u32[]{:S(2)}, u32[]{:S(2)}) collective-permute-start(f32[2,96,384]{2,1,0:T(8,128)} %get-tuple-element.222), channel_id=1, source_target_pairs={{0,16},{4,20},{8,24},{12,28},{16,0},{20,4},{24,8},{28,12},{1,17},{... | collective-permute-start | bytes 884744 | tf_op jit(solution)/shard_map/ppermute | solution.py:978
  333.5 13.0 %collective-permute-start.34 = (f32[1,96,384]{2,1,0:T(8,128)}, f32[1,96,384]{2,1,0:T(8,128)S(1)}, u32[]{:S(2)}, u32[]{:S(2)}) collective-permute-start(f32[1,96,384]{2,1,0:T(8,128)} %get-tuple-element.223), channel_id=1, source_target_pairs={{0,16},{4,20},{8,24},{12,28},{16,0},{20,4},{24,8},{28,12},{1,17},{... | collective-permute-start | bytes 442376 | tf_op jit(solution)/shard_map/ppermute | solution.py:978
  333.8 13.4 %copy-start.38 = (f32[2,96,768]{2,1,0:T(8,128)S(1)}, f32[2,96,768]{2,1,0:T(8,128)}, u32[]{:S(2)}) copy-start(f32[2,96,768]{2,1,0:T(8,128)} %copy-done.37) | copy-start | bytes 1769476
  (52 other events, 171.4 us)

commit v6 on v5

--- a/solution.py
+++ b/solution.py
@@ -118,8 +118,17 @@
     return jnp.sum(values, axis=0, keepdims=True)
 
 
-def rows_of(w, n=T, stride=C):
-    return pl.ds(w, n, stride=stride)
+def rows_of(w, n, stride=C):
+    return pl.ds(w, n, stride=stride) if n > 1 else pl.ds(w, 1)
+
+
+WHOLE = T // 8 * 8
+
+
+def move_rows(dest, g, to, to_stride, src, first, stride, scale=None):
+    for start, n in ((0, WHOLE), (WHOLE, T - WHOLE)):
+        v = src[g, rows_of(first + stride * start, n, stride), :]
+        dest[g, rows_of(to + to_stride * start, n, to_stride), :] = v if scale is None else v * scale
 
 
 def lanes_at(n, width):
@@ -193,7 +202,7 @@
                 crop = HALF * c + k
                 keep = jnp.where(crop < n[0], 1.0, 0.0).astype(F32)
                 for g in range(NG):
-                    out[g, rows_of(k, stride=HALF), :] = s[g, rows_of(crop), :] * keep
+                    move_rows(out, g, k, HALF, s, crop, C, keep)
 
     return call(
         body, (core, count, crops), [SM, SM, VM], [shape((NG, PIECE, LANE), F32)] * 2, [VM] * 2, cost(2.5), "crop_rows", after, scratch=[pltpu.VMEM((NG, ROWS, LANE), F32)],
@@ -204,7 +213,7 @@
     for b, piece in enumerate(pieces):
         for k in range(HALF):
             for g in range(NG):
-                dest[g, rows_of(HALF * b + k), :] = piece[g, rows_of(k, stride=HALF), :]
+                move_rows(dest, g, HALF * b + k, C, piece, k, HALF)
 
 
 def own_quadrants(x_at, both_halves, rolled, after=()):
@@ -218,7 +227,7 @@
         for b, out in enumerate((mine, other)):
             for k in range(HALF):
                 for g in range(NG):
-                    out[g, rows_of(k, stride=HALF), :] = s[g, rows_of(HALF * b + k), :]
+                    move_rows(out, g, k, HALF, s, HALF * b + k, C)
 
     return call(
         body, (x_at, both_halves), [SM, VM], [shape((NG, PIECE, LANE), F32)] * 2, [VM] * 2, cost(3), "own_quadrants", after, scratch=[pltpu.VMEM((ROWS, D), F32), pltpu.VMEM((NG, ROWS, LANE), F32)],
@@ -232,7 +241,7 @@
                 crop = HALF * c + k
                 keep = jnp.where(crop < n[0], 1.0, 0.0).astype(F32)
                 for g in range(NG):
-                    s[g, rows_of(crop), :] = src[g, rows_of(k, stride=HALF), :] * keep
+                    move_rows(s, g, crop, C, src, k, HALF, keep)
         for g in range(NG):
             out[:, :, LANE * g : LANE * (g + 1)] = s[g].reshape(T, C, LANE).astype(BF16)
 
@@ -246,7 +255,9 @@
         for k in range(HALF):
             for src, c in ((a, at[0]), (b, 1 - at[0])):
                 for g in range(NG):
-                    out[pl.ds((HALF * c + k) * (T * NG) + g, T, stride=NG), :] = src[g, rows_of(k, stride=HALF), :]
+                    for start, n in ((0, WHOLE), (WHOLE, T - WHOLE)):
+                        to = (HALF * c + k) * (T * NG) + g + NG * start
+                        out[rows_of(to, n, NG), :] = src[g, rows_of(k + HALF * start, n, HALF), :]
 
     return call(
         body, (core, mine, theirs), [SM, VM, VM], shape((C * T * NG, LANE), F32), VM, cost(2.5), "crop_major", after,

time: 358 us -> 358 us (level)
  no operation moved by 1% of the time
where the time goes in v6:
time: 358 us; the launch traced here: 354 us
  Pallas kernels  222 us (62%)
  waiting for transfers between devices  81.5 us (23%)
  starting transfers between devices  25.7 us (7%)
  local copies, waits for them, and re-layouts  22.3 us (6%)
    pallas_call x31, Pallas kernels, call(): pl.pallas_call(wrapped, grid_spec=pltpu.PrefetchScalarGridSpec(num_scalar...  222 us
    ppermute x19, waiting for transfers between devices, send(): self.kept, self.recv = (kept, lax.ppermute(out, axis, perm))  76.6 us
    unnamed x131, local copies, waits for them, and re-layouts  21 us
    ppermute x19, starting transfers between devices, send(): self.kept, self.recv = (kept, lax.ppermute(out, axis, perm))  17.7 us
    ppermute x17, starting transfers between devices, over(): return lax.ppermute(a, 'win', [(i, i ^ way) for i in range(4)])  8.03 us
  transfers between devices with their start and end apart: 36, of which 16 were waited for; matrix products, arithmetic and copies ran while one was open for 0% of the time, Pallas kernels for 54%

profile of v6, /device:TPU:0, one launch (start us, length us, event | category | flops | bytes accessed | tf_op | source)
XLA Modules:
  0.0 353.9 jit_solution(18075682877026048333)
XLA Ops:
  1.7 1.4 crop_rows.2
  3.6 2.6 collective-permute-start.1
  6.9 1.3 crop_rows.3
  8.3 2.0 collective-permute-start.5
  10.4 1.7 window_bias.1.refs_3_.refs_2_.refs_7_
  12.3 19.7 %forward_0.2 = (f32[2,392,768]{2,1,0:T(8,128)}, bf16[2,392,768]{2,1,0:T(8,128)(2,1)S(1)}, bf16[2,8,18,64,128]{4,3,2,1,0:T(8,128)(2,1)}, bf16[2,392,768]{2,1,0:T(...) custom-call(s32[1]{0:T(128)} %bitcast.1.refs_0_, ...), custom_call_target="tpu_custom_call" | custom-call | flops 9660000256 | tf_op jit(solution)/shard_map/forward_0/pallas_call | solution.py:178
  32.1 2.1 collective-permute-done.refs_1_
  34.2 1.3 copy-done.1
  35.5 19.0 %forward_0.3 = (f32[2,392,768]{2,1,0:T(8,128)}, bf16[2,392,768]{2,1,0:T(8,128)(2,1)S(1)}, bf16[2,8,18,64,128]{4,3,2,1,0:T(8,128)(2,1)}, bf16[2,392,768]{2,1,0:T(...) custom-call(s32[1]{0:T(128)} %bitcast.1.refs_0_, ...), custom_call_target="tpu_custom_call", output_to_operand_aliasing={{0}: (17, {}), {1}: (18, {}), {2}: (19, {}), {3}: (20, {}),... | custom-call | flops 9660000256 | tf_op jit(solution)/shard_map/forward_0/pallas_call | solution.py:178
  55.6 36.5 %forward_1.1 = (f32[2,392,768]{2,1,0:T(8,128)}, bf16[2,392,768]{2,1,0:T(8,128)(2,1)S(1)}, bf16[2,8,18,64,128]{4,3,2,1,0:T(8,128)(2,1)}, bf16[2,392,768]{2,1,0:T(...) custom-call(s32[1]{0:T(128)} %bitcast.refs_0_.refs_1_, ...), custom_call_target="tpu_custom_call" | custom-call | flops 16560000000 | tf_op jit(solution)/shard_map/forward_1/pallas_call | solution.py:178
  92.2 25.2 %mlp_back_1.1 = (bf16[2,2,392,192]{3,2,1,0:T(8,128)(2,1)S(1)}, bf16[2,392,1536]{2,1,0:T(8,128)(2,1)}, f32[2,392,768]{2,1,0:T(8,128)}, f32[8,768]{1,0:T(8,128)S(1...) custom-call(s32[1]{0:T(128)} %bitcast.1.refs_0_, s32[1]{0:T(128)} %bitcast.refs_0_.refs_1_, ...), custom_call_target="tpu_custom_call" | custom-call | flops 10119999488 | tf_op jit(solution)/shard_map/mlp_back_1/pallas_call | solution.py:178
  119.4 1.7 copy-done.27
  121.1 28.0 %attn_back_1.1 = (bf16[2,2,392,768]{3,2,1,0:T(8,128)(2,1)}, f32[4,768]{1,0:T(4,128)S(1)}, f32[4,8,256]{2,1,0:T(8,128)S(1)}, f32[2,49,8,768]{3,2,1,0:T(8,128)}, f...) custom-call(s32[1]{0:T(128)} %bitcast.1.refs_0_, s32[1]{0:T(128)} %bitcast.refs_0_.refs_1_, ...), custom_call_target="tpu_custom_call" | custom-call | flops 14259999744 | tf_op jit(solution)/shard_map/attn_back_1/pallas_call | solution.py:178
  150.9 2.4 copy-done
  155.1 3.7 %down_mine.2 = (f32[4,96,768]{2,1,0:T(8,128)S(1)}, f32[4,96,768]{2,1,0:T(8,128)S(1)}) custom-call(s32[4]{0:T(128)S(1)} %pad_add_fusion.refs_0_, bf16[2,2,392,192]{3,2,1,0:T(8,128)(2,1)S(1)} %copy-done.11, bf16[2,392,3072]{2,1,0:T(8,128)(2,1)S(1)} %copy-done, bf16[2,392,3072]{2,1,0:T(8,128)(2,1)S(1)} %copy-done, ...), custom_call_target="tpu_custom_call" | custom-call | flops 3174000128 | tf_op jit(solution)/shard_map/down_mine/pallas_call | solution.py:178
  158.9 4.1 %up_mine.2 = (f32[4,96,768]{2,1,0:T(8,128)S(1)}, f32[4,96,768]{2,1,0:T(8,128)S(1)}) custom-call(s32[4]{0:T(128)S(1)} %pad_add_fusion.refs_0_, bf16[2,392,768]{2,1,0:T(8,128)(2,1)S(1)} %copy-done.40, bf16[2,392,1536]{2,1,0:T(8,128)(2,1)S(1)} %copy-done.36, f32[8,96,768]{2,1,0:T(8,128)} %collective-permute-done.10.refs_3_, ...), custom_call_target="tpu_custom_call" | custom-call | flops 2622000128 | tf_op jit(solution)/shard_map/up_mine/pallas_call | solution.py:178
  163.0 2.2 collective-permute-start.11
  165.3 1.5 collective-permute-start.9
  166.9 24.2 %mlp_back_0.1 = (bf16[2,2,392,192]{3,2,1,0:T(8,128)(2,1)S(1)}, bf16[2,392,1536]{2,1,0:T(8,128)(2,1)}, f32[2,392,768]{2,1,0:T(8,128)}, f32[8,768]{1,0:T(8,128)S(1...) custom-call(s32[1]{0:T(128)} %bitcast.1.refs_0_, s32[1]{0:T(128)} %bitcast.refs_0_.refs_1_, ...), custom_call_target="tpu_custom_call" | custom-call | flops 10119999488 | tf_op jit(solution)/shard_map/mlp_back_0/pallas_call | solution.py:178
  191.4 1.5 collective-permute-done.9.refs_2_.refs_4_
  194.3 1.5 collective-permute-start.14
  196.5 6.0 %attn_mine.3 = (f32[4,96,768]{2,1,0:T(8,128)S(1)}, f32[4,96,768]{2,1,0:T(8,128)}) custom-call(s32[4]{0:T(128)S(1)} %pad_add_fusion.refs_0_, bf16[2,392,768]{2,1,0:T(8,128)(2,1)S(1)} %copy-done.54, bf16[2,392,768]{2,1,0:T(8,128)(2,1)S(1)} %copy-done.56, bf16[2,2,392,768]{3,2,1,0:T(8,128)(2,1)S(1)} %copy-done.50, ...), custom_call_target="tpu_custom_call" | custom-call | flops 3265999872 | tf_op jit(solution)/shard_map/attn_mine/pallas_call | solution.py:178
  203.2 7.3 %collective-permute-done.14.refs_3_ = f32[2,96,768]{2,1,0:T(8,128)S(1)} collective-permute-done((f32[2,96,768]{2,1,0:T(8,128)S(1)}, f32[2,96,768]{2,1,0:T(8,128)S(1)}, u32[]{:S(2)}, u32[]{:S(2)}) %collective-permute-start.14) | collective-permute-done | bytes 589856 | tf_op jit(solution)/shard_map/ppermute | solution.py:989
  211.6 2.7 collective-permute-start.20
  214.3 3.8 %down_mine.3 = (f32[4,96,768]{2,1,0:T(8,128)S(1)}, f32[4,96,768]{2,1,0:T(8,128)S(1)}) custom-call(s32[4]{0:T(128)S(1)} %pad_add_fusion.refs_0_, bf16[2,2,392,192]{3,2,1,0:T(8,128)(2,1)S(1)} %get-tuple-element.171.refs_1_, bf16[2,392,3072]{2,1,0:T(8,128)(2,1)S(1)} %bitcast.31, bf16[2,392,3072]{2,1,0:T(8,128)(2,1)S(1)} %bitcast.31, ...), custom_call_target="tpu_custom_call" | custom-call | flops 3174000128 | tf_op jit(solution)/shard_map/down_mine/pallas_call | solution.py:178
  218.2 3.8 %up_mine.3 = (f32[4,96,768]{2,1,0:T(8,128)S(1)}, f32[4,96,768]{2,1,0:T(8,128)}) custom-call(s32[4]{0:T(128)S(1)} %pad_add_fusion.refs_0_, bf16[2,392,768]{2,1,0:T(8,128)(2,1)S(1)} %copy-done.3, bf16[2,392,1536]{2,1,0:T(8,128)(2,1)S(1)} %copy-done.26, f32[8,96,768]{2,1,0:T(8,128)S(1)} %collective-permute-done.17.refs_3_, ...), custom_call_target="tpu_custom_call" | custom-call | flops 2622000128 | tf_op jit(solution)/shard_map/up_mine/pallas_call | solution.py:178
  223.7 27.4 %attn_back_0.1 = (bf16[2,2,392,768]{3,2,1,0:T(8,128)(2,1)}, f32[4,768]{1,0:T(4,128)S(1)}, f32[96,384]{1,0:T(8,128)S(1)}, f32[2,49,8,768]{3,2,1,0:T(8,128)}, f32[...) custom-call(s32[1]{0:T(128)} %bitcast.1.refs_0_, s32[1]{0:T(128)} %bitcast.refs_0_.refs_1_, ...), custom_call_target="tpu_custom_call" | custom-call | flops 14259999744 | tf_op jit(solution)/shard_map/attn_back_0/pallas_call | solution.py:178
  251.2 9.0 %collective-permute-done.18.refs_6_.refs_8_ = f32[4,96,768]{2,1,0:T(8,128)S(1)} collective-permute-done((f32[4,96,768]{2,1,0:T(8,128)}, f32[4,96,768]{2,1,0:T(8,128)S(1)}, u32[]{:S(2)}, u32[]{:S(2)}) %collective-permute-start.18) | collective-permute-done | bytes 1179680 | tf_op jit(solution)/shard_map/ppermute | solution.py:989
  261.4 1.4 split_sum.8
  263.9 2.7 collective-permute-done.12.refs_3_
  266.6 1.4 collective-permute-start.24
  268.0 1.3 token_major.1.refs_2_
  270.8 1.5 copy-done.34
  272.3 1.6 attn_mine.4
  274.6 5.5 %collective-permute-done.23.refs_3_ = f32[2,96,768]{2,1,0:T(8,128)S(1)} collective-permute-done((f32[2,96,768]{2,1,0:T(8,128)S(1)}, f32[2,96,768]{2,1,0:T(8,128)S(1)}, u32[]{:S(2)}, u32[]{:S(2)}) %collective-permute-start.23) | collective-permute-done | bytes 589856 | tf_op jit(solution)/shard_map/ppermute | solution.py:989
  280.1 2.7 collective-permute-done.24.refs_4_
  283.6 2.5 attn_mine.5
  286.0 1.5 collective-permute-start.27
  287.5 1.5 collective-permute-start.32
  289.0 9.6 %collective-permute-done.29.refs_2_.refs_4_ = f32[5,96,384]{2,1,0:T(8,128)S(1)} collective-permute-done((f32[5,96,384]{2,1,0:T(8,128)S(1)}, f32[5,96,384]{2,1,0:T(8,128)S(1)}, u32[]{:S(2)}, u32[]{:S(2)}) %collective-permute-start.29) | collective-permute-done | bytes 737312 | tf_op jit(solution)/shard_map/ppermute | solution.py:989
  299.7 10.7 %collective-permute-done.27.refs_2_.refs_4_ = f32[4,96,384]{2,1,0:T(8,128)S(1)} collective-permute-done((f32[4,96,384]{2,1,0:T(8,128)S(1)}, f32[4,96,384]{2,1,0:T(8,128)S(1)}, u32[]{:S(2)}, u32[]{:S(2)}) %collective-permute-start.27) | collective-permute-done | bytes 589856 | tf_op jit(solution)/shard_map/ppermute | solution.py:989
  310.6 1.8 collective-permute-start.35
  312.5 3.0 collective-permute-done.32.refs_6_.refs_1_
  315.4 11.9 %collective-permute-done.31.refs_2_.refs_4_ = f32[3,96,384]{2,1,0:T(8,128)S(1)} collective-permute-done((f32[3,96,384]{2,1,0:T(8,128)S(1)}, f32[3,96,384]{2,1,0:T(8,128)S(1)}, u32[]{:S(2)}, u32[]{:S(2)}) %collective-permute-start.31) | collective-permute-done | bytes 442400 | tf_op jit(solution)/shard_map/ppermute | solution.py:989
  328.1 4.0 %collective-permute-done.30.refs_2_.refs_4_ = f32[2,96,384]{2,1,0:T(8,128)S(1)} collective-permute-done((f32[2,96,384]{2,1,0:T(8,128)S(1)}, f32[2,96,384]{2,1,0:T(8,128)S(1)}, u32[]{:S(2)}, u32[]{:S(2)}) %collective-permute-start.30) | collective-permute-done | bytes 294944 | tf_op jit(solution)/shard_map/ppermute | solution.py:989
  337.0 9.5 %collective-permute-done.34.refs_7_ = f32[1,96,384]{2,1,0:T(8,128)S(1)} collective-permute-done((f32[1,96,384]{2,1,0:T(8,128)}, f32[1,96,384]{2,1,0:T(8,128)S(1)}, u32[]{:S(2)}, u32[]{:S(2)}) %collective-permute-start.34) | collective-permute-done | bytes 147488 | tf_op jit(solution)/shard_map/ppermute | solution.py:989
  348.1 1.3 copy-done.32
  349.4 2.3 last_sums.1
  (201 shorter events, 30.0 us)
Async XLA Ops:
  3.2 9.0 %collective-permute-start.2 = (f32[6,196,128]{2,1,0:T(8,128)}, f32[6,196,128]{2,1,0:T(8,128)}, u32[]{:S(2)}, u32[]{:S(2)}) collective-permute-start(f32[6,196,128]{2,1,0:T(8,128)} %get-tuple-element.124), channel_id=1, source_target_pairs={{0,1},{1,0},{2,3},{3,2},{4,5},{5,4},{6,7},{7,6},{8,9},{9,8},{10,11... | collective-permute-start | bytes 1806344 | tf_op jit(solution)/shard_map/ppermute | solution.py:1091
  3.6 30.6 %collective-permute-start.1 = (f32[6,196,128]{2,1,0:T(8,128)}, f32[6,196,128]{2,1,0:T(8,128)S(1)}, u32[]{:S(2)}, u32[]{:S(2)}) collective-permute-start(f32[6,196,128]{2,1,0:T(8,128)} %get-tuple-element.124), channel_id=1, source_target_pairs={{0,3},{1,2},{2,1},{3,0},{4,7},{5,6},{6,5},{7,4},{8,11},{9,10},{10,... | collective-permute-start | bytes 1806344 | tf_op jit(solution)/shard_map/ppermute | solution.py:1091
  6.2 28.0 %collective-permute-start = (f32[6,196,128]{2,1,0:T(8,128)}, f32[6,196,128]{2,1,0:T(8,128)S(1)}, u32[]{:S(2)}, u32[]{:S(2)}) collective-permute-start(f32[6,196,128]{2,1,0:T(8,128)} %get-tuple-element.123.refs_3_.refs_1_), channel_id=1, source_target_pairs={{0,2},{1,3},{2,0},{3,1},{4,6},{5,7},{6,4},{7,5},{8,10},{9,11},{10,... | collective-permute-start | bytes 1806344 | tf_op jit(solution)/shard_map/ppermute | solution.py:1091
  8.1 84.0 %collective-permute-start.3 = (f32[6,196,128]{2,1,0:T(8,128)}, f32[6,196,128]{2,1,0:T(8,128)S(1)}, u32[]{:S(2)}, u32[]{:S(2)}) collective-permute-start(f32[6,196,128]{2,1,0:T(8,128)} %get-tuple-element.139), channel_id=1, source_target_pairs={{0,1},{1,0},{2,3},{3,2},{4,5},{5,4},{6,7},{7,6},{8,9},{9,8},{10,11... | collective-permute-start | bytes 1806344 | tf_op jit(solution)/shard_map/ppermute | solution.py:1091
  8.3 83.9 %collective-permute-start.5 = (f32[6,196,128]{2,1,0:T(8,128)}, f32[6,196,128]{2,1,0:T(8,128)S(1)}, u32[]{:S(2)}, u32[]{:S(2)}) collective-permute-start(f32[6,196,128]{2,1,0:T(8,128)} %get-tuple-element.139), channel_id=1, source_target_pairs={{0,3},{1,2},{2,1},{3,0},{4,7},{5,6},{6,5},{7,4},{8,11},{9,10},{10,... | collective-permute-start | bytes 1806344 | tf_op jit(solution)/shard_map/ppermute | solution.py:1091
  12.1 107.3 %copy-start.12 = (f32[12,56,256]{2,1,0:T(8,128)}, f32[12,56,256]{2,1,0:T(8,128)S(1)}, u32[]{:S(2)}) copy-start(f32[12,56,256]{2,1,0:T(8,128)S(1)} %window_bias.1.refs_3_.refs_2_.refs_7_) | copy-start | bytes 2064388
  12.2 80.0 %collective-permute-start.4 = (f32[6,196,128]{2,1,0:T(8,128)S(1)}, f32[6,196,128]{2,1,0:T(8,128)S(1)}, u32[]{:S(2)}, u32[]{:S(2)}) collective-permute-start(f32[6,196,128]{2,1,0:T(8,128)S(1)} %get-tuple-element.125.refs_17_.refs_2_), channel_id=1, source_target_pairs={{0,2},{1,3},{2,0},{3,1},{4,6},{5,7},{6,4},{7,5},{8,10},{9,11},{10,... | collective-permute-start | bytes 1806344 | tf_op jit(solution)/shard_map/ppermute | solution.py:1091
  55.6 36.5 %copy-start.6 = (bf16[2,392,768]{2,1,0:T(8,128)(2,1)}, bf16[2,392,768]{2,1,0:T(8,128)(2,1)S(1)}, u32[]{:S(2)}) copy-start(bf16[2,392,768]{2,1,0:T(8,128)(2,1)S(1)} %get-tuple-element.187.refs_5_.refs_1_) | copy-start | bytes 3612676
  55.6 36.5 %copy-start.8 = (bf16[2,392,768]{2,1,0:T(8,128)(2,1)}, bf16[2,392,768]{2,1,0:T(8,128)(2,1)S(1)}, u32[]{:S(2)}) copy-start(bf16[2,392,768]{2,1,0:T(8,128)(2,1)S(1)} %get-tuple-element.188.refs_6_.refs_2_) | copy-start | bytes 3612676
  92.1 25.3 %copy-start.39 = (bf16[2,392,768]{2,1,0:T(8,128)(2,1)}, bf16[2,392,768]{2,1,0:T(8,128)(2,1)S(1)}, u32[]{:S(2)}) copy-start(bf16[2,392,768]{2,1,0:T(8,128)(2,1)S(1)} %get-tuple-element.143.refs_9_.refs_1_) | copy-start | bytes 3612676
  92.1 27.3 %copy-start.53 = (bf16[2,392,768]{2,1,0:T(8,128)(2,1)}, bf16[2,392,768]{2,1,0:T(8,128)(2,1)S(1)}, u32[]{:S(2)}) copy-start(bf16[2,392,768]{2,1,0:T(8,128)(2,1)S(1)} %get-tuple-element.137.refs_5_.refs_1_) | copy-start | bytes 3612676
  92.1 27.3 %copy-start.55 = (bf16[2,392,768]{2,1,0:T(8,128)(2,1)}, bf16[2,392,768]{2,1,0:T(8,128)(2,1)S(1)}, u32[]{:S(2)}) copy-start(bf16[2,392,768]{2,1,0:T(8,128)(2,1)S(1)} %get-tuple-element.138.refs_6_.refs_2_) | copy-start | bytes 3612676
  92.2 27.3 %copy-start.4 = (bf16[2,768,768]{2,1,0:T(8,128)(2,1)S(1)}, bf16[2,768,768]{2,1,0:T(8,128)(2,1)}, u32[]{:S(2)}) copy-start(bf16[2,768,768]{2,1,0:T(8,128)(2,1)} %refs_13_.7) | copy-start | bytes 7077892
  118.9 32.0 %collective-permute-start.8 = (f32[8,96,768]{2,1,0:T(8,128)}, f32[8,96,768]{2,1,0:T(8,128)S(1)}, u32[]{:S(2)}, u32[]{:S(2)}) collective-permute-start(f32[8,96,768]{2,1,0:T(8,128)} %get-tuple-element.147.refs_11_), channel_id=1, source_target_pairs={{0,1},{1,0},{2,3},{3,2},{4,5},{5,4},{6,7},{7,6},{8,9},{9,8},{10,11... | collective-permute-start | bytes 7077896 | tf_op jit(solution)/shard_map/ppermute | solution.py:1091
  118.9 40.0 %collective-permute-start.10 = (f32[8,96,768]{2,1,0:T(8,128)}, f32[8,96,768]{2,1,0:T(8,128)}, u32[]{:S(2)}, u32[]{:S(2)}) collective-permute-start(f32[8,96,768]{2,1,0:T(8,128)} %get-tuple-element.156), channel_id=1, source_target_pairs={{0,1},{1,0},{2,3},{3,2},{4,5},{5,4},{6,7},{7,6},{8,9},{9,8},{10,11... | collective-permute-start | bytes 7077896 | tf_op jit(solution)/shard_map/ppermute | solution.py:1091
  150.3 16.6 %collective-permute-start.6 = (f32[8,96,384]{2,1,0:T(8,128)}, f32[8,96,384]{2,1,0:T(8,128)S(1)}, u32[]{:S(2)}, u32[]{:S(2)}) collective-permute-start(f32[8,96,384]{2,1,0:T(8,128)} %get-tuple-element.149), channel_id=1, source_target_pairs={{0,1},{1,0},{2,3},{3,2},{4,5},{5,4},{6,7},{7,6},{8,9},{9,8},{10,11... | collective-permute-start | bytes 3538952 | tf_op jit(solution)/shard_map/ppermute | solution.py:1091
  150.3 16.6 %collective-permute-start.7 = (f32[8,96,384]{2,1,0:T(8,128)}, f32[8,96,384]{2,1,0:T(8,128)}, u32[]{:S(2)}, u32[]{:S(2)}) collective-permute-start(f32[8,96,384]{2,1,0:T(8,128)} %get-tuple-element.150), channel_id=1, source_target_pairs={{0,1},{1,0},{2,3},{3,2},{4,5},{5,4},{6,7},{7,6},{8,9},{9,8},{10,11... | collective-permute-start | bytes 3538952 | tf_op jit(solution)/shard_map/ppermute | solution.py:1091
  163.0 28.4 %collective-permute-start.11 = (f32[4,96,768]{2,1,0:T(8,128)S(1)}, f32[4,96,768]{2,1,0:T(8,128)S(1)}, u32[]{:S(2)}, u32[]{:S(2)}) collective-permute-start(f32[4,96,768]{2,1,0:T(8,128)S(1)} %get-tuple-element.158), channel_id=1, source_target_pairs={{0,8},{4,12},{8,0},{12,4},{16,24},{20,28},{24,16},{28,20},{1,9},{5... | collective-permute-start | bytes 3538952 | tf_op jit(solution)/shard_map/ppermute | solution.py:989
  165.3 27.6 %collective-permute-start.9 = (f32[4,96,768]{2,1,0:T(8,128)S(1)}, f32[4,96,768]{2,1,0:T(8,128)S(1)}, u32[]{:S(2)}, u32[]{:S(2)}) collective-permute-start(f32[4,96,768]{2,1,0:T(8,128)S(1)} %get-tuple-element.154), channel_id=1, source_target_pairs={{0,4},{4,0},{8,12},{12,8},{16,20},{20,16},{24,28},{28,24},{1,5},{5... | collective-permute-start | bytes 3538952 | tf_op jit(solution)/shard_map/ppermute | solution.py:989
  193.8 20.5 %collective-permute-start.13 = (f32[8,96,768]{2,1,0:T(8,128)}, f32[8,96,768]{2,1,0:T(8,128)S(1)}, u32[]{:S(2)}, u32[]{:S(2)}) collective-permute-start(f32[8,96,768]{2,1,0:T(8,128)} %get-tuple-element.172), channel_id=1, source_target_pairs={{0,1},{1,0},{2,3},{3,2},{4,5},{5,4},{6,7},{7,6},{8,9},{9,8},{10,11... | collective-permute-start | bytes 7077896 | tf_op jit(solution)/shard_map/ppermute | solution.py:1091
  193.8 24.3 %collective-permute-start.17 = (f32[8,96,768]{2,1,0:T(8,128)}, f32[8,96,768]{2,1,0:T(8,128)S(1)}, u32[]{:S(2)}, u32[]{:S(2)}) collective-permute-start(f32[8,96,768]{2,1,0:T(8,128)} %get-tuple-element.180), channel_id=1, source_target_pairs={{0,1},{1,0},{2,3},{3,2},{4,5},{5,4},{6,7},{7,6},{8,9},{9,8},{10,11... | collective-permute-start | bytes 7077896 | tf_op jit(solution)/shard_map/ppermute | solution.py:1091
  194.3 16.2 %collective-permute-start.14 = (f32[2,96,768]{2,1,0:T(8,128)S(1)}, f32[2,96,768]{2,1,0:T(8,128)S(1)}, u32[]{:S(2)}, u32[]{:S(2)}) collective-permute-start(f32[2,96,768]{2,1,0:T(8,128)S(1)} %get-tuple-element.174), channel_id=1, source_target_pairs={{0,4},{4,0},{8,12},{12,8},{16,20},{20,16},{24,28},{28,24},{1,5},{5... | collective-permute-start | bytes 1769480 | tf_op jit(solution)/shard_map/ppermute | solution.py:989
  195.9 15.0 %collective-permute-start.15 = (f32[2,96,768]{2,1,0:T(8,128)S(1)}, f32[2,96,768]{2,1,0:T(8,128)S(1)}, u32[]{:S(2)}, u32[]{:S(2)}) collective-permute-start(f32[2,96,768]{2,1,0:T(8,128)S(1)} %get-tuple-element.175), channel_id=1, source_target_pairs={{0,8},{4,12},{8,0},{12,4},{16,24},{20,28},{24,16},{28,20},{1,9},{5... | collective-permute-start | bytes 1769480 | tf_op jit(solution)/shard_map/ppermute | solution.py:989
  196.5 17.8 %slice-start = ((s8[4816896]{0:T(1024)(128)(4,1)}), s8[4194304]{0:T(1024)(128)(4,1)S(1)}, s32[]{:S(2)}) async-start(s8[4816896]{0:T(1024)(128)(4,1)} %bitcast.30), calls=%async_computation | async-start | bytes 8388608
  196.5 17.8 %slice-start.1 = ((s8[4816896]{0:T(1024)(128)(4,1)}), s8[622592]{0:T(1024)(128)(4,1)S(1)}, s32[]{:S(2)}) async-start(s8[4816896]{0:T(1024)(128)(4,1)} %bitcast.30), calls=%async_computation.1 | async-start | bytes 1245184
  202.5 48.7 %collective-permute-start.19 = (f32[4,96,768]{2,1,0:T(8,128)}, f32[4,96,768]{2,1,0:T(8,128)S(1)}, u32[]{:S(2)}, u32[]{:S(2)}) collective-permute-start(f32[4,96,768]{2,1,0:T(8,128)} %get-tuple-element.183), channel_id=1, source_target_pairs={{0,4},{4,0},{8,12},{12,8},{16,20},{20,16},{24,28},{28,24},{1,5},{5... | collective-permute-start | bytes 3538952 | tf_op jit(solution)/shard_map/ppermute | solution.py:989
  203.2 14.9 %copy-start.43 = (f32[6,196,128]{2,1,0:T(8,128)}, f32[6,196,128]{2,1,0:T(8,128)S(1)}, u32[]{:S(2)}) copy-start(f32[6,196,128]{2,1,0:T(8,128)S(1)} %get-tuple-element.169.refs_5_.refs_2_) | copy-start | bytes 1806340
  211.6 39.6 %collective-permute-start.20 = (f32[2,96,768]{2,1,0:T(8,128)S(1)}, f32[2,96,768]{2,1,0:T(8,128)S(1)}, u32[]{:S(2)}, u32[]{:S(2)}) collective-permute-start(f32[2,96,768]{2,1,0:T(8,128)S(1)} %get-tuple-element.195), channel_id=1, source_target_pairs={{0,16},{4,20},{8,24},{12,28},{16,0},{20,4},{24,8},{28,12},{1,17},{... | collective-permute-start | bytes 1769480 | tf_op jit(solution)/shard_map/ppermute | solution.py:989
  222.1 38.1 %collective-permute-start.18 = (f32[4,96,768]{2,1,0:T(8,128)}, f32[4,96,768]{2,1,0:T(8,128)S(1)}, u32[]{:S(2)}, u32[]{:S(2)}) collective-permute-start(f32[4,96,768]{2,1,0:T(8,128)} %get-tuple-element.182), channel_id=1, source_target_pairs={{0,4},{4,0},{8,12},{12,8},{16,20},{20,16},{24,28},{28,24},{1,5},{5... | collective-permute-start | bytes 3538952 | tf_op jit(solution)/shard_map/ppermute | solution.py:989
  223.2 38.2 %collective-permute-start.16 = (f32[4,96,768]{2,1,0:T(8,128)S(1)}, f32[4,96,768]{2,1,0:T(8,128)S(1)}, u32[]{:S(2)}, u32[]{:S(2)}) collective-permute-start(f32[4,96,768]{2,1,0:T(8,128)S(1)} %get-tuple-element.178), channel_id=1, source_target_pairs={{0,8},{4,12},{8,0},{12,4},{16,24},{20,28},{24,16},{28,20},{1,9},{5... | collective-permute-start | bytes 3538952 | tf_op jit(solution)/shard_map/ppermute | solution.py:989
  262.8 7.9 %collective-permute-start.25 = (f32[8,96,384]{2,1,0:T(8,128)S(1)}, f32[8,96,384]{2,1,0:T(8,128)S(1)}, u32[]{:S(2)}, u32[]{:S(2)}) collective-permute-start(f32[8,96,384]{2,1,0:T(8,128)S(1)} %get-tuple-element.205), channel_id=1, source_target_pairs={{0,1},{1,0},{2,3},{3,2},{4,5},{5,4},{6,7},{7,6},{8,9},{9,8},{10,11... | collective-permute-start | bytes 3538952 | tf_op jit(solution)/shard_map/ppermute | solution.py:1091
  262.9 3.7 %collective-permute-start.12 = (f32[6,196,128]{2,1,0:T(8,128)S(1)}, f32[6,196,128]{2,1,0:T(8,128)S(1)}, u32[]{:S(2)}, u32[]{:S(2)}) collective-permute-start(f32[6,196,128]{2,1,0:T(8,128)S(1)} %get-tuple-element.170), channel_id=1, source_target_pairs={{0,1},{1,0},{2,3},{3,2},{4,5},{5,4},{6,7},{7,6},{8,9},{9,8},{10,11... | collective-permute-start | bytes 1806344 | tf_op jit(solution)/shard_map/ppermute | solution.py:1091
  263.4 20.1 %collective-permute-start.22 = (f32[8,96,384]{2,1,0:T(8,128)S(1)}, f32[8,96,384]{2,1,0:T(8,128)S(1)}, u32[]{:S(2)}, u32[]{:S(2)}) collective-permute-start(f32[8,96,384]{2,1,0:T(8,128)S(1)} %get-tuple-element.201), channel_id=1, source_target_pairs={{0,1},{1,0},{2,3},{3,2},{4,5},{5,4},{6,7},{7,6},{8,9},{9,8},{10,11... | collective-permute-start | bytes 3538952 | tf_op jit(solution)/shard_map/ppermute | solution.py:1091
  263.5 7.2 %collective-permute-start.26 = (f32[96,384]{1,0:T(8,128)S(1)}, f32[96,384]{1,0:T(8,128)S(1)}, u32[]{:S(2)}, u32[]{:S(2)}) collective-permute-start(f32[96,384]{1,0:T(8,128)S(1)} %get-tuple-element.206.refs_5_), channel_id=1, source_target_pairs={{0,1},{1,0},{2,3},{3,2},{4,5},{5,4},{6,7},{7,6},{8,9},{9,8},{10,11... | collective-permute-start | bytes 442376 | tf_op jit(solution)/shard_map/ppermute | solution.py:1091
  263.9 16.2 %collective-permute-start.23 = (f32[2,96,768]{2,1,0:T(8,128)S(1)}, f32[2,96,768]{2,1,0:T(8,128)S(1)}, u32[]{:S(2)}, u32[]{:S(2)}) collective-permute-start(f32[2,96,768]{2,1,0:T(8,128)S(1)} %get-tuple-element.203), channel_id=1, source_target_pairs={{0,8},{4,12},{8,0},{12,4},{16,24},{20,28},{24,16},{28,20},{1,9},{5... | collective-permute-start | bytes 1769480 | tf_op jit(solution)/shard_map/ppermute | solution.py:989
  266.6 16.2 %collective-permute-start.24 = (f32[2,96,768]{2,1,0:T(8,128)S(1)}, f32[2,96,768]{2,1,0:T(8,128)S(1)}, u32[]{:S(2)}, u32[]{:S(2)}) collective-permute-start(f32[2,96,768]{2,1,0:T(8,128)S(1)} %get-tuple-element.204), channel_id=1, source_target_pairs={{0,4},{4,0},{8,12},{12,8},{16,20},{20,16},{24,28},{28,24},{1,5},{5... | collective-permute-start | bytes 1769480 | tf_op jit(solution)/shard_map/ppermute | solution.py:989
  273.9 24.7 %collective-permute-start.29 = (f32[5,96,384]{2,1,0:T(8,128)S(1)}, f32[5,96,384]{2,1,0:T(8,128)S(1)}, u32[]{:S(2)}, u32[]{:S(2)}) collective-permute-start(f32[5,96,384]{2,1,0:T(8,128)S(1)} %get-tuple-element.213), channel_id=1, source_target_pairs={{0,4},{4,0},{8,12},{12,8},{16,20},{20,16},{24,28},{28,24},{1,5},{5... | collective-permute-start | bytes 2211848 | tf_op jit(solution)/shard_map/ppermute | solution.py:989
  274.6 24.3 %collective-permute-start.28 = (f32[2,96,768]{2,1,0:T(8,128)S(1)}, f32[2,96,768]{2,1,0:T(8,128)S(1)}, u32[]{:S(2)}, u32[]{:S(2)}) collective-permute-start(f32[2,96,768]{2,1,0:T(8,128)S(1)} %get-tuple-element.212), channel_id=1, source_target_pairs={{0,8},{4,12},{8,0},{12,4},{16,24},{20,28},{24,16},{28,20},{1,9},{5... | collective-permute-start | bytes 1769480 | tf_op jit(solution)/shard_map/ppermute | solution.py:989
  286.0 24.4 %collective-permute-start.27 = (f32[4,96,384]{2,1,0:T(8,128)S(1)}, f32[4,96,384]{2,1,0:T(8,128)S(1)}, u32[]{:S(2)}, u32[]{:S(2)}) collective-permute-start(f32[4,96,384]{2,1,0:T(8,128)S(1)} %get-tuple-element.210), channel_id=1, source_target_pairs={{0,4},{4,0},{8,12},{12,8},{16,20},{20,16},{24,28},{28,24},{1,5},{5... | collective-permute-start | bytes 1769480 | tf_op jit(solution)/shard_map/ppermute | solution.py:989
  287.5 27.9 %collective-permute-start.32 = (f32[2,96,768]{2,1,0:T(8,128)S(1)}, f32[2,96,768]{2,1,0:T(8,128)S(1)}, u32[]{:S(2)}, u32[]{:S(2)}) collective-permute-start(f32[2,96,768]{2,1,0:T(8,128)S(1)} %get-tuple-element.219), channel_id=1, source_target_pairs={{0,16},{4,20},{8,24},{12,28},{16,0},{20,4},{24,8},{28,12},{1,17},{... | collective-permute-start | bytes 1769480 | tf_op jit(solution)/shard_map/ppermute | solution.py:989
  298.8 28.6 %collective-permute-start.31 = (f32[3,96,384]{2,1,0:T(8,128)S(1)}, f32[3,96,384]{2,1,0:T(8,128)S(1)}, u32[]{:S(2)}, u32[]{:S(2)}) collective-permute-start(f32[3,96,384]{2,1,0:T(8,128)S(1)} %get-tuple-element.218), channel_id=1, source_target_pairs={{0,8},{4,12},{8,0},{12,4},{16,24},{20,28},{24,16},{28,20},{1,9},{5... | collective-permute-start | bytes 1327112 | tf_op jit(solution)/shard_map/ppermute | solution.py:989
  298.8 34.9 %collective-permute-start.21 = (f32[6,196,128]{2,1,0:T(8,128)S(1)}, f32[6,196,128]{2,1,0:T(8,128)S(1)}, u32[]{:S(2)}, u32[]{:S(2)}) collective-permute-start(f32[6,196,128]{2,1,0:T(8,128)S(1)} %get-tuple-element.199), channel_id=1, source_target_pairs={{0,1},{1,0},{2,3},{3,2},{4,5},{5,4},{6,7},{7,6},{8,9},{9,8},{10,11... | collective-permute-start | bytes 1806344 | tf_op jit(solution)/shard_map/ppermute | solution.py:1091
  299.7 28.4 %copy-start.48 = (f32[1,96,768]{2,1,0:T(8,128)}, f32[1,96,768]{2,1,0:T(8,128)S(1)}, u32[]{:S(2)}) copy-start(f32[1,96,768]{2,1,0:T(8,128)S(1)} %get-tuple-element.215.refs_5_.refs_8_) | copy-start | bytes 884740
  310.6 21.6 %collective-permute-start.30 = (f32[2,96,384]{2,1,0:T(8,128)S(1)}, f32[2,96,384]{2,1,0:T(8,128)S(1)}, u32[]{:S(2)}, u32[]{:S(2)}) collective-permute-start(f32[2,96,384]{2,1,0:T(8,128)S(1)} %get-tuple-element.217), channel_id=1, source_target_pairs={{0,8},{4,12},{8,0},{12,4},{16,24},{20,28},{24,16},{28,20},{1,9},{5... | collective-permute-start | bytes 884744 | tf_op jit(solution)/shard_map/ppermute | solution.py:989
  310.6 26.3 %collective-permute-start.35 = (f32[1,96,768]{2,1,0:T(8,128)}, f32[1,96,768]{2,1,0:T(8,128)S(1)}, u32[]{:S(2)}, u32[]{:S(2)}) collective-permute-start(f32[1,96,768]{2,1,0:T(8,128)} %get-tuple-element.224), channel_id=1, source_target_pairs={{0,16},{4,20},{8,24},{12,28},{16,0},{20,4},{24,8},{28,12},{1,17},{... | collective-permute-start | bytes 884744 | tf_op jit(solution)/shard_map/ppermute | solution.py:989
  328.1 19.0 %collective-permute-start.33 = (f32[2,96,384]{2,1,0:T(8,128)}, f32[2,96,384]{2,1,0:T(8,128)}, u32[]{:S(2)}, u32[]{:S(2)}) collective-permute-start(f32[2,96,384]{2,1,0:T(8,128)} %get-tuple-element.222), channel_id=1, source_target_pairs={{0,16},{4,20},{8,24},{12,28},{16,0},{20,4},{24,8},{28,12},{1,17},{... | collective-permute-start | bytes 884744 | tf_op jit(solution)/shard_map/ppermute | solution.py:989
  333.5 13.0 %collective-permute-start.34 = (f32[1,96,384]{2,1,0:T(8,128)}, f32[1,96,384]{2,1,0:T(8,128)S(1)}, u32[]{:S(2)}, u32[]{:S(2)}) collective-permute-start(f32[1,96,384]{2,1,0:T(8,128)} %get-tuple-element.223), channel_id=1, source_target_pairs={{0,16},{4,20},{8,24},{12,28},{16,0},{20,4},{24,8},{28,12},{1,17},{... | collective-permute-start | bytes 442376 | tf_op jit(solution)/shard_map/ppermute | solution.py:989
  333.8 13.4 %copy-start.38 = (f32[2,96,768]{2,1,0:T(8,128)S(1)}, f32[2,96,768]{2,1,0:T(8,128)}, u32[]{:S(2)}) copy-start(f32[2,96,768]{2,1,0:T(8,128)} %copy-done.37) | copy-start | bytes 1769476
  (52 other events, 171.5 us)

commit v7 on v6

--- a/solution.py
+++ b/solution.py
@@ -512,20 +512,22 @@
                 dd_o[c, 0] = dd[:, MINE * w : MINE * (w + 1)]
 
     def step(n, _):
-        wait(cp_d(n))
-        grad_act = nt(dd[...], wdown[lanes_at(n, D), :])
-        da = (grad_act * gp[0, :, lanes_at(n, D)].astype(F32)).astype(BF16)
-
-        da_s[:, lanes_at(n, D)] = da
-
-        @pl.when(n // 2 == x_at[0])
+        wait(cp_d(2 * n))
+        wait(cp_d(2 * n + 1))
+        grad_act = nt(dd[...], wdown[lanes_at(n, 2 * D), :])
+        da = (grad_act * gp[0, :, lanes_at(n, 2 * D)].astype(F32)).astype(BF16)
+        da_s[:, lanes_at(n, 2 * D)] = da
+
+        @pl.when(n == x_at[0])
         def _():
-            da_o[0, :, lanes_at(n % 2, D)] = da
-
-        sv_o[pl.ds(4 + n, 1), :] += colsum(da.astype(F32))
+            da_o[0] = da
+
+        sums = colsum(da.astype(F32))
+        for k in range(2):
+            sv_o[pl.ds(4 + 2 * n + k, 1), :] += sums[:, D * k : D * (k + 1)]
         return 0
 
-    lax.fori_loop(0, 4, step, 0)
+    lax.fori_loop(0, 2, step, 0)
     for n in range(4):
         wait(cp_u(n))
     dh2 = nt(da_s[...], wup[...])

time: 358 us -> 357 us (level)
  no operation moved by 1% of the time
where the time goes in v7:
time: 357 us; the launch traced here: 353 us
  Pallas kernels  221 us (62%)
  waiting for transfers between devices  81.6 us (23%)
  starting transfers between devices  25.8 us (7%)
  local copies, waits for them, and re-layouts  22.3 us (6%)
    pallas_call x31, Pallas kernels, call(): pl.pallas_call(wrapped, grid_spec=pltpu.PrefetchScalarGridSpec(num_scalar...  221 us
    ppermute x19, waiting for transfers between devices, send(): self.kept, self.recv = (kept, lax.ppermute(out, axis, perm))  76.7 us
    unnamed x131, local copies, waits for them, and re-layouts  21 us
    ppermute x19, starting transfers between devices, send(): self.kept, self.recv = (kept, lax.ppermute(out, axis, perm))  17.7 us
    ppermute x17, starting transfers between devices, over(): return lax.ppermute(a, 'win', [(i, i ^ way) for i in range(4)])  8.03 us
  transfers between devices with their start and end apart: 36, of which 16 were waited for; matrix products, arithmetic and copies ran while one was open for 0% of the time, Pallas kernels for 54%

profile of v7, /device:TPU:0, one launch (start us, length us, event | category | flops | bytes accessed | tf_op | source)
XLA Modules:
  0.0 353.0 jit_solution(13219507322222760216)
XLA Ops:
  1.7 1.4 crop_rows.2
  3.6 2.6 collective-permute-start.1
  6.9 1.3 crop_rows.3
  8.3 2.0 collective-permute-start.5
  10.4 1.7 window_bias.1.refs_3_.refs_2_.refs_7_
  12.3 19.7 %forward_0.2 = (f32[2,392,768]{2,1,0:T(8,128)}, bf16[2,392,768]{2,1,0:T(8,128)(2,1)S(1)}, bf16[2,8,18,64,128]{4,3,2,1,0:T(8,128)(2,1)}, bf16[2,392,768]{2,1,0:T(...) custom-call(s32[1]{0:T(128)} %bitcast.1.refs_0_, ...), custom_call_target="tpu_custom_call" | custom-call | flops 9660000256 | tf_op jit(solution)/shard_map/forward_0/pallas_call | solution.py:178
  32.1 2.1 collective-permute-done.refs_1_
  34.2 1.3 copy-done.1
  35.5 19.0 %forward_0.3 = (f32[2,392,768]{2,1,0:T(8,128)}, bf16[2,392,768]{2,1,0:T(8,128)(2,1)S(1)}, bf16[2,8,18,64,128]{4,3,2,1,0:T(8,128)(2,1)}, bf16[2,392,768]{2,1,0:T(...) custom-call(s32[1]{0:T(128)} %bitcast.1.refs_0_, ...), custom_call_target="tpu_custom_call", output_to_operand_aliasing={{0}: (17, {}), {1}: (18, {}), {2}: (19, {}), {3}: (20, {}),... | custom-call | flops 9660000256 | tf_op jit(solution)/shard_map/forward_0/pallas_call | solution.py:178
  55.6 36.5 %forward_1.1 = (f32[2,392,768]{2,1,0:T(8,128)}, bf16[2,392,768]{2,1,0:T(8,128)(2,1)S(1)}, bf16[2,8,18,64,128]{4,3,2,1,0:T(8,128)(2,1)}, bf16[2,392,768]{2,1,0:T(...) custom-call(s32[1]{0:T(128)} %bitcast.refs_0_.refs_1_, ...), custom_call_target="tpu_custom_call" | custom-call | flops 16560000000 | tf_op jit(solution)/shard_map/forward_1/pallas_call | solution.py:178
  92.2 24.6 %mlp_back_1.1 = (bf16[2,2,392,192]{3,2,1,0:T(8,128)(2,1)S(1)}, bf16[2,392,1536]{2,1,0:T(8,128)(2,1)}, f32[2,392,768]{2,1,0:T(8,128)}, f32[8,768]{1,0:T(8,128)S(1...) custom-call(s32[1]{0:T(128)} %bitcast.1.refs_0_, s32[1]{0:T(128)} %bitcast.refs_0_.refs_1_, ...), custom_call_target="tpu_custom_call" | custom-call | flops 10119999488 | tf_op jit(solution)/shard_map/mlp_back_1/pallas_call | solution.py:178
  118.8 1.7 copy-done.27
  120.5 28.0 %attn_back_1.1 = (bf16[2,2,392,768]{3,2,1,0:T(8,128)(2,1)}, f32[4,768]{1,0:T(4,128)S(1)}, f32[4,8,256]{2,1,0:T(8,128)S(1)}, f32[2,49,8,768]{3,2,1,0:T(8,128)}, f...) custom-call(s32[1]{0:T(128)} %bitcast.1.refs_0_, s32[1]{0:T(128)} %bitcast.refs_0_.refs_1_, ...), custom_call_target="tpu_custom_call" | custom-call | flops 14259999744 | tf_op jit(solution)/shard_map/attn_back_1/pallas_call | solution.py:178
  150.3 2.4 copy-done
  154.5 3.7 %down_mine.2 = (f32[4,96,768]{2,1,0:T(8,128)S(1)}, f32[4,96,768]{2,1,0:T(8,128)S(1)}) custom-call(s32[4]{0:T(128)S(1)} %pad_add_fusion.refs_0_, bf16[2,2,392,192]{3,2,1,0:T(8,128)(2,1)S(1)} %copy-done.11, bf16[2,392,3072]{2,1,0:T(8,128)(2,1)S(1)} %copy-done, bf16[2,392,3072]{2,1,0:T(8,128)(2,1)S(1)} %copy-done, ...), custom_call_target="tpu_custom_call" | custom-call | flops 3174000128 | tf_op jit(solution)/shard_map/down_mine/pallas_call | solution.py:178
  158.3 4.1 %up_mine.2 = (f32[4,96,768]{2,1,0:T(8,128)S(1)}, f32[4,96,768]{2,1,0:T(8,128)S(1)}) custom-call(s32[4]{0:T(128)S(1)} %pad_add_fusion.refs_0_, bf16[2,392,768]{2,1,0:T(8,128)(2,1)S(1)} %copy-done.40, bf16[2,392,1536]{2,1,0:T(8,128)(2,1)S(1)} %copy-done.36, f32[8,96,768]{2,1,0:T(8,128)} %collective-permute-done.10.refs_3_, ...), custom_call_target="tpu_custom_call" | custom-call | flops 2622000128 | tf_op jit(solution)/shard_map/up_mine/pallas_call | solution.py:178
  162.4 2.2 collective-permute-start.11
  164.7 1.5 collective-permute-start.9
  166.3 24.0 %mlp_back_0.1 = (bf16[2,2,392,192]{3,2,1,0:T(8,128)(2,1)S(1)}, bf16[2,392,1536]{2,1,0:T(8,128)(2,1)}, f32[2,392,768]{2,1,0:T(8,128)}, f32[8,768]{1,0:T(8,128)S(1...) custom-call(s32[1]{0:T(128)} %bitcast.1.refs_0_, s32[1]{0:T(128)} %bitcast.refs_0_.refs_1_, ...), custom_call_target="tpu_custom_call" | custom-call | flops 10119999488 | tf_op jit(solution)/shard_map/mlp_back_0/pallas_call | solution.py:178
  190.8 1.5 collective-permute-done.9.refs_2_.refs_4_
  193.8 1.5 collective-permute-start.14
  195.9 6.0 %attn_mine.3 = (f32[4,96,768]{2,1,0:T(8,128)S(1)}, f32[4,96,768]{2,1,0:T(8,128)}) custom-call(s32[4]{0:T(128)S(1)} %pad_add_fusion.refs_0_, bf16[2,392,768]{2,1,0:T(8,128)(2,1)S(1)} %copy-done.54, bf16[2,392,768]{2,1,0:T(8,128)(2,1)S(1)} %copy-done.56, bf16[2,2,392,768]{3,2,1,0:T(8,128)(2,1)S(1)} %copy-done.50, ...), custom_call_target="tpu_custom_call" | custom-call | flops 3265999872 | tf_op jit(solution)/shard_map/attn_mine/pallas_call | solution.py:178
  202.6 7.3 %collective-permute-done.14.refs_3_ = f32[2,96,768]{2,1,0:T(8,128)S(1)} collective-permute-done((f32[2,96,768]{2,1,0:T(8,128)S(1)}, f32[2,96,768]{2,1,0:T(8,128)S(1)}, u32[]{:S(2)}, u32[]{:S(2)}) %collective-permute-start.14) | collective-permute-done | bytes 589856 | tf_op jit(solution)/shard_map/ppermute | solution.py:991
  211.0 2.7 collective-permute-start.20
  213.7 3.8 %down_mine.3 = (f32[4,96,768]{2,1,0:T(8,128)S(1)}, f32[4,96,768]{2,1,0:T(8,128)S(1)}) custom-call(s32[4]{0:T(128)S(1)} %pad_add_fusion.refs_0_, bf16[2,2,392,192]{3,2,1,0:T(8,128)(2,1)S(1)} %get-tuple-element.171.refs_1_, bf16[2,392,3072]{2,1,0:T(8,128)(2,1)S(1)} %bitcast.31, bf16[2,392,3072]{2,1,0:T(8,128)(2,1)S(1)} %bitcast.31, ...), custom_call_target="tpu_custom_call" | custom-call | flops 3174000128 | tf_op jit(solution)/shard_map/down_mine/pallas_call | solution.py:178
  217.6 3.8 %up_mine.3 = (f32[4,96,768]{2,1,0:T(8,128)S(1)}, f32[4,96,768]{2,1,0:T(8,128)}) custom-call(s32[4]{0:T(128)S(1)} %pad_add_fusion.refs_0_, bf16[2,392,768]{2,1,0:T(8,128)(2,1)S(1)} %copy-done.3, bf16[2,392,1536]{2,1,0:T(8,128)(2,1)S(1)} %copy-done.26, f32[8,96,768]{2,1,0:T(8,128)S(1)} %collective-permute-done.17.refs_3_, ...), custom_call_target="tpu_custom_call" | custom-call | flops 2622000128 | tf_op jit(solution)/shard_map/up_mine/pallas_call | solution.py:178
  223.1 27.6 %attn_back_0.1 = (bf16[2,2,392,768]{3,2,1,0:T(8,128)(2,1)}, f32[4,768]{1,0:T(4,128)S(1)}, f32[96,384]{1,0:T(8,128)S(1)}, f32[2,49,8,768]{3,2,1,0:T(8,128)}, f32[...) custom-call(s32[1]{0:T(128)} %bitcast.1.refs_0_, s32[1]{0:T(128)} %bitcast.refs_0_.refs_1_, ...), custom_call_target="tpu_custom_call" | custom-call | flops 14259999744 | tf_op jit(solution)/shard_map/attn_back_0/pallas_call | solution.py:178
  250.7 8.9 %collective-permute-done.18.refs_6_.refs_8_ = f32[4,96,768]{2,1,0:T(8,128)S(1)} collective-permute-done((f32[4,96,768]{2,1,0:T(8,128)}, f32[4,96,768]{2,1,0:T(8,128)S(1)}, u32[]{:S(2)}, u32[]{:S(2)}) %collective-permute-start.18) | collective-permute-done | bytes 1179680 | tf_op jit(solution)/shard_map/ppermute | solution.py:991
  259.6 1.2 collective-permute-done.16.refs_2_.refs_4_
  263.1 2.7 collective-permute-done.12.refs_3_
  265.8 1.4 collective-permute-start.24
  267.2 1.3 token_major.1.refs_2_
  269.9 1.5 copy-done.34
  271.4 1.6 attn_mine.4
  273.7 5.5 %collective-permute-done.23.refs_3_ = f32[2,96,768]{2,1,0:T(8,128)S(1)} collective-permute-done((f32[2,96,768]{2,1,0:T(8,128)S(1)}, f32[2,96,768]{2,1,0:T(8,128)S(1)}, u32[]{:S(2)}, u32[]{:S(2)}) %collective-permute-start.23) | collective-permute-done | bytes 589856 | tf_op jit(solution)/shard_map/ppermute | solution.py:991
  279.2 2.7 collective-permute-done.24.refs_4_
  282.7 2.5 attn_mine.5
  285.2 1.5 collective-permute-start.27
  286.6 1.5 collective-permute-start.32
  288.1 9.6 %collective-permute-done.29.refs_2_.refs_4_ = f32[5,96,384]{2,1,0:T(8,128)S(1)} collective-permute-done((f32[5,96,384]{2,1,0:T(8,128)S(1)}, f32[5,96,384]{2,1,0:T(8,128)S(1)}, u32[]{:S(2)}, u32[]{:S(2)}) %collective-permute-start.29) | collective-permute-done | bytes 737312 | tf_op jit(solution)/shard_map/ppermute | solution.py:991
  298.8 10.7 %collective-permute-done.27.refs_2_.refs_4_ = f32[4,96,384]{2,1,0:T(8,128)S(1)} collective-permute-done((f32[4,96,384]{2,1,0:T(8,128)S(1)}, f32[4,96,384]{2,1,0:T(8,128)S(1)}, u32[]{:S(2)}, u32[]{:S(2)}) %collective-permute-start.27) | collective-permute-done | bytes 589856 | tf_op jit(solution)/shard_map/ppermute | solution.py:991
  309.8 1.8 collective-permute-start.35
  311.6 3.0 collective-permute-done.32.refs_6_.refs_1_
  314.6 11.9 %collective-permute-done.31.refs_2_.refs_4_ = f32[3,96,384]{2,1,0:T(8,128)S(1)} collective-permute-done((f32[3,96,384]{2,1,0:T(8,128)S(1)}, f32[3,96,384]{2,1,0:T(8,128)S(1)}, u32[]{:S(2)}, u32[]{:S(2)}) %collective-permute-start.31) | collective-permute-done | bytes 442400 | tf_op jit(solution)/shard_map/ppermute | solution.py:991
  327.2 4.0 %collective-permute-done.30.refs_2_.refs_4_ = f32[2,96,384]{2,1,0:T(8,128)S(1)} collective-permute-done((f32[2,96,384]{2,1,0:T(8,128)S(1)}, f32[2,96,384]{2,1,0:T(8,128)S(1)}, u32[]{:S(2)}, u32[]{:S(2)}) %collective-permute-start.30) | collective-permute-done | bytes 294944 | tf_op jit(solution)/shard_map/ppermute | solution.py:991
  336.1 9.5 %collective-permute-done.34.refs_7_ = f32[1,96,384]{2,1,0:T(8,128)S(1)} collective-permute-done((f32[1,96,384]{2,1,0:T(8,128)}, f32[1,96,384]{2,1,0:T(8,128)S(1)}, u32[]{:S(2)}, u32[]{:S(2)}) %collective-permute-start.34) | collective-permute-done | bytes 147488 | tf_op jit(solution)/shard_map/ppermute | solution.py:991
  347.2 1.3 copy-done.32
  348.5 2.3 last_sums.1
  (201 shorter events, 30.1 us)
Async XLA Ops:
  3.2 9.0 %collective-permute-start.2 = (f32[6,196,128]{2,1,0:T(8,128)}, f32[6,196,128]{2,1,0:T(8,128)}, u32[]{:S(2)}, u32[]{:S(2)}) collective-permute-start(f32[6,196,128]{2,1,0:T(8,128)} %get-tuple-element.124), channel_id=1, source_target_pairs={{0,1},{1,0},{2,3},{3,2},{4,5},{5,4},{6,7},{7,6},{8,9},{9,8},{10,11... | collective-permute-start | bytes 1806344 | tf_op jit(solution)/shard_map/ppermute | solution.py:1093
  3.6 30.6 %collective-permute-start.1 = (f32[6,196,128]{2,1,0:T(8,128)}, f32[6,196,128]{2,1,0:T(8,128)S(1)}, u32[]{:S(2)}, u32[]{:S(2)}) collective-permute-start(f32[6,196,128]{2,1,0:T(8,128)} %get-tuple-element.124), channel_id=1, source_target_pairs={{0,3},{1,2},{2,1},{3,0},{4,7},{5,6},{6,5},{7,4},{8,11},{9,10},{10,... | collective-permute-start | bytes 1806344 | tf_op jit(solution)/shard_map/ppermute | solution.py:1093
  6.2 28.0 %collective-permute-start = (f32[6,196,128]{2,1,0:T(8,128)}, f32[6,196,128]{2,1,0:T(8,128)S(1)}, u32[]{:S(2)}, u32[]{:S(2)}) collective-permute-start(f32[6,196,128]{2,1,0:T(8,128)} %get-tuple-element.123.refs_3_.refs_1_), channel_id=1, source_target_pairs={{0,2},{1,3},{2,0},{3,1},{4,6},{5,7},{6,4},{7,5},{8,10},{9,11},{10,... | collective-permute-start | bytes 1806344 | tf_op jit(solution)/shard_map/ppermute | solution.py:1093
  8.1 84.0 %collective-permute-start.3 = (f32[6,196,128]{2,1,0:T(8,128)}, f32[6,196,128]{2,1,0:T(8,128)S(1)}, u32[]{:S(2)}, u32[]{:S(2)}) collective-permute-start(f32[6,196,128]{2,1,0:T(8,128)} %get-tuple-element.139), channel_id=1, source_target_pairs={{0,1},{1,0},{2,3},{3,2},{4,5},{5,4},{6,7},{7,6},{8,9},{9,8},{10,11... | collective-permute-start | bytes 1806344 | tf_op jit(solution)/shard_map/ppermute | solution.py:1093
  8.3 83.9 %collective-permute-start.5 = (f32[6,196,128]{2,1,0:T(8,128)}, f32[6,196,128]{2,1,0:T(8,128)S(1)}, u32[]{:S(2)}, u32[]{:S(2)}) collective-permute-start(f32[6,196,128]{2,1,0:T(8,128)} %get-tuple-element.139), channel_id=1, source_target_pairs={{0,3},{1,2},{2,1},{3,0},{4,7},{5,6},{6,5},{7,4},{8,11},{9,10},{10,... | collective-permute-start | bytes 1806344 | tf_op jit(solution)/shard_map/ppermute | solution.py:1093
  12.1 106.7 %copy-start.12 = (f32[12,56,256]{2,1,0:T(8,128)}, f32[12,56,256]{2,1,0:T(8,128)S(1)}, u32[]{:S(2)}) copy-start(f32[12,56,256]{2,1,0:T(8,128)S(1)} %window_bias.1.refs_3_.refs_2_.refs_7_) | copy-start | bytes 2064388
  12.2 80.0 %collective-permute-start.4 = (f32[6,196,128]{2,1,0:T(8,128)S(1)}, f32[6,196,128]{2,1,0:T(8,128)S(1)}, u32[]{:S(2)}, u32[]{:S(2)}) collective-permute-start(f32[6,196,128]{2,1,0:T(8,128)S(1)} %get-tuple-element.125.refs_17_.refs_2_), channel_id=1, source_target_pairs={{0,2},{1,3},{2,0},{3,1},{4,6},{5,7},{6,4},{7,5},{8,10},{9,11},{10,... | collective-permute-start | bytes 1806344 | tf_op jit(solution)/shard_map/ppermute | solution.py:1093
  55.6 36.5 %copy-start.6 = (bf16[2,392,768]{2,1,0:T(8,128)(2,1)}, bf16[2,392,768]{2,1,0:T(8,128)(2,1)S(1)}, u32[]{:S(2)}) copy-start(bf16[2,392,768]{2,1,0:T(8,128)(2,1)S(1)} %get-tuple-element.187.refs_5_.refs_1_) | copy-start | bytes 3612676
  55.6 36.5 %copy-start.8 = (bf16[2,392,768]{2,1,0:T(8,128)(2,1)}, bf16[2,392,768]{2,1,0:T(8,128)(2,1)S(1)}, u32[]{:S(2)}) copy-start(bf16[2,392,768]{2,1,0:T(8,128)(2,1)S(1)} %get-tuple-element.188.refs_6_.refs_2_) | copy-start | bytes 3612676
  92.1 24.7 %copy-start.39 = (bf16[2,392,768]{2,1,0:T(8,128)(2,1)}, bf16[2,392,768]{2,1,0:T(8,128)(2,1)S(1)}, u32[]{:S(2)}) copy-start(bf16[2,392,768]{2,1,0:T(8,128)(2,1)S(1)} %get-tuple-element.143.refs_9_.refs_1_) | copy-start | bytes 3612676
  92.1 26.7 %copy-start.53 = (bf16[2,392,768]{2,1,0:T(8,128)(2,1)}, bf16[2,392,768]{2,1,0:T(8,128)(2,1)S(1)}, u32[]{:S(2)}) copy-start(bf16[2,392,768]{2,1,0:T(8,128)(2,1)S(1)} %get-tuple-element.137.refs_5_.refs_1_) | copy-start | bytes 3612676
  92.1 26.7 %copy-start.55 = (bf16[2,392,768]{2,1,0:T(8,128)(2,1)}, bf16[2,392,768]{2,1,0:T(8,128)(2,1)S(1)}, u32[]{:S(2)}) copy-start(bf16[2,392,768]{2,1,0:T(8,128)(2,1)S(1)} %get-tuple-element.138.refs_6_.refs_2_) | copy-start | bytes 3612676
  92.2 26.7 %copy-start.4 = (bf16[2,768,768]{2,1,0:T(8,128)(2,1)S(1)}, bf16[2,768,768]{2,1,0:T(8,128)(2,1)}, u32[]{:S(2)}) copy-start(bf16[2,768,768]{2,1,0:T(8,128)(2,1)} %refs_13_.7) | copy-start | bytes 7077892
  118.3 32.0 %collective-permute-start.8 = (f32[8,96,768]{2,1,0:T(8,128)}, f32[8,96,768]{2,1,0:T(8,128)S(1)}, u32[]{:S(2)}, u32[]{:S(2)}) collective-permute-start(f32[8,96,768]{2,1,0:T(8,128)} %get-tuple-element.147.refs_11_), channel_id=1, source_target_pairs={{0,1},{1,0},{2,3},{3,2},{4,5},{5,4},{6,7},{7,6},{8,9},{9,8},{10,11... | collective-permute-start | bytes 7077896 | tf_op jit(solution)/shard_map/ppermute | solution.py:1093
  118.3 40.0 %collective-permute-start.10 = (f32[8,96,768]{2,1,0:T(8,128)}, f32[8,96,768]{2,1,0:T(8,128)}, u32[]{:S(2)}, u32[]{:S(2)}) collective-permute-start(f32[8,96,768]{2,1,0:T(8,128)} %get-tuple-element.156), channel_id=1, source_target_pairs={{0,1},{1,0},{2,3},{3,2},{4,5},{5,4},{6,7},{7,6},{8,9},{9,8},{10,11... | collective-permute-start | bytes 7077896 | tf_op jit(solution)/shard_map/ppermute | solution.py:1093
  149.7 16.6 %collective-permute-start.6 = (f32[8,96,384]{2,1,0:T(8,128)}, f32[8,96,384]{2,1,0:T(8,128)S(1)}, u32[]{:S(2)}, u32[]{:S(2)}) collective-permute-start(f32[8,96,384]{2,1,0:T(8,128)} %get-tuple-element.149), channel_id=1, source_target_pairs={{0,1},{1,0},{2,3},{3,2},{4,5},{5,4},{6,7},{7,6},{8,9},{9,8},{10,11... | collective-permute-start | bytes 3538952 | tf_op jit(solution)/shard_map/ppermute | solution.py:1093
  149.7 16.6 %collective-permute-start.7 = (f32[8,96,384]{2,1,0:T(8,128)}, f32[8,96,384]{2,1,0:T(8,128)}, u32[]{:S(2)}, u32[]{:S(2)}) collective-permute-start(f32[8,96,384]{2,1,0:T(8,128)} %get-tuple-element.150), channel_id=1, source_target_pairs={{0,1},{1,0},{2,3},{3,2},{4,5},{5,4},{6,7},{7,6},{8,9},{9,8},{10,11... | collective-permute-start | bytes 3538952 | tf_op jit(solution)/shard_map/ppermute | solution.py:1093
  162.4 28.4 %collective-permute-start.11 = (f32[4,96,768]{2,1,0:T(8,128)S(1)}, f32[4,96,768]{2,1,0:T(8,128)S(1)}, u32[]{:S(2)}, u32[]{:S(2)}) collective-permute-start(f32[4,96,768]{2,1,0:T(8,128)S(1)} %get-tuple-element.158), channel_id=1, source_target_pairs={{0,8},{4,12},{8,0},{12,4},{16,24},{20,28},{24,16},{28,20},{1,9},{5... | collective-permute-start | bytes 3538952 | tf_op jit(solution)/shard_map/ppermute | solution.py:991
  164.7 27.6 %collective-permute-start.9 = (f32[4,96,768]{2,1,0:T(8,128)S(1)}, f32[4,96,768]{2,1,0:T(8,128)S(1)}, u32[]{:S(2)}, u32[]{:S(2)}) collective-permute-start(f32[4,96,768]{2,1,0:T(8,128)S(1)} %get-tuple-element.154), channel_id=1, source_target_pairs={{0,4},{4,0},{8,12},{12,8},{16,20},{20,16},{24,28},{28,24},{1,5},{5... | collective-permute-start | bytes 3538952 | tf_op jit(solution)/shard_map/ppermute | solution.py:991
  193.2 20.5 %collective-permute-start.13 = (f32[8,96,768]{2,1,0:T(8,128)}, f32[8,96,768]{2,1,0:T(8,128)S(1)}, u32[]{:S(2)}, u32[]{:S(2)}) collective-permute-start(f32[8,96,768]{2,1,0:T(8,128)} %get-tuple-element.172), channel_id=1, source_target_pairs={{0,1},{1,0},{2,3},{3,2},{4,5},{5,4},{6,7},{7,6},{8,9},{9,8},{10,11... | collective-permute-start | bytes 7077896 | tf_op jit(solution)/shard_map/ppermute | solution.py:1093
  193.3 24.3 %collective-permute-start.17 = (f32[8,96,768]{2,1,0:T(8,128)}, f32[8,96,768]{2,1,0:T(8,128)S(1)}, u32[]{:S(2)}, u32[]{:S(2)}) collective-permute-start(f32[8,96,768]{2,1,0:T(8,128)} %get-tuple-element.180), channel_id=1, source_target_pairs={{0,1},{1,0},{2,3},{3,2},{4,5},{5,4},{6,7},{7,6},{8,9},{9,8},{10,11... | collective-permute-start | bytes 7077896 | tf_op jit(solution)/shard_map/ppermute | solution.py:1093
  193.8 16.2 %collective-permute-start.14 = (f32[2,96,768]{2,1,0:T(8,128)S(1)}, f32[2,96,768]{2,1,0:T(8,128)S(1)}, u32[]{:S(2)}, u32[]{:S(2)}) collective-permute-start(f32[2,96,768]{2,1,0:T(8,128)S(1)} %get-tuple-element.174), channel_id=1, source_target_pairs={{0,4},{4,0},{8,12},{12,8},{16,20},{20,16},{24,28},{28,24},{1,5},{5... | collective-permute-start | bytes 1769480 | tf_op jit(solution)/shard_map/ppermute | solution.py:991
  195.3 15.0 %collective-permute-start.15 = (f32[2,96,768]{2,1,0:T(8,128)S(1)}, f32[2,96,768]{2,1,0:T(8,128)S(1)}, u32[]{:S(2)}, u32[]{:S(2)}) collective-permute-start(f32[2,96,768]{2,1,0:T(8,128)S(1)} %get-tuple-element.175), channel_id=1, source_target_pairs={{0,8},{4,12},{8,0},{12,4},{16,24},{20,28},{24,16},{28,20},{1,9},{5... | collective-permute-start | bytes 1769480 | tf_op jit(solution)/shard_map/ppermute | solution.py:991
  195.9 17.8 %slice-start = ((s8[4816896]{0:T(1024)(128)(4,1)}), s8[4194304]{0:T(1024)(128)(4,1)S(1)}, s32[]{:S(2)}) async-start(s8[4816896]{0:T(1024)(128)(4,1)} %bitcast.30), calls=%async_computation | async-start | bytes 8388608
  195.9 17.8 %slice-start.1 = ((s8[4816896]{0:T(1024)(128)(4,1)}), s8[622592]{0:T(1024)(128)(4,1)S(1)}, s32[]{:S(2)}) async-start(s8[4816896]{0:T(1024)(128)(4,1)} %bitcast.30), calls=%async_computation.1 | async-start | bytes 1245184
  201.9 48.8 %collective-permute-start.19 = (f32[4,96,768]{2,1,0:T(8,128)}, f32[4,96,768]{2,1,0:T(8,128)S(1)}, u32[]{:S(2)}, u32[]{:S(2)}) collective-permute-start(f32[4,96,768]{2,1,0:T(8,128)} %get-tuple-element.183), channel_id=1, source_target_pairs={{0,4},{4,0},{8,12},{12,8},{16,20},{20,16},{24,28},{28,24},{1,5},{5... | collective-permute-start | bytes 3538952 | tf_op jit(solution)/shard_map/ppermute | solution.py:991
  202.6 14.9 %copy-start.43 = (f32[6,196,128]{2,1,0:T(8,128)}, f32[6,196,128]{2,1,0:T(8,128)S(1)}, u32[]{:S(2)}) copy-start(f32[6,196,128]{2,1,0:T(8,128)S(1)} %get-tuple-element.169.refs_5_.refs_2_) | copy-start | bytes 1806340
  211.0 39.7 %collective-permute-start.20 = (f32[2,96,768]{2,1,0:T(8,128)S(1)}, f32[2,96,768]{2,1,0:T(8,128)S(1)}, u32[]{:S(2)}, u32[]{:S(2)}) collective-permute-start(f32[2,96,768]{2,1,0:T(8,128)S(1)} %get-tuple-element.195), channel_id=1, source_target_pairs={{0,16},{4,20},{8,24},{12,28},{16,0},{20,4},{24,8},{28,12},{1,17},{... | collective-permute-start | bytes 1769480 | tf_op jit(solution)/shard_map/ppermute | solution.py:991
  221.5 38.2 %collective-permute-start.18 = (f32[4,96,768]{2,1,0:T(8,128)}, f32[4,96,768]{2,1,0:T(8,128)S(1)}, u32[]{:S(2)}, u32[]{:S(2)}) collective-permute-start(f32[4,96,768]{2,1,0:T(8,128)} %get-tuple-element.182), channel_id=1, source_target_pairs={{0,4},{4,0},{8,12},{12,8},{16,20},{20,16},{24,28},{28,24},{1,5},{5... | collective-permute-start | bytes 3538952 | tf_op jit(solution)/shard_map/ppermute | solution.py:991
  222.6 38.2 %collective-permute-start.16 = (f32[4,96,768]{2,1,0:T(8,128)S(1)}, f32[4,96,768]{2,1,0:T(8,128)S(1)}, u32[]{:S(2)}, u32[]{:S(2)}) collective-permute-start(f32[4,96,768]{2,1,0:T(8,128)S(1)} %get-tuple-element.178), channel_id=1, source_target_pairs={{0,8},{4,12},{8,0},{12,4},{16,24},{20,28},{24,16},{28,20},{1,9},{5... | collective-permute-start | bytes 3538952 | tf_op jit(solution)/shard_map/ppermute | solution.py:991
  262.0 7.9 %collective-permute-start.25 = (f32[8,96,384]{2,1,0:T(8,128)S(1)}, f32[8,96,384]{2,1,0:T(8,128)S(1)}, u32[]{:S(2)}, u32[]{:S(2)}) collective-permute-start(f32[8,96,384]{2,1,0:T(8,128)S(1)} %get-tuple-element.205), channel_id=1, source_target_pairs={{0,1},{1,0},{2,3},{3,2},{4,5},{5,4},{6,7},{7,6},{8,9},{9,8},{10,11... | collective-permute-start | bytes 3538952 | tf_op jit(solution)/shard_map/ppermute | solution.py:1093
  262.0 3.7 %collective-permute-start.12 = (f32[6,196,128]{2,1,0:T(8,128)S(1)}, f32[6,196,128]{2,1,0:T(8,128)S(1)}, u32[]{:S(2)}, u32[]{:S(2)}) collective-permute-start(f32[6,196,128]{2,1,0:T(8,128)S(1)} %get-tuple-element.170), channel_id=1, source_target_pairs={{0,1},{1,0},{2,3},{3,2},{4,5},{5,4},{6,7},{7,6},{8,9},{9,8},{10,11... | collective-permute-start | bytes 1806344 | tf_op jit(solution)/shard_map/ppermute | solution.py:1093
  262.5 20.1 %collective-permute-start.22 = (f32[8,96,384]{2,1,0:T(8,128)S(1)}, f32[8,96,384]{2,1,0:T(8,128)S(1)}, u32[]{:S(2)}, u32[]{:S(2)}) collective-permute-start(f32[8,96,384]{2,1,0:T(8,128)S(1)} %get-tuple-element.201), channel_id=1, source_target_pairs={{0,1},{1,0},{2,3},{3,2},{4,5},{5,4},{6,7},{7,6},{8,9},{9,8},{10,11... | collective-permute-start | bytes 3538952 | tf_op jit(solution)/shard_map/ppermute | solution.py:1093
  262.6 7.2 %collective-permute-start.26 = (f32[96,384]{1,0:T(8,128)S(1)}, f32[96,384]{1,0:T(8,128)S(1)}, u32[]{:S(2)}, u32[]{:S(2)}) collective-permute-start(f32[96,384]{1,0:T(8,128)S(1)} %get-tuple-element.206.refs_5_), channel_id=1, source_target_pairs={{0,1},{1,0},{2,3},{3,2},{4,5},{5,4},{6,7},{7,6},{8,9},{9,8},{10,11... | collective-permute-start | bytes 442376 | tf_op jit(solution)/shard_map/ppermute | solution.py:1093
  263.1 16.2 %collective-permute-start.23 = (f32[2,96,768]{2,1,0:T(8,128)S(1)}, f32[2,96,768]{2,1,0:T(8,128)S(1)}, u32[]{:S(2)}, u32[]{:S(2)}) collective-permute-start(f32[2,96,768]{2,1,0:T(8,128)S(1)} %get-tuple-element.203), channel_id=1, source_target_pairs={{0,8},{4,12},{8,0},{12,4},{16,24},{20,28},{24,16},{28,20},{1,9},{5... | collective-permute-start | bytes 1769480 | tf_op jit(solution)/shard_map/ppermute | solution.py:991
  265.8 16.2 %collective-permute-start.24 = (f32[2,96,768]{2,1,0:T(8,128)S(1)}, f32[2,96,768]{2,1,0:T(8,128)S(1)}, u32[]{:S(2)}, u32[]{:S(2)}) collective-permute-start(f32[2,96,768]{2,1,0:T(8,128)S(1)} %get-tuple-element.204), channel_id=1, source_target_pairs={{0,4},{4,0},{8,12},{12,8},{16,20},{20,16},{24,28},{28,24},{1,5},{5... | collective-permute-start | bytes 1769480 | tf_op jit(solution)/shard_map/ppermute | solution.py:991
  273.0 24.7 %collective-permute-start.29 = (f32[5,96,384]{2,1,0:T(8,128)S(1)}, f32[5,96,384]{2,1,0:T(8,128)S(1)}, u32[]{:S(2)}, u32[]{:S(2)}) collective-permute-start(f32[5,96,384]{2,1,0:T(8,128)S(1)} %get-tuple-element.213), channel_id=1, source_target_pairs={{0,4},{4,0},{8,12},{12,8},{16,20},{20,16},{24,28},{28,24},{1,5},{5... | collective-permute-start | bytes 2211848 | tf_op jit(solution)/shard_map/ppermute | solution.py:991
  273.7 24.3 %collective-permute-start.28 = (f32[2,96,768]{2,1,0:T(8,128)S(1)}, f32[2,96,768]{2,1,0:T(8,128)S(1)}, u32[]{:S(2)}, u32[]{:S(2)}) collective-permute-start(f32[2,96,768]{2,1,0:T(8,128)S(1)} %get-tuple-element.212), channel_id=1, source_target_pairs={{0,8},{4,12},{8,0},{12,4},{16,24},{20,28},{24,16},{28,20},{1,9},{5... | collective-permute-start | bytes 1769480 | tf_op jit(solution)/shard_map/ppermute | solution.py:991
  285.2 24.4 %collective-permute-start.27 = (f32[4,96,384]{2,1,0:T(8,128)S(1)}, f32[4,96,384]{2,1,0:T(8,128)S(1)}, u32[]{:S(2)}, u32[]{:S(2)}) collective-permute-start(f32[4,96,384]{2,1,0:T(8,128)S(1)} %get-tuple-element.210), channel_id=1, source_target_pairs={{0,4},{4,0},{8,12},{12,8},{16,20},{20,16},{24,28},{28,24},{1,5},{5... | collective-permute-start | bytes 1769480 | tf_op jit(solution)/shard_map/ppermute | solution.py:991
  286.6 27.9 %collective-permute-start.32 = (f32[2,96,768]{2,1,0:T(8,128)S(1)}, f32[2,96,768]{2,1,0:T(8,128)S(1)}, u32[]{:S(2)}, u32[]{:S(2)}) collective-permute-start(f32[2,96,768]{2,1,0:T(8,128)S(1)} %get-tuple-element.219), channel_id=1, source_target_pairs={{0,16},{4,20},{8,24},{12,28},{16,0},{20,4},{24,8},{28,12},{1,17},{... | collective-permute-start | bytes 1769480 | tf_op jit(solution)/shard_map/ppermute | solution.py:991
  297.9 28.6 %collective-permute-start.31 = (f32[3,96,384]{2,1,0:T(8,128)S(1)}, f32[3,96,384]{2,1,0:T(8,128)S(1)}, u32[]{:S(2)}, u32[]{:S(2)}) collective-permute-start(f32[3,96,384]{2,1,0:T(8,128)S(1)} %get-tuple-element.218), channel_id=1, source_target_pairs={{0,8},{4,12},{8,0},{12,4},{16,24},{20,28},{24,16},{28,20},{1,9},{5... | collective-permute-start | bytes 1327112 | tf_op jit(solution)/shard_map/ppermute | solution.py:991
  298.0 34.9 %collective-permute-start.21 = (f32[6,196,128]{2,1,0:T(8,128)S(1)}, f32[6,196,128]{2,1,0:T(8,128)S(1)}, u32[]{:S(2)}, u32[]{:S(2)}) collective-permute-start(f32[6,196,128]{2,1,0:T(8,128)S(1)} %get-tuple-element.199), channel_id=1, source_target_pairs={{0,1},{1,0},{2,3},{3,2},{4,5},{5,4},{6,7},{7,6},{8,9},{9,8},{10,11... | collective-permute-start | bytes 1806344 | tf_op jit(solution)/shard_map/ppermute | solution.py:1093
  298.8 28.4 %copy-start.48 = (f32[1,96,768]{2,1,0:T(8,128)}, f32[1,96,768]{2,1,0:T(8,128)S(1)}, u32[]{:S(2)}) copy-start(f32[1,96,768]{2,1,0:T(8,128)S(1)} %get-tuple-element.215.refs_5_.refs_8_) | copy-start | bytes 884740
  309.7 21.6 %collective-permute-start.30 = (f32[2,96,384]{2,1,0:T(8,128)S(1)}, f32[2,96,384]{2,1,0:T(8,128)S(1)}, u32[]{:S(2)}, u32[]{:S(2)}) collective-permute-start(f32[2,96,384]{2,1,0:T(8,128)S(1)} %get-tuple-element.217), channel_id=1, source_target_pairs={{0,8},{4,12},{8,0},{12,4},{16,24},{20,28},{24,16},{28,20},{1,9},{5... | collective-permute-start | bytes 884744 | tf_op jit(solution)/shard_map/ppermute | solution.py:991
  309.8 26.3 %collective-permute-start.35 = (f32[1,96,768]{2,1,0:T(8,128)}, f32[1,96,768]{2,1,0:T(8,128)S(1)}, u32[]{:S(2)}, u32[]{:S(2)}) collective-permute-start(f32[1,96,768]{2,1,0:T(8,128)} %get-tuple-element.224), channel_id=1, source_target_pairs={{0,16},{4,20},{8,24},{12,28},{16,0},{20,4},{24,8},{28,12},{1,17},{... | collective-permute-start | bytes 884744 | tf_op jit(solution)/shard_map/ppermute | solution.py:991
  327.2 19.0 %collective-permute-start.33 = (f32[2,96,384]{2,1,0:T(8,128)}, f32[2,96,384]{2,1,0:T(8,128)}, u32[]{:S(2)}, u32[]{:S(2)}) collective-permute-start(f32[2,96,384]{2,1,0:T(8,128)} %get-tuple-element.222), channel_id=1, source_target_pairs={{0,16},{4,20},{8,24},{12,28},{16,0},{20,4},{24,8},{28,12},{1,17},{... | collective-permute-start | bytes 884744 | tf_op jit(solution)/shard_map/ppermute | solution.py:991
  332.6 13.0 %collective-permute-start.34 = (f32[1,96,384]{2,1,0:T(8,128)}, f32[1,96,384]{2,1,0:T(8,128)S(1)}, u32[]{:S(2)}, u32[]{:S(2)}) collective-permute-start(f32[1,96,384]{2,1,0:T(8,128)} %get-tuple-element.223), channel_id=1, source_target_pairs={{0,16},{4,20},{8,24},{12,28},{16,0},{20,4},{24,8},{28,12},{1,17},{... | collective-permute-start | bytes 442376 | tf_op jit(solution)/shard_map/ppermute | solution.py:991
  332.9 13.4 %copy-start.38 = (f32[2,96,768]{2,1,0:T(8,128)S(1)}, f32[2,96,768]{2,1,0:T(8,128)}, u32[]{:S(2)}) copy-start(f32[2,96,768]{2,1,0:T(8,128)} %copy-done.37) | copy-start | bytes 1769476
  (52 other events, 171.2 us)
